TPU v7x, 32 devices: a whole 2x2x4 slice. The times are simulated.
32 devices in a mesh: dp: 8 (over y, x, core), mp: 4 (over z).
Axes of the slice: x: 2, y: 2, z: 4, core: 2. Of those that a mesh axis runs over, the one named last changes fastest.
Arguments:
- inputs: bfloat16 [8, 1024, 1024], P('dp', 'mp'), may hold values from -6 to 6
- block_size: int32 [8], P('dp'), may hold values from 256 to 512, as said below
- gain_attn: float32 [1024], replicated, may hold values from 0.5 to 1.5
- qkv_weight: bfloat16 [1024, 3, 1024], P(None, None, 'mp'), may hold values from -0.1875 to 0.1875
- ssm_rate: float32 [1024, 16], P('mp'), may hold values from 0.001 to 0.1
- ssm_coef: float32 [1024, 16], P('mp'), may hold values from -0.15 to 0.15
- ssm_skip: float32 [1024], P('mp'), may hold values from -3 to 3
- out_weight: bfloat16 [1024, 1024], P('mp'), may hold values from -1.5 to 1.5
- gain_mlp: float32 [1024], replicated, may hold values from 0.5 to 1.5
- up_weight: bfloat16 [1024, 4096], P(None, 'mp'), may hold values from -0.1875 to 0.1875
- down_weight: bfloat16 [4096, 1024], P('mp'), may hold values from -0.09375 to 0.09375
- cotangent: bfloat16 [8, 1024, 1024], P('dp', 'mp'), may hold values from -6 to 6
Outputs:
- output: bfloat16 [8, 1024, 1024], P('dp', 'mp')
- input_grad: float32 [8, 1024, 1024], P('dp', 'mp')
- gain_attn_grad: float32 [1024], replicated
- qkv_weight_grad: float32 [1024, 3, 1024], P(None, None, 'mp')
- ssm_rate_grad: float32 [1024, 16], P('mp')
- ssm_coef_grad: float32 [1024, 16], P('mp')
- ssm_skip_grad: float32 [1024], P('mp')
- out_weight_grad: float32 [1024, 1024], P('mp')
- gain_mlp_grad: float32 [1024], replicated
- up_weight_grad: float32 [1024, 4096], P(None, 'mp')
- down_weight_grad: float32 [4096, 1024], P('mp')
Inputs may be any that keep to these rules, and one draw needn't show every extreme that they name: `block_size`: each row's attention blocks hold 256 or 512 tokens, and both lengths occur among the rows.
All inputs are finite; a program needn't handle non-finite values.
Results may differ from a plain program's by a relative error of at most 0.014.
Values may be sent and summed in bfloat16 or wider, within the bound.
No kernel may reach another device: no remote copies, remote signals or barrier semaphores. Data moves between devices by JAX's collectives and lax.ppermute only.
A program may use at most 192 MiB of HBM per device.

v0:
```python
from functools import partial
import math

import jax
import jax.numpy as jnp
from jax import lax
from jax.sharding import PartitionSpec as P

HD = 128
CTX = 128
BLOCK = 256
SSM_BLOCK = 128


epsilon = 1e-05
masked_score = -1e30
highest = lax.Precision.HIGHEST


def layer_norm(values, row_gain):
    row_mean = jnp.mean(values, axis=-1, keepdims=True)
    centred = values - row_mean
    spread = jnp.mean(centred * centred, axis=-1, keepdims=True)
    return centred * lax.rsqrt(spread + epsilon) * row_gain


def exact_gelu(values):
    return jax.nn.gelu(values, approximate=False)


def ssm_mix(signal, rates, coefs, skips):
    total_rows, channels = signal.shape
    blocks = total_rows // SSM_BLOCK
    rate_t = rates.T
    coef_t = coefs.T
    lag_steps = jnp.arange(SSM_BLOCK, dtype=jnp.float32)
    kernel = jnp.sum(coef_t * jnp.exp(-lag_steps[:, None, None] * rate_t), axis=1)
    offsets = (
        jnp.arange(SSM_BLOCK, dtype=jnp.int32)[:, None]
        - jnp.arange(SSM_BLOCK, dtype=jnp.int32)[None, :]
    )
    lag_ids = jnp.arange(SSM_BLOCK, dtype=jnp.int32)
    lag_table = (
        (offsets[:, :, None] == lag_ids[None, None, :])
        .astype(jnp.float32)
        .reshape(SSM_BLOCK * SSM_BLOCK, SSM_BLOCK)
    )
    toeplitz = jnp.dot(lag_table, kernel, precision=highest).reshape(SSM_BLOCK, SSM_BLOCK, channels)
    pieces = signal.reshape(blocks, SSM_BLOCK, channels)
    inside = jnp.einsum("ijc,bjc->bic", toeplitz, pieces, precision=highest)
    end_power = jnp.exp(-(SSM_BLOCK - 1.0 - lag_steps)[:, None, None] * rate_t)
    local_state = jnp.einsum("jnc,bjc->bnc", end_power, pieces, precision=highest)
    block_ids = jnp.arange(blocks, dtype=jnp.int32)
    block_gaps = block_ids[:, None] - block_ids[None, :] - 1
    earlier = (block_gaps >= 0)[:, :, None, None]
    gap_steps = (SSM_BLOCK * jnp.maximum(block_gaps, 0)).astype(jnp.float32)
    carried = jnp.where(earlier, jnp.exp(-gap_steps[:, :, None, None] * rate_t), 0.0)
    prior_state = jnp.einsum("abnc,bnc->anc", carried, local_state, precision=highest)
    in_power = coef_t * jnp.exp(-(lag_steps + 1.0)[:, None, None] * rate_t)
    outside = jnp.einsum("inc,bnc->bic", in_power, prior_state, precision=highest)
    return (inside + outside).reshape(total_rows, channels) + skips * signal


def key_mask(tile_start, block_len):
    tile_len = 2 * BLOCK
    query_pos = tile_start + jnp.arange(tile_len, dtype=jnp.int32)
    block_start = query_pos // block_len * block_len
    key_pos = jnp.concatenate(
        [
            tile_start - CTX + jnp.arange(CTX, dtype=jnp.int32),
            tile_start + BLOCK - CTX + jnp.arange(CTX, dtype=jnp.int32),
            tile_start + jnp.arange(tile_len, dtype=jnp.int32),
        ]
    )
    from_context = jnp.arange(2 * CTX + tile_len, dtype=jnp.int32) < 2 * CTX
    context_ok = (
        (key_pos[None] >= block_start[:, None] - CTX)
        & (key_pos[None] < block_start[:, None])
        & (key_pos[None] >= 0)
    )
    own_ok = (key_pos[None] >= block_start[:, None]) & (key_pos[None] <= query_pos[:, None])
    return jnp.where(from_context[None], context_ok, own_ok)


def tile_scores(tile_q, all_keys, tile_start, block_len):
    score_scale = 1.0 / math.sqrt(HD)
    scores = (
        jnp.einsum("ihd,jhd->hij", tile_q, all_keys, preferred_element_type=jnp.float32)
        * score_scale
    )
    return jnp.where(key_mask(tile_start, block_len)[None], scores, masked_score)


def tile_forward(tile_item, block_len):
    tile_q, tile_k, tile_v, first_ctx, second_ctx, tile_start = tile_item
    all_keys = jnp.concatenate([first_ctx, second_ctx, tile_k], axis=0)
    all_values = jnp.concatenate([first_ctx, second_ctx, tile_v], axis=0)
    scores = tile_scores(tile_q, all_keys, tile_start, block_len)
    row_max = jnp.max(scores, axis=-1, keepdims=True)
    weights = jnp.exp(scores - row_max)
    weight_total = jnp.sum(weights, axis=-1, keepdims=True)
    prob_rows = weights / weight_total
    mixed_out = jnp.einsum(
        "hij,jhd->ihd",
        prob_rows.astype(jnp.bfloat16),
        all_values,
        preferred_element_type=jnp.float32,
    )
    log_total = row_max[..., 0] + jnp.log(weight_total[..., 0])
    return (mixed_out.astype(jnp.bfloat16), log_total)


def tile_backward(tile_item, block_len):
    tile_q, tile_k, tile_v, first_ctx, second_ctx, tile_start, log_total, out_grad = tile_item
    score_scale = 1.0 / math.sqrt(HD)
    all_keys = jnp.concatenate([first_ctx, second_ctx, tile_k], axis=0)
    all_values = jnp.concatenate([first_ctx, second_ctx, tile_v], axis=0)
    scores = tile_scores(tile_q, all_keys, tile_start, block_len)
    prob_rows = jnp.exp(scores - log_total[..., None])
    prob_grad = jnp.einsum("ihd,jhd->hij", out_grad, all_values, preferred_element_type=jnp.float32)
    centre = jnp.sum(prob_rows * prob_grad, axis=-1, keepdims=True)
    score_grad = (prob_rows * (prob_grad - centre)).astype(jnp.bfloat16)
    query_grad = (
        jnp.einsum("hij,jhd->ihd", score_grad, all_keys, preferred_element_type=jnp.float32)
        * score_scale
    ).astype(jnp.bfloat16)
    key_grad = (
        jnp.einsum("hij,ihd->jhd", score_grad, tile_q, preferred_element_type=jnp.float32)
        * score_scale
    )
    value_grad = jnp.einsum(
        "hij,ihd->jhd", prob_rows.astype(jnp.bfloat16), out_grad, preferred_element_type=jnp.float32
    )
    ctx_grad = key_grad[: 2 * CTX] + value_grad[: 2 * CTX]
    return (
        query_grad,
        key_grad[2 * CTX :].astype(jnp.bfloat16),
        value_grad[2 * CTX :].astype(jnp.bfloat16),
        ctx_grad[:CTX],
        ctx_grad[CTX:],
    )


def per_device(
    inputs,
    block_size,
    gain_attn,
    qkv_weight,
    ssm_rate,
    ssm_coef,
    ssm_skip,
    out_weight,
    gain_mlp,
    up_weight,
    down_weight,
    cotangent,
):
    shard_in = inputs[0].astype(jnp.float32)
    block_len = block_size[0]
    shard_rows, model_dim = shard_in.shape
    channels = qkv_weight.shape[2]
    local_heads = channels // HD
    col_start = lax.axis_index("mp") * channels
    flat_qkv_weight = qkv_weight.reshape(model_dim, 3 * channels)
    normed_one, norm_one_pull = jax.vjp(layer_norm, shard_in, gain_attn)
    whole_one = lax.all_gather(normed_one.astype(jnp.bfloat16), "mp", axis=0, tiled=True)
    total_rows = whole_one.shape[0]
    tile_len = 2 * BLOCK
    tile_count = total_rows // tile_len
    qkv = jnp.dot(whole_one, flat_qkv_weight, preferred_element_type=jnp.float32)
    qkv = qkv.astype(jnp.bfloat16).reshape(total_rows, 3, local_heads, HD)
    queries = qkv[:, 0].reshape(tile_count, tile_len, local_heads, HD)
    key_rows = qkv[:, 1].reshape(tile_count, tile_len, local_heads, HD)
    value_rows = qkv[:, 2].reshape(tile_count, tile_len, local_heads, HD)
    signal = lax.dynamic_slice_in_dim(whole_one, col_start, channels, 1).astype(jnp.float32)
    mixed_full, ssm_pull = jax.vjp(ssm_mix, signal, ssm_rate, ssm_coef, ssm_skip)
    context = mixed_full.astype(jnp.bfloat16).reshape(total_rows, local_heads, HD)
    shifted = jnp.concatenate(
        [jnp.zeros((CTX, local_heads, HD), jnp.bfloat16), context[: total_rows - CTX]], axis=0
    )
    ctx_first = shifted.reshape(tile_count, tile_len, local_heads, HD)[:, :CTX]
    ctx_second = context.reshape(tile_count, tile_len, local_heads, HD)[:, BLOCK - CTX : BLOCK]
    starts = jnp.arange(tile_count, dtype=jnp.int32) * tile_len
    attended_tiles, log_totals = lax.map(
        partial(tile_forward, block_len=block_len),
        (queries, key_rows, value_rows, ctx_first, ctx_second, starts),
    )
    attended = attended_tiles.reshape(total_rows, channels)
    picked = attended
    middle = shard_in + lax.psum_scatter(
        jnp.dot(picked, out_weight, preferred_element_type=jnp.float32),
        "mp",
        scatter_dimension=0,
        tiled=True,
    )
    normed_two, norm_two_pull = jax.vjp(layer_norm, middle, gain_mlp)
    whole_two = lax.all_gather(normed_two.astype(jnp.bfloat16), "mp", axis=0, tiled=True)
    gate = jnp.dot(whole_two, up_weight, preferred_element_type=jnp.float32)
    activated_full, gelu_pull = jax.vjp(exact_gelu, gate)
    activated = activated_full.astype(jnp.bfloat16)
    picked = activated
    result = middle + lax.psum_scatter(
        jnp.dot(picked, down_weight, preferred_element_type=jnp.float32).astype(jnp.bfloat16),
        "mp",
        scatter_dimension=0,
        tiled=True,
    ).astype(jnp.float32)
    output = result.astype(jnp.bfloat16)[None]
    cot_rows = cotangent[0]
    cot_whole = lax.all_gather(cot_rows, "mp", axis=0, tiled=True)
    down_grad = jnp.einsum("tf,td->fd", activated, cot_whole, preferred_element_type=jnp.float32)
    activated_grad = jnp.einsum(
        "td,fd->tf", cot_whole, down_weight, preferred_element_type=jnp.float32
    )
    gate_grad = gelu_pull(activated_grad)[0].astype(jnp.bfloat16)
    up_grad = jnp.einsum("td,tf->df", whole_two, gate_grad, preferred_element_type=jnp.float32)
    picked = gate_grad
    normed_two_grad = lax.psum_scatter(
        jnp.einsum("tf,df->td", picked, up_weight, preferred_element_type=jnp.float32),
        "mp",
        scatter_dimension=0,
        tiled=True,
    )
    middle_norm_grad, gain_mlp_grad = norm_two_pull(normed_two_grad)
    middle_grad = cot_rows.astype(jnp.float32) + middle_norm_grad
    attn_back = lax.all_gather(middle_grad.astype(jnp.bfloat16), "mp", axis=0, tiled=True)
    out_grad = jnp.einsum("tc,td->cd", attended, attn_back, preferred_element_type=jnp.float32)
    attended_grad = jnp.einsum(
        "td,cd->tc", attn_back, out_weight, preferred_element_type=jnp.float32
    ).astype(jnp.bfloat16)
    query_grad, key_grad, value_grad, first_grad, second_grad = lax.map(
        partial(tile_backward, block_len=block_len),
        (
            queries,
            key_rows,
            value_rows,
            ctx_first,
            ctx_second,
            starts,
            log_totals,
            attended_grad.reshape(tile_count, tile_len, local_heads, HD),
        ),
    )
    qkv_grad = jnp.stack(
        [
            query_grad.reshape(total_rows, channels),
            key_grad.reshape(total_rows, channels),
            value_grad.reshape(total_rows, channels),
        ],
        axis=1,
    ).reshape(total_rows, 3 * channels)
    context_grad = jnp.zeros((tile_count, tile_len, local_heads, HD), jnp.float32)
    context_grad = context_grad.at[:, BLOCK - CTX : BLOCK].add(second_grad)
    context_grad = context_grad.at[:-1, tile_len - CTX :].add(first_grad[1:])
    signal_grad, rate_grad, coef_grad, skip_grad = ssm_pull(
        context_grad.reshape(total_rows, channels)
    )
    qkv_grad_weight = jnp.einsum(
        "td,tk->dk", whole_one, qkv_grad, preferred_element_type=jnp.float32
    ).reshape(model_dim, 3, channels)
    picked = qkv_grad
    product_rows = jnp.einsum(
        "tk,dk->td", picked, flat_qkv_weight, preferred_element_type=jnp.float32
    )
    current = lax.dynamic_slice_in_dim(product_rows, col_start, channels, 1)
    normed_one_grad = lax.psum_scatter(
        lax.dynamic_update_slice_in_dim(product_rows, current + signal_grad, col_start, 1).astype(
            jnp.bfloat16
        ),
        "mp",
        scatter_dimension=0,
        tiled=True,
    ).astype(jnp.float32)
    input_norm_grad, gain_attn_grad = norm_one_pull(normed_one_grad)
    input_grad = (middle_grad + input_norm_grad)[None]
    qkv_grad_weight, rate_grad, coef_grad, skip_grad, out_grad, up_grad, down_grad = lax.psum(
        (qkv_grad_weight, rate_grad, coef_grad, skip_grad, out_grad, up_grad, down_grad), "dp"
    )
    gain_attn_grad, gain_mlp_grad = lax.psum((gain_attn_grad, gain_mlp_grad), ("dp", "mp"))
    return (
        output,
        input_grad,
        gain_attn_grad,
        qkv_grad_weight,
        rate_grad,
        coef_grad,
        skip_grad,
        out_grad,
        gain_mlp_grad,
        up_grad,
        down_grad,
    )


def solution(mesh):
    return jax.shard_map(
        per_device,
        mesh=mesh,
        in_specs=(
            P("dp", "mp", None),
            P("dp"),
            P(),
            P(None, None, "mp"),
            P("mp", None),
            P("mp", None),
            P("mp"),
            P("mp", None),
            P(),
            P(None, "mp"),
            P("mp", None),
            P("dp", "mp", None),
        ),
        out_specs=(
            P("dp", "mp", None),
            P("dp", "mp", None),
            P(),
            P(None, None, "mp"),
            P("mp", None),
            P("mp", None),
            P("mp"),
            P("mp", None),
            P(),
            P(None, "mp"),
            P("mp", None),
        ),
        check_vma=False,
    )
```

profile of v0, /device:TPU:0, one launch (start us, length us, event | category | flops | bytes accessed | tf_op | source)
XLA Modules:
  0.0 843.1 jit_solution(15823164485079725597)
XLA Ops:
  11.0 2.1 fusion.104
  15.6 2.6 copy.150
  18.7 1.7 multiply_reduce_fusion.3
  20.4 9.6 %fusion.55 = f32[128,128,256]{2,1,0:T(8,128)} fusion(s32[128,128]{1,0:T(8,128)S(1)} %iota_subtract_fusion, f32[128,256]{0,1:T(8,128)S(1)} %multiply_reduce_fusion.3), kind=kOutput, calls=%fused_computation.109 | convolution fusion | flops 6446645248 | bytes 16973824 | tf_op jit(solution)/shard_map/jvp()/dot_general | solution.py:48
  30.1 18.0 %copy.146 = f32[128,128,256]{1,0,2:T(8,128)} copy(f32[128,128,256]{2,1,0:T(8,128)} %fusion.55) | data formatting | bytes 33554432 | tf_op jit(solution)/shard_map/jvp()/dot_general | solution.py:48
  48.2 13.8 %all-gather.6.cloned.1.call-done = bf16[1024,1024]{1,0:T(8,128)(2,1)} async-done(((bf16[256,1024]{1,0:T(8,128)(2,1)}), bf16[1024,1024]{1,0:T(8,128)(2,1)}) %all-gather.6.cloned.1.call-update) | async-done | bytes 2097168 | tf_op jit(solution)/shard_map/all_gather | solution.py:166
  63.4 2.9 fusion.86
  69.5 4.1 fusion.81
  73.6 17.0 %fusion.92 = f32[8,128,256]{1,0,2:T(8,128)} fusion(f32[256,8,128]{2,1,0:T(8,128)S(1)} %fusion.81, bf16[8,128,256]{1,0,2:T(8,128)(2,1)S(1)} %copy.206, f32[128,128,256]{1,0,2:T(8,128)} %copy.146), kind=kOutput, calls=%fused_computation.164 | convolution fusion | flops 402915328 | bytes 19398656 | tf_op jit(solution)/shard_map/jvp(ijc,bjc->bic)/dot_general | solution.py:50
  90.7 2.5 copy.208
  96.4 3.9 convolution_convert_fusion.1
  108.6 35.1 %while.42 = (s32[]{:T(128)}, bf16[2,512,2,128]{3,2,1,0:T(2,128)(2,1)}, f32[2,2,512]{2,1,0:T(2,128)}, bf16[2,128,2,128]{3,1,2,0:T(8,128)(2,1)}, bf16[2,128,2,128]...) while((s32[]{:T(128)}, ...), condition=%wide.region_6.7_spmd, body=%wide.region_3.6_spmd.sunk | while | flops 417736448 | bytes 17166820 | solution.py:184
  119.2 2.0 fusion.204
  122.1 2.0 fusion.206
  136.8 2.0 fusion.204
  139.7 2.0 fusion.206
  143.7 4.3 fusion.137
  148.1 75.6 %reduce-scatter.5.cloned.1.call-done = f32[256,1024]{1,0:T(8,128)} async-done(((f32[1024,1024]{1,0:T(8,128)}), f32[256,1024]{1,0:T(8,128)}) %reduce-scatter.5.cloned.1.call-update) | async-done | bytes 1048592 | tf_op jit(solution)/shard_map/reduce_scatter | solution.py:190
  223.7 1.5 fusion.147
  227.2 46.0 %all-gather.8.cloned.1.call-done = bf16[1024,1024]{1,0:T(8,128)(2,1)} async-done(((bf16[256,1024]{1,0:T(8,128)(2,1)}), bf16[1024,1024]{1,0:T(8,128)(2,1)}) %all-gather.8.cloned.1.call-update) | async-done | bytes 2097168 | tf_op jit(solution)/shard_map/all_gather | solution.py:197
  273.2 14.4 %multiply_convert_fusion.1 = (bf16[1024,1024]{1,0:T(8,128)(2,1)}, f32[1024,1024]{1,0:T(8,128)}, f32[1024,1024]{1,0:T(8,128)}) fusion(bf16[1024,1024]{1,0:T(8,128)(2,1)} %all-gather.8.cloned.1.call-done, bf16[1024,1024]{1,0:T(8,128)(2,1)S(1)} %copy-done), kind=kOutput, calls=%fused_computation.111 | convolution fusion | flops 2215641088 | bytes 14680064 | tf_op jit(solution)/shard_map/dot_general | solution.py:198
  287.6 31.7 %all-gather.12.cloned.1.call-done = bf16[1,1024,1024]{2,1,0:T(8,128)(2,1)} async-done(((bf16[1,256,1024]{2,1,0:T(8,128)(2,1)}), bf16[1,1024,1024]{2,1,0:T(8,128)(2,1)}) %all-gather.12.cloned.1.call-update) | async-done | bytes 2097168 | tf_op jit(solution)/shard_map/all_gather | solution.py:210
  319.4 8.1 add_convert_fusion
  328.8 4.4 fusion.151
  334.8 5.2 convolution_convert_fusion
  340.1 68.7 %reduce-scatter.9.cloned.1.call-done = f32[256,1024]{1,0:T(8,128)} async-done(((f32[1024,1024]{1,0:T(8,128)}), f32[256,1024]{1,0:T(8,128)}) %reduce-scatter.9.cloned.1.call-update) | async-done | bytes 1048592 | tf_op jit(solution)/shard_map/reduce_scatter | solution.py:218
  408.8 1.6 multiply_reduce_fusion.6
  410.4 45.5 %reduce-scatter.7.cloned.1.call-done = bf16[256,1024]{1,0:T(8,128)(2,1)} async-done(((bf16[1024,1024]{1,0:T(8,128)(2,1)}), bf16[256,1024]{1,0:T(8,128)(2,1)}) %reduce-scatter.7.cloned.1.call-update) | async-done | bytes 524304 | tf_op jit(solution)/shard_map/reduce_scatter | solution.py:202
  456.0 2.5 fusion.145
  461.2 43.9 %all-gather.10.cloned.1.call-done = bf16[1024,1024]{1,0:T(8,128)(2,1)} async-done(((bf16[256,1024]{1,0:T(8,128)(2,1)}), bf16[1024,1024]{1,0:T(8,128)(2,1)}) %all-gather.10.cloned.1.call-update) | async-done | bytes 2097168 | tf_op jit(solution)/shard_map/all_gather | solution.py:226
  505.1 2.3 convolution_convert_fusion.2
  511.5 33.2 %while.43 = (s32[]{:T(128)}, bf16[2,512,2,128]{3,2,1,0:T(2,128)(2,1)}, bf16[2,512,2,128]{3,2,1,0:T(2,128)(2,1)}, bf16[2,512,2,128]{3,2,1,0:T(2,128)(2,1)}, f32[2...) while((s32[]{:T(128)}, ...), condition=%wide.region_16.17_spmd, body=%wide.region_14.16_spmd.sunk | while | flops 1020929792 | bytes 35832092 | solution.py:231
  519.1 2.3 multiply_reduce_fusion.10
  535.7 2.3 multiply_reduce_fusion.10
  545.8 3.0 add_select_fusion.2
  548.8 1.7 scatter-add.9
  551.1 1.8 reshape_reshape.7
  552.9 1.6 copy.169
  554.6 17.3 %fusion.152 = f32[256,8,128]{2,1,0:T(8,128)} fusion(f32[256,8,128]{2,1,0:T(8,128)S(1)} %copy.169, f32[128,128,256]{1,0,2:T(8,128)} %copy.146), kind=kOutput, calls=%fused_computation.266 | convolution fusion | flops 402653184 | bytes 18874368 | tf_op jit(solution)/shard_map/transpose(jvp(ijc,bjc->bic))/dot_general | solution.py:50
  571.9 5.4 fusion.89
  579.0 2.2 stack_reshape.11
  585.1 4.6 fusion.88
  589.7 2.5 copy.172
  593.8 1.8 convolution_bitcast_fusion.1
  595.7 1.6 fusion.109
  597.2 1.7 convert_element_type.149
  599.1 6.8 fusion.72
  605.8 4.4 fusion.153
  610.3 3.1 copy.173
  613.4 3.5 fusion.135
  616.9 3.5 fusion.70
  621.9 2.8 fusion.65
  624.8 13.4 %convolution_bitcast_fusion = f32[128,128,256]{1,0,2:T(8,128)S(1)} fusion(f32[256,8,128]{2,1,0:T(8,128)S(1)} %copy.169, bf16[8,128,256]{1,0,2:T(8,128)(2,1)S(1)} %copy-done.11), kind=kOutput, calls=%fused_computation.104 | convolution fusion | flops 402653184 | bytes 18350080 | tf_op jit(solution)/shard_map/transpose(jvp(ijc,bjc->bic))/dot_general | solution.py:50
  638.2 18.4 %fusion.101 = f32[128,256]{0,1:T(8,128)S(1)} fusion(f32[128,128,256]{1,0,2:T(8,128)S(1)} %convolution_bitcast_fusion, s32[128,128]{1,0:T(8,128)S(1)} %copy-done.29), kind=kOutput, calls=%fused_computation.180 | convolution fusion | flops 6444548096 | bytes 16973824 | tf_op jit(solution)/shard_map/transpose(jvp())/dot_general | solution.py:48
  656.6 6.6 multiply_reduce_fusion.1
  663.3 34.6 %all-reduce.3 = (f32[256,16]{1,0:T(8,128)S(1)}, f32[256,16]{1,0:T(8,128)S(1)}, f32[256]{0:T(256)}) all-reduce(f32[256,16]{1,0:T(8,128)S(1)} %get-tuple-element.875, f32[256,16]{1,0:T(8,128)S(1)} %get-tuple-element.874, f32[256]{0:T(256)S(1)} %get-tuple-element.868), channel_id=1, replica_groups=mesh['dp'=8,'mp'=4] {'dp'}, use_global_device_ids=true, to_apply=%region_28.29 | all-reduce | flops 8448 | bytes 67584 | tf_op jit(solution)/shard_map/psum | solution.py:276
  700.7 1.7 fusion.110
  702.4 38.3 %all-reduce.2 = (f32[1024]{0:T(1024)}, f32[1024]{0:T(1024)}) all-reduce(f32[1024]{0:T(1024)S(1)} %get-tuple-element.772, f32[1024]{0:T(1024)S(1)} %get-tuple-element.770), channel_id=1, replica_groups=mesh['dp'=8,'mp'=4] {'dp','mp'}, use_global_device_ids=true, to_apply=%region_22.23 | all-reduce | flops 2048 | bytes 16384 | tf_op jit(solution)/shard_map/psum | solution.py:279
  740.7 2.5 add_bitcast_fusion
  743.2 82.6 %all-reduce.7.cloned.1.call-done = (f32[1024,3,256]{2,0,1:T(8,128)}, f32[256,1024]{1,0:T(8,128)}, f32[1024,1024]{1,0:T(8,128)}, f32[1024,1024]{1,0:T(8,128)}) async-done(((f32[1024,3,256]{2,0,1:T(8,128)}, f32[256,1024]{1,0:T(8,128)}, f32[1024,1024]{1,0:T(8,128)}, f32[1024,1024]{1,0:T(8,128)}), (f32[1024,3,256]{2,0,1:T(8,128)}, f32[256,1024]{1,0:T(8,128)}, f32[1024,1024]{1,0:T(8,128)}, ...) | async-done | bytes 12582928 | tf_op jit(solution)/shard_map/psum | solution.py:276
  825.8 3.9 copy.314
  830.7 2.1 copy.316
  832.8 1.6 copy-done.15
  834.4 2.0 copy.317
  (340 shorter events, 98.0 us)
Async XLA Ops:
  7.2 266.0 %copy-start = (bf16[1024,1024]{1,0:T(8,128)(2,1)S(1)}, bf16[1024,1024]{1,0:T(8,128)(2,1)}, u32[]{:S(2)}) copy-start(bf16[1024,1024]{1,0:T(8,128)(2,1)} %param.29) | copy-start | bytes 6291460
  7.2 54.8 %all-gather.6.cloned.1.call-start = ((), (), s32[]{:S(2)}) async-start(), calls=%async_computation.4 | async-start | bytes 2621440 | tf_op jit(solution)/shard_map/all_gather | solution.py:166
  13.2 210.5 %reduce-scatter.5.cloned.1.call-start = ((), (), s32[]{:S(2)}) async-start(), calls=%async_computation.5 | async-start | bytes 5242880 | tf_op jit(solution)/shard_map/reduce_scatter | solution.py:190
  14.7 54.7 %copy-start.31 = (f32[16,256]{0,1:T(8,128)}, f32[16,256]{0,1:T(8,128)S(1)}, u32[]{:S(2)}) copy-start(f32[16,256]{0,1:T(8,128)S(1)} %copy.143) | copy-start | bytes 49156
  15.6 53.9 %copy-start.35 = (f32[16,256]{0,1:T(8,128)}, f32[16,256]{0,1:T(8,128)S(1)}, u32[]{:S(2)}) copy-start(f32[16,256]{0,1:T(8,128)S(1)} %copy.142) | copy-start | bytes 49156
  48.1 19.7 %copy-start.45 = (f32[256,16]{0,1:T(8,128)S(1)}, f32[256,16]{0,1:T(8,128)}, u32[]{:S(2)}) copy-start(f32[256,16]{0,1:T(8,128)} %param.24) | copy-start | bytes 49156
  48.1 21.4 %copy-start.56 = (f32[128]{0:T(128)}, f32[128]{0:T(128)S(1)}, u32[]{:S(2)}) copy-start(f32[128]{0:T(128)S(1)} %subtract_negate_fusion) | copy-start | bytes 1540
  48.1 21.3 %copy-start.68 = (f32[128]{0:T(128)}, f32[128]{0:T(128)S(1)}, u32[]{:S(2)}) copy-start(f32[128]{0:T(128)S(1)} %add_negate_fusion) | copy-start | bytes 1540
  48.2 21.3 %copy-start.64 = (pred[8,8]{1,0:T(8,128)(4,1)}, pred[8,8]{1,0:T(8,128)(4,1)S(1)}, u32[]{:S(2)}) copy-start(pred[8,8]{1,0:T(8,128)(4,1)S(1)} %fusion.142) | copy-start | bytes 196
  48.2 21.3 %copy-start.53 = (f32[8,8]{1,0:T(8,128)}, f32[8,8]{1,0:T(8,128)S(1)}, u32[]{:S(2)}) copy-start(f32[8,8]{1,0:T(8,128)S(1)} %convert_negate_fusion) | copy-start | bytes 772
  63.4 10.2 %copy-start.10 = (bf16[8,128,256]{1,0,2:T(8,128)(2,1)}, bf16[8,128,256]{1,0,2:T(8,128)(2,1)S(1)}, u32[]{:S(2)}) copy-start(bf16[8,128,256]{1,0,2:T(8,128)(2,1)S(1)} %copy.206) | copy-start | bytes 1572868
  67.8 22.8 %copy-start.33 = (f32[16,256,8]{1,0,2:T(8,128)}, f32[16,256,8]{1,0,2:T(8,128)S(1)}, u32[]{:S(2)}) copy-start(f32[16,256,8]{1,0,2:T(8,128)S(1)} %copy.226) | copy-start | bytes 393220
  73.6 19.6 %copy-start.51 = (f32[256]{0:T(256)S(1)}, f32[256]{0:T(256)}, u32[]{:S(2)}) copy-start(f32[256]{0:T(256)} %param.26) | copy-start | bytes 3076
  101.3 3.8 slice-start
  119.2 2.9 copy-start.9
  122.1 4.1 copy-start.61
  136.7 2.9 copy-start.9
  139.7 4.1 copy-start.61
  143.7 4.3 copy-start.3
  143.7 4.4 copy-start.5
  143.7 4.4 copy-start.62
  148.0 77.5 %copy-start.42 = (f32[1024]{0:T(1024)S(1)}, f32[1024]{0:T(1024)}, u32[]{:S(2)}) copy-start(f32[1024]{0:T(1024)} %param.28) | copy-start | bytes 12292
  148.1 125.1 %all-gather.8.cloned.1.call-start = ((), (), s32[]{:S(2)}) async-start(), calls=%async_computation.6 | async-start | bytes 2621440 | tf_op jit(solution)/shard_map/all_gather | solution.py:197
  226.6 92.8 %all-gather.12.cloned.1.call-start = ((), (), s32[]{:S(2)}) async-start(), calls=%async_computation.11 | async-start | bytes 2621440 | tf_op jit(solution)/shard_map/all_gather | solution.py:210
  227.1 181.7 %reduce-scatter.9.cloned.1.call-start = ((), (), s32[]{:S(2)}) async-start(), calls=%async_computation.8 | async-start | bytes 5242880 | tf_op jit(solution)/shard_map/reduce_scatter | solution.py:218
  333.2 122.8 %reduce-scatter.7.cloned.1.call-start = ((), (), s32[]{:S(2)}) async-start(), calls=%async_computation.7 | async-start | bytes 2621440 | tf_op jit(solution)/shard_map/reduce_scatter | solution.py:202
  340.0 118.5 %copy-start.13 = (bf16[1,256,1024]{2,1,0:T(8,128)(2,1)S(1)}, bf16[1,256,1024]{2,1,0:T(8,128)(2,1)}, u32[]{:S(2)}) copy-start(bf16[1,256,1024]{2,1,0:T(8,128)(2,1)} %param.31) | copy-start | bytes 1572868
  340.0 165.0 %all-gather.10.cloned.1.call-start = ((), (), s32[]{:S(2)}) async-start(), calls=%async_computation.9 | async-start | bytes 2621440 | tf_op jit(solution)/shard_map/all_gather | solution.py:226
  410.4 50.0 %copy-start.55 = (s32[4]{0:T(128)S(1)}, s32[4]{0:T(128)}, u32[]{:S(2)}) copy-start(s32[4]{0:T(128)} %constant.355.clone.1) | copy-start | bytes 52
  410.4 94.6 %copy-start.30 = (bf16[256,1024]{1,0:T(8,128)(2,1)S(1)}, bf16[256,1024]{1,0:T(8,128)(2,1)}, u32[]{:S(2)}) copy-start(bf16[256,1024]{1,0:T(8,128)(2,1)} %param.27) | copy-start | bytes 1572868
  458.5 48.9 %copy-start.7 = (f32[256,1024]{1,0:T(8,128)}, f32[256,1024]{1,0:T(8,128)S(1)}, u32[]{:S(2)}) copy-start(f32[256,1024]{1,0:T(8,128)S(1)} %get-tuple-element.842) | copy-start | bytes 3145732
  459.6 239.6 %reduce-scatter.11.cloned.1.call-start = ((), (), s32[]{:S(2)}) async-start(), calls=%async_computation.10 | async-start | bytes 2621440 | tf_op jit(solution)/shard_map/reduce_scatter | solution.py:266
  461.2 50.4 %copy-start.4 = (bf16[2,512,2,128]{3,1,2,0:T(8,128)(2,1)S(1)}, bf16[2,512,2,128]{3,1,2,0:T(8,128)(2,1)}, u32[]{:S(2)}) copy-start(bf16[2,512,2,128]{3,1,2,0:T(8,128)(2,1)} %copy-done.3) | copy-start | bytes 1572868
  461.2 50.4 %copy-start.6 = (bf16[2,512,2,128]{3,1,0,2:T(8,128)(2,1)S(1)}, bf16[2,512,2,128]{3,1,0,2:T(8,128)(2,1)}, u32[]{:S(2)}) copy-start(bf16[2,512,2,128]{3,1,0,2:T(8,128)(2,1)} %copy-done.5) | copy-start | bytes 1572868
  461.2 50.4 %copy-start.41 = (f32[2,2,512]{2,1,0:T(2,128)S(1)}, f32[2,2,512]{2,1,0:T(2,128)}, u32[]{:S(2)}) copy-start(f32[2,2,512]{2,1,0:T(2,128)} %get-tuple-element.1131) | copy-start | bytes 24580
  461.2 50.4 %copy-start.63 = (s32[2]{0:T(128)S(1)}, s32[2]{0:T(128)}, u32[]{:S(2)}) copy-start(s32[2]{0:T(128)} %copy-done.62) | copy-start | bytes 28
  554.5 17.4 %copy-start.32 = (f32[16,256]{0,1:T(8,128)S(1)}, f32[16,256]{0,1:T(8,128)}, u32[]{:S(2)}) copy-start(f32[16,256]{0,1:T(8,128)} %copy-done.31) | copy-start | bytes 49156
  554.6 17.4 %copy-start.36 = (f32[16,256]{0,1:T(8,128)S(1)}, f32[16,256]{0,1:T(8,128)}, u32[]{:S(2)}) copy-start(f32[16,256]{0,1:T(8,128)} %copy-done.35) | copy-start | bytes 49156
  554.6 17.4 %copy-start.69 = (f32[128]{0:T(128)S(1)}, f32[128]{0:T(128)}, u32[]{:S(2)}) copy-start(f32[128]{0:T(128)} %copy-done.68) | copy-start | bytes 1540
  571.9 5.4 copy-start.20
  577.3 5.4 copy-start.54
  577.3 7.8 copy-start.57
  599.0 226.8 %all-reduce.7.cloned.1.call-start = ((), (), s32[]{:S(2)}) async-start(), calls=%async_computation.12 | async-start | bytes 25165824 | tf_op jit(solution)/shard_map/psum | solution.py:276
  599.0 6.8 copy-start.59
  599.0 6.8 copy-start.72
  610.3 3.1 copy-start.12
  613.4 3.5 copy-start.24
  613.4 3.5 copy-start.25
  624.7 13.4 %copy-start.29 = (s32[128,128]{1,0:T(8,128)S(1)}, s32[128,128]{1,0:T(8,128)}, u32[]{:S(2)}) copy-start(s32[128,128]{1,0:T(8,128)} %copy-done.28) | copy-start | bytes 196612
  638.1 18.4 %copy-start.26 = (f32[16,256,8]{0,2,1:T(8,128)S(1)}, f32[16,256,8]{0,2,1:T(8,128)}, u32[]{:S(2)}) copy-start(f32[16,256,8]{0,2,1:T(8,128)} %copy.196) | copy-start | bytes 393220
  638.2 18.4 %copy-start.37 = (f32[16,256]{0,1:T(8,128)S(1)}, f32[16,256]{0,1:T(8,128)}, u32[]{:S(2)}) copy-start(f32[16,256]{0,1:T(8,128)} %copy-done.35) | copy-start | bytes 49156
  638.2 18.4 %copy-start.67 = (f32[128]{0:T(128)S(1)}, f32[128]{0:T(128)}, u32[]{:S(2)}) copy-start(f32[128]{0:T(128)} %copy-done.66) | copy-start | bytes 1540
  638.2 18.4 %copy-start.70 = (f32[128]{0:T(128)S(1)}, f32[128]{0:T(128)}, u32[]{:S(2)}) copy-start(f32[128]{0:T(128)} %copy-done.68) | copy-start | bytes 1540
  656.6 42.7 %copy-start.2 = (bf16[1,256,1024]{2,1,0:T(8,128)(2,1)S(1)}, bf16[1,256,1024]{2,1,0:T(8,128)(2,1)}, u32[]{:S(2)}) copy-start(bf16[1,256,1024]{2,1,0:T(8,128)(2,1)} %param.20) | copy-start | bytes 1572868
  656.6 42.7 %copy-start.38 = (f32[1024]{0:T(1024)S(1)}, f32[1024]{0:T(1024)}, u32[]{:S(2)}) copy-start(f32[1024]{0:T(1024)} %param.22) | copy-start | bytes 12292
  656.6 42.7 %copy-start.44 = (f32[256]{0:T(256)S(1)}, f32[256]{0:T(256)}, u32[]{:S(2)}) copy-start(f32[256]{0:T(256)} %copy-done.43) | copy-start | bytes 3076
  656.6 44.0 %copy-start.50 = (f32[256]{0:T(256)S(1)}, f32[256]{0:T(256)}, u32[]{:S(2)}) copy-start(f32[256]{0:T(256)} %copy-done.49) | copy-start | bytes 3076
  656.6 44.1 %copy-start.48 = (f32[256]{0:T(256)S(1)}, f32[256]{0:T(256)}, u32[]{:S(2)}) copy-start(f32[256]{0:T(256)} %copy-done.47) | copy-start | bytes 3076
  663.3 77.4 %copy-start.8 = (f32[256,1024]{1,0:T(8,128)S(1)}, f32[256,1024]{1,0:T(8,128)}, u32[]{:S(2)}) copy-start(f32[256,1024]{1,0:T(8,128)} %copy-done.7) | copy-start | bytes 3145732
  663.3 77.4 %copy-start.14 = (bf16[1,256,1024]{2,1,0:T(8,128)(2,1)S(1)}, bf16[1,256,1024]{2,1,0:T(8,128)(2,1)}, u32[]{:S(2)}) copy-start(bf16[1,256,1024]{2,1,0:T(8,128)(2,1)} %param.31) | copy-start | bytes 1572868
  825.8 3.9 copy-start.27
  825.8 4.9 copy-start.16
  830.7 3.7 copy-start.15
  830.7 5.7 copy-start.1
  (26 other events, 44.2 us)
Sparse Core Ops, SparseCore 0:
  13.3 48.6 all-gather.5
  148.2 75.4 reduce-scatter.4
  226.7 46.4 all-gather.7
  274.7 44.6 all-gather.11
  333.3 75.4 reduce-scatter.8
  411.5 44.3 reduce-scatter.6
  459.8 45.2 all-gather.9
  599.1 42.6 reduce-scatter.10
  646.9 178.8 all-reduce.6
where the time goes:
time: 854 us; the launch traced here: 843 us
  waiting for transfers between devices  408 us (48%)
  matrix products  183 us (21%)
  local copies, waits for them, and re-layouts  109 us (13%)
  blocking collectives  72.9 us (9%)
  other arithmetic  47.8 us (6%)
  between operations  15.5 us (2%)
    psum x1, waiting for transfers between devices, per_device(): lax.psum((qkv_grad_weight, rate_grad, coef_grad, skip_grad, out_grad, up_...  82.6 us
    reduce_scatter x1, waiting for transfers between devices, per_device(): lax.psum_scatter(jnp.dot(picked, out_weight, preferred_element_type=jnp.f...  75.6 us
    reduce_scatter x1, waiting for transfers between devices, per_device(): lax.psum_scatter(jnp.einsum('tf,df->td', picked, up_weight, preferred_ele...  68.7 us
    dot_general x3, matrix products, ssm_mix(): inside = jnp.einsum('ijc,bjc->bic', toeplitz, pieces, precision=highest)  47.7 us
    all_gather x1, waiting for transfers between devices, per_device(): lax.all_gather(normed_two.astype(jnp.bfloat16), 'mp', axis=0, tiled=True)  46 us
    reduce_scatter x1, waiting for transfers between devices, per_device(): lax.psum_scatter(jnp.dot(picked, down_weight, preferred_element_type=jnp....  45.5 us
    all_gather x1, waiting for transfers between devices, per_device(): lax.all_gather(middle_grad.astype(jnp.bfloat16), 'mp', axis=0, tiled=True)  43.9 us
    psum x1, blocking collectives, per_device(): lax.psum((gain_attn_grad, gain_mlp_grad), ('dp', 'mp'))  38.3 us
  transfers between devices with their start and end apart: 9, of which 8 were waited for; matrix products, arithmetic and copies ran while one was open for 15% of the time, Pallas kernels for 0%

commit v1 on v0

v1 whole, which is shorter than its diff:
```python
from functools import partial
import math

import jax
import jax.numpy as jnp
from jax import lax
from jax.experimental import pallas as pl
from jax.experimental.pallas import tpu as pltpu
from jax.sharding import PartitionSpec as P

HD = 128
CTX = 128
GROUP = 8

f32 = jnp.float32
bf16 = jnp.bfloat16
epsilon = 1e-05
masked_score = -1e30
score_scale = 1.0 / math.sqrt(HD)
VMEM_LIMIT = 56 * 1024 * 1024

NT = (((1,), (1,)), ((), ()))
TN = (((0,), (0,)), ((), ()))
NN = (((1,), (0,)), ((), ()))


def mm(a, b, dims=NN):
    return lax.dot_general(a, b, dims, preferred_element_type=f32)


def call(kernel, out_shape, scratch=(), n_scalar=0, flops=0, moved=0):
    specs = [pl.BlockSpec(memory_space=pltpu.SMEM)] * n_scalar

    def run(*args):
        in_specs = specs + [pl.BlockSpec(memory_space=pltpu.VMEM)] * (len(args) - n_scalar)
        out_specs = jax.tree.map(lambda s: pl.BlockSpec(memory_space=pltpu.VMEM), out_shape)
        return pl.pallas_call(
            kernel,
            out_shape=out_shape,
            in_specs=in_specs,
            out_specs=out_specs,
            scratch_shapes=scratch,
            compiler_params=pltpu.CompilerParams(vmem_limit_bytes=VMEM_LIMIT),
            cost_estimate=pl.CostEstimate(flops=flops, bytes_accessed=moved, transcendentals=0),
        )(*args)

    return run


def shape(dims, dtype=f32):
    return jax.ShapeDtypeStruct(dims, dtype)


def ssm_forward(x_ref, rate_ref, coef_ref, skip_ref, win_ref, state_ref, xs):
    xs[...] = x_ref[...].astype(f32)
    decay = jnp.exp(-rate_ref[...])
    coef = coef_ref[...]
    skip = skip_ref[...]
    zero = jnp.zeros_like(decay)

    def step(eight, carry, window):
        state, slope = carry
        x8 = xs[pl.ds(pl.multiple_of(eight * 8, 8), 8), :]
        rows = []
        for k in range(8):
            slope = decay * (slope + state)
            state = decay * state + x8[k : k + 1]
            if window is not None:
                rows.append(jnp.sum(coef * state, axis=0, keepdims=True))
        if window is not None:
            at = pl.multiple_of((eight - (2 * window + 1) * 16) * 8, 8)
            win_ref[window, pl.ds(at, 8), :] = jnp.concatenate(rows, axis=0) + skip * x8
        return state, slope

    carry = (zero, zero)
    for chunk in range(4):
        window = chunk // 2 if chunk % 2 else None
        carry = lax.fori_loop(
            chunk * 16, chunk * 16 + 16, partial(step, window=window), carry
        )
    state_ref[0] = carry[0]
    state_ref[1] = carry[1]


def ssm_carry_in(local_ref, enter_ref, rate_ref, coef_ref, out_ref, acc):
    rate = rate_ref[...]
    decay = jnp.exp(-rate)
    coef = coef_ref[...]

    def step(eight, state):
        rows = []
        for k in range(8):
            rows.append(jnp.sum(coef * state, axis=0, keepdims=True))
            state = decay * state
        acc[pl.ds(pl.multiple_of(eight * 8, 8), 8), :] = jnp.concatenate(rows, axis=0)
        return state

    lax.fori_loop(0, 16, step, enter_ref[...] * jnp.exp(-129.0 * rate))
    out_ref[...] = (local_ref[...] + acc[...]).astype(bf16)


def ssm_adjoint_exit(grad_ref, rate_ref, out_ref):
    rate = rate_ref[...]
    decay = jnp.exp(-rate)

    def step(j, adj):
        eight = 15 - j
        g8 = grad_ref[pl.ds(pl.multiple_of(eight * 8, 8), 8), :]
        for k in range(7, -1, -1):
            adj = decay * adj + g8[k : k + 1]
        return adj

    adj = lax.fori_loop(0, 16, step, jnp.zeros_like(rate))
    out_ref[...] = adj * jnp.exp(-128.0 * rate)


def ssm_signal_grad(near_ref, far_ref, enter_ref, rate_ref, coef_ref, skip_ref, out_ref):
    decay = jnp.exp(-rate_ref[...])
    coef = coef_ref[...]
    skip = skip_ref[...]

    def step(j, adj, chunk):
        eight = 15 - j
        local = pl.multiple_of(eight * 8, 8)
        if chunk % 2:
            g8 = (near_ref, far_ref)[chunk // 2][pl.ds(local, 8), :]
        rows = [None] * 8
        for k in range(7, -1, -1):
            adj = decay * adj
            if chunk % 2:
                adj = adj + g8[k : k + 1]
            rows[k] = jnp.sum(coef * adj, axis=0, keepdims=True)
        y8 = jnp.concatenate(rows, axis=0)
        if chunk % 2:
            y8 = y8 + skip * g8
        out_ref[pl.ds(pl.multiple_of(chunk * 128 + eight * 8, 8), 8), :] = y8
        return adj

    adj = enter_ref[...]
    for chunk in (3, 2, 1, 0):
        adj = lax.fori_loop(0, 16, partial(step, chunk=chunk), adj)


def ssm_param_grad(
    x_ref, near_ref, far_ref, enter_ref, rate_ref, coef_ref, out_ref, skip_out_ref, xs
):
    xs[...] = x_ref[...].astype(f32)
    decay = jnp.exp(-rate_ref[...])
    zero = jnp.zeros_like(decay)

    def step(eight, carry, chunk):
        state, slope, for_coef, for_rate = carry
        x8 = xs[pl.ds(pl.multiple_of(eight * 8 + chunk * 128, 8), 8), :]
        if chunk % 2:
            g8 = (near_ref, far_ref)[chunk // 2][pl.ds(pl.multiple_of(eight * 8, 8), 8), :]
        for k in range(8):
            slope = decay * (slope + state)
            state = decay * state + x8[k : k + 1]
            if chunk % 2:
                for_coef = for_coef + state * g8[k : k + 1]
                for_rate = for_rate + slope * g8[k : k + 1]
        return state, slope, for_coef, for_rate

    carry = (enter_ref[0], enter_ref[1], zero, zero)
    for chunk in range(4):
        carry = lax.fori_loop(0, 16, partial(step, chunk=chunk), carry)
    out_ref[0] = -coef_ref[...] * carry[3]
    out_ref[1] = carry[2]
    skip_out_ref[...] = jnp.sum(xs[128:256] * near_ref[...], axis=0, keepdims=True) + jnp.sum(
        xs[384:512] * far_ref[...], axis=0, keepdims=True
    )


def causal(scores):
    rows = lax.broadcasted_iota(jnp.int32, scores.shape, 0)
    cols = lax.broadcasted_iota(jnp.int32, scores.shape, 1)
    return jnp.where(cols <= rows, scores, masked_score)


def softmax_parts(parts):
    top = parts[0].max(axis=-1, keepdims=True)
    for part in parts[1:]:
        top = jnp.maximum(top, part.max(axis=-1, keepdims=True))
    weights = [jnp.exp(part - top) for part in parts]
    total = weights[0].sum(axis=-1, keepdims=True)
    for weight in weights[1:]:
        total = total + weight.sum(axis=-1, keepdims=True)
    return [weight / total for weight in weights]


def block_probs(query, key, first, second, whole, late):
    q0, q1 = query[:256], query[256:]
    k0, k1 = key[:256], key[256:]
    has_first = late > 0
    is_whole = whole > 0
    chosen = jnp.where(is_whole, first, second)
    chosen_ok = jnp.logical_or(jnp.logical_not(is_whole), has_first)
    s00 = causal(mm(q0, k0, NT) * score_scale)
    s0c = jnp.where(has_first, mm(q0, first, NT) * score_scale, masked_score)
    s11 = causal(mm(q1, k1, NT) * score_scale)
    s10 = jnp.where(is_whole, mm(q1, k0, NT) * score_scale, masked_score)
    s1c = jnp.where(chosen_ok, mm(q1, chosen, NT) * score_scale, masked_score)
    return softmax_parts([s00, s0c]), softmax_parts([s11, s10, s1c]), chosen


def attention_forward(flag_ref, qkv_ref, first_ref, second_ref, out_ref):
    channels = first_ref.shape[1]
    for head in range(channels // HD):
        at = head * HD
        query = qkv_ref[:, at : at + HD]
        key = qkv_ref[:, channels + at : channels + at + HD]
        value = qkv_ref[:, 2 * channels + at : 2 * channels + at + HD]
        first = first_ref[:, at : at + HD]
        second = second_ref[:, at : at + HD]
        (p00, p0c), (p11, p10, p1c), chosen = block_probs(
            query, key, first, second, flag_ref[0], flag_ref[1]
        )
        v0, v1 = value[:256], value[256:]
        out_ref[:256, at : at + HD] = (
            mm(p00.astype(bf16), v0) + mm(p0c.astype(bf16), first)
        ).astype(bf16)
        out_ref[256:, at : at + HD] = (
            mm(p11.astype(bf16), v1) + mm(p10.astype(bf16), v0) + mm(p1c.astype(bf16), chosen)
        ).astype(bf16)


def attention_backward(
    flag_ref, qkv_ref, first_ref, second_ref, grad_ref, out_ref, first_out_ref, second_out_ref
):
    channels = first_ref.shape[1]
    is_whole = flag_ref[0] > 0
    for head in range(channels // HD):
        at = head * HD
        query = qkv_ref[:, at : at + HD]
        key = qkv_ref[:, channels + at : channels + at + HD]
        value = qkv_ref[:, 2 * channels + at : 2 * channels + at + HD]
        first = first_ref[:, at : at + HD]
        second = second_ref[:, at : at + HD]
        grad = grad_ref[:, at : at + HD]
        early, later, chosen = block_probs(
            query, key, first, second, flag_ref[0], flag_ref[1]
        )
        q0, q1 = query[:256], query[256:]
        k0, k1 = key[:256], key[256:]
        v0, v1 = value[:256], value[256:]
        g0, g1 = grad[:256], grad[256:]

        def score_grads(probs, rows, values):
            prob_grads = [mm(rows, v, NT) for v in values]
            centre = sum(
                (p * d).sum(axis=-1, keepdims=True) for p, d in zip(probs, prob_grads)
            )
            return [(p * (d - centre)).astype(bf16) for p, d in zip(probs, prob_grads)]

        d00, d0c = score_grads(early, g0, (v0, first))
        d11, d10, d1c = score_grads(later, g1, (v1, v0, chosen))
        p00, p0c = [p.astype(bf16) for p in early]
        p11, p10, p1c = [p.astype(bf16) for p in later]
        out_ref[:256, at : at + HD] = ((mm(d00, k0) + mm(d0c, first)) * score_scale).astype(bf16)
        out_ref[256:, at : at + HD] = (
            (mm(d11, k1) + mm(d10, k0) + mm(d1c, chosen)) * score_scale
        ).astype(bf16)
        at_k = channels + at
        out_ref[:256, at_k : at_k + HD] = (
            (mm(d00, q0, TN) + mm(d10, q1, TN)) * score_scale
        ).astype(bf16)
        out_ref[256:, at_k : at_k + HD] = (mm(d11, q1, TN) * score_scale).astype(bf16)
        at_v = 2 * channels + at
        out_ref[:256, at_v : at_v + HD] = (mm(p00, g0, TN) + mm(p10, g1, TN)).astype(bf16)
        out_ref[256:, at_v : at_v + HD] = mm(p11, g1, TN).astype(bf16)
        from_early = mm(d0c, q0, TN) * score_scale + mm(p0c, g0, TN)
        from_later = mm(d1c, q1, TN) * score_scale + mm(p1c, g1, TN)
        first_out_ref[:, at : at + HD] = from_early + jnp.where(is_whole, from_later, 0.0)
        second_out_ref[:, at : at + HD] = jnp.where(is_whole, 0.0, from_later)


def feed_forward(
    n_ref, c_ref, up0_ref, up1_ref, down0_ref, down1_ref, act_ref, gate_ref,
    down_own_ref, down_send_ref, back_own_ref, back_send_ref, acc_down, acc_back,
):
    step = pl.program_id(0)
    steps = pl.num_programs(0)
    half = n_ref.shape[0] // 2

    @pl.when(step == 0)
    def _():
        acc_down[...] = jnp.zeros_like(acc_down)
        acc_back[...] = jnp.zeros_like(acc_back)

    def body(up_ref, down_ref):
        up = up_ref[...]
        down = down_ref[...]
        gate = mm(n_ref[...], up)
        cdf = 0.5 * (1.0 + lax.erf(gate * (1.0 / math.sqrt(2.0))))
        act = (gate * cdf).astype(bf16)
        slope = cdf + gate * jnp.exp(-0.5 * gate * gate) * (1.0 / math.sqrt(2.0 * math.pi))
        act_ref[...] = act
        acc_down[...] += mm(act, down)
        grad = (mm(c_ref[...], down, NT) * slope).astype(bf16)
        gate_ref[...] = grad
        acc_back[...] += mm(grad, up, NT)

    @pl.when(step < steps // 2)
    def _():
        body(up0_ref, down0_ref)

    @pl.when(step >= steps // 2)
    def _():
        body(up1_ref, down1_ref)

    @pl.when(step == steps - 1)
    def _():
        down_own_ref[...] = acc_down[:half]
        down_send_ref[...] = acc_down[half:].astype(bf16)
        back_own_ref[...] = acc_back[:half]
        back_send_ref[...] = acc_back[half:].astype(bf16)


def run_feed_forward(rows, cot, up0, up1, down0, down1):
    tokens, width = rows.shape
    hidden = up0.shape[1]
    block = 512
    per = hidden // block
    half = tokens // 2

    def slot0(j):
        return jnp.minimum(j, per - 1)

    def slot1(j):
        return jnp.maximum(j - per, 0)

    whole = pl.BlockSpec((tokens, width), lambda j: (0, 0))
    part = pl.BlockSpec((half, width), lambda j: (0, 0))
    return pl.pallas_call(
        feed_forward,
        grid=(2 * per,),
        out_shape=(
            shape((tokens, 2 * hidden), bf16),
            shape((tokens, 2 * hidden), bf16),
            shape((half, width)),
            shape((half, width), bf16),
            shape((half, width)),
            shape((half, width), bf16),
        ),
        in_specs=[
            whole,
            whole,
            pl.BlockSpec((width, block), lambda j: (0, slot0(j))),
            pl.BlockSpec((width, block), lambda j: (0, slot1(j))),
            pl.BlockSpec((block, width), lambda j: (slot0(j), 0)),
            pl.BlockSpec((block, width), lambda j: (slot1(j), 0)),
        ],
        out_specs=(
            pl.BlockSpec((tokens, block), lambda j: (0, j)),
            pl.BlockSpec((tokens, block), lambda j: (0, j)),
            part,
            part,
            part,
            part,
        ),
        scratch_shapes=[pltpu.VMEM((tokens, width), f32), pltpu.VMEM((tokens, width), f32)],
        compiler_params=pltpu.CompilerParams(
            vmem_limit_bytes=VMEM_LIMIT, dimension_semantics=("arbitrary",)
        ),
        cost_estimate=pl.CostEstimate(
            flops=2 * 4 * tokens * width * 2 * hidden,
            bytes_accessed=16 * 1024 * 1024,
            transcendentals=0,
        ),
    )(rows, cot, up0, up1, down0, down1)


def weight_grad(place_ref, *refs, plan, n_args):
    args, (keep_ref, send_ref) = refs[:n_args], refs[n_args:]
    place = place_ref[0]
    rows = keep_ref.shape[2]
    for mat, pieces in enumerate(plan):
        for lhs_at, rhs_at, lhs_col, rhs_col, cols, out_col in pieces:
            rhs = args[rhs_at][:, rhs_col : rhs_col + cols]
            for pair in range(GROUP // 2):
                start = lhs_col + pair * 2 * rows
                block = mm(args[lhs_at][:, start : start + 2 * rows], rhs, TN).astype(bf16)
                for side in range(2):
                    target = jnp.bitwise_xor(place, 2 * pair + side)
                    slot = target // 2
                    value = block[side * rows : (side + 1) * rows]

                    @pl.when(target % 2 == 0)
                    def _():
                        keep_ref[mat, slot, :, out_col : out_col + cols] = value

                    @pl.when(target % 2 == 1)
                    def _():
                        send_ref[mat, slot, :, out_col : out_col + cols] = value


def run_weight_grad(place, args, plan, rows=128, cols=1024):
    out = shape((len(plan), GROUP // 2, rows, cols), bf16)
    tokens = args[0].shape[0]
    return call(
        partial(weight_grad, plan=plan, n_args=len(args)),
        (out, out),
        n_scalar=1,
        flops=2 * len(plan) * tokens * GROUP * rows * cols,
        moved=4 * len(plan) * GROUP * rows * cols,
    )(place, *args)


def normalise(values):
    mean = jnp.mean(values, axis=-1, keepdims=True)
    centred = values - mean
    spread = jnp.mean(centred * centred, axis=-1, keepdims=True)
    inverse = lax.rsqrt(spread + epsilon)
    return centred * inverse, inverse


def normalise_back(grad, gain, hat, inverse):
    inner = grad * gain
    back = (
        inner
        - jnp.mean(inner, axis=-1, keepdims=True)
        - hat * jnp.mean(inner * hat, axis=-1, keepdims=True)
    ) * inverse
    return back, jnp.sum(grad * hat, axis=0)


def per_device(
    inputs,
    block_size,
    gain_attn,
    qkv_weight,
    ssm_rate,
    ssm_coef,
    ssm_skip,
    out_weight,
    gain_mlp,
    up_weight,
    down_weight,
    cotangent,
    dp_size,
):
    z = lax.axis_index("mp")
    place = jnp.bitwise_and(lax.axis_index("dp"), GROUP - 1)
    odd = jnp.bitwise_and(z, 1)
    late = jnp.right_shift(z, 1)
    is_odd = odd > 0
    is_late = late > 0
    groups = [[g * GROUP + k for k in range(GROUP)] for g in range(dp_size // GROUP)]
    groups = groups if len(groups) > 1 else None

    def swap_mp(value, mask):
        return lax.ppermute(value, "mp", [(k, k ^ mask) for k in range(4)])

    def swap_dp(value, mask):
        return lax.ppermute(value, "dp", [(k, k ^ mask) for k in range(dp_size)])

    def gather(value):
        return lax.all_gather(value, "dp", axis=0, tiled=True, axis_index_groups=groups)

    def by_position(own, other):
        return jnp.where(
            is_odd, jnp.concatenate([other, own], 0), jnp.concatenate([own, other], 0)
        )

    def halves(tile):
        size = tile.shape[0] // 2
        own = lax.dynamic_slice_in_dim(tile, odd * size, size, 0)
        other = lax.dynamic_slice_in_dim(tile, (1 - odd) * size, size, 0)
        return own, other

    def swap_slots(value):
        size = value.shape[-1] // 2
        return jnp.concatenate([value[..., size:], value[..., :size]], -1)

    model_dim = inputs.shape[2]
    channels = qkv_weight.shape[2]
    rows = model_dim // GROUP
    row = inputs[0].astype(f32)
    cot = cotangent[0]
    whole = (block_size[0] > 2 * CTX).astype(jnp.int32)
    flags = jnp.stack([whole, late])
    place_arg = place.reshape(1)

    attn_slice = jnp.concatenate(
        [
            lax.dynamic_slice_in_dim(qkv_weight, place * rows, rows, 0).reshape(rows, 3 * channels),
            lax.dynamic_slice_in_dim(out_weight, place * rows, rows, 1).T,
        ],
        1,
    )
    attn_far = gather(swap_mp(attn_slice, 2))
    mlp_rows = up_weight.shape[0] // GROUP
    mlp_slice = jnp.concatenate(
        [
            lax.dynamic_slice_in_dim(up_weight, place * mlp_rows, mlp_rows, 0),
            lax.dynamic_slice_in_dim(down_weight, place * mlp_rows, mlp_rows, 0),
        ],
        0,
    )
    ssm_pack = jnp.concatenate(
        [ssm_rate.T, ssm_coef.T, ssm_skip[None], jnp.zeros((7, channels), f32)], 0
    )
    ssm_both = jnp.concatenate([ssm_pack, swap_mp(ssm_pack, 2)], 1)
    rate_t, coef_t, skip_t = ssm_both[:16], ssm_both[16:32], ssm_both[32:33]

    hat_one, inverse_one = normalise(row)
    normed_one = (hat_one * gain_attn).astype(bf16)
    tile_one = by_position(normed_one, swap_mp(normed_one, 1))
    tokens = tile_one.shape[0]
    wide = 2 * channels

    z_far = jnp.bitwise_xor(z, 2)
    signal = jnp.concatenate(
        [
            lax.dynamic_slice_in_dim(tile_one, z * channels, channels, 1),
            lax.dynamic_slice_in_dim(tile_one, z_far * channels, channels, 1),
        ],
        1,
    )
    windows, exit_state = call(
        ssm_forward,
        (shape((2, CTX, wide)), shape((2, 16, wide))),
        scratch=[pltpu.VMEM((tokens, wide), f32)],
        flops=4 * tokens * wide * 64,
        moved=4 * tokens * wide,
    )(signal, rate_t, coef_t, skip_t)
    handed = jnp.concatenate([exit_state.reshape(32, wide), windows[1]], 0)
    handed = swap_slots(lax.ppermute(handed, "mp", [(0, 2), (1, 3)]))
    enter_state = handed[:32].reshape(2, 16, wide)
    ctx_first = handed[32:].astype(bf16)
    ctx_second = call(
        ssm_carry_in,
        shape((CTX, wide), bf16),
        scratch=[pltpu.VMEM((CTX, wide), f32)],
        flops=CTX * wide * 64,
        moved=CTX * wide * 8,
    )(windows[0], enter_state[0], rate_t, coef_t)

    near_qkv = qkv_weight.reshape(model_dim, 3 * channels)
    far_qkv = attn_far[:, : 3 * channels]
    far_out = attn_far[:, 3 * channels :]
    cot_tile = jnp.concatenate([cot, swap_mp(cot, 1)], 0)
    mlp_far = gather(swap_mp(mlp_slice, 2)).reshape(GROUP, 2, mlp_rows, up_weight.shape[1])
    up_far = mlp_far[:, 0].reshape(up_weight.shape)
    down_far = mlp_far[:, 1].reshape(down_weight.shape)

    def attend(qkv, slot):
        at = slot * channels
        return call(
            attention_forward,
            shape((tokens, channels), bf16),
            n_scalar=1,
            flops=4 * tokens * channels * 512,
            moved=2 * tokens * channels * 4,
        )(flags, qkv, ctx_first[:, at : at + channels], ctx_second[:, at : at + channels])

    qkv_near = mm(tile_one, near_qkv).astype(bf16)
    attended_near = attend(qkv_near, 0)
    qkv_far = mm(tile_one, far_qkv).astype(bf16)
    attended_far = attend(qkv_far, 1)
    projected = mm(attended_near, out_weight) + mm(attended_far, far_out, NT)
    out_own, out_other = halves(projected)
    middle = row + out_own + swap_mp(out_other.astype(bf16), 1).astype(f32)

    hat_two, inverse_two = normalise(middle)
    normed_two = (hat_two * gain_mlp).astype(bf16)
    tile_two = jnp.concatenate([normed_two, swap_mp(normed_two, 1)], 0)
    activated, gate_grad, down_own, down_send, back_own, back_send = run_feed_forward(
        tile_two, cot_tile, up_weight, up_far, down_weight, down_far
    )
    normed_two_grad = back_own + swap_mp(back_send, 1).astype(f32)
    result = middle + down_own + swap_mp(down_send, 1).astype(f32)
    output = result.astype(bf16)[None]
    middle_back, gain_mlp_grad = normalise_back(normed_two_grad, gain_mlp, hat_two, inverse_two)
    middle_grad = cot.astype(f32) + middle_back
    attn_grad = middle_grad.astype(bf16)
    tile_back = by_position(attn_grad, swap_mp(attn_grad, 1))

    def reduce_over_plane(keep, send):
        total = keep.astype(f32) + swap_dp(send, 1).astype(f32)
        own = total[:, 0]
        for slot in range(1, GROUP // 2):
            own = own + swap_dp(total[:, slot].astype(bf16), 2 * slot).astype(f32)
        count = own.shape[0] // 2
        own = own[:count] + swap_mp(own[count:].astype(bf16), 2).astype(f32)
        mask = GROUP
        while mask < dp_size:
            own = own + swap_dp(own.astype(bf16), mask).astype(f32)
            mask *= 2
        own = own.astype(bf16)
        full = gather(own.reshape(count * own.shape[1], own.shape[2]))
        full = full.reshape(GROUP, count, own.shape[1], own.shape[2])
        return [
            full[:, k].reshape(GROUP * own.shape[1], own.shape[2]).astype(f32)
            for k in range(count)
        ]

    hidden = up_weight.shape[1]
    up_plan = [[(0, 1, 0, s * hidden, hidden, 0)] for s in range(2)]
    down_plan = [[(2, 3, s * hidden, 0, hidden, 0)] for s in range(2)]
    mlp_plan = [up_plan[0], down_plan[0], up_plan[1], down_plan[1]]
    mlp_keep, mlp_send = run_weight_grad(
        place_arg, (tile_two, gate_grad, activated, cot_tile), mlp_plan
    )
    up_grad, down_grad = reduce_over_plane(mlp_keep, mlp_send)

    attended_grad_near = mm(tile_back, out_weight, NT).astype(bf16)
    attended_grad_far = mm(tile_back, far_out).astype(bf16)

    def attend_back(qkv, grad, slot):
        at = slot * channels
        return call(
            attention_backward,
            (
                shape((tokens, 3 * channels), bf16),
                shape((CTX, channels)),
                shape((CTX, channels)),
            ),
            n_scalar=1,
            flops=10 * tokens * channels * 512,
            moved=2 * tokens * channels * 8,
        )(flags, qkv, ctx_first[:, at : at + channels], ctx_second[:, at : at + channels], grad)

    dqkv_near, first_near, second_near = attend_back(qkv_near, attended_grad_near, 0)
    dqkv_far, first_far, second_far = attend_back(qkv_far, attended_grad_far, 1)
    second_grad = jnp.concatenate([second_near, second_far], 1)
    exit_adjoint = call(
        ssm_adjoint_exit, shape((16, wide)), flops=CTX * wide * 32, moved=CTX * wide * 4
    )(second_grad, rate_t)
    returned = jnp.concatenate(
        [exit_adjoint, jnp.concatenate([first_near, first_far], 1)], 0
    )
    returned = swap_slots(lax.ppermute(returned, "mp", [(2, 0), (3, 1)]))
    enter_adjoint, last_grad = returned[:16], returned[16:]
    signal_grad = call(
        ssm_signal_grad,
        shape((tokens, wide)),
        flops=tokens * wide * 64,
        moved=tokens * wide * 4,
    )(second_grad, last_grad, enter_adjoint, rate_t, coef_t, skip_t)
    param_grad, skip_grad = call(
        ssm_param_grad,
        (shape((2, 16, wide)), shape((1, wide))),
        scratch=[pltpu.VMEM((tokens, wide), f32)],
        flops=tokens * wide * 96,
        moved=tokens * wide * 4,
    )(signal, second_grad, last_grad, enter_state, rate_t, coef_t)

    placed = jnp.concatenate(
        [
            jnp.where(
                z == b,
                signal_grad[:, :channels],
                jnp.where(z_far == b, signal_grad[:, channels:], 0.0),
            )
            for b in range(4)
        ],
        1,
    )
    one_back = mm(dqkv_near, near_qkv, NT) + mm(dqkv_far, far_qkv, NT) + placed
    one_own, one_other = halves(one_back)
    normed_one_grad = one_own + swap_mp(one_other.astype(bf16), 1).astype(f32)
    input_back, gain_attn_grad = normalise_back(normed_one_grad, gain_attn, hat_one, inverse_one)
    input_grad = (middle_grad + input_back)[None]

    attn_plan = [
        [(0, 1, 0, 0, 3 * channels, 0), (2, 3, 0, 0, channels, 3 * channels)],
        [(0, 4, 0, 0, 3 * channels, 0), (2, 5, 0, 0, channels, 3 * channels)],
    ]
    attn_keep, attn_send = run_weight_grad(
        place_arg,
        (tile_one, dqkv_near, tile_back, attended_near, dqkv_far, attended_far),
        attn_plan,
    )
    (attn_full,) = reduce_over_plane(attn_keep, attn_send)
    qkv_grad = attn_full[:, : 3 * channels].reshape(model_dim, 3, channels)
    out_grad = attn_full[:, 3 * channels :].T

    small = jnp.concatenate([param_grad.reshape(32, wide), skip_grad], 0)
    small = small[:, :channels] + swap_mp(small[:, channels:], 2)
    gains = jnp.stack([gain_attn_grad, gain_mlp_grad])
    for mask in (1, 2):
        gains = gains + swap_mp(gains, mask)
    packed = jnp.concatenate([small, gains.reshape(-1, channels)], 0)
    mask = 1
    while mask < dp_size:
        packed = packed + swap_dp(packed, mask)
        mask *= 2
    rate_grad = packed[:16].T
    coef_grad = packed[16:32].T
    skip_sum = packed[32]
    gains = packed[33:].reshape(2, model_dim)
    return (
        output,
        input_grad,
        gains[0],
        qkv_grad,
        rate_grad,
        coef_grad,
        skip_sum,
        out_grad,
        gains[1],
        up_grad,
        down_grad,
    )


def solution(mesh):
    return jax.shard_map(
        partial(per_device, dp_size=mesh.shape["dp"]),
        mesh=mesh,
        in_specs=(
            P("dp", "mp", None),
            P("dp"),
            P(),
            P(None, None, "mp"),
            P("mp", None),
            P("mp", None),
            P("mp"),
            P("mp", None),
            P(),
            P(None, "mp"),
            P("mp", None),
            P("dp", "mp", None),
        ),
        out_specs=(
            P("dp", "mp", None),
            P("dp", "mp", None),
            P(),
            P(None, None, "mp"),
            P("mp", None),
            P("mp", None),
            P("mp"),
            P("mp", None),
            P(),
            P(None, "mp"),
            P("mp", None),
        ),
        check_vma=False,
    )
```

time: 854 us -> 485 us (0.57)
  matrix products: 183 us -> 17.9 us
  waiting for transfers between devices: 408 us -> 251 us
  Pallas kernels: 0 us -> 79.6 us
  blocking collectives: 72.9 us -> 0 us
  local copies, waits for them, and re-layouts: 109 us -> 37.2 us
  starting transfers between devices: 0.37 us -> 39.8 us
    ppermute x0 -> x29, waiting for transfers between devices: none -> 251 us  [the longest x16 157 us: swap_mp(): return lax.ppermute(value, 'mp', [(k, k ^ mask) for k in range(4)])]
    reduce_scatter x4 -> x0, waiting for transfers between devices: 190 us -> none  [the longest x1 75.6 us: per_device(): lax.psum_scatter(jnp.dot(picked, out_weight, preferred_element_type=jnp.f...]
    dot_general x37 -> x8, matrix products: 183 us -> 17.9 us  [mm(): return lax.dot_general(a, b, dims, preferred_element_type=f32)]
    all_gather x4, waiting for transfers between devices: 135 us -> 0.03 us  [gather(): lax.all_gather(value, 'dp', axis=0, tiled=True, axis_index_groups=groups)]
    psum x1 -> x0, waiting for transfers between devices: 82.6 us -> none  [per_device(): lax.psum((qkv_grad_weight, rate_grad, coef_grad, skip_grad, out_grad, up_...]
    pallas_call x0 -> x12, Pallas kernels: none -> 79.6 us  [the longest x11 63.8 us: run(): pl.pallas_call(kernel, out_shape=out_shape, in_specs=in_specs, out_specs=...]
    psum x2 -> x0, blocking collectives: 72.9 us -> none  [the longest x1 38.3 us: per_device(): lax.psum((gain_attn_grad, gain_mlp_grad), ('dp', 'mp'))]
    ppermute x0 -> x29, starting transfers between devices: none -> 39.7 us  [the longest x16 24.3 us: swap_mp(): return lax.ppermute(value, 'mp', [(k, k ^ mask) for k in range(4)])]
  transfers between devices with their start and end apart: 9 -> 33, of which waited for: 8 -> 27; matrix products, arithmetic and copies ran while one was open for 15% -> 14% of each run, Pallas kernels for 0% -> 9%
where the time goes in v1:
time: 485 us; the launch traced here: 481 us
  waiting for transfers between devices  251 us (52%)
  Pallas kernels  79.6 us (16%)
  other arithmetic  40.1 us (8%)
  starting transfers between devices  39.8 us (8%)
  local copies, waits for them, and re-layouts  37.2 us (8%)
  matrix products  17.9 us (4%)
  between operations  15.3 us (3%)
    ppermute x16, waiting for transfers between devices, swap_mp(): return lax.ppermute(value, 'mp', [(k, k ^ mask) for k in range(4)])  157 us
    ppermute x11, waiting for transfers between devices, swap_dp(): return lax.ppermute(value, 'dp', [(k, k ^ mask) for k in range(dp_size)])  82.5 us
    pallas_call x11, Pallas kernels, run(): pl.pallas_call(kernel, out_shape=out_shape, in_specs=in_specs, out_specs=...  63.8 us
    ppermute x16, starting transfers between devices, swap_mp(): return lax.ppermute(value, 'mp', [(k, k ^ mask) for k in range(4)])  24.3 us
    dot_general x8, matrix products, mm(): return lax.dot_general(a, b, dims, preferred_element_type=f32)  17.9 us
    pallas_call x1, Pallas kernels, run_feed_forward(): pl.pallas_call(feed_forward, grid=(2 * per,), out_shape=(shape((tokens, 2...  15.9 us
    unnamed x61, local copies, waits for them, and re-layouts  14.7 us
    ppermute x1, waiting for transfers between devices, per_device(): returned = swap_slots(lax.ppermute(returned, 'mp', [(2, 0), (3, 1)]))  11 us
  transfers between devices with their start and end apart: 33, of which 27 were waited for; matrix products, arithmetic and copies ran while one was open for 14% of the time, Pallas kernels for 9%

profile of v1, /device:TPU:0, one launch (start us, length us, event | category | flops | bytes accessed | tf_op | source)
XLA Modules:
  0.0 481.4 jit_solution(4954547771852148532)
XLA Ops:
  7.2 1.8 copy.36
  9.2 4.1 collective-permute-start.3
  13.3 11.9 %collective-permute-done.3 = bf16[128,1024]{0,1:T(8,128)(2,1)S(1)} collective-permute-done((bf16[128,1024]{0,1:T(8,128)(2,1)S(1)}, bf16[128,1024]{0,1:T(8,128)(2,1)S(1)}, u32[]{:S(2)}, u32[]{:S(2)}) %collective-permute-start.3) | collective-permute-done | bytes 262176 | tf_op jit(solution)/shard_map/ppermute | solution.py:452
  27.2 25.2 %collective-permute-done.7 = bf16[256,1024]{1,0:T(8,128)(2,1)S(1)} collective-permute-done((bf16[256,1024]{1,0:T(8,128)(2,1)S(1)}, bf16[256,1024]{1,0:T(8,128)(2,1)S(1)}, u32[]{:S(2)}, u32[]{:S(2)}) %collective-permute-start.7) | collective-permute-done | bytes 524320 | tf_op jit(solution)/shard_map/ppermute | solution.py:452
  54.2 1.8 collective-permute-start.1
  56.7 8.4 %collective-permute-done.1 = f32[40,256]{1,0:T(8,128)S(1)} collective-permute-done((f32[40,256]{1,0:T(8,128)S(1)}, f32[40,256]{1,0:T(8,128)S(1)}, u32[]{:S(2)}, u32[]{:S(2)}) %collective-permute-start.1) | collective-permute-done | bytes 40992 | tf_op jit(solution)/shard_map/ppermute | solution.py:452
  68.8 6.0 %shard_map.203 = (f32[2,128,512]{2,1,0:T(8,128)}, f32[2,16,512]{2,1,0:T(8,128)}) custom-call(bf16[512,512]{1,0:T(8,128)(2,1)} %pad_maximum_fusion.2.x_ref, f32[16,512]{1,0:T(8,128)} %get-tuple-element.115.rate_ref, f32[16,512]{1,0:T(8,128)} %get-tuple-element.114.coef_ref, f32[1,512]{1,0:T(1,128)} %pad_maximum_fusion.13.skip_ref), custom_call_target="tpu_custom_call" | custom-call | flops 67108864 | bytes 1048576 | tf_op jit(solution)/shard_map/pallas_call | solution.py:37
  74.8 1.8 slice_bitcast_fusion.9
  77.4 4.5 collective-permute-start.2
  82.5 3.3 convolution_convert_fusion.1.qkv_ref
  87.4 2.6 shard_map.204
  90.0 1.6 fusion.47
  91.6 3.2 shard_map.205.refs_3_
  96.3 3.7 convolution_convert_fusion.qkv_ref
  100.0 3.2 shard_map.206.refs_5_
  103.2 1.6 convolution_add_fusion
  106.2 8.5 %collective-permute-start.4 = (bf16[256,1024]{1,0:T(8,128)(2,1)S(1)}, bf16[256,1024]{1,0:T(8,128)(2,1)S(1)}, u32[]{:S(2)}, u32[]{:S(2)}) collective-permute-start(bf16[256,1024]{1,0:T(8,128)(2,1)S(1)} %dynamic-slice_convert_fusion.1), channel_id=1, source_target_pairs={{0,1},{1,0},{2,3},{3,2},{4,5},{5,4},{6,7},{7,6},{8,9},{9,8},{10,11... | collective-permute-start | bytes 1572872 | tf_op jit(solution)/shard_map/ppermute | solution.py:452
  114.7 12.6 %collective-permute-done.4 = bf16[256,1024]{1,0:T(8,128)(2,1)S(1)} collective-permute-done((bf16[256,1024]{1,0:T(8,128)(2,1)S(1)}, bf16[256,1024]{1,0:T(8,128)(2,1)S(1)}, u32[]{:S(2)}, u32[]{:S(2)}) %collective-permute-start.4) | collective-permute-done | bytes 524320 | tf_op jit(solution)/shard_map/ppermute | solution.py:452
  129.4 2.1 collective-permute-start.5
  131.5 7.2 %collective-permute-done.6 = bf16[256,1024]{1,0:T(8,128)(2,1)} collective-permute-done((bf16[256,1024]{1,0:T(8,128)(2,1)}, bf16[256,1024]{1,0:T(8,128)(2,1)}, u32[]{:S(2)}, u32[]{:S(2)}) %collective-permute-start.6) | collective-permute-done | bytes 524320 | tf_op jit(solution)/shard_map/ppermute | solution.py:452
  138.7 2.3 pad_maximum_fusion.1.c_ref.refs_3_
  141.0 8.2 %collective-permute-done.5 = bf16[256,1024]{1,0:T(8,128)(2,1)S(1)} collective-permute-done((bf16[256,1024]{1,0:T(8,128)(2,1)S(1)}, bf16[256,1024]{1,0:T(8,128)(2,1)S(1)}, u32[]{:S(2)}, u32[]{:S(2)}) %collective-permute-start.5) | collective-permute-done | bytes 524320 | tf_op jit(solution)/shard_map/ppermute | solution.py:452
  150.3 4.8 %fusion.44 = (bf16[8,1,128,1024]{3,2,1,0:T(8,128)(2,1)}, bf16[8,1,128,1024]{3,2,1,0:T(8,128)(2,1)}) fusion(bf16[8,2,128,1024]{3,2,1,0:T(8,128)(2,1)} %bitcast.152), kind=kLoop, calls=%fused_computation.134 | loop fusion | bytes 8388608 | tf_op jit(solution)/shard_map/slice | solution.py:545
  155.1 15.9 %shard_map.207 = (bf16[512,2048]{1,0:T(8,128)(2,1)}, bf16[512,2048]{1,0:T(8,128)(2,1)}, f32[256,1024]{1,0:T(8,128)}, bf16[256,1024]{1,0:T(8,128)(2,1)}, f32[256,1024]{1,0:T(8,128)}, /*index=5*/bf16[256,1024]{1,0:T(8,128)(2,1)}) custom-call(bf16[512,1024]{1,0:T(8,128)(2,1)} %pad_maximum_fusion.n_ref.refs_0_, ...), custom_call_target="tpu_custom_call" | custom-call | flops 8589934592 | bytes 16777216 | tf_op jit(solution)/shard_map/pallas_call | solution.py:334
  171.0 1.8 collective-permute-start.9
  173.1 13.0 %collective-permute-done.9 = bf16[256,1024]{1,0:T(8,128)(2,1)S(1)} collective-permute-done((bf16[256,1024]{1,0:T(8,128)(2,1)}, bf16[256,1024]{1,0:T(8,128)(2,1)S(1)}, u32[]{:S(2)}, u32[]{:S(2)}) %collective-permute-start.9) | collective-permute-done | bytes 524320 | tf_op jit(solution)/shard_map/ppermute | solution.py:452
  186.2 1.7 multiply_reduce_fusion
  187.9 8.0 %collective-permute-done.8 = bf16[256,1024]{1,0:T(8,128)(2,1)S(1)} collective-permute-done((bf16[256,1024]{1,0:T(8,128)(2,1)}, bf16[256,1024]{1,0:T(8,128)(2,1)S(1)}, u32[]{:S(2)}, u32[]{:S(2)}) %collective-permute-start.8) | collective-permute-done | bytes 524320 | tf_op jit(solution)/shard_map/ppermute | solution.py:452
  195.9 2.7 fusion.40
  200.0 11.0 %collective-permute-done.10 = bf16[256,1024]{1,0:T(8,128)(2,1)S(1)} collective-permute-done((bf16[256,1024]{1,0:T(8,128)(2,1)S(1)}, bf16[256,1024]{1,0:T(8,128)(2,1)S(1)}, u32[]{:S(2)}, u32[]{:S(2)}) %collective-permute-start.10) | collective-permute-done | bytes 524320 | tf_op jit(solution)/shard_map/ppermute | solution.py:452
  212.6 2.2 convolution_convert_fusion.2.grad_ref
  214.9 4.6 shard_map.209
  219.4 4.6 shard_map.208
  224.0 10.8 %shard_map.213 = (bf16[2,4,128,1024]{3,2,1,0:T(8,128)(2,1)}, bf16[2,4,128,1024]{3,2,1,0:T(8,128)(2,1)}) custom-call(s32[1]{0:T(128)} %bitcast.21.place_ref, bf16[512,1024]{1,0:T(8,128)(2,1)} %copy-done.9, bf16[512,768]{1,0:T(8,128)(2,1)} %get-tuple-element.37.refs_1_, bf16[512,1024]{1,0:T(8,128)(2,1)} %copy-done.13, bf16[512,256]{1,0:T(8,128)(2,1)} %shard_map.205.refs_3_, ...), custom_call_target="tpu_custom_call" | custom-call | flops 2147483648 | bytes 8388608 | tf_op jit(solution)/shard_map/pallas_call | solution.py:37
  234.8 15.1 %shard_map.214 = (bf16[4,4,128,1024]{3,2,1,0:T(8,128)(2,1)}, bf16[4,4,128,1024]{3,2,1,0:T(8,128)(2,1)}) custom-call(s32[1]{0:T(128)} %bitcast.21.place_ref, bf16[512,1024]{1,0:T(8,128)(2,1)} %pad_maximum_fusion.n_ref.refs_0_, bf16[512,2048]{1,0:T(8,128)(2,1)} %get-tuple-element.47.refs_1_, bf16[512,2048]{1,0:T(8,128)(2,1)} %get-tuple-element.48.refs_2_, ...), custom_call_target="tpu_custom_call" | custom-call | flops 4294967296 | bytes 16777216 | tf_op jit(solution)/shard_map/pallas_call | solution.py:37
  255.2 11.3 %collective-permute-done.20 = bf16[2,128,1024]{2,1,0:T(8,128)(2,1)S(1)} collective-permute-done((bf16[2,128,1024]{2,1,0:T(8,128)(2,1)S(1)}, bf16[2,128,1024]{2,1,0:T(8,128)(2,1)S(1)}, u32[]{:S(2)}, u32[]{:S(2)}) %collective-permute-start.20) | collective-permute-done | bytes 524320 | tf_op jit(solution)/shard_map/ppermute | solution.py:455
  266.5 11.2 %collective-permute-done.22 = bf16[2,128,1024]{2,1,0:T(8,128)(2,1)S(1)} collective-permute-done((bf16[2,128,1024]{2,1,0:T(8,128)(2,1)S(1)}, bf16[2,128,1024]{2,1,0:T(8,128)(2,1)S(1)}, u32[]{:S(2)}, u32[]{:S(2)}) %collective-permute-start.22) | collective-permute-done | bytes 524320 | tf_op jit(solution)/shard_map/ppermute | solution.py:455
  279.4 3.5 collective-permute-start.23
  282.9 9.9 %collective-permute-done.23 = bf16[1,128,1024]{2,1,0:T(8,128)(2,1)S(1)} collective-permute-done((bf16[1,128,1024]{2,1,0:T(8,128)(2,1)S(1)}, bf16[1,128,1024]{2,1,0:T(8,128)(2,1)S(1)}, u32[]{:S(2)}, u32[]{:S(2)}) %collective-permute-start.23) | collective-permute-done | bytes 262176 | tf_op jit(solution)/shard_map/ppermute | solution.py:452
  293.6 6.0 %fusion.39 = (bf16[4,4,128,1024]{3,2,1,0:T(8,128)(2,1)S(1)}, f32[4,4,128,1024]{3,2,1,0:T(8,128)S(1)}) fusion(bf16[4,4,128,1024]{3,2,1,0:T(8,128)(2,1)} %collective-permute-done.24, bf16[4,4,128,1024]{3,2,1,0:T(8,128)(2,1)} %get-tuple-element.49), kind=kLoop, calls=%fused_computation.130 | loop fusion | flops 8388608 | bytes 20971520 | tf_op jit(solution)/shard_map/convert.5
  299.9 1.5 collective-permute-start.25
  303.4 31.0 %collective-permute-done.25 = bf16[4,128,1024]{2,1,0:T(8,128)(2,1)S(1)} collective-permute-done((bf16[4,128,1024]{2,1,0:T(8,128)(2,1)S(1)}, bf16[4,128,1024]{2,1,0:T(8,128)(2,1)S(1)}, u32[]{:S(2)}, u32[]{:S(2)}) %collective-permute-start.25) | collective-permute-done | bytes 1048608 | tf_op jit(solution)/shard_map/ppermute | solution.py:455
  334.5 21.0 %collective-permute-done.27 = bf16[4,128,1024]{2,1,0:T(8,128)(2,1)S(1)} collective-permute-done((bf16[4,128,1024]{2,1,0:T(8,128)(2,1)S(1)}, bf16[4,128,1024]{2,1,0:T(8,128)(2,1)S(1)}, u32[]{:S(2)}, u32[]{:S(2)}) %collective-permute-start.27) | collective-permute-done | bytes 1048608 | tf_op jit(solution)/shard_map/ppermute | solution.py:455
  357.7 25.2 %collective-permute-done.28 = bf16[2,128,1024]{2,1,0:T(8,128)(2,1)S(1)} collective-permute-done((bf16[2,128,1024]{2,1,0:T(8,128)(2,1)S(1)}, bf16[2,128,1024]{2,1,0:T(8,128)(2,1)S(1)}, u32[]{:S(2)}, u32[]{:S(2)}) %collective-permute-start.28) | collective-permute-done | bytes 524320 | tf_op jit(solution)/shard_map/ppermute | solution.py:452
  386.5 1.9 shard_map.210
  390.9 3.4 fusion.51
  394.4 11.0 %collective-permute-done.11 = f32[144,512]{1,0:T(8,128)S(1)} collective-permute-done((f32[144,512]{1,0:T(8,128)S(1)}, f32[144,512]{1,0:T(8,128)S(1)}, u32[]{:S(2)}, u32[]{:S(2)}) %collective-permute-start.11) | collective-permute-done | bytes 294944 | tf_op jit(solution)/shard_map/ppermute | solution.py:633
  406.8 6.3 %shard_map.211 = f32[512,512]{1,0:T(8,128)} custom-call(f32[128,512]{1,0:T(8,128)} %copy-done.8, f32[128,512]{1,0:T(8,128)} %fusion.31.far_ref, f32[16,512]{1,0:T(8,128)} %pad_maximum_fusion.11.enter_ref, f32[16,512]{1,0:T(8,128)} %get-tuple-element.115.rate_ref, f32[16,512]{1,0:T(8,128)} %get-tuple-element.114.coef_ref, f32[1,512]{1,0:T(1,128)} %pad_maximum_fusion.13.skip_ref), custom_call_target="tpu_custom_call" | custom-call | flops 16777216 | bytes 1048576 | tf_op jit(solution)/shard_map/pallas_call | solution.py:37
  413.1 1.5 select_select_fusion.3
  417.0 5.6 %shard_map.212 = (f32[2,16,512]{2,1,0:T(8,128)}, f32[1,512]{1,0:T(1,128)}) custom-call(bf16[512,512]{1,0:T(8,128)(2,1)} %pad_maximum_fusion.2.x_ref, f32[128,512]{1,0:T(8,128)} %copy-done.8, f32[128,512]{1,0:T(8,128)} %fusion.31.far_ref, f32[2,16,512]{2,1,0:T(8,128)} %bitcast.161, f32[16,512]{1,0:T(8,128)} %get-tuple-element.115.rate_ref, ...), custom_call_target="tpu_custom_call" | custom-call | flops 25165824 | bytes 1048576 | tf_op jit(solution)/shard_map/pallas_call | solution.py:37
  422.6 7.5 %collective-permute-done.12 = bf16[256,1024]{1,0:T(8,128)(2,1)S(1)} collective-permute-done((bf16[256,1024]{1,0:T(8,128)(2,1)S(1)}, bf16[256,1024]{1,0:T(8,128)(2,1)S(1)}, u32[]{:S(2)}, u32[]{:S(2)}) %collective-permute-start.12) | collective-permute-done | bytes 524320 | tf_op jit(solution)/shard_map/ppermute | solution.py:452
  431.1 3.3 collective-permute-done.14
  434.5 1.6 collective-permute-done.13
  436.1 2.9 collective-permute-done.15
  441.7 2.8 collective-permute-done.17
  444.9 2.6 fusion.18
  451.1 2.0 bitcast_convert_fusion.2
  453.1 2.0 copy-done.3
  455.1 2.0 slice.244
  457.1 3.5 copy.43
  460.6 3.5 copy.49
  466.8 2.7 fusion.43
  469.5 2.6 bitcast_convert_fusion
  472.1 2.6 bitcast_convert_fusion.1
  (167 shorter events, 52.3 us)
Async XLA Ops:
  7.2 1.9 copy-start
  7.2 89.1 %all-gather.6.cloned.1.call-start = ((), (), s32[]{:S(2)}) async-start(), calls=%async_computation | async-start | bytes 2359296 | tf_op jit(solution)/shard_map/all_gather | solution.py:458
  9.0 44.5 %copy-start.11 = (bf16[1024,3,256]{0,2,1:T(8,128)(2,1)}, bf16[1024,3,256]{0,2,1:T(8,128)(2,1)S(1)}, u32[]{:S(2)}) copy-start(bf16[1024,3,256]{0,2,1:T(8,128)(2,1)S(1)} %copy.36) | copy-start | bytes 4718596
  9.0 44.3 %copy-start.2 = (bf16[1,256,1024]{2,1,0:T(8,128)(2,1)S(1)}, bf16[1,256,1024]{2,1,0:T(8,128)(2,1)}, u32[]{:S(2)}) copy-start(bf16[1,256,1024]{2,1,0:T(8,128)(2,1)} %param.12) | copy-start | bytes 1572868
  9.2 44.6 %copy-start.22 = (f32[1024]{0:T(1024)S(1)}, f32[1024]{0:T(1024)}, u32[]{:S(2)}) copy-start(f32[1024]{0:T(1024)} %param.14) | copy-start | bytes 12292
  9.2 16.0 %collective-permute-start.3 = (bf16[128,1024]{0,1:T(8,128)(2,1)S(1)}, bf16[128,1024]{0,1:T(8,128)(2,1)S(1)}, u32[]{:S(2)}, u32[]{:S(2)}) collective-permute-start(bf16[128,1024]{0,1:T(8,128)(2,1)S(1)} %pad_maximum_fusion.6), channel_id=1, source_target_pairs={{0,2},{1,3},{2,0},{3,1},{4,6},{5,7},{6,4},{7,5},{8,10},{9,11},{10,... | collective-permute-start | bytes 786440 | tf_op jit(solution)/shard_map/ppermute | solution.py:452
  25.2 0.7 copy-start.17
  25.9 124.3 %all-gather.8.cloned.1.call-start = ((), (), s32[]{:S(2)}) async-start(), calls=%async_computation.1 | async-start | bytes 4718592 | tf_op jit(solution)/shard_map/all_gather | solution.py:458
  27.1 27.1 %copy-start.18 = (f32[256,16]{0,1:T(8,128)S(1)}, f32[256,16]{0,1:T(8,128)}, u32[]{:S(2)}) copy-start(f32[256,16]{0,1:T(8,128)} %param.17) | copy-start | bytes 49156
  27.1 27.1 %copy-start.19 = (f32[256,16]{0,1:T(8,128)S(1)}, f32[256,16]{0,1:T(8,128)}, u32[]{:S(2)}) copy-start(f32[256,16]{0,1:T(8,128)} %param.16) | copy-start | bytes 49156
  27.1 27.1 %copy-start.23 = (f32[256]{0:T(256)S(1)}, f32[256]{0:T(256)}, u32[]{:S(2)}) copy-start(f32[256]{0:T(256)} %param.18) | copy-start | bytes 3076
  27.1 25.3 %collective-permute-start.7 = (bf16[256,1024]{1,0:T(8,128)(2,1)S(1)}, bf16[256,1024]{1,0:T(8,128)(2,1)S(1)}, u32[]{:S(2)}, u32[]{:S(2)}) collective-permute-start(bf16[256,1024]{1,0:T(8,128)(2,1)S(1)} %pad_maximum_fusion.3), channel_id=1, source_target_pairs={{0,2},{1,3},{2,0},{3,1},{4,6},{5,7},{6,4},{7,5},{8,10},{9,11},{10,... | collective-permute-start | bytes 1572872 | tf_op jit(solution)/shard_map/ppermute | solution.py:452
  52.5 0.8 copy-start.15
  53.3 397.8 %all-gather.12.cloned.1.call-start = ((), (), s32[]{:S(2)}) async-start(), calls=%async_computation.3 | async-start | bytes 2359296 | tf_op jit(solution)/shard_map/all_gather | solution.py:458
  54.1 13.1 %collective-permute-start = (bf16[256,1024]{1,0:T(8,128)(2,1)S(1)}, bf16[256,1024]{1,0:T(8,128)(2,1)S(1)}, u32[]{:S(2)}, u32[]{:S(2)}) collective-permute-start(bf16[256,1024]{1,0:T(8,128)(2,1)S(1)} %fusion.13), channel_id=1, source_target_pairs={{0,1},{1,0},{2,3},{3,2},{4,5},{5,4},{6,7},{7,6},{8,9},{9,8},{10,11... | collective-permute-start | bytes 1572872 | tf_op jit(solution)/shard_map/ppermute | solution.py:452
  54.2 10.8 %collective-permute-start.1 = (f32[40,256]{1,0:T(8,128)S(1)}, f32[40,256]{1,0:T(8,128)S(1)}, u32[]{:S(2)}, u32[]{:S(2)}) collective-permute-start(f32[40,256]{1,0:T(8,128)S(1)} %pad_maximum_fusion.10), channel_id=1, source_target_pairs={{0,2},{1,3},{2,0},{3,1},{4,6},{5,7},{6,4},{7,5},{8,10},{9,11},{10,... | collective-permute-start | bytes 122888 | tf_op jit(solution)/shard_map/ppermute | solution.py:452
  67.7 14.8 %copy-start.9 = (bf16[512,1024]{1,0:T(8,128)(2,1)}, bf16[512,1024]{1,0:T(8,128)(2,1)S(1)}, u32[]{:S(2)}) copy-start(bf16[512,1024]{1,0:T(8,128)(2,1)S(1)} %maximum_select_fusion.refs_0_) | copy-start | bytes 3145732
  77.4 9.4 %collective-permute-start.2 = (f32[160,512]{1,0:T(8,128)S(1)}, f32[160,512]{1,0:T(8,128)S(1)}, u32[]{:S(2)}, u32[]{:S(2)}) collective-permute-start(f32[160,512]{1,0:T(8,128)S(1)} %pad_maximum_fusion.5), channel_id=1, source_target_pairs={{0,2},{1,3},{4,6},{5,7},{8,10},{9,11},{12,14},{13,15},{16,18},{17,... | collective-permute-start | bytes 983048 | tf_op jit(solution)/shard_map/ppermute | solution.py:528
  104.8 1.3 copy-start.4
  106.2 21.2 %collective-permute-start.4 = (bf16[256,1024]{1,0:T(8,128)(2,1)S(1)}, bf16[256,1024]{1,0:T(8,128)(2,1)S(1)}, u32[]{:S(2)}, u32[]{:S(2)}) collective-permute-start(bf16[256,1024]{1,0:T(8,128)(2,1)S(1)} %dynamic-slice_convert_fusion.1), channel_id=1, source_target_pairs={{0,1},{1,0},{2,3},{3,2},{4,5},{5,4},{6,7},{7,6},{8,9},{9,8},{10,11... | collective-permute-start | bytes 1572872 | tf_op jit(solution)/shard_map/ppermute | solution.py:452
  114.7 24.1 %collective-permute-start.6 = (bf16[256,1024]{1,0:T(8,128)(2,1)}, bf16[256,1024]{1,0:T(8,128)(2,1)}, u32[]{:S(2)}, u32[]{:S(2)}) collective-permute-start(bf16[256,1024]{1,0:T(8,128)(2,1)} %bitcast.11), channel_id=1, source_target_pairs={{0,1},{1,0},{2,3},{3,2},{4,5},{5,4},{6,7},{7,6},{8,9},{9,8},{10,11... | collective-permute-start | bytes 1572872 | tf_op jit(solution)/shard_map/ppermute | solution.py:452
  114.7 14.4 %copy-start.21 = (f32[1024]{0:T(1024)S(1)}, f32[1024]{0:T(1024)}, u32[]{:S(2)}) copy-start(f32[1024]{0:T(1024)} %param.20) | copy-start | bytes 12292
  129.4 19.9 %collective-permute-start.5 = (bf16[256,1024]{1,0:T(8,128)(2,1)S(1)}, bf16[256,1024]{1,0:T(8,128)(2,1)S(1)}, u32[]{:S(2)}, u32[]{:S(2)}) collective-permute-start(bf16[256,1024]{1,0:T(8,128)(2,1)S(1)} %multiply_convert_fusion), channel_id=1, source_target_pairs={{0,1},{1,0},{2,3},{3,2},{4,5},{5,4},{6,7},{7,6},{8,9},{9,8},{10,11... | collective-permute-start | bytes 1572872 | tf_op jit(solution)/shard_map/ppermute | solution.py:452
  171.0 24.9 %copy-start.6 = (f32[256,1024]{1,0:T(8,128)S(1)}, f32[256,1024]{1,0:T(8,128)}, u32[]{:S(2)}) copy-start(f32[256,1024]{1,0:T(8,128)} %get-tuple-element.35) | copy-start | bytes 3145732
  171.0 24.8 %copy-start.14 = (f32[256,1024]{1,0:T(8,128)S(1)}, f32[256,1024]{1,0:T(8,128)}, u32[]{:S(2)}) copy-start(f32[256,1024]{1,0:T(8,128)} %get-tuple-element.33) | copy-start | bytes 3145732
  171.0 15.1 %collective-permute-start.9 = (bf16[256,1024]{1,0:T(8,128)(2,1)}, bf16[256,1024]{1,0:T(8,128)(2,1)S(1)}, u32[]{:S(2)}, u32[]{:S(2)}) collective-permute-start(bf16[256,1024]{1,0:T(8,128)(2,1)} %get-tuple-element.36), channel_id=1, source_target_pairs={{0,1},{1,0},{2,3},{3,2},{4,5},{5,4},{6,7},{7,6},{8,9},{9,8},{10,11... | collective-permute-start | bytes 1572872 | tf_op jit(solution)/shard_map/ppermute | solution.py:452
  172.8 23.0 %collective-permute-start.8 = (bf16[256,1024]{1,0:T(8,128)(2,1)}, bf16[256,1024]{1,0:T(8,128)(2,1)S(1)}, u32[]{:S(2)}, u32[]{:S(2)}) collective-permute-start(bf16[256,1024]{1,0:T(8,128)(2,1)} %get-tuple-element.34), channel_id=1, source_target_pairs={{0,1},{1,0},{2,3},{3,2},{4,5},{5,4},{6,7},{7,6},{8,9},{9,8},{10,11... | collective-permute-start | bytes 1572872 | tf_op jit(solution)/shard_map/ppermute | solution.py:452
  198.6 12.4 %collective-permute-start.10 = (bf16[256,1024]{1,0:T(8,128)(2,1)S(1)}, bf16[256,1024]{1,0:T(8,128)(2,1)S(1)}, u32[]{:S(2)}, u32[]{:S(2)}) collective-permute-start(bf16[256,1024]{1,0:T(8,128)(2,1)S(1)} %get-tuple-element.79), channel_id=1, source_target_pairs={{0,1},{1,0},{2,3},{3,2},{4,5},{5,4},{6,7},{7,6},{8,9},{9,8},{10,11... | collective-permute-start | bytes 1572872 | tf_op jit(solution)/shard_map/ppermute | solution.py:452
  211.4 8.0 %copy-start.13 = (bf16[512,1024]{1,0:T(8,128)(2,1)}, bf16[512,1024]{1,0:T(8,128)(2,1)S(1)}, u32[]{:S(2)}) copy-start(bf16[512,1024]{1,0:T(8,128)(2,1)S(1)} %maximum_select_fusion.1.refs_2_) | copy-start | bytes 3145732
  234.8 15.5 %collective-permute-start.19 = (bf16[2,4,128,1024]{3,2,1,0:T(8,128)(2,1)}, bf16[2,4,128,1024]{3,2,1,0:T(8,128)(2,1)S(1)}, u32[]{:S(2)}, u32[]{:S(2)}) collective-permute-start(bf16[2,4,128,1024]{3,2,1,0:T(8,128)(2,1)} %get-tuple-element.46), channel_id=1, source_target_pairs={{0,4},{4,0},{8,12},{12,8},{16,20},{20,16},{24,28},{28,24},{1,5},{5... | collective-permute-start | bytes 6291464 | tf_op jit(solution)/shard_map/ppermute | solution.py:455
  234.8 15.5 %copy-start.10 = (bf16[2,4,128,1024]{3,2,1,0:T(8,128)(2,1)S(1)}, bf16[2,4,128,1024]{3,2,1,0:T(8,128)(2,1)}, u32[]{:S(2)}) copy-start(bf16[2,4,128,1024]{3,2,1,0:T(8,128)(2,1)} %get-tuple-element.45) | copy-start | bytes 6291460
  249.9 43.7 %collective-permute-start.24 = (bf16[4,4,128,1024]{3,2,1,0:T(8,128)(2,1)}, bf16[4,4,128,1024]{3,2,1,0:T(8,128)(2,1)}, u32[]{:S(2)}, u32[]{:S(2)}) collective-permute-start(bf16[4,4,128,1024]{3,2,1,0:T(8,128)(2,1)} %get-tuple-element.50), channel_id=1, source_target_pairs={{0,4},{4,0},{8,12},{12,8},{16,20},{20,16},{24,28},{28,24},{1,5},{5... | collective-permute-start | bytes 12582920 | tf_op jit(solution)/shard_map/ppermute | solution.py:455
  251.7 14.8 %collective-permute-start.20 = (bf16[2,128,1024]{2,1,0:T(8,128)(2,1)S(1)}, bf16[2,128,1024]{2,1,0:T(8,128)(2,1)S(1)}, u32[]{:S(2)}, u32[]{:S(2)}) collective-permute-start(bf16[2,128,1024]{2,1,0:T(8,128)(2,1)S(1)} %get-tuple-element.94), channel_id=1, source_target_pairs={{0,8},{4,12},{8,0},{12,4},{16,24},{20,28},{24,16},{28,20},{1,9},{5... | collective-permute-start | bytes 1572872 | tf_op jit(solution)/shard_map/ppermute | solution.py:455
  253.0 24.6 %collective-permute-start.22 = (bf16[2,128,1024]{2,1,0:T(8,128)(2,1)S(1)}, bf16[2,128,1024]{2,1,0:T(8,128)(2,1)S(1)}, u32[]{:S(2)}, u32[]{:S(2)}) collective-permute-start(bf16[2,128,1024]{2,1,0:T(8,128)(2,1)S(1)} %get-tuple-element.95), channel_id=1, source_target_pairs={{0,24},{4,28},{8,16},{12,20},{16,8},{20,12},{24,0},{28,4},{1,25},{... | collective-permute-start | bytes 1572872 | tf_op jit(solution)/shard_map/ppermute | solution.py:455
  254.5 24.5 %collective-permute-start.21 = (bf16[2,128,1024]{2,1,0:T(8,128)(2,1)S(1)}, bf16[2,128,1024]{2,1,0:T(8,128)(2,1)S(1)}, u32[]{:S(2)}, u32[]{:S(2)}) collective-permute-start(bf16[2,128,1024]{2,1,0:T(8,128)(2,1)S(1)} %get-tuple-element.96), channel_id=1, source_target_pairs={{0,16},{4,20},{8,24},{12,28},{16,0},{20,4},{24,8},{28,12},{1,17},{... | collective-permute-start | bytes 1572872 | tf_op jit(solution)/shard_map/ppermute | solution.py:455
  279.4 13.3 %collective-permute-start.23 = (bf16[1,128,1024]{2,1,0:T(8,128)(2,1)S(1)}, bf16[1,128,1024]{2,1,0:T(8,128)(2,1)S(1)}, u32[]{:S(2)}, u32[]{:S(2)}) collective-permute-start(bf16[1,128,1024]{2,1,0:T(8,128)(2,1)S(1)} %slice.336), channel_id=1, source_target_pairs={{0,2},{1,3},{2,0},{3,1},{4,6},{5,7},{6,4},{7,5},{8,10},{9,11},{10,... | collective-permute-start | bytes 786440 | tf_op jit(solution)/shard_map/ppermute | solution.py:452
  293.5 173.2 %all-gather.10.cloned.1.call-start = ((), (), s32[]{:S(2)}) async-start(), calls=%async_computation.2 | async-start | bytes 4718592 | tf_op jit(solution)/shard_map/all_gather | solution.py:458
  299.9 34.6 %collective-permute-start.25 = (bf16[4,128,1024]{2,1,0:T(8,128)(2,1)S(1)}, bf16[4,128,1024]{2,1,0:T(8,128)(2,1)S(1)}, u32[]{:S(2)}, u32[]{:S(2)}) collective-permute-start(bf16[4,128,1024]{2,1,0:T(8,128)(2,1)S(1)} %get-tuple-element.87), channel_id=1, source_target_pairs={{0,8},{4,12},{8,0},{12,4},{16,24},{20,28},{24,16},{28,20},{1,9},{5... | collective-permute-start | bytes 3145736 | tf_op jit(solution)/shard_map/ppermute | solution.py:455
  301.4 54.1 %collective-permute-start.27 = (bf16[4,128,1024]{2,1,0:T(8,128)(2,1)S(1)}, bf16[4,128,1024]{2,1,0:T(8,128)(2,1)S(1)}, u32[]{:S(2)}, u32[]{:S(2)}) collective-permute-start(bf16[4,128,1024]{2,1,0:T(8,128)(2,1)S(1)} %get-tuple-element.88), channel_id=1, source_target_pairs={{0,24},{4,28},{8,16},{12,20},{16,8},{20,12},{24,0},{28,4},{1,25},{... | collective-permute-start | bytes 3145736 | tf_op jit(solution)/shard_map/ppermute | solution.py:455
  302.1 54.8 %collective-permute-start.26 = (bf16[4,128,1024]{2,1,0:T(8,128)(2,1)S(1)}, bf16[4,128,1024]{2,1,0:T(8,128)(2,1)S(1)}, u32[]{:S(2)}, u32[]{:S(2)}) collective-permute-start(bf16[4,128,1024]{2,1,0:T(8,128)(2,1)S(1)} %get-tuple-element.89), channel_id=1, source_target_pairs={{0,16},{4,20},{8,24},{12,28},{16,0},{20,4},{24,8},{28,12},{1,17},{... | collective-permute-start | bytes 3145736 | tf_op jit(solution)/shard_map/ppermute | solution.py:455
  357.7 33.3 %copy-start.12 = (bf16[1024,3,256]{0,2,1:T(8,128)(2,1)S(1)}, bf16[1024,3,256]{0,2,1:T(8,128)(2,1)}, u32[]{:S(2)}) copy-start(bf16[1024,3,256]{0,2,1:T(8,128)(2,1)} %copy-done.11) | copy-start | bytes 4718596
  357.7 25.3 %collective-permute-start.28 = (bf16[2,128,1024]{2,1,0:T(8,128)(2,1)S(1)}, bf16[2,128,1024]{2,1,0:T(8,128)(2,1)S(1)}, u32[]{:S(2)}, u32[]{:S(2)}) collective-permute-start(bf16[2,128,1024]{2,1,0:T(8,128)(2,1)S(1)} %slice.335), channel_id=1, source_target_pairs={{0,2},{1,3},{2,0},{3,1},{4,6},{5,7},{6,4},{7,5},{8,10},{9,11},{10,... | collective-permute-start | bytes 1572872 | tf_op jit(solution)/shard_map/ppermute | solution.py:452
  385.8 0.7 copy-start.8
  389.4 15.9 %collective-permute-start.11 = (f32[144,512]{1,0:T(8,128)S(1)}, f32[144,512]{1,0:T(8,128)S(1)}, u32[]{:S(2)}, u32[]{:S(2)}) collective-permute-start(f32[144,512]{1,0:T(8,128)S(1)} %maximum_maximum_fusion), channel_id=1, source_target_pairs={{2,0},{3,1},{6,4},{7,5},{10,8},{11,9},{14,12},{15,13},{18,16},{19,... | collective-permute-start | bytes 884744 | tf_op jit(solution)/shard_map/ppermute | solution.py:633
  406.0 8.6 %copy-start.26 = (bf16[512,768]{1,0:T(8,128)(2,1)S(1)}, bf16[512,768]{1,0:T(8,128)(2,1)}, u32[]{:S(2)}) copy-start(bf16[512,768]{1,0:T(8,128)(2,1)} %get-tuple-element.38.refs_4_) | copy-start | bytes 2359300
  406.8 7.8 %copy-start.20 = (bf16[1024,1024]{0,1:T(8,128)(2,1)S(1)}, bf16[1024,1024]{0,1:T(8,128)(2,1)}, u32[]{:S(2)}) copy-start(bf16[1024,1024]{0,1:T(8,128)(2,1)} %all-gather.6.cloned.1.call-done) | copy-start | bytes 6291460
  413.1 1.9 copy-start.25
  416.1 14.6 %copy-start.7 = (f32[512,1024]{1,0:T(8,128)}, f32[512,1024]{1,0:T(8,128)S(1)}, u32[]{:S(2)}) copy-start(f32[512,1024]{1,0:T(8,128)S(1)} %maximum_add_fusion) | copy-start | bytes 6291460
  416.2 13.9 %collective-permute-start.12 = (bf16[256,1024]{1,0:T(8,128)(2,1)S(1)}, bf16[256,1024]{1,0:T(8,128)(2,1)S(1)}, u32[]{:S(2)}, u32[]{:S(2)}) collective-permute-start(bf16[256,1024]{1,0:T(8,128)(2,1)S(1)} %dynamic-slice_convert_fusion), channel_id=1, source_target_pairs={{0,1},{1,0},{2,3},{3,2},{4,5},{5,4},{6,7},{7,6},{8,9},{9,8},{10,11... | collective-permute-start | bytes 1572872 | tf_op jit(solution)/shard_map/ppermute | solution.py:452
  417.0 27.8 %copy-start.5 = (f32[256,1024]{1,0:T(8,128)S(1)}, f32[256,1024]{1,0:T(8,128)}, u32[]{:S(2)}) copy-start(f32[256,1024]{1,0:T(8,128)} %get-tuple-element.80) | copy-start | bytes 3145732
  422.6 8.4 %copy-start.16 = (f32[2,16,512]{2,1,0:T(8,128)S(1)}, f32[2,16,512]{2,1,0:T(8,128)}, u32[]{:S(2)}) copy-start(f32[2,16,512]{2,1,0:T(8,128)} %get-tuple-element.43) | copy-start | bytes 196612
  422.6 8.4 %copy-start.24 = (f32[1,512]{1,0:T(1,128)S(1)}, f32[1,512]{1,0:T(1,128)}, u32[]{:S(2)}) copy-start(f32[1,512]{1,0:T(1,128)} %get-tuple-element.44) | copy-start | bytes 6148
  430.6 3.7 collective-permute-start.14
  431.0 5.1 %collective-permute-start.13 = (f32[33,256]{1,0:T(8,128)S(1)}, f32[33,256]{1,0:T(8,128)S(1)}, u32[]{:S(2)}, u32[]{:S(2)}) collective-permute-start(f32[33,256]{1,0:T(8,128)S(1)} %pad_maximum_fusion.9), channel_id=1, source_target_pairs={{0,2},{1,3},{2,0},{3,1},{4,6},{5,7},{6,4},{7,5},{8,10},{9,11},{10,... | collective-permute-start | bytes 101384 | tf_op jit(solution)/shard_map/ppermute | solution.py:452
  434.4 4.6 collective-permute-start.15
  439.0 1.3 collective-permute-start.16
  440.3 4.2 collective-permute-start.17
  444.5 4.2 collective-permute-start.18
  453.1 2.0 copy-start.3
  472.1 2.6 copy-start.1
Sparse Core Ops, SparseCore 0:
  26.1 29.3 all-gather.5
  57.9 36.7 all-gather.7
  293.7 36.1 all-gather.11
  384.1 34.8 all-gather.9

commit v2 on v1

v2 whole, which is shorter than its diff:
```python
from functools import partial
import math

import jax
import jax.numpy as jnp
from jax import lax
from jax.experimental import pallas as pl
from jax.experimental.pallas import tpu as pltpu
from jax.sharding import PartitionSpec as P

HD = 128
CTX = 128
HALF = 256
STATES = 16
GROUP = 8

f32 = jnp.float32
bf16 = jnp.bfloat16
epsilon = 1e-05
masked_score = -1e30
score_scale = 1.0 / math.sqrt(HD)
VMEM_LIMIT = 16 * 1024 * 1024

NT = (((1,), (1,)), ((), ()))
TN = (((0,), (0,)), ((), ()))
NN = (((1,), (0,)), ((), ()))

WHOLE, LATE, ODD, NEAR, FAR, PLACE = range(6)


def mm(a, b, dims=NN):
    return lax.dot_general(a, b, dims, preferred_element_type=f32)


def shape(dims, dtype=f32):
    return jax.ShapeDtypeStruct(dims, dtype)


def call(kernel, out_shape, scratch=()):
    def run(flags, *args):
        vmem = pl.BlockSpec(memory_space=pltpu.VMEM)
        return pl.pallas_call(
            kernel,
            out_shape=out_shape,
            in_specs=[pl.BlockSpec(memory_space=pltpu.SMEM)] + [vmem] * len(args),
            out_specs=jax.tree.map(lambda _: vmem, out_shape),
            scratch_shapes=scratch,
            compiler_params=pltpu.CompilerParams(vmem_limit_bytes=VMEM_LIMIT),
            cost_estimate=pl.CostEstimate(flops=0, bytes_accessed=0, transcendentals=0),
        )(flags, *args)

    return run


SENT = (1, 5, 3, 7, 0, 4, 2, 6)


def in_sent_order(flag_ref, value_ref, out_ref, masks=SENT):
    width = value_ref.shape[1] // GROUP
    for k, mask in enumerate(masks):
        source = jnp.bitwise_xor(flag_ref[PLACE], mask)
        out_ref[:, k * width : (k + 1) * width] = value_ref[:, aligned(source * width, width)]


def aligned(start, size):
    return pl.ds(pl.multiple_of(start, size), size)


def cut_slices(flag_ref, qkv_ref, out_ref, up_ref, down_ref, attn_ref, mlp_ref):
    channels = qkv_ref.shape[2]
    rows = attn_ref.shape[0]
    for part in range(3):
        attn_ref[:, part * channels : (part + 1) * channels] = qkv_ref[part]
    attn_ref[:, 3 * channels :] = out_ref[...].T
    mlp_ref[:rows, :] = up_ref[...]
    mlp_ref[rows:, :] = down_ref[...]


def run_cut_slices(flags, qkv_parts, out_weight, up_weight, down_weight):
    channels = qkv_parts.shape[2]
    width = out_weight.shape[1]
    rows = width // GROUP
    here = lambda j, flag_ref: (flag_ref[PLACE], 0)
    return pl.pallas_call(
        cut_slices,
        grid_spec=pltpu.PrefetchScalarGridSpec(
            num_scalar_prefetch=1,
            grid=(1,),
            in_specs=[
                pl.BlockSpec((3, rows, channels), lambda j, flag_ref: (0, flag_ref[PLACE], 0)),
                pl.BlockSpec((channels, rows), lambda j, flag_ref: (0, flag_ref[PLACE])),
                pl.BlockSpec((rows, width), here),
                pl.BlockSpec((rows, width), here),
            ],
            out_specs=(
                pl.BlockSpec((rows, 4 * channels), lambda j, flag_ref: (0, 0)),
                pl.BlockSpec((2 * rows, width), lambda j, flag_ref: (0, 0)),
            ),
        ),
        out_shape=(shape((rows, 4 * channels), bf16), shape((2 * rows, width), bf16)),
        compiler_params=pltpu.CompilerParams(vmem_limit_bytes=VMEM_LIMIT),
        cost_estimate=pl.CostEstimate(flops=0, bytes_accessed=0, transcendentals=0),
    )(flags, qkv_parts, out_weight, up_weight, down_weight)


def normalise(values):
    mean = jnp.mean(values, axis=-1, keepdims=True)
    centred = values - mean
    spread = jnp.mean(centred * centred, axis=-1, keepdims=True)
    inverse = lax.rsqrt(spread + epsilon)
    return centred * inverse, inverse


def normalise_back(grad, gain, hat, inverse):
    inner = grad * gain
    return (
        inner
        - jnp.mean(inner, axis=-1, keepdims=True)
        - hat * jnp.mean(inner * hat, axis=-1, keepdims=True)
    ) * inverse


def by_rows(body, rows, block=64):
    for k in range(rows // block):
        body(slice(k * block, (k + 1) * block))


def norm_one(flag_ref, x_ref, gain_ref, out_ref):
    def body(at):
        hat, _ = normalise(x_ref[at, :].astype(f32))
        out_ref[at, :] = (hat * gain_ref[...]).astype(bf16)

    by_rows(body, x_ref.shape[0])


def norm_two(flag_ref, x_ref, own_ref, received_ref, gain_ref, middle_ref, out_ref):
    def body(at):
        middle = x_ref[at, :].astype(f32) + own_ref[at, :] + received_ref[at, :].astype(f32)
        middle_ref[at, :] = middle
        hat, _ = normalise(middle)
        out_ref[at, :] = (hat * gain_ref[...]).astype(bf16)

    by_rows(body, x_ref.shape[0])


def norm_two_back(
    flag_ref, middle_ref, own_ref, received_ref, cot_ref, gain_ref, grad_ref, low_ref, gain_out_ref
):
    sums = []

    def body(at):
        hat, inverse = normalise(middle_ref[at, :])
        grad = own_ref[at, :] + received_ref[at, :].astype(f32)
        sums.append(jnp.sum(grad * hat, axis=0, keepdims=True))
        total = cot_ref[at, :].astype(f32) + normalise_back(grad, gain_ref[...], hat, inverse)
        grad_ref[at, :] = total
        low_ref[at, :] = total.astype(bf16)

    by_rows(body, middle_ref.shape[0])
    gain_out_ref[...] = sum(sums)


def norm_one_back(
    flag_ref, x_ref, own_ref, received_ref, middle_ref, gain_ref, gain_two_grad_ref, grad_ref,
    gain_out_ref,
):
    sums = []

    def body(at):
        hat, inverse = normalise(x_ref[at, :].astype(f32))
        grad = own_ref[at, :] + received_ref[at, :].astype(f32)
        sums.append(jnp.sum(grad * hat, axis=0, keepdims=True))
        grad_ref[at, :] = middle_ref[at, :] + normalise_back(grad, gain_ref[...], hat, inverse)

    by_rows(body, x_ref.shape[0])
    width = gain_out_ref.shape[1]
    pieces = x_ref.shape[1] // width
    for which, value in enumerate((sum(sums), gain_two_grad_ref[...])):
        for k in range(pieces):
            row = which * pieces + k
            gain_out_ref[row : row + 1, :] = value[:, k * width : (k + 1) * width]


def split_three(value):
    high = value.astype(bf16)
    rest = value - high.astype(f32)
    middle = rest.astype(bf16)
    return [high, middle, (rest - middle.astype(f32)).astype(bf16)]


def join_three(ref, start, lanes):
    parts = [ref[start + k * STATES : start + (k + 1) * STATES, lanes] for k in range(3)]
    return (parts[0].astype(f32) + parts[1].astype(f32)) + parts[2].astype(f32)


def load_signal(flag_ref, tile_ref, xs):
    channels = xs.shape[1] // 2
    for half in range(2):
        source = jnp.bitwise_xor(flag_ref[ODD], half)
        for slot, name in enumerate((NEAR, FAR)):
            xs[half * HALF : (half + 1) * HALF, slot * channels : (slot + 1) * channels] = tile_ref[
                source, :, aligned(flag_ref[name] * channels, channels)
            ].astype(f32)


def ssm_forward(
    flag_ref, own_ref, other_ref, rate_ref, coef_ref, skip_ref, tile_ref, sent_ref,
    second_ref, handed_ref, xs,
):
    tile_ref[0] = own_ref[...]
    tile_ref[1] = other_ref[...]
    in_sent_order(flag_ref, own_ref, sent_ref.at[0])
    in_sent_order(flag_ref, other_ref, sent_ref.at[1])
    load_signal(flag_ref, tile_ref, xs)
    decay = jnp.exp(-rate_ref[...])
    coef = coef_ref[...]
    skip = skip_ref[...]
    zero = jnp.zeros_like(decay)

    def step(eight, carry, chunk):
        state, slope = carry
        x8 = xs[aligned((chunk * 16 + eight) * 8, 8), :]
        rows = []
        for k in range(8):
            slope = decay * (slope + state)
            state = decay * state + x8[k : k + 1]
            if chunk % 2:
                rows.append(jnp.sum(coef * state, axis=0, keepdims=True))
        if chunk % 2:
            y8 = jnp.concatenate(rows, axis=0) + skip * x8
            at = aligned(eight * 8, 8)
            if chunk == 1:
                second_ref[at, :] = y8
            else:
                xs[at, :] = y8
        return state, slope

    carry = (zero, zero)
    for chunk in range(4):
        carry = lax.fori_loop(0, 16, partial(step, chunk=chunk), carry)
    handed_ref[:CTX, :] = xs[:CTX, :].astype(bf16)
    for k, part in enumerate(split_three(carry[0]) + split_three(carry[1])):
        handed_ref[CTX + k * STATES : CTX + (k + 1) * STATES, :] = part


def project(flag_ref, tile_ref, weight_ref, qkv_ref):
    for half in range(2):
        qkv_ref[half] = mm(tile_ref[half], weight_ref[...]).astype(bf16)


def ssm_carry_in(
    flag_ref, local_ref, handed_ref, rate_ref, coef_ref, first_ref, second_ref, enter_ref, acc
):
    channels = rate_ref.shape[1] // 2
    for slot in range(2):
        to = slice(slot * channels, (slot + 1) * channels)
        source = slice((1 - slot) * channels, (2 - slot) * channels)
        first_ref[:, to] = handed_ref[:CTX, source]
        enter_ref[0, :, to] = join_three(handed_ref, CTX, source)
        enter_ref[1, :, to] = join_three(handed_ref, CTX + 3 * STATES, source)
    rate = rate_ref[...]
    decay = jnp.exp(-rate)
    coef = coef_ref[...]

    def step(eight, state):
        rows = []
        for k in range(8):
            rows.append(jnp.sum(coef * state, axis=0, keepdims=True))
            state = decay * state
        acc[aligned(eight * 8, 8), :] = jnp.concatenate(rows, axis=0)
        return state

    lax.fori_loop(0, 16, step, enter_ref[0] * jnp.exp(-129.0 * rate))
    second_ref[...] = (local_ref[...] + acc[...]).astype(bf16)


def ssm_signal_grad(
    flag_ref, near_ref, returned_ref, rate_ref, coef_ref, skip_ref, dqkv_ref, near_weight_ref,
    far_weight_ref, own_ref, send_ref, last_ref, rows_out, total,
):
    channels = rate_ref.shape[1] // 2
    adjoints = []
    for slot in range(2):
        to = slice(slot * channels, (slot + 1) * channels)
        source = slice((1 - slot) * channels, (2 - slot) * channels)
        last_ref[:, to] = returned_ref[:CTX, source].astype(f32)
        adjoints.append(join_three(returned_ref, CTX, source))
    decay = jnp.exp(-rate_ref[...])
    coef = coef_ref[...]
    skip = skip_ref[...]

    def step(j, adjoint, chunk):
        eight = 15 - j
        at = aligned(eight * 8, 8)
        if chunk % 2:
            g8 = (near_ref, last_ref)[chunk // 2][at, :]
        rows = [None] * 8
        for k in range(7, -1, -1):
            adjoint = decay * adjoint
            if chunk % 2:
                adjoint = adjoint + g8[k : k + 1]
            rows[k] = jnp.sum(coef * adjoint, axis=0, keepdims=True)
        y8 = jnp.concatenate(rows, axis=0)
        if chunk % 2:
            y8 = y8 + skip * g8
        rows_out[aligned((chunk * 16 + eight) * 8, 8), :] = y8
        return adjoint

    adjoint = jnp.concatenate(adjoints, axis=1)
    for chunk in (3, 2, 1, 0):
        adjoint = lax.fori_loop(0, 16, partial(step, chunk=chunk), adjoint)
    split = near_weight_ref.shape[1]
    for half in (1, 0):
        total[...] = mm(dqkv_ref[half, :, :split], near_weight_ref[...], NT) + mm(
            dqkv_ref[half, :, split:], far_weight_ref[...], NT
        )
        source = aligned(jnp.bitwise_xor(flag_ref[ODD], half) * HALF, HALF)
        for slot, name in enumerate((NEAR, FAR)):
            total[:, aligned(flag_ref[name] * channels, channels)] += rows_out[
                source, slot * channels : (slot + 1) * channels
            ]
        if half:
            send_ref[...] = total[...].astype(bf16)
        else:
            own_ref[...] = total[...]


def ssm_param_grad(
    flag_ref, tile_ref, near_ref, last_ref, enter_ref, rate_ref, coef_ref, out_ref, xs
):
    load_signal(flag_ref, tile_ref, xs)
    decay = jnp.exp(-rate_ref[...])
    zero = jnp.zeros_like(decay)

    def step(eight, carry, chunk):
        state, slope, for_coef, for_rate = carry
        x8 = xs[aligned((chunk * 16 + eight) * 8, 8), :]
        if chunk % 2:
            g8 = (near_ref, last_ref)[chunk // 2][aligned(eight * 8, 8), :]
        for k in range(8):
            slope = decay * (slope + state)
            state = decay * state + x8[k : k + 1]
            if chunk % 2:
                for_coef = for_coef + state * g8[k : k + 1]
                for_rate = for_rate + slope * g8[k : k + 1]
        return state, slope, for_coef, for_rate

    carry = (enter_ref[0], enter_ref[1], zero, zero)
    for chunk in range(4):
        carry = lax.fori_loop(0, 16, partial(step, chunk=chunk), carry)
    out_ref[:STATES, :] = -coef_ref[...] * carry[3]
    out_ref[STATES : 2 * STATES, :] = carry[2]
    skip = jnp.sum(xs[CTX : 2 * CTX] * near_ref[...], axis=0, keepdims=True) + jnp.sum(
        xs[3 * CTX :] * last_ref[...], axis=0, keepdims=True
    )
    out_ref[2 * STATES :, :] = jnp.concatenate(
        [skip, jnp.zeros((out_ref.shape[0] - 2 * STATES - 1, skip.shape[1]), f32)], axis=0
    )


def causal(scores):
    rows = lax.broadcasted_iota(jnp.int32, scores.shape, 0)
    cols = lax.broadcasted_iota(jnp.int32, scores.shape, 1)
    return jnp.where(cols <= rows, scores, masked_score)


def softmax_parts(parts):
    top = parts[0].max(axis=-1, keepdims=True)
    for part in parts[1:]:
        top = jnp.maximum(top, part.max(axis=-1, keepdims=True))
    weights = [jnp.exp(part - top) for part in parts]
    total = weights[0].sum(axis=-1, keepdims=True)
    for weight in weights[1:]:
        total = total + weight.sum(axis=-1, keepdims=True)
    return [weight / total for weight in weights]


def block_probs(q0, q1, k0, k1, first, second, whole, late):
    has_first = late > 0
    is_whole = whole > 0
    chosen = jnp.where(is_whole, first, second)
    chosen_ok = jnp.logical_or(jnp.logical_not(is_whole), has_first)
    s00 = causal(mm(q0, k0, NT) * score_scale)
    s0c = jnp.where(has_first, mm(q0, first, NT) * score_scale, masked_score)
    s11 = causal(mm(q1, k1, NT) * score_scale)
    s10 = jnp.where(is_whole, mm(q1, k0, NT) * score_scale, masked_score)
    s1c = jnp.where(chosen_ok, mm(q1, chosen, NT) * score_scale, masked_score)
    return softmax_parts([s00, s0c]), softmax_parts([s11, s10, s1c]), chosen


def head_parts(qkv_ref, head, half):
    channels = qkv_ref.shape[2] // 3
    return [
        qkv_ref[half, :, part * channels + head * HD : part * channels + (head + 1) * HD]
        for part in range(3)
    ]


def attention_forward(
    flag_ref, near_ref, far_ref, first_ref, second_ref, out_near_ref, out_far_ref, att_ref, own_ref,
    send_ref,
):
    half0 = flag_ref[ODD]
    half1 = 1 - half0
    heads = near_ref.shape[2] // (3 * HD)
    for index in range(2 * heads):
        qkv_ref = (near_ref, far_ref)[index // heads]
        q0, k0, v0 = head_parts(qkv_ref, index % heads, half0)
        q1, k1, v1 = head_parts(qkv_ref, index % heads, half1)
        at = slice(index * HD, (index + 1) * HD)
        first = first_ref[:, at]
        second = second_ref[:, at]
        (p00, p0c), (p11, p10, p1c), chosen = block_probs(
            q0, q1, k0, k1, first, second, flag_ref[WHOLE], flag_ref[LATE]
        )
        att_ref[half0, :, at] = (mm(p00.astype(bf16), v0) + mm(p0c.astype(bf16), first)).astype(
            bf16
        )
        att_ref[half1, :, at] = (
            mm(p11.astype(bf16), v1) + mm(p10.astype(bf16), v0) + mm(p1c.astype(bf16), chosen)
        ).astype(bf16)
    split = heads * HD

    def projected(half):
        return mm(att_ref[half, :, :split], out_near_ref[...]) + mm(
            att_ref[half, :, split:], out_far_ref[...], NT
        )

    send_ref[...] = projected(1).astype(bf16)
    own_ref[...] = projected(0)


def attended_grads(flag_ref, own_ref, other_ref, out_near_ref, out_far_ref, grad_ref, sent_ref):
    split = out_near_ref.shape[0]
    for half, ref in enumerate((own_ref, other_ref)):
        grad_ref[half, :, :split] = mm(ref[...], out_near_ref[...], NT).astype(bf16)
        grad_ref[half, :, split:] = mm(ref[...], out_far_ref[...]).astype(bf16)
        in_sent_order(flag_ref, ref, sent_ref.at[half])


def attention_backward(
    flag_ref, near_ref, far_ref, first_ref, second_ref, grad_ref, rate_ref, out_ref, second_out_ref,
    returned_ref,
):
    half0 = flag_ref[ODD]
    half1 = 1 - half0
    is_whole = flag_ref[WHOLE] > 0
    heads = near_ref.shape[2] // (3 * HD)
    for index in range(2 * heads):
        slot, head = index // heads, index % heads
        qkv_ref = (near_ref, far_ref)[slot]
        q0, k0, v0 = head_parts(qkv_ref, head, half0)
        q1, k1, v1 = head_parts(qkv_ref, head, half1)
        at = slice(index * HD, (index + 1) * HD)
        g0 = grad_ref[half0, :, at]
        g1 = grad_ref[half1, :, at]
        first = first_ref[:, at]
        second = second_ref[:, at]
        early, later, chosen = block_probs(
            q0, q1, k0, k1, first, second, flag_ref[WHOLE], flag_ref[LATE]
        )

        def score_grads(probs, rows, values):
            prob_grads = [mm(rows, v, NT) for v in values]
            centre = sum((p * d).sum(axis=-1, keepdims=True) for p, d in zip(probs, prob_grads))
            return [(p * (d - centre)).astype(bf16) for p, d in zip(probs, prob_grads)]

        d00, d0c = score_grads(early, g0, (v0, first))
        d11, d10, d1c = score_grads(later, g1, (v1, v0, chosen))
        p00, p0c = [p.astype(bf16) for p in early]
        p11, p10, p1c = [p.astype(bf16) for p in later]
        base = slot * 3 * heads * HD + head * HD
        for_q, for_k, for_v = [
            slice(base + part * heads * HD, base + part * heads * HD + HD) for part in range(3)
        ]
        out_ref[half0, :, for_q] = ((mm(d00, k0) + mm(d0c, first)) * score_scale).astype(bf16)
        out_ref[half1, :, for_q] = (
            (mm(d11, k1) + mm(d10, k0) + mm(d1c, chosen)) * score_scale
        ).astype(bf16)
        out_ref[half0, :, for_k] = ((mm(d00, q0, TN) + mm(d10, q1, TN)) * score_scale).astype(bf16)
        out_ref[half1, :, for_k] = (mm(d11, q1, TN) * score_scale).astype(bf16)
        out_ref[half0, :, for_v] = (mm(p00, g0, TN) + mm(p10, g1, TN)).astype(bf16)
        out_ref[half1, :, for_v] = mm(p11, g1, TN).astype(bf16)
        from_early = mm(d0c, q0, TN) * score_scale + mm(p0c, g0, TN)
        from_later = mm(d1c, q1, TN) * score_scale + mm(p1c, g1, TN)
        returned_ref[:CTX, at] = (from_early + jnp.where(is_whole, from_later, 0.0)).astype(bf16)
        second_out_ref[:, at] = jnp.where(is_whole, 0.0, from_later)

    rate = rate_ref[...]
    decay = jnp.exp(-rate)

    def step(j, adjoint):
        g8 = second_out_ref[aligned((15 - j) * 8, 8), :]
        for k in range(7, -1, -1):
            adjoint = decay * adjoint + g8[k : k + 1]
        return adjoint

    adjoint = lax.fori_loop(0, 16, step, jnp.zeros_like(rate)) * jnp.exp(-float(CTX) * rate)
    for k, part in enumerate(split_three(adjoint)):
        returned_ref[CTX + k * STATES : CTX + (k + 1) * STATES, :] = part


def flat(ref):
    if len(ref.shape) == 2:
        return ref[...]
    part = ref[:, 0]
    return part.reshape(part.shape[0] * part.shape[1], part.shape[2])


def feed_forward(
    flag_ref, n_ref, c_ref, up0_ref, down0_ref, up1_ref, down1_ref, act_ref, gate_ref, sent_ref,
    down_out_ref, back_out_ref, acc_down, acc_back,
):
    step = pl.program_id(0)
    steps = pl.num_programs(0)
    per = steps // 2

    @pl.when(step == 0)
    def _():
        acc_down[...] = jnp.zeros_like(acc_down)
        acc_back[...] = jnp.zeros_like(acc_back)
        in_sent_order(flag_ref, n_ref, sent_ref)

    def body(up, down, slot):
        gate = mm(n_ref[...], up)
        cdf = 0.5 * (1.0 + lax.erf(gate * (1.0 / math.sqrt(2.0))))
        act = (gate * cdf).astype(bf16)
        slope = cdf + gate * jnp.exp(-0.5 * gate * gate) * (1.0 / math.sqrt(2.0 * math.pi))
        grad = (mm(c_ref[...], down, NT) * slope).astype(bf16)
        gate_ref[...] = grad
        hidden = act_ref.shape[1] // 2
        width = hidden // GROUP
        count = act.shape[1] // width
        for k in range(count):
            mask = jnp.bitwise_xor(flag_ref[PLACE], (step - slot * per) * count + k)
            to = (1 - mask % 2) * 4 + (mask // 2 % 2) * 2 + mask // 4
            act_ref[:, aligned(slot * hidden + to * width, width)] = act[
                :, k * width : (k + 1) * width
            ]
        acc_down[...] += mm(act, down)
        acc_back[...] += mm(grad, up, NT)

    @pl.when(step < per)
    def _():
        body(up0_ref[...], down0_ref[...], 0)

    @pl.when(step >= per)
    def _():
        body(flat(up1_ref), flat(down1_ref), 1)

    @pl.when(step == steps - 1)
    def _():
        down_out_ref[...] = acc_down[...].astype(down_out_ref.dtype)
        back_out_ref[...] = acc_back[...].astype(back_out_ref.dtype)


def run_feed_forward(flags, rows, cot, up, down, far, kind):
    tokens, width = rows.shape
    block = 512
    hidden = up.shape[1]
    per = hidden // block
    slices, slice_rows = far.shape[0], far.shape[2]

    def near_at(j):
        return jnp.minimum(j, per - 1)

    def far_at(j):
        return jnp.maximum(j - per, 0)

    whole = pl.BlockSpec((tokens, width), lambda j: (0, 0))
    return pl.pallas_call(
        feed_forward,
        grid=(2 * per,),
        out_shape=(
            shape((tokens, 2 * hidden), bf16),
            shape((tokens, 2 * hidden), bf16),
            shape((tokens, width), bf16),
            shape((tokens, width), kind),
            shape((tokens, width), kind),
        ),
        in_specs=[
            pl.BlockSpec(memory_space=pltpu.SMEM),
            whole,
            whole,
            pl.BlockSpec((width, block), lambda j: (0, near_at(j))),
            pl.BlockSpec((block, width), lambda j: (near_at(j), 0)),
            pl.BlockSpec((slices, 1, slice_rows, block), lambda j: (0, 0, 0, far_at(j))),
            pl.BlockSpec((slices // per, 1, slice_rows, width), lambda j: (far_at(j), 1, 0, 0)),
        ],
        out_specs=(
            pl.BlockSpec((tokens, 2 * hidden), lambda j: (0, 0)),
            pl.BlockSpec((tokens, block), lambda j: (0, j)),
            whole,
            whole,
            whole,
        ),
        scratch_shapes=[pltpu.VMEM((tokens, width), f32), pltpu.VMEM((tokens, width), f32)],
        compiler_params=pltpu.CompilerParams(
            vmem_limit_bytes=24 * 1024 * 1024, dimension_semantics=("arbitrary",)
        ),
        cost_estimate=pl.CostEstimate(flops=0, bytes_accessed=0, transcendentals=0),
    )(flags, rows, cot, up, down, far, far)


def products(lhs_refs, rhs_refs, columns, split=None):
    total = None
    for lhs_ref, rhs_ref in zip(lhs_refs, rhs_refs):
        term = mm(lhs_ref[:, columns], rhs_ref[...], TN)
        total = term if total is None else total + term
    return total


def down_pass(flag_ref, act0, act1, cot0, cot1, out_ref):
    hidden = act0.shape[1] // 2
    part = hidden // 4
    for slot in range(2):
        value = products(
            (act0, act1), (cot0, cot1), slice(slot * hidden, slot * hidden + hidden // 2)
        ).astype(bf16)
        out_ref[slot * part : (slot + 1) * part, :] = value[part:]
        out_ref[(2 + slot) * part : (3 + slot) * part, :] = value[:part]


def down_keep(flag_ref, act0, act1, cot0, cot1, core_ref, send_ref, left_ref):
    hidden = act0.shape[1] // 2
    part = hidden // 4
    for slot in range(2):
        value = products(
            (act0, act1), (cot0, cot1), slice(slot * hidden + hidden // 2, (slot + 1) * hidden)
        )
        to = slice(slot * part, (slot + 1) * part)
        send_ref[to, :] = (value[part:] + core_ref[to, :].astype(f32)).astype(bf16)
        left_ref[to, :] = value[:part] + core_ref[2 * part + to.start : 2 * part + to.stop, :].astype(
            f32
        )


def down_step(flag_ref, left_ref, received_ref, own_ref, send_ref):
    rows = own_ref.shape[0] // 2
    for slot in range(2):
        to = slice(slot * rows, (slot + 1) * rows)
        own = slice(2 * slot * rows, (2 * slot + 1) * rows)
        send = slice((2 * slot + 1) * rows, (2 * slot + 2) * rows)
        own_ref[to, :] = left_ref[own, :] + received_ref[own, :].astype(f32)
        send_ref[to, :] = (left_ref[send, :] + received_ref[send, :].astype(f32)).astype(bf16)


def y_first(value, rows):
    parts = [value[k * rows : (k + 1) * rows] for k in (1, 3, 0, 2)]
    return jnp.concatenate(parts[:2], 0), jnp.concatenate(parts[2:], 0)


def rows_pass(flag_ref, lhs0, lhs1, rhs0, rhs1, out_ref):
    half = lhs0.shape[1] // 2
    value = products((lhs0, lhs1), (rhs0, rhs1), slice(0, half)).astype(bf16)
    send, left = y_first(value, half // 4)
    out_ref[: half // 2, :] = send
    out_ref[half // 2 :, :] = left


def rows_keep(flag_ref, lhs0, lhs1, rhs0, rhs1, core_ref, send_ref, left_ref):
    half = lhs0.shape[1] // 2
    value = products((lhs0, lhs1), (rhs0, rhs1), slice(half, 2 * half))
    send, left = y_first(value, half // 4)
    send_ref[...] = (send + core_ref[: half // 2, :].astype(f32)).astype(bf16)
    left_ref[...] = left + core_ref[half // 2 :, :].astype(f32)


def rows_step(
    flag_ref, up_left, out_left, up_received, out_received, up_own, out_own, send_ref
):
    rows = up_own.shape[0]
    at = 0
    for left, received, own in ((up_left, up_received, up_own), (out_left, out_received, out_own)):
        own[...] = left[:rows, :] + received[:rows, :].astype(f32)
        width = own.shape[1]
        send_ref[:, at : at + width] = (left[rows:, :] + received[rows:, :].astype(f32)).astype(bf16)
        at += width


def own_slices(
    flag_ref, down_own, down_received, up_own, out_own, rows_received, near_ref, far_ref
):
    rows, hidden, channels = up_own.shape[0], up_own.shape[1] // 2, out_own.shape[1] // 2
    down = down_own[...] + down_received[...].astype(f32)
    up = up_own[...] + rows_received[:, : 2 * hidden].astype(f32)
    out = out_own[...] + rows_received[:, 2 * hidden :].astype(f32)
    width = down.shape[1]
    for slot, ref in enumerate((near_ref, far_ref)):
        ref[:, :width] = down[slot * rows : (slot + 1) * rows].astype(ref.dtype)
        ref[:, width : width + hidden] = up[:, slot * hidden : (slot + 1) * hidden].astype(ref.dtype)
        ref[:, width + hidden :] = out[:, slot * channels : (slot + 1) * channels].astype(ref.dtype)


def attn_pass(flag_ref, lhs0, lhs1, rhs0, rhs1, out_ref):
    half = lhs0.shape[1] // 2
    out_ref[...] = products((lhs0, lhs1), (rhs0, rhs1), slice(0, half)).astype(bf16)


def attn_keep(flag_ref, lhs0, lhs1, rhs0, rhs1, core_ref, own_ref, *send_refs):
    half = lhs0.shape[1] // 2
    rows = half // 4
    value = products((lhs0, lhs1), (rhs0, rhs1), slice(half, 2 * half)) + core_ref[...].astype(f32)
    own_ref[...] = value[:rows]
    for k, ref in enumerate(send_refs):
        ref[...] = value[(k + 1) * rows : (k + 2) * rows].astype(bf16)


def attn_own(flag_ref, own_ref, r1_ref, r2_ref, r3_ref, near_ref, far_ref):
    total = own_ref[...] + (
        r1_ref[...].astype(f32) + r2_ref[...].astype(f32) + r3_ref[...].astype(f32)
    )
    width = near_ref.shape[1]
    near_ref[...] = total[:, :width]
    far_ref[...] = total[:, width:].astype(bf16)


def add_two(flag_ref, a_ref, b_ref, out_ref):
    out_ref[...] = (a_ref[...].astype(f32) + b_ref[...].astype(f32)).astype(out_ref.dtype)


def add_three(flag_ref, a_ref, b_ref, c_ref, out_ref):
    out_ref[...] = (a_ref[...] + b_ref[...] + c_ref[...].astype(f32)).astype(out_ref.dtype)


def pack_small(flag_ref, param_ref, gains_ref, received_ref, near_ref, far_ref):
    gains = gains_ref[...] + received_ref[...]
    width = gains.shape[1]
    rows = param_ref.shape[0]
    for slot, ref in enumerate((near_ref, far_ref)):
        ref[:rows, :] = param_ref[:, slot * width : (slot + 1) * width]
        ref[rows:, :] = gains


def widen(flag_ref, all_ref, down_ref, up_ref, out_ref):
    down, up = down_ref.shape[1], up_ref.shape[1]
    down_ref[...] = all_ref[:, :down].astype(f32)
    up_ref[...] = all_ref[:, down : down + up].astype(f32)
    out_ref[...] = all_ref[:, down + up :].astype(f32).T


def sources(flag_ref, even_ref, odd_ref):
    for pair in range(GROUP // 2):
        for side, ref in enumerate((even_ref, odd_ref)):
            source = jnp.bitwise_xor(flag_ref[PLACE], 2 * pair + side)
            yield ref, pair, aligned(source * even_ref.shape[1], even_ref.shape[1])


def assemble_weight(flag_ref, even_ref, odd_ref, tile_ref, weight_ref, out_ref, qkv_ref):
    split = weight_ref.shape[1]
    for ref, pair, at in sources(flag_ref, even_ref, odd_ref):
        weight_ref[at, :] = ref[pair, :, :split]
        out_ref[at, :] = ref[pair, :, split:]
    project(flag_ref, tile_ref, weight_ref, qkv_ref)


def assemble_grad(flag_ref, even_ref, odd_ref, qkv_ref):
    channels = qkv_ref.shape[2]
    for ref, pair, at in sources(flag_ref, even_ref, odd_ref):
        for part in range(3):
            qkv_ref[part, at, :] = ref[pair, :, part * channels : (part + 1) * channels].astype(f32)


class Order:
    def __init__(self):
        self.last = ()

    def __call__(self, *values):
        tied = lax.optimization_barrier((values, self.last))[0]
        return tied[0] if len(tied) == 1 else tied

    def done(self, result):
        self.last = result
        return result


def per_device(
    inputs,
    block_size,
    gain_attn,
    qkv_weight,
    ssm_rate,
    ssm_coef,
    ssm_skip,
    out_weight,
    gain_mlp,
    up_weight,
    down_weight,
    cotangent,
    dp_size,
):
    z = lax.axis_index("mp")
    place = jnp.bitwise_and(lax.axis_index("dp"), GROUP - 1)
    groups = [[g * GROUP + k for k in range(GROUP)] for g in range(dp_size // GROUP)]
    groups = groups if len(groups) > 1 else None

    def swap_mp(value, mask):
        return lax.ppermute(value, "mp", [(k, k ^ mask) for k in range(4)])

    def swap_dp(value, mask):
        return lax.ppermute(value, "dp", [(k, k ^ mask) for k in range(dp_size)])

    def gather(value):
        return lax.all_gather(value, "dp", axis=0, tiled=True, axis_index_groups=groups)

    def gather_by_xor(piece):
        return [piece] + [swap_dp(piece, 2 * k) for k in range(1, GROUP // 2)]

    def over_groups(own):
        mask = GROUP
        while mask < dp_size:
            own = own + swap_dp(own.astype(bf16), mask).astype(f32)
            mask *= 2
        return own.astype(bf16)

    model_dim = inputs.shape[2]
    channels = qkv_weight.shape[2]
    hidden = up_weight.shape[1]
    wide = 2 * channels
    rows = model_dim // GROUP
    row = inputs[0]
    cot = cotangent[0]
    z_far = jnp.bitwise_xor(z, 2)
    whole = (block_size[0] > HALF).astype(jnp.int32)
    flags = jnp.stack(
        [whole, jnp.right_shift(z, 1), jnp.bitwise_and(z, 1), z, z_far, place]
    ).astype(jnp.int32)
    gain_one = gain_attn[None]
    gain_two = gain_mlp[None]
    order = Order()
    half = shape((HALF, model_dim))
    half_low = shape((HALF, model_dim), bf16)

    normed_one = order.done(call(norm_one, half_low)(flags, row, gain_one))
    paired_one = swap_mp(normed_one, 1)
    qkv_parts = jnp.transpose(qkv_weight, (1, 0, 2))
    attn_slice, mlp_slice = order.done(
        run_cut_slices(flags, order(qkv_parts), out_weight, up_weight, down_weight)
    )
    attn_across = swap_mp(attn_slice, 2)
    ssm_pack = jnp.concatenate(
        [ssm_rate.T, ssm_coef.T, ssm_skip[None], jnp.zeros((7, channels), f32)], 0
    )
    ssm_both = jnp.concatenate([ssm_pack, swap_mp(ssm_pack, 2)], 1)
    rate_t, coef_t, skip_t = ssm_both[:16], ssm_both[16:32], ssm_both[32:33]
    near_qkv = order.done(jnp.concatenate(list(order(*[qkv_parts[k] for k in range(3)])), 1))

    paired_one, attn_across = order.done(order(paired_one, attn_across))
    attn_pieces = gather_by_xor(attn_across)
    mlp_across = swap_mp(order(mlp_slice), 2)
    tile_one, one_sent, second_local, handed = order.done(
        call(
            ssm_forward,
            (
                shape((2, HALF, model_dim), bf16),
                shape((2, HALF, model_dim), bf16),
                shape((CTX, wide)),
                shape((CTX + 6 * STATES, wide), bf16),
            ),
            scratch=[pltpu.VMEM((2 * HALF, wide), f32)],
        )(flags, normed_one, order(paired_one), rate_t, coef_t, skip_t)
    )
    handed = lax.ppermute(handed, "mp", [(0, 2), (1, 3)])

    qkv_shape = shape((2, HALF, 3 * channels), bf16)
    qkv_near = order.done(call(project, qkv_shape)(flags, order(tile_one), near_qkv))
    even = order.done(jnp.stack(list(order(*attn_pieces))))
    odd_part = swap_dp(even, 1)
    far_qkv, far_out, qkv_far = order.done(
        call(
            assemble_weight,
            (
                shape((model_dim, 3 * channels), bf16),
                shape((model_dim, channels), bf16),
                qkv_shape,
            ),
        )(flags, even, order(odd_part), tile_one)
    )
    ctx_first, ctx_second, enter_state = order.done(
        call(
            ssm_carry_in,
            (shape((CTX, wide), bf16), shape((CTX, wide), bf16), shape((2, STATES, wide))),
            scratch=[pltpu.VMEM((CTX, wide), f32)],
        )(flags, second_local, order(handed), rate_t, coef_t)
    )
    mlp_far = gather(order(mlp_across)).reshape(GROUP, 2, rows, model_dim)
    paired_cot = swap_mp(order(cot), 1)
    attended, out_own, out_send = order.done(
        call(attention_forward, (shape((2, HALF, wide), bf16), half, half_low))(
            flags, order(qkv_near), qkv_far, ctx_first, ctx_second, out_weight, far_out
        )
    )
    out_received = swap_mp(out_send, 1)
    paired_cot = order.done(order(paired_cot))
    middle, normed_two = order.done(
        call(norm_two, (half, half_low))(flags, row, out_own, order(out_received), gain_two)
    )

    paired_two = swap_mp(normed_two, 1)
    mlp = (up_weight, down_weight, mlp_far)
    act_own, gate_own, two_own, down_own, back_own = order.done(
        run_feed_forward(flags, order(normed_two), cot, *mlp, f32)
    )
    act_other, gate_other, two_other, down_send, back_send = order.done(
        run_feed_forward(flags, order(paired_two), paired_cot, *mlp, bf16)
    )
    back_received = swap_mp(back_send, 1)

    def low(*dims):
        return shape(dims, bf16)

    side = model_dim // 2
    acts = (act_own, act_other, cot, paired_cot)
    passed = order.done(call(down_pass, low(hidden, model_dim))(flags, order(act_own), *acts[1:]))
    down_core = swap_dp(passed, 1)
    middle_grad, attn_grad, gain_mlp_grad = order.done(
        call(norm_two_back, (half, half_low, shape((1, model_dim))))(
            flags, middle, back_own, order(back_received), cot, gain_two
        )
    )
    paired_back = swap_mp(attn_grad, 1)
    passed = order.done(
        call(rows_pass, low(side, 2 * hidden))(
            flags, order(two_own), two_other, gate_own, gate_other
        )
    )
    up_core = swap_dp(passed, 1)
    down_send_x, down_left = order.done(
        call(down_keep, (low(side, model_dim), shape((side, model_dim))))(
            flags, *acts, order(down_core)
        )
    )
    down_x = swap_dp(down_send_x, 2)
    up_send_y, up_left = order.done(
        call(rows_keep, (low(side // 2, 2 * hidden), shape((side // 2, 2 * hidden))))(
            flags, two_own, two_other, gate_own, gate_other, order(up_core)
        )
    )
    up_y = swap_dp(up_send_y, 4)

    att_grad, back_sent = order.done(
        call(
            attended_grads,
            (shape((2, HALF, wide), bf16), shape((2, HALF, model_dim), bf16)),
        )(flags, attn_grad, order(paired_back), out_weight, far_out)
    )
    down_received = swap_mp(order(down_send), 1)
    outs = (back_sent[0], back_sent[1], attended[0], attended[1])
    passed = order.done(call(rows_pass, low(side, wide))(flags, *outs))
    out_core = swap_dp(passed, 1)
    dqkv, second_grad, returned = order.done(
        call(
            attention_backward,
            (
                shape((2, HALF, 6 * channels), bf16),
                shape((CTX, wide)),
                shape((CTX + 3 * STATES, wide), bf16),
            ),
        )(flags, qkv_near, qkv_far, ctx_first, ctx_second, order(att_grad), rate_t)
    )
    returned = lax.ppermute(returned, "mp", [(2, 0), (3, 1)])
    out_send_y, out_left = order.done(
        call(rows_keep, (low(side // 2, wide), shape((side // 2, wide))))(
            flags, *outs, order(out_core)
        )
    )
    out_y = swap_dp(out_send_y, 4)
    ones = (one_sent[0], one_sent[1], dqkv[0], dqkv[1])
    passed = order.done(call(attn_pass, low(side, 6 * channels))(flags, order(ones[0]), *ones[1:]))
    attn_core = swap_dp(passed, 1)
    down_mine, down_send_y = order.done(
        call(down_step, (shape((2 * rows, model_dim)), low(2 * rows, model_dim)))(
            flags, down_left, order(down_x)
        )
    )
    down_y = swap_dp(down_send_y, 4)
    one_own, one_send, last_grad = order.done(
        call(
            ssm_signal_grad,
            (half, half_low, shape((CTX, wide))),
            scratch=[pltpu.VMEM((2 * HALF, wide), f32), pltpu.VMEM((HALF, model_dim), f32)],
        )(
            flags, second_grad, order(returned), rate_t, coef_t, skip_t, dqkv, near_qkv, far_qkv
        )
    )
    one_received = swap_mp(one_send, 1)
    up_mine, out_mine, rows_send_x = order.done(
        call(
            rows_step,
            (shape((rows, 2 * hidden)), shape((rows, wide)), low(rows, 2 * hidden + wide)),
        )(flags, up_left, out_left, *order(up_y, out_y))
    )
    rows_x = swap_dp(rows_send_x, 2)
    attn_mine, *attn_sends = order.done(
        call(attn_keep, (shape((rows, 6 * channels)),) + (low(rows, 6 * channels),) * 3)(
            flags, *ones, order(attn_core)
        )
    )
    attn_sent = [swap_dp(part, SENT[5 + k]) for k, part in enumerate(attn_sends)]
    param_grad = order.done(
        call(
            ssm_param_grad,
            shape((40, wide)),
            scratch=[pltpu.VMEM((2 * HALF, wide), f32)],
        )(flags, order(tile_one), second_grad, last_grad, enter_state, rate_t, coef_t)
    )
    input_grad, gains = order.done(
        call(norm_one_back, (half, shape((2 * model_dim // channels, channels))))(
            flags, row, one_own, order(one_received), middle_grad, gain_one, gain_mlp_grad
        )
    )
    mlp_width = model_dim + hidden + channels
    mlp_near, mlp_send = order.done(
        call(own_slices, (shape((rows, mlp_width)), low(rows, mlp_width)))(
            flags, down_mine, order(down_y), up_mine, out_mine, order(rows_x)
        )
    )
    mlp_received = swap_mp(mlp_send, 2)
    attn_near, attn_send = order.done(
        call(attn_own, (shape((rows, 3 * channels)), low(rows, 3 * channels)))(
            flags, attn_mine, *order(*attn_sent)
        )
    )
    attn_received = swap_mp(attn_send, 2)
    gains_received = swap_mp(order(gains), 1)
    output = order.done(
        call(add_three, half_low)(flags, middle, down_own, order(down_received))
    )
    attn_slice_grad = order.done(
        call(add_two, low(rows, 3 * channels))(flags, attn_near, order(attn_received))
    )
    attn_pieces = gather_by_xor(over_groups(attn_slice_grad))
    mlp_slice_grad = order.done(
        call(add_two, low(rows, mlp_width))(flags, mlp_near, order(mlp_received))
    )
    mlp_full = gather(over_groups(mlp_slice_grad))
    small = shape((48, channels))
    packed, packed_far = order.done(
        call(pack_small, (small, small))(flags, param_grad, gains, order(gains_received))
    )
    packed = order.done(call(add_two, small)(flags, packed, order(swap_mp(packed_far, 2))))
    packed = order.done(call(add_two, small)(flags, packed, order(swap_dp(packed, 1))))
    even = order.done(jnp.stack(list(order(*attn_pieces))))
    odd_part = swap_dp(even, 1)
    mask = 2
    while mask < dp_size:
        packed = order.done(call(add_two, small)(flags, packed, order(swap_dp(packed, mask))))
        mask *= 2
    qkv_grad = order.done(
        call(assemble_grad, shape((3, model_dim, channels)))(flags, even, order(odd_part))
    )
    down_grad, up_grad, out_grad = call(
        widen, (shape(down_weight.shape), shape(up_weight.shape), shape(out_weight.shape))
    )(flags, order(mlp_full))
    gains = packed[40:].reshape(2, model_dim)
    return (
        output[None],
        input_grad[None],
        gains[0],
        jnp.transpose(qkv_grad, (1, 0, 2)),
        packed[:16].T,
        packed[16:32].T,
        packed[32],
        out_grad,
        gains[1],
        up_grad,
        down_grad,
    )


def solution(mesh):
    return jax.shard_map(
        partial(per_device, dp_size=mesh.shape["dp"]),
        mesh=mesh,
        in_specs=(
            P("dp", "mp", None),
            P("dp"),
            P(),
            P(None, None, "mp"),
            P("mp", None),
            P("mp", None),
            P("mp"),
            P("mp", None),
            P(),
            P(None, "mp"),
            P("mp", None),
            P("dp", "mp", None),
        ),
        out_specs=(
            P("dp", "mp", None),
            P("dp", "mp", None),
            P(),
            P(None, None, "mp"),
            P("mp", None),
            P("mp", None),
            P("mp"),
            P("mp", None),
            P(),
            P(None, "mp"),
            P("mp", None),
        ),
        check_vma=False,
    )
```

time: 485 us -> 316 us (0.65)
  waiting for transfers between devices: 251 us -> 145 us
  other arithmetic: 40.1 us -> 0.26 us
  matrix products: 17.9 us -> 0 us
  local copies, waits for them, and re-layouts: 37.2 us -> 22.4 us
  starting transfers between devices: 39.8 us -> 47.7 us
  Pallas kernels: 79.6 us -> 84.9 us
    ppermute x16 -> x15, waiting for transfers between devices: 157 us -> 84.4 us  [swap_mp(): return lax.ppermute(value, 'mp', [(k, k ^ mask) for k in range(4)])]
    ppermute x11 -> x23, waiting for transfers between devices: 82.5 us -> 26.5 us  [swap_dp(): return lax.ppermute(value, 'dp', [(k, k ^ mask) for k in range(dp_size)])]
    dot_general x8 -> x0, matrix products: 17.9 us -> none  [mm(): return lax.dot_general(a, b, dims, preferred_element_type=f32)]
    all_gather x4 -> x2, waiting for transfers between devices: 0.03 us -> 15.2 us  [gather(): lax.all_gather(value, 'dp', axis=0, tiled=True, axis_index_groups=groups)]
    slice x10 -> x1, local copies, waits for them, and re-layouts: 15.3 us -> 0.56 us  [per_device(): packed[32]]
    convert_element_type x8 -> x0, other arithmetic: 12.2 us -> none  [the longest x3 7.26 us: reduce_over_plane(): full[:, k].reshape(GROUP * own.shape[1], own.shape[2]).astype(f32)]
    ppermute x11 -> x23, starting transfers between devices: 9.34 us -> 19.9 us  [swap_dp(): return lax.ppermute(value, 'dp', [(k, k ^ mask) for k in range(dp_size)])]
    concatenate x13 -> x0, other arithmetic: 8.99 us -> none  [the longest x4 2.76 us: swap_slots(): return jnp.concatenate([value[..., size:], value[..., :size]], -1)]
  transfers between devices with their start and end apart: 33 -> 42, of which waited for: 27 -> 25; matrix products, arithmetic and copies ran while one was open for 14% -> 1% of each run, Pallas kernels for 9% -> 22%
where the time goes in v2:
time: 316 us; the launch traced here: 315 us
  waiting for transfers between devices  145 us (46%)
  Pallas kernels  84.9 us (27%)
  starting transfers between devices  47.7 us (15%)
  local copies, waits for them, and re-layouts  22.4 us (7%)
  between operations  15.4 us (5%)
    ppermute x15, waiting for transfers between devices, swap_mp(): return lax.ppermute(value, 'mp', [(k, k ^ mask) for k in range(4)])  84.4 us
    pallas_call x35, Pallas kernels, run(): pl.pallas_call(kernel, out_shape=out_shape, in_specs=[pl.BlockSpec(memory...  68.6 us
    ppermute x23, waiting for transfers between devices, swap_dp(): return lax.ppermute(value, 'dp', [(k, k ^ mask) for k in range(dp_size)])  26.5 us
    ppermute x15, starting transfers between devices, swap_mp(): return lax.ppermute(value, 'mp', [(k, k ^ mask) for k in range(4)])  21.4 us
    unnamed x85, local copies, waits for them, and re-layouts  20.7 us
    ppermute x23, starting transfers between devices, swap_dp(): return lax.ppermute(value, 'dp', [(k, k ^ mask) for k in range(dp_size)])  19.9 us
    pallas_call x2, Pallas kernels, run_feed_forward(): pl.pallas_call(feed_forward, grid=(2 * per,), out_shape=(shape((tokens, 2...  15.6 us
    all_gather x2, waiting for transfers between devices, gather(): lax.all_gather(value, 'dp', axis=0, tiled=True, axis_index_groups=groups)  15.2 us
  transfers between devices with their start and end apart: 42, of which 25 were waited for; matrix products, arithmetic and copies ran while one was open for 1% of the time, Pallas kernels for 22%

profile of v2, /device:TPU:0, one launch (start us, length us, event | category | flops | bytes accessed | tf_op | source)
XLA Modules:
  0.0 315.4 jit_solution(11467350540603988930)
XLA Ops:
  10.6 3.1 collective-permute-start
  13.7 1.6 copy-done.2
  15.3 1.6 copy-done.4
  16.9 1.4 copy-done.10
  20.0 2.7 collective-permute-start.1
  23.3 12.8 %collective-permute-done.2 = f32[40,256]{1,0:T(8,128)S(1)} collective-permute-done((f32[40,256]{1,0:T(8,128)S(1)}, f32[40,256]{1,0:T(8,128)S(1)}, u32[]{:S(2)}, u32[]{:S(2)}) %collective-permute-start.2) | collective-permute-done | bytes 40992 | tf_op jit(solution)/shard_map/ppermute | solution.py:798
  36.2 1.6 collective-permute-start.4
  37.7 1.5 collective-permute-start.5
  39.7 5.1 %shard_map.205 = (bf16[2,256,1024]{2,1,0:T(8,128)(2,1)S(1)}, bf16[2,256,1024]{2,1,0:T(8,128)(2,1)S(1)}, f32[128,512]{1,0:T(8,128)S(1)}, bf16[224,512]{1,0:T(8,128)(2,1)S(1)}) custom-call(s32[6]{0:T(128)S(1)} %stack.54.flag_ref, bf16[256,1024]{1,0:T(8,128)(2,1)S(1)} %shard_map.203.own_ref, bf16[256,1024]{1,0:T(8,128)(2,1)S(1)} %collective-permute-done.other_ref, ...), custom_call_target="tpu_custom_call" | custom-call | tf_op jit(solution)/shard_map/pallas_call | solution.py:42
  44.8 1.6 shard_map.206.near_ref
  46.4 3.5 %collective-permute-done.5 = bf16[128,1024]{1,0:T(8,128)(2,1)S(1)} collective-permute-done((bf16[128,1024]{1,0:T(8,128)(2,1)S(1)}, bf16[128,1024]{1,0:T(8,128)(2,1)S(1)}, u32[]{:S(2)}, u32[]{:S(2)}) %collective-permute-start.5) | collective-permute-done | bytes 262176 | tf_op jit(solution)/shard_map/ppermute | solution.py:801
  50.3 4.8 %collective-permute-start.3 = (bf16[224,512]{1,0:T(8,128)(2,1)S(1)}, bf16[224,512]{1,0:T(8,128)(2,1)S(1)}, u32[]{:S(2)}, u32[]{:S(2)}) collective-permute-start(bf16[224,512]{1,0:T(8,128)(2,1)S(1)} %get-tuple-element.146), channel_id=1, source_target_pairs={{0,2},{1,3},{4,6},{5,7},{8,10},{9,11},{12,14},{13,15},{16,18},{17,... | collective-permute-start | bytes 688136 | tf_op jit(solution)/shard_map/ppermute | solution.py:863
  55.1 1.7 shard_map.207
  58.7 8.5 %collective-permute-done.3.handed_ref = bf16[224,512]{1,0:T(8,128)(2,1)S(1)} collective-permute-done((bf16[224,512]{1,0:T(8,128)(2,1)S(1)}, bf16[224,512]{1,0:T(8,128)(2,1)S(1)}, u32[]{:S(2)}, u32[]{:S(2)}) %collective-permute-start.3) | collective-permute-done | bytes 229408 | tf_op jit(solution)/shard_map/ppermute | solution.py:863
  67.3 1.5 shard_map.208
  68.8 7.8 %collective-permute-done.10 = bf16[256,1024]{1,0:T(8,128)(2,1)} collective-permute-done((bf16[256,1024]{1,0:T(8,128)(2,1)S(1)}, bf16[256,1024]{1,0:T(8,128)(2,1)}, u32[]{:S(2)}, u32[]{:S(2)}) %collective-permute-start.10) | collective-permute-done | bytes 524320 | tf_op jit(solution)/shard_map/ppermute | solution.py:798
  76.9 9.9 %collective-permute-start.9 = (bf16[256,1024]{1,0:T(8,128)(2,1)}, bf16[256,1024]{1,0:T(8,128)(2,1)S(1)}, u32[]{:S(2)}, u32[]{:S(2)}) collective-permute-start(bf16[256,1024]{1,0:T(8,128)(2,1)} %bitcast.18.c_ref.cot0.cot_ref), channel_id=1, source_target_pairs={{0,1},{1,0},{2,3},{3,2},{4,5},{5,4},{6,7},{7,6},{8,9},{9,8},{10,11... | collective-permute-start | bytes 1572872 | tf_op jit(solution)/shard_map/ppermute | solution.py:798
  87.8 3.7 %shard_map.209 = (bf16[2,256,512]{2,1,0:T(8,128)(2,1)S(1)}, f32[256,1024]{1,0:T(8,128)S(1)}, bf16[256,1024]{1,0:T(8,128)(2,1)S(1)}) custom-call(s32[6]{0:T(128)S(1)} %stack.54.flag_ref, bf16[2,256,768]{2,1,0:T(8,128)(2,1)S(1)} %shard_map.206.near_ref, bf16[2,256,768]{2,1,0:T(8,128)(2,1)S(1)} %get-tuple-element.155.far_ref, ...), custom_call_target="tpu_custom_call" | custom-call | tf_op jit(solution)/shard_map/pallas_call | solution.py:42
  92.3 7.3 %collective-permute-done.9.c_ref.cot1 = bf16[256,1024]{1,0:T(8,128)(2,1)S(1)} collective-permute-done((bf16[256,1024]{1,0:T(8,128)(2,1)}, bf16[256,1024]{1,0:T(8,128)(2,1)S(1)}, u32[]{:S(2)}, u32[]{:S(2)}) %collective-permute-start.9) | collective-permute-done | bytes 524320 | tf_op jit(solution)/shard_map/ppermute | solution.py:798
  100.5 9.8 %collective-permute-done.8.received_ref = bf16[256,1024]{1,0:T(8,128)(2,1)S(1)} collective-permute-done((bf16[256,1024]{1,0:T(8,128)(2,1)S(1)}, bf16[256,1024]{1,0:T(8,128)(2,1)S(1)}, u32[]{:S(2)}, u32[]{:S(2)}) %collective-permute-start.8) | collective-permute-done | bytes 524320 | tf_op jit(solution)/shard_map/ppermute | solution.py:798
  110.3 1.8 shard_map.210
  113.1 1.7 collective-permute-start.11
  114.8 8.0 %all-gather.3.cloned.1.call-done = bf16[2048,1024]{1,0:T(8,128)(2,1)} async-done(((bf16[256,1024]{1,0:T(8,128)(2,1)}), bf16[2048,1024]{1,0:T(8,128)(2,1)}) %all-gather.3.cloned.1.call-update) | async-done | bytes 4194320 | tf_op jit(solution)/shard_map/all_gather | solution.py:804
  122.8 2.2 copy-done
  125.0 1.6 copy-done.5
  126.6 7.9 %shard_map.211 = (bf16[256,2048]{1,0:T(8,128)(2,1)S(1)}, bf16[256,2048]{1,0:T(8,128)(2,1)S(1)}, bf16[256,1024]{1,0:T(8,128)(2,1)S(1)}, f32[256,1024]{1,0:T(8,128)S(1)}, f32[256,1024]{1,0:T(8,128)S(1)}) custom-call(s32[6]{0:T(128)S(1)} %stack.54.flag_ref, bf16[256,1024]{1,0:T(8,128)(2,1)} %get-tuple-element.169.n_ref, ...), custom_call_target="tpu_custom_call" | custom-call | tf_op jit(solution)/shard_map/pallas_call | solution.py:571
  134.5 7.7 %shard_map.212 = (bf16[256,2048]{1,0:T(8,128)(2,1)S(1)}, bf16[256,2048]{1,0:T(8,128)(2,1)S(1)}, bf16[256,1024]{1,0:T(8,128)(2,1)S(1)}, bf16[256,1024]{1,0:T(8,128)(2,1)S(1)}, bf16[256,1024]{1,0:T(8,128)(2,1)S(1)}) custom-call(s32[6]{0:T(128)S(1)} %stack.54.flag_ref, bf16[256,1024]{1,0:T(8,128)(2,1)} %collective-permute-done.11.n_ref, ...), custom_call_target="tpu_custom_call" | custom-call | tf_op jit(solution)/shard_map/pallas_call | solution.py:571
  142.2 1.6 collective-permute-start.12
  143.8 2.4 shard_map.213
  146.3 10.1 %collective-permute-done.12.received_ref = bf16[256,1024]{1,0:T(8,128)(2,1)S(1)} collective-permute-done((bf16[256,1024]{1,0:T(8,128)(2,1)S(1)}, bf16[256,1024]{1,0:T(8,128)(2,1)S(1)}, u32[]{:S(2)}, u32[]{:S(2)}) %collective-permute-start.12) | collective-permute-done | bytes 524320 | tf_op jit(solution)/shard_map/ppermute | solution.py:798
  156.4 1.9 shard_map.214
  158.3 1.8 shard_map.215
  160.2 1.6 collective-permute-start.13
  161.9 2.3 shard_map.216
  164.3 1.5 collective-permute-start.22
  165.8 1.9 shard_map.217
  168.2 6.3 %collective-permute-done.13.other_ref = bf16[256,1024]{1,0:T(8,128)(2,1)S(1)} collective-permute-done((bf16[256,1024]{1,0:T(8,128)(2,1)S(1)}, bf16[256,1024]{1,0:T(8,128)(2,1)S(1)}, u32[]{:S(2)}, u32[]{:S(2)}) %collective-permute-start.13) | collective-permute-done | bytes 524320 | tf_op jit(solution)/shard_map/ppermute | solution.py:798
  174.6 1.4 shard_map.218
  177.4 5.7 %shard_map.220 = (bf16[2,256,1536]{2,1,0:T(8,128)(2,1)S(1)}, f32[128,512]{1,0:T(8,128)S(1)}, bf16[176,512]{1,0:T(8,128)(2,1)S(1)}) custom-call(s32[6]{0:T(128)S(1)} %stack.54.flag_ref, bf16[2,256,768]{2,1,0:T(8,128)(2,1)S(1)} %copy-done.9, bf16[2,256,768]{2,1,0:T(8,128)(2,1)S(1)} %copy-done.24, bf16[128,512]{1,0:T(8,128)(2,1)S(1)} %get-tuple-element.157.first_ref, ...), custom_call_target="tpu_custom_call" | custom-call | tf_op jit(solution)/shard_map/pallas_call | solution.py:42
  184.2 1.5 shard_map.222
  190.3 10.2 %collective-permute-done.21.returned_ref = bf16[176,512]{1,0:T(8,128)(2,1)S(1)} collective-permute-done((bf16[176,512]{1,0:T(8,128)(2,1)S(1)}, bf16[176,512]{1,0:T(8,128)(2,1)S(1)}, u32[]{:S(2)}, u32[]{:S(2)}) %collective-permute-start.21) | collective-permute-done | bytes 180256 | tf_op jit(solution)/shard_map/ppermute | solution.py:961
  200.5 6.8 %shard_map.224 = (f32[256,1024]{1,0:T(8,128)S(1)}, bf16[256,1024]{1,0:T(8,128)(2,1)S(1)}, f32[128,512]{1,0:T(8,128)S(1)}) custom-call(s32[6]{0:T(128)S(1)} %stack.54.flag_ref, f32[128,512]{1,0:T(8,128)S(1)} %get-tuple-element.201.near_ref, bf16[176,512]{1,0:T(8,128)(2,1)S(1)} %collective-permute-done.21.returned_ref, ...), custom_call_target="tpu_custom_call" | custom-call | tf_op jit(solution)/shard_map/pallas_call | solution.py:42
  210.4 1.6 shard_map.226
  213.9 4.3 %shard_map.227.param_ref = f32[40,512]{1,0:T(8,128)S(1)} custom-call(s32[6]{0:T(128)S(1)} %stack.54.flag_ref, bf16[2,256,1024]{2,1,0:T(8,128)(2,1)S(1)} %get-tuple-element.224.tile_ref, f32[128,512]{1,0:T(8,128)S(1)} %get-tuple-element.201.near_ref, f32[128,512]{1,0:T(8,128)S(1)} %get-tuple-element.213.last_ref, ...), custom_call_target="tpu_custom_call" | custom-call | tf_op jit(solution)/shard_map/pallas_call | solution.py:42
  218.2 3.5 %collective-permute-done.27.received_ref = bf16[256,1024]{1,0:T(8,128)(2,1)S(1)} collective-permute-done((bf16[256,1024]{1,0:T(8,128)(2,1)S(1)}, bf16[256,1024]{1,0:T(8,128)(2,1)S(1)}, u32[]{:S(2)}, u32[]{:S(2)}) %collective-permute-start.27) | collective-permute-done | bytes 524320 | tf_op jit(solution)/shard_map/ppermute | solution.py:798
  221.7 1.6 collective-permute-start.25
  223.4 2.4 shard_map.228
  227.0 3.2 %collective-permute-done.23.r1_ref = bf16[128,1536]{1,0:T(8,128)(2,1)S(1)} collective-permute-done((bf16[128,1536]{1,0:T(8,128)(2,1)S(1)}, bf16[128,1536]{1,0:T(8,128)(2,1)S(1)}, u32[]{:S(2)}, u32[]{:S(2)}) %collective-permute-start.23) | collective-permute-done | bytes 393248 | tf_op jit(solution)/shard_map/ppermute | solution.py:801
  230.1 4.2 %collective-permute-done.24.r2_ref = bf16[128,1536]{1,0:T(8,128)(2,1)S(1)} collective-permute-done((bf16[128,1536]{1,0:T(8,128)(2,1)S(1)}, bf16[128,1536]{1,0:T(8,128)(2,1)S(1)}, u32[]{:S(2)}, u32[]{:S(2)}) %collective-permute-start.24) | collective-permute-done | bytes 393248 | tf_op jit(solution)/shard_map/ppermute | solution.py:801
  234.3 7.0 %collective-permute-done.25.r3_ref = bf16[128,1536]{1,0:T(8,128)(2,1)S(1)} collective-permute-done((bf16[128,1536]{1,0:T(8,128)(2,1)S(1)}, bf16[128,1536]{1,0:T(8,128)(2,1)S(1)}, u32[]{:S(2)}, u32[]{:S(2)}) %collective-permute-start.25) | collective-permute-done | bytes 393248 | tf_op jit(solution)/shard_map/ppermute | solution.py:801
  242.1 8.8 %collective-permute-done.16.c_ref = bf16[256,1024]{1,0:T(8,128)(2,1)S(1)} collective-permute-done((bf16[256,1024]{1,0:T(8,128)(2,1)S(1)}, bf16[256,1024]{1,0:T(8,128)(2,1)S(1)}, u32[]{:S(2)}, u32[]{:S(2)}) %collective-permute-start.16) | collective-permute-done | bytes 524320 | tf_op jit(solution)/shard_map/ppermute | solution.py:798
  250.8 1.5 shard_map.231
  252.3 9.3 %collective-permute-done.31.b_ref = bf16[128,768]{1,0:T(8,128)(2,1)S(1)} collective-permute-done((bf16[128,768]{1,0:T(8,128)(2,1)S(1)}, bf16[128,768]{1,0:T(8,128)(2,1)S(1)}, u32[]{:S(2)}, u32[]{:S(2)}) %collective-permute-start.31) | collective-permute-done | bytes 196640 | tf_op jit(solution)/shard_map/ppermute | solution.py:798
  262.2 1.5 shard_map.233
  265.4 1.8 collective-permute-start.37
  267.2 3.6 %collective-permute-done.29.received_ref = f32[8,256]{1,0:T(8,128)S(1)} collective-permute-done((f32[8,256]{1,0:T(8,128)S(1)}, f32[8,256]{1,0:T(8,128)S(1)}, u32[]{:S(2)}, u32[]{:S(2)}) %collective-permute-start.29) | collective-permute-done | bytes 8224 | tf_op jit(solution)/shard_map/ppermute | solution.py:798
  271.5 5.0 %collective-permute-done.32.b_ref = f32[48,256]{1,0:T(8,128)S(1)} collective-permute-done((f32[48,256]{1,0:T(8,128)S(1)}, f32[48,256]{1,0:T(8,128)S(1)}, u32[]{:S(2)}, u32[]{:S(2)}) %collective-permute-start.32) | collective-permute-done | bytes 49184 | tf_op jit(solution)/shard_map/ppermute | solution.py:798
  280.5 3.1 collective-permute-done.34.b_ref
  284.1 1.8 collective-permute-start.38
  285.8 3.2 %collective-permute-done.38.b_ref = f32[48,256]{1,0:T(8,128)S(1)} collective-permute-done((f32[48,256]{1,0:T(8,128)S(1)}, f32[48,256]{1,0:T(8,128)S(1)}, u32[]{:S(2)}, u32[]{:S(2)}) %collective-permute-start.38) | collective-permute-done | bytes 49184 | tf_op jit(solution)/shard_map/ppermute | solution.py:801
  291.9 2.4 shard_map.239
  294.3 7.2 %all-gather.5.cloned.1.call-done.all_ref = bf16[1024,2304]{1,0:T(8,128)(2,1)} async-done(((bf16[128,2304]{1,0:T(8,128)(2,1)}), bf16[1024,2304]{1,0:T(8,128)(2,1)}) %all-gather.5.cloned.1.call-update) | async-done | bytes 4718608 | tf_op jit(solution)/shard_map/all_gather | solution.py:804
  301.5 2.3 copy-done.15
  303.9 4.7 %shard_map.240 = (f32[1024,1024]{1,0:T(8,128)}, f32[1024,1024]{1,0:T(8,128)}, f32[256,1024]{1,0:T(8,128)}) custom-call(s32[6]{0:T(128)S(1)} %stack.54.flag_ref, bf16[1024,2304]{1,0:T(8,128)(2,1)S(1)} %copy-done.15), custom_call_target="tpu_custom_call" | custom-call | tf_op jit(solution)/shard_map/pallas_call | solution.py:42
  (161 shorter events, 37.1 us)
Async XLA Ops:
  7.2 115.6 %all-gather.3.cloned.1.call-start = ((), (), s32[]{:S(2)}) async-start(), calls=%async_computation | async-start | bytes 4718592 | tf_op jit(solution)/shard_map/all_gather | solution.py:804
  10.6 25.6 %collective-permute-start = (bf16[256,1024]{1,0:T(8,128)(2,1)S(1)}, bf16[256,1024]{1,0:T(8,128)(2,1)S(1)}, u32[]{:S(2)}, u32[]{:S(2)}) collective-permute-start(bf16[256,1024]{1,0:T(8,128)(2,1)S(1)} %shard_map.203.own_ref), channel_id=1, source_target_pairs={{0,1},{1,0},{2,3},{3,2},{4,5},{5,4},{6,7},{7,6},{8,9},{9,8},{10,11... | collective-permute-start | bytes 1572872 | tf_op jit(solution)/shard_map/ppermute | solution.py:798
  19.3 3.3 %copy-start.37 = (f32[256,16]{0,1:T(8,128)S(1)}, f32[256,16]{0,1:T(8,128)}, u32[]{:S(2)}) copy-start(f32[256,16]{0,1:T(8,128)} %param.17) | copy-start | bytes 49156
  19.3 3.3 %copy-start.38 = (f32[256,16]{0,1:T(8,128)S(1)}, f32[256,16]{0,1:T(8,128)}, u32[]{:S(2)}) copy-start(f32[256,16]{0,1:T(8,128)} %param.16) | copy-start | bytes 49156
  19.3 3.3 %copy-start.39 = (f32[256]{0:T(256)S(1)}, f32[256]{0:T(256)}, u32[]{:S(2)}) copy-start(f32[256]{0:T(256)} %param.18) | copy-start | bytes 3076
  19.3 3.7 %copy-start.11 = (bf16[1024,3,256]{2,0,1:T(8,128)(2,1)S(1)}, bf16[1024,3,256]{2,0,1:T(8,128)(2,1)}, u32[]{:S(2)}) copy-start(bf16[1024,3,256]{2,0,1:T(8,128)(2,1)} %param.15) | copy-start | bytes 4718596
  20.0 16.2 %collective-permute-start.1 = (bf16[128,1024]{1,0:T(8,128)(2,1)S(1)}, bf16[128,1024]{1,0:T(8,128)(2,1)S(1)}, u32[]{:S(2)}, u32[]{:S(2)}) collective-permute-start(bf16[128,1024]{1,0:T(8,128)(2,1)S(1)} %get-tuple-element.135), channel_id=1, source_target_pairs={{0,2},{1,3},{2,0},{3,1},{4,6},{5,7},{6,4},{7,5},{8,10},{9,11},{10,... | collective-permute-start | bytes 786440 | tf_op jit(solution)/shard_map/ppermute | solution.py:798
  22.7 13.5 %collective-permute-start.2 = (f32[40,256]{1,0:T(8,128)S(1)}, f32[40,256]{1,0:T(8,128)S(1)}, u32[]{:S(2)}, u32[]{:S(2)}) collective-permute-start(f32[40,256]{1,0:T(8,128)S(1)} %pad_maximum_fusion.3), channel_id=1, source_target_pairs={{0,2},{1,3},{2,0},{3,1},{4,6},{5,7},{6,4},{7,5},{8,10},{9,11},{10,... | collective-permute-start | bytes 122888 | tf_op jit(solution)/shard_map/ppermute | solution.py:798
  23.3 23.1 %copy-start.6 = (bf16[1024,768]{1,0:T(8,128)(2,1)}, bf16[1024,768]{1,0:T(8,128)(2,1)S(1)}, u32[]{:S(2)}) copy-start(bf16[1024,768]{1,0:T(8,128)(2,1)S(1)} %constant_dynamic-update-slice_fusion.weight_ref.near_weight_ref) | copy-start | bytes 4718596
  36.2 10.2 %collective-permute-start.4 = (bf16[128,1024]{1,0:T(8,128)(2,1)S(1)}, bf16[128,1024]{1,0:T(8,128)(2,1)S(1)}, u32[]{:S(2)}, u32[]{:S(2)}) collective-permute-start(bf16[128,1024]{1,0:T(8,128)(2,1)S(1)} %collective-permute-done.1), channel_id=1, source_target_pairs={{0,8},{4,12},{8,0},{12,4},{16,24},{20,28},{24,16},{28,20},{1,9},{5... | collective-permute-start | bytes 786440 | tf_op jit(solution)/shard_map/ppermute | solution.py:801
  37.7 12.2 %collective-permute-start.5 = (bf16[128,1024]{1,0:T(8,128)(2,1)S(1)}, bf16[128,1024]{1,0:T(8,128)(2,1)S(1)}, u32[]{:S(2)}, u32[]{:S(2)}) collective-permute-start(bf16[128,1024]{1,0:T(8,128)(2,1)S(1)} %collective-permute-done.1), channel_id=1, source_target_pairs={{0,16},{4,20},{8,24},{12,28},{16,0},{20,4},{24,8},{28,12},{1,17},{... | collective-permute-start | bytes 786440 | tf_op jit(solution)/shard_map/ppermute | solution.py:801
  39.2 10.7 %collective-permute-start.6 = (bf16[128,1024]{1,0:T(8,128)(2,1)S(1)}, bf16[128,1024]{1,0:T(8,128)(2,1)S(1)}, u32[]{:S(2)}, u32[]{:S(2)}) collective-permute-start(bf16[128,1024]{1,0:T(8,128)(2,1)S(1)} %collective-permute-done.1), channel_id=1, source_target_pairs={{0,24},{4,28},{8,16},{12,20},{16,8},{20,12},{24,0},{28,4},{1,25},{... | collective-permute-start | bytes 786440 | tf_op jit(solution)/shard_map/ppermute | solution.py:801
  46.4 40.3 %copy-start.8 = (bf16[2,256,768]{2,1,0:T(8,128)(2,1)}, bf16[2,256,768]{2,1,0:T(8,128)(2,1)S(1)}, u32[]{:S(2)}) copy-start(bf16[2,256,768]{2,1,0:T(8,128)(2,1)S(1)} %shard_map.206.near_ref) | copy-start | bytes 2359300
  50.1 36.6 %copy-start.13 = (bf16[256,1024]{1,0:T(8,128)(2,1)S(1)}, bf16[256,1024]{1,0:T(8,128)(2,1)}, u32[]{:S(2)}) copy-start(bf16[256,1024]{1,0:T(8,128)(2,1)} %out_near_ref.3) | copy-start | bytes 1572868
  50.1 5.0 %collective-permute-start.7 = (bf16[4,128,1024]{2,1,0:T(8,128)(2,1)S(1)}, bf16[4,128,1024]{2,1,0:T(8,128)(2,1)S(1)}, u32[]{:S(2)}, u32[]{:S(2)}) collective-permute-start(bf16[4,128,1024]{2,1,0:T(8,128)(2,1)S(1)} %pad_maximum_fusion.even_ref), channel_id=1, source_target_pairs={{0,4},{4,0},{8,12},{12,8},{16,20},{20,16},{24,28},{28,24},{1,5},{5... | collective-permute-start | bytes 3145736 | tf_op jit(solution)/shard_map/ppermute | solution.py:801
  50.2 26.4 %collective-permute-start.10 = (bf16[256,1024]{1,0:T(8,128)(2,1)S(1)}, bf16[256,1024]{1,0:T(8,128)(2,1)}, u32[]{:S(2)}, u32[]{:S(2)}) collective-permute-start(bf16[256,1024]{1,0:T(8,128)(2,1)S(1)} %get-tuple-element.170), channel_id=1, source_target_pairs={{0,2},{1,3},{2,0},{3,1},{4,6},{5,7},{6,4},{7,5},{8,10},{9,11},{10,... | collective-permute-start | bytes 1572872 | tf_op jit(solution)/shard_map/ppermute | solution.py:798
  50.3 17.0 %collective-permute-start.3 = (bf16[224,512]{1,0:T(8,128)(2,1)S(1)}, bf16[224,512]{1,0:T(8,128)(2,1)S(1)}, u32[]{:S(2)}, u32[]{:S(2)}) collective-permute-start(bf16[224,512]{1,0:T(8,128)(2,1)S(1)} %get-tuple-element.146), channel_id=1, source_target_pairs={{0,2},{1,3},{4,6},{5,7},{8,10},{9,11},{12,14},{13,15},{16,18},{17,... | collective-permute-start | bytes 688136 | tf_op jit(solution)/shard_map/ppermute | solution.py:863
  58.7 28.0 %copy-start.23 = (bf16[2,256,768]{2,1,0:T(8,128)(2,1)}, bf16[2,256,768]{2,1,0:T(8,128)(2,1)S(1)}, u32[]{:S(2)}) copy-start(bf16[2,256,768]{2,1,0:T(8,128)(2,1)S(1)} %get-tuple-element.155.far_ref) | copy-start | bytes 2359300
  76.6 33.7 %copy-start.34 = (f32[1024]{0:T(1024)S(1)}, f32[1024]{0:T(1024)}, u32[]{:S(2)}) copy-start(f32[1024]{0:T(1024)} %param.20) | copy-start | bytes 12292
  76.6 224.9 %all-gather.5.cloned.1.call-start = ((), (), s32[]{:S(2)}) async-start(), calls=%async_computation.1 | async-start | bytes 5308416 | tf_op jit(solution)/shard_map/all_gather | solution.py:804
  76.8 33.5 %copy-start.17 = (bf16[1,256,1024]{2,1,0:T(8,128)(2,1)S(1)}, bf16[1,256,1024]{2,1,0:T(8,128)(2,1)}, u32[]{:S(2)}) copy-start(bf16[1,256,1024]{2,1,0:T(8,128)(2,1)} %param.12) | copy-start | bytes 1572868
  76.9 22.8 %collective-permute-start.9 = (bf16[256,1024]{1,0:T(8,128)(2,1)}, bf16[256,1024]{1,0:T(8,128)(2,1)S(1)}, u32[]{:S(2)}, u32[]{:S(2)}) collective-permute-start(bf16[256,1024]{1,0:T(8,128)(2,1)} %bitcast.18.c_ref.cot0.cot_ref), channel_id=1, source_target_pairs={{0,1},{1,0},{2,3},{3,2},{4,5},{5,4},{6,7},{7,6},{8,9},{9,8},{10,11... | collective-permute-start | bytes 1572872 | tf_op jit(solution)/shard_map/ppermute | solution.py:798
  92.3 30.5 %copy-start.3 = (bf16[1024,1024]{1,0:T(8,128)(2,1)S(1)}, bf16[1024,1024]{1,0:T(8,128)(2,1)}, u32[]{:S(2)}) copy-start(bf16[1024,1024]{1,0:T(8,128)(2,1)} %up0_ref.3) | copy-start | bytes 6291460
  92.3 18.0 %collective-permute-start.8 = (bf16[256,1024]{1,0:T(8,128)(2,1)S(1)}, bf16[256,1024]{1,0:T(8,128)(2,1)S(1)}, u32[]{:S(2)}, u32[]{:S(2)}) collective-permute-start(bf16[256,1024]{1,0:T(8,128)(2,1)S(1)} %get-tuple-element.162), channel_id=1, source_target_pairs={{0,1},{1,0},{2,3},{3,2},{4,5},{5,4},{6,7},{7,6},{8,9},{9,8},{10,11... | collective-permute-start | bytes 1572872 | tf_op jit(solution)/shard_map/ppermute | solution.py:798
  113.1 21.4 %collective-permute-start.11 = (bf16[256,1024]{1,0:T(8,128)(2,1)}, bf16[256,1024]{1,0:T(8,128)(2,1)}, u32[]{:S(2)}, u32[]{:S(2)}) collective-permute-start(bf16[256,1024]{1,0:T(8,128)(2,1)} %get-tuple-element.169.n_ref), channel_id=1, source_target_pairs={{0,1},{1,0},{2,3},{3,2},{4,5},{5,4},{6,7},{7,6},{8,9},{9,8},{10,11... | collective-permute-start | bytes 1572872 | tf_op jit(solution)/shard_map/ppermute | solution.py:798
  126.6 7.9 %copy-start.1 = (bf16[2048,1024]{1,0:T(8,128)(2,1)S(1)}, bf16[2048,1024]{1,0:T(8,128)(2,1)}, u32[]{:S(2)}) copy-start(bf16[2048,1024]{1,0:T(8,128)(2,1)} %all-gather.3.cloned.1.call-done) | copy-start | bytes 12582916
  126.6 7.9 %copy-start.20 = (bf16[256,1024]{1,0:T(8,128)(2,1)S(1)}, bf16[256,1024]{1,0:T(8,128)(2,1)}, u32[]{:S(2)}) copy-start(bf16[256,1024]{1,0:T(8,128)(2,1)} %copy-done.19) | copy-start | bytes 1572868
  142.2 14.2 %collective-permute-start.12 = (bf16[256,1024]{1,0:T(8,128)(2,1)S(1)}, bf16[256,1024]{1,0:T(8,128)(2,1)S(1)}, u32[]{:S(2)}, u32[]{:S(2)}) collective-permute-start(bf16[256,1024]{1,0:T(8,128)(2,1)S(1)} %get-tuple-element.179), channel_id=1, source_target_pairs={{0,1},{1,0},{2,3},{3,2},{4,5},{5,4},{6,7},{7,6},{8,9},{9,8},{10,11... | collective-permute-start | bytes 1572872 | tf_op jit(solution)/shard_map/ppermute | solution.py:798
  143.8 12.6 %copy-start.22 = (f32[256,1024]{1,0:T(8,128)S(1)}, f32[256,1024]{1,0:T(8,128)}, u32[]{:S(2)}) copy-start(f32[256,1024]{1,0:T(8,128)} %copy-done.21) | copy-start | bytes 3145732
  146.2 15.7 %collective-permute-start.15 = (bf16[1024,1024]{1,0:T(8,128)(2,1)S(1)}, bf16[1024,1024]{1,0:T(8,128)(2,1)S(1)}, u32[]{:S(2)}, u32[]{:S(2)}) collective-permute-start(bf16[1024,1024]{1,0:T(8,128)(2,1)S(1)} %shard_map.213), channel_id=1, source_target_pairs={{0,4},{4,0},{8,12},{12,8},{16,20},{20,16},{24,28},{28,24},{1,5},{5... | collective-permute-start | bytes 6291464 | tf_op jit(solution)/shard_map/ppermute | solution.py:801
  158.3 3.5 %copy-start.31 = (bf16[2,256,1024]{2,1,0:T(8,128)(2,1)S(1)}, bf16[2,256,1024]{2,1,0:T(8,128)(2,1)}, u32[]{:S(2)}) copy-start(bf16[2,256,1024]{2,1,0:T(8,128)(2,1)} %copy-done.30) | copy-start | bytes 3145732
  160.1 5.6 %collective-permute-start.14 = (bf16[512,2048]{1,0:T(8,128)(2,1)S(1)}, bf16[512,2048]{1,0:T(8,128)(2,1)S(1)}, u32[]{:S(2)}, u32[]{:S(2)}) collective-permute-start(bf16[512,2048]{1,0:T(8,128)(2,1)S(1)} %shard_map.215), channel_id=1, source_target_pairs={{0,4},{4,0},{8,12},{12,8},{16,20},{20,16},{24,28},{28,24},{1,5},{5... | collective-permute-start | bytes 6291464 | tf_op jit(solution)/shard_map/ppermute | solution.py:801
  160.2 14.3 %collective-permute-start.13 = (bf16[256,1024]{1,0:T(8,128)(2,1)S(1)}, bf16[256,1024]{1,0:T(8,128)(2,1)S(1)}, u32[]{:S(2)}, u32[]{:S(2)}) collective-permute-start(bf16[256,1024]{1,0:T(8,128)(2,1)S(1)} %get-tuple-element.185.own_ref), channel_id=1, source_target_pairs={{0,1},{1,0},{2,3},{3,2},{4,5},{5,4},{6,7},{7,6},{8,9},{9,8},{10,11... | collective-permute-start | bytes 1572872 | tf_op jit(solution)/shard_map/ppermute | solution.py:798
  164.3 25.3 %collective-permute-start.22 = (bf16[512,1024]{1,0:T(8,128)(2,1)S(1)}, bf16[512,1024]{1,0:T(8,128)(2,1)S(1)}, u32[]{:S(2)}, u32[]{:S(2)}) collective-permute-start(bf16[512,1024]{1,0:T(8,128)(2,1)S(1)} %get-tuple-element.190), channel_id=1, source_target_pairs={{0,8},{4,12},{8,0},{12,4},{16,24},{20,28},{24,16},{28,20},{1,9},{5... | collective-permute-start | bytes 3145736 | tf_op jit(solution)/shard_map/ppermute | solution.py:801
  165.8 8.8 %copy-start.14 = (bf16[256,1024]{1,0:T(8,128)(2,1)S(1)}, bf16[256,1024]{1,0:T(8,128)(2,1)}, u32[]{:S(2)}) copy-start(bf16[256,1024]{1,0:T(8,128)(2,1)} %out_near_ref.3) | copy-start | bytes 1572868
  165.8 8.8 %copy-start.27 = (bf16[1024,256]{1,0:T(8,128)(2,1)S(1)}, bf16[1024,256]{1,0:T(8,128)(2,1)}, u32[]{:S(2)}) copy-start(bf16[1024,256]{1,0:T(8,128)(2,1)} %copy-done.25) | copy-start | bytes 1572868
  167.6 39.7 %collective-permute-start.19 = (bf16[256,2048]{1,0:T(8,128)(2,1)S(1)}, bf16[256,2048]{1,0:T(8,128)(2,1)S(1)}, u32[]{:S(2)}, u32[]{:S(2)}) collective-permute-start(bf16[256,2048]{1,0:T(8,128)(2,1)S(1)} %get-tuple-element.193), channel_id=1, source_target_pairs={{0,16},{4,20},{8,24},{12,28},{16,0},{20,4},{24,8},{28,12},{1,17},{... | collective-permute-start | bytes 3145736 | tf_op jit(solution)/shard_map/ppermute | solution.py:801
  177.1 6.1 %collective-permute-start.17 = (bf16[512,512]{1,0:T(8,128)(2,1)S(1)}, bf16[512,512]{1,0:T(8,128)(2,1)S(1)}, u32[]{:S(2)}, u32[]{:S(2)}) collective-permute-start(bf16[512,512]{1,0:T(8,128)(2,1)S(1)} %shard_map.219), channel_id=1, source_target_pairs={{0,4},{4,0},{8,12},{12,8},{16,20},{20,16},{24,28},{28,24},{1,5},{5... | collective-permute-start | bytes 1572872 | tf_op jit(solution)/shard_map/ppermute | solution.py:801
  185.8 14.7 %copy-start.7 = (bf16[1024,768]{1,0:T(8,128)(2,1)S(1)}, bf16[1024,768]{1,0:T(8,128)(2,1)}, u32[]{:S(2)}) copy-start(bf16[1024,768]{1,0:T(8,128)(2,1)} %copy-done.6) | copy-start | bytes 4718596
  185.8 14.7 %copy-start.29 = (bf16[1024,768]{1,0:T(8,128)(2,1)S(1)}, bf16[1024,768]{1,0:T(8,128)(2,1)}, u32[]{:S(2)}) copy-start(bf16[1024,768]{1,0:T(8,128)(2,1)} %copy-done.28) | copy-start | bytes 4718596
  185.8 24.5 %collective-permute-start.18 = (bf16[512,1536]{1,0:T(8,128)(2,1)S(1)}, bf16[512,1536]{1,0:T(8,128)(2,1)S(1)}, u32[]{:S(2)}, u32[]{:S(2)}) collective-permute-start(bf16[512,1536]{1,0:T(8,128)(2,1)S(1)} %shard_map.222), channel_id=1, source_target_pairs={{0,4},{4,0},{8,12},{12,8},{16,20},{20,16},{24,28},{28,24},{1,5},{5... | collective-permute-start | bytes 4718600 | tf_op jit(solution)/shard_map/ppermute | solution.py:801
  186.1 21.2 %collective-permute-start.20 = (bf16[256,512]{1,0:T(8,128)(2,1)S(1)}, bf16[256,512]{1,0:T(8,128)(2,1)S(1)}, u32[]{:S(2)}, u32[]{:S(2)}) collective-permute-start(bf16[256,512]{1,0:T(8,128)(2,1)S(1)} %get-tuple-element.204), channel_id=1, source_target_pairs={{0,16},{4,20},{8,24},{12,28},{16,0},{20,4},{24,8},{28,12},{1,17},{... | collective-permute-start | bytes 786440 | tf_op jit(solution)/shard_map/ppermute | solution.py:801
  187.4 13.1 %collective-permute-start.21 = (bf16[176,512]{1,0:T(8,128)(2,1)S(1)}, bf16[176,512]{1,0:T(8,128)(2,1)S(1)}, u32[]{:S(2)}, u32[]{:S(2)}) collective-permute-start(bf16[176,512]{1,0:T(8,128)(2,1)S(1)} %get-tuple-element.202), channel_id=1, source_target_pairs={{2,0},{3,1},{6,4},{7,5},{10,8},{11,9},{14,12},{15,13},{18,16},{19,... | collective-permute-start | bytes 540680 | tf_op jit(solution)/shard_map/ppermute | solution.py:961
  208.1 17.7 %collective-permute-start.28 = (bf16[128,2560]{1,0:T(8,128)(2,1)S(1)}, bf16[128,2560]{1,0:T(8,128)(2,1)S(1)}, u32[]{:S(2)}, u32[]{:S(2)}) collective-permute-start(bf16[128,2560]{1,0:T(8,128)(2,1)S(1)} %get-tuple-element.218), channel_id=1, source_target_pairs={{0,8},{4,12},{8,0},{12,4},{16,24},{20,28},{24,16},{28,20},{1,9},{5... | collective-permute-start | bytes 1966088 | tf_op jit(solution)/shard_map/ppermute | solution.py:801
  209.0 12.7 %collective-permute-start.27 = (bf16[256,1024]{1,0:T(8,128)(2,1)S(1)}, bf16[256,1024]{1,0:T(8,128)(2,1)S(1)}, u32[]{:S(2)}, u32[]{:S(2)}) collective-permute-start(bf16[256,1024]{1,0:T(8,128)(2,1)S(1)} %get-tuple-element.212), channel_id=1, source_target_pairs={{0,1},{1,0},{2,3},{3,2},{4,5},{5,4},{6,7},{7,6},{8,9},{9,8},{10,11... | collective-permute-start | bytes 1572872 | tf_op jit(solution)/shard_map/ppermute | solution.py:798
  209.0 16.8 %collective-permute-start.26 = (bf16[256,1024]{1,0:T(8,128)(2,1)S(1)}, bf16[256,1024]{1,0:T(8,128)(2,1)S(1)}, u32[]{:S(2)}, u32[]{:S(2)}) collective-permute-start(bf16[256,1024]{1,0:T(8,128)(2,1)S(1)} %get-tuple-element.209), channel_id=1, source_target_pairs={{0,16},{4,20},{8,24},{12,28},{16,0},{20,4},{24,8},{28,12},{1,17},{... | collective-permute-start | bytes 1572872 | tf_op jit(solution)/shard_map/ppermute | solution.py:801
  211.9 11.4 %copy-start.18 = (bf16[1,256,1024]{2,1,0:T(8,128)(2,1)S(1)}, bf16[1,256,1024]{2,1,0:T(8,128)(2,1)}, u32[]{:S(2)}) copy-start(bf16[1,256,1024]{2,1,0:T(8,128)(2,1)} %param.12) | copy-start | bytes 1572868
  211.9 11.4 %copy-start.36 = (f32[1024]{0:T(1024)S(1)}, f32[1024]{0:T(1024)}, u32[]{:S(2)}) copy-start(f32[1024]{0:T(1024)} %param.14) | copy-start | bytes 12292
  212.0 18.2 %collective-permute-start.23 = (bf16[128,1536]{1,0:T(8,128)(2,1)S(1)}, bf16[128,1536]{1,0:T(8,128)(2,1)S(1)}, u32[]{:S(2)}, u32[]{:S(2)}) collective-permute-start(bf16[128,1536]{1,0:T(8,128)(2,1)S(1)} %get-tuple-element.221), channel_id=1, source_target_pairs={{0,16},{4,20},{8,24},{12,28},{16,0},{20,4},{24,8},{28,12},{1,17},{... | collective-permute-start | bytes 1179656 | tf_op jit(solution)/shard_map/ppermute | solution.py:801
  212.7 21.6 %collective-permute-start.24 = (bf16[128,1536]{1,0:T(8,128)(2,1)S(1)}, bf16[128,1536]{1,0:T(8,128)(2,1)S(1)}, u32[]{:S(2)}, u32[]{:S(2)}) collective-permute-start(bf16[128,1536]{1,0:T(8,128)(2,1)S(1)} %get-tuple-element.222), channel_id=1, source_target_pairs={{0,8},{4,12},{8,0},{12,4},{16,24},{20,28},{24,16},{28,20},{1,9},{5... | collective-permute-start | bytes 1179656 | tf_op jit(solution)/shard_map/ppermute | solution.py:801
  221.7 19.6 %collective-permute-start.25 = (bf16[128,1536]{1,0:T(8,128)(2,1)S(1)}, bf16[128,1536]{1,0:T(8,128)(2,1)S(1)}, u32[]{:S(2)}, u32[]{:S(2)}) collective-permute-start(bf16[128,1536]{1,0:T(8,128)(2,1)S(1)} %get-tuple-element.223), channel_id=1, source_target_pairs={{0,24},{4,28},{8,16},{12,20},{16,8},{20,12},{24,0},{28,4},{1,25},{... | collective-permute-start | bytes 1179656 | tf_op jit(solution)/shard_map/ppermute | solution.py:801
  226.6 35.5 %collective-permute-start.30 = (bf16[128,2304]{1,0:T(8,128)(2,1)S(1)}, bf16[128,2304]{1,0:T(8,128)(2,1)S(1)}, u32[]{:S(2)}, u32[]{:S(2)}) collective-permute-start(bf16[128,2304]{1,0:T(8,128)(2,1)S(1)} %get-tuple-element.231), channel_id=1, source_target_pairs={{0,2},{1,3},{2,0},{3,1},{4,6},{5,7},{6,4},{7,5},{8,10},{9,11},{10,... | collective-permute-start | bytes 1769480 | tf_op jit(solution)/shard_map/ppermute | solution.py:798
  226.7 24.1 %collective-permute-start.16 = (bf16[256,1024]{1,0:T(8,128)(2,1)S(1)}, bf16[256,1024]{1,0:T(8,128)(2,1)S(1)}, u32[]{:S(2)}, u32[]{:S(2)}) collective-permute-start(bf16[256,1024]{1,0:T(8,128)(2,1)S(1)} %get-tuple-element.198), channel_id=1, source_target_pairs={{0,1},{1,0},{2,3},{3,2},{4,5},{5,4},{6,7},{7,6},{8,9},{9,8},{10,11... | collective-permute-start | bytes 1572872 | tf_op jit(solution)/shard_map/ppermute | solution.py:798
  242.0 19.6 %collective-permute-start.31 = (bf16[128,768]{1,0:T(8,128)(2,1)S(1)}, bf16[128,768]{1,0:T(8,128)(2,1)S(1)}, u32[]{:S(2)}, u32[]{:S(2)}) collective-permute-start(bf16[128,768]{1,0:T(8,128)(2,1)S(1)} %get-tuple-element.236), channel_id=1, source_target_pairs={{0,2},{1,3},{2,0},{3,1},{4,6},{5,7},{6,4},{7,5},{8,10},{9,11},{10,... | collective-permute-start | bytes 589832 | tf_op jit(solution)/shard_map/ppermute | solution.py:798
  263.7 15.2 %collective-permute-start.35 = (bf16[128,768]{1,0:T(8,128)(2,1)S(1)}, bf16[128,768]{1,0:T(8,128)(2,1)S(1)}, u32[]{:S(2)}, u32[]{:S(2)}) collective-permute-start(bf16[128,768]{1,0:T(8,128)(2,1)S(1)} %shard_map.232), channel_id=1, source_target_pairs={{0,8},{4,12},{8,0},{12,4},{16,24},{20,28},{24,16},{28,20},{1,9},{5... | collective-permute-start | bytes 589832 | tf_op jit(solution)/shard_map/ppermute | solution.py:801
  264.7 14.2 %collective-permute-start.36 = (bf16[128,768]{1,0:T(8,128)(2,1)S(1)}, bf16[128,768]{1,0:T(8,128)(2,1)S(1)}, u32[]{:S(2)}, u32[]{:S(2)}) collective-permute-start(bf16[128,768]{1,0:T(8,128)(2,1)S(1)} %shard_map.232), channel_id=1, source_target_pairs={{0,16},{4,20},{8,24},{12,28},{16,0},{20,4},{24,8},{28,12},{1,17},{... | collective-permute-start | bytes 589832 | tf_op jit(solution)/shard_map/ppermute | solution.py:801
  265.4 13.7 %collective-permute-start.37 = (bf16[128,768]{1,0:T(8,128)(2,1)S(1)}, bf16[128,768]{1,0:T(8,128)(2,1)S(1)}, u32[]{:S(2)}, u32[]{:S(2)}) collective-permute-start(bf16[128,768]{1,0:T(8,128)(2,1)S(1)} %shard_map.232), channel_id=1, source_target_pairs={{0,24},{4,28},{8,16},{12,20},{16,8},{20,12},{24,0},{28,4},{1,25},{... | collective-permute-start | bytes 589832 | tf_op jit(solution)/shard_map/ppermute | solution.py:801
  267.2 3.7 %collective-permute-start.29 = (f32[8,256]{1,0:T(8,128)S(1)}, f32[8,256]{1,0:T(8,128)S(1)}, u32[]{:S(2)}, u32[]{:S(2)}) collective-permute-start(f32[8,256]{1,0:T(8,128)S(1)} %get-tuple-element.238.gains_ref), channel_id=1, source_target_pairs={{0,1},{1,0},{2,3},{3,2},{4,5},{5,4},{6,7},{7,6},{8,9},{9,8},{10,11... | collective-permute-start | bytes 24584 | tf_op jit(solution)/shard_map/ppermute | solution.py:798
  271.4 5.1 %collective-permute-start.32 = (f32[48,256]{1,0:T(8,128)S(1)}, f32[48,256]{1,0:T(8,128)S(1)}, u32[]{:S(2)}, u32[]{:S(2)}) collective-permute-start(f32[48,256]{1,0:T(8,128)S(1)} %get-tuple-element.243), channel_id=1, source_target_pairs={{0,2},{1,3},{2,0},{3,1},{4,6},{5,7},{6,4},{7,5},{8,10},{9,11},{10,... | collective-permute-start | bytes 147464 | tf_op jit(solution)/shard_map/ppermute | solution.py:798
  277.0 1.3 collective-permute-start.33
  279.3 12.6 %collective-permute-start.39 = (bf16[4,128,768]{2,1,0:T(8,128)(2,1)S(1)}, bf16[4,128,768]{2,1,0:T(8,128)(2,1)S(1)}, u32[]{:S(2)}, u32[]{:S(2)}) collective-permute-start(bf16[4,128,768]{2,1,0:T(8,128)(2,1)S(1)} %pad_maximum_fusion.1.even_ref), channel_id=1, source_target_pairs={{0,4},{4,0},{8,12},{12,8},{16,20},{20,16},{24,28},{28,24},{1,5},{5... | collective-permute-start | bytes 2359304 | tf_op jit(solution)/shard_map/ppermute | solution.py:801
  279.4 4.2 %collective-permute-start.34 = (f32[48,256]{1,0:T(8,128)S(1)}, f32[48,256]{1,0:T(8,128)S(1)}, u32[]{:S(2)}, u32[]{:S(2)}) collective-permute-start(f32[48,256]{1,0:T(8,128)S(1)} %shard_map.236.a_ref), channel_id=1, source_target_pairs={{0,8},{4,12},{8,0},{12,4},{16,24},{20,28},{24,16},{28,20},{1,9},{5... | collective-permute-start | bytes 147464 | tf_op jit(solution)/shard_map/ppermute | solution.py:801
  284.1 4.9 %collective-permute-start.38 = (f32[48,256]{1,0:T(8,128)S(1)}, f32[48,256]{1,0:T(8,128)S(1)}, u32[]{:S(2)}, u32[]{:S(2)}) collective-permute-start(f32[48,256]{1,0:T(8,128)S(1)} %shard_map.237.a_ref), channel_id=1, source_target_pairs={{0,16},{4,20},{8,24},{12,28},{16,0},{20,4},{24,8},{28,12},{1,17},{... | collective-permute-start | bytes 147464 | tf_op jit(solution)/shard_map/ppermute | solution.py:801
  301.5 2.3 copy-start.15
  (18 other events, 22.5 us)
Sparse Core Ops, SparseCore 0:
  76.7 46.0 all-gather.2
  263.8 37.6 all-gather.4

commit v3 on v2

--- a/solution.py
+++ b/solution.py
@@ -36,7 +36,11 @@
     return jax.ShapeDtypeStruct(dims, dtype)
 
 
-def call(kernel, out_shape, scratch=()):
+def length(micros):
+    return pl.CostEstimate(flops=int(micros * 1e9), bytes_accessed=0, transcendentals=0)
+
+
+def call(kernel, out_shape, scratch=(), micros=0):
     def run(flags, *args):
         vmem = pl.BlockSpec(memory_space=pltpu.VMEM)
         return pl.pallas_call(
@@ -46,7 +50,7 @@
             out_specs=jax.tree.map(lambda _: vmem, out_shape),
             scratch_shapes=scratch,
             compiler_params=pltpu.CompilerParams(vmem_limit_bytes=VMEM_LIMIT),
-            cost_estimate=pl.CostEstimate(flops=0, bytes_accessed=0, transcendentals=0),
+            cost_estimate=length(micros),
         )(flags, *args)
 
     return run
@@ -66,41 +70,62 @@
     return pl.ds(pl.multiple_of(start, size), size)
 
 
-def cut_slices(flag_ref, qkv_ref, out_ref, up_ref, down_ref, attn_ref, mlp_ref):
-    channels = qkv_ref.shape[2]
-    rows = attn_ref.shape[0]
-    for part in range(3):
-        attn_ref[:, part * channels : (part + 1) * channels] = qkv_ref[part]
-    attn_ref[:, 3 * channels :] = out_ref[...].T
-    mlp_ref[:rows, :] = up_ref[...]
-    mlp_ref[rows:, :] = down_ref[...]
-
-
-def run_cut_slices(flags, qkv_parts, out_weight, up_weight, down_weight):
+def cut_slices(
+    flag_ref, qkv_ref, out_ref, up_ref, down_ref, ssm_ref, attn_ref, mlp_ref, out_slice, *sems
+):
+    rows = mlp_ref.shape[0] // 2
+    channels = out_slice.shape[0]
+    count = ssm_ref.shape[0]
+    for k, part in enumerate(split_three(ssm_ref[...])):
+        attn_ref[rows : rows + count, k * channels : (k + 1) * channels] = part
+    attn_ref[rows : rows + count, 3 * channels :] = jnp.zeros((count, channels), bf16)
+    at = aligned(flag_ref[PLACE] * rows, rows)
+    copies = [
+        pltpu.make_async_copy(
+            qkv_ref.at[part, at, :],
+            attn_ref.at[:rows, part * channels : (part + 1) * channels],
+            sems[part],
+        )
+        for part in range(3)
+    ] + [
+        pltpu.make_async_copy(out_ref.at[:, at], out_slice, sems[3]),
+        pltpu.make_async_copy(up_ref.at[at, :], mlp_ref.at[:rows, :], sems[4]),
+        pltpu.make_async_copy(down_ref.at[at, :], mlp_ref.at[rows:, :], sems[5]),
+    ]
+    for copy in copies:
+        copy.start()
+    for copy in copies:
+        copy.wait()
+    attn_ref[:rows, 3 * channels :] = out_slice[...].T
+
+
+def join_ssm(flag_ref, own_ref, across_ref, out_ref):
+    channels = own_ref.shape[1]
+    start = across_ref.shape[0] - own_ref.shape[0]
+    out_ref[:, :channels] = own_ref[...]
+    parts = [across_ref[start:, k * channels : (k + 1) * channels].astype(f32) for k in range(3)]
+    out_ref[:, channels:] = (parts[0] + parts[1]) + parts[2]
+
+
+def run_cut_slices(flags, qkv_parts, out_weight, up_weight, down_weight, ssm_pack):
     channels = qkv_parts.shape[2]
     width = out_weight.shape[1]
     rows = width // GROUP
-    here = lambda j, flag_ref: (flag_ref[PLACE], 0)
+    vmem = pl.BlockSpec(memory_space=pltpu.VMEM)
     return pl.pallas_call(
         cut_slices,
-        grid_spec=pltpu.PrefetchScalarGridSpec(
-            num_scalar_prefetch=1,
-            grid=(1,),
-            in_specs=[
-                pl.BlockSpec((3, rows, channels), lambda j, flag_ref: (0, flag_ref[PLACE], 0)),
-                pl.BlockSpec((channels, rows), lambda j, flag_ref: (0, flag_ref[PLACE])),
-                pl.BlockSpec((rows, width), here),
-                pl.BlockSpec((rows, width), here),
-            ],
-            out_specs=(
-                pl.BlockSpec((rows, 4 * channels), lambda j, flag_ref: (0, 0)),
-                pl.BlockSpec((2 * rows, width), lambda j, flag_ref: (0, 0)),
-            ),
+        in_specs=[pl.BlockSpec(memory_space=pltpu.SMEM)]
+        + [pl.BlockSpec(memory_space=pltpu.HBM)] * 4
+        + [vmem],
+        out_specs=(vmem, vmem),
+        out_shape=(
+            shape((rows + ssm_pack.shape[0], 4 * channels), bf16),
+            shape((2 * rows, width), bf16),
         ),
-        out_shape=(shape((rows, 4 * channels), bf16), shape((2 * rows, width), bf16)),
-        compiler_params=pltpu.CompilerParams(vmem_limit_bytes=VMEM_LIMIT),
-        cost_estimate=pl.CostEstimate(flops=0, bytes_accessed=0, transcendentals=0),
-    )(flags, qkv_parts, out_weight, up_weight, down_weight)
+        scratch_shapes=[pltpu.VMEM((channels, rows), bf16)] + [pltpu.SemaphoreType.DMA] * 6,
+        compiler_params=pltpu.CompilerParams(vmem_limit_bytes=56 * 1024 * 1024),
+        cost_estimate=length(0),
+    )(flags, qkv_parts, out_weight, up_weight, down_weight, ssm_pack)
 
 
 def normalise(values):
@@ -133,6 +158,12 @@
     by_rows(body, x_ref.shape[0])
 
 
+def touch(flag_ref, up_ref, down_ref, cot_ref, paired_ref, out_ref):
+    out_ref[...] = (
+        up_ref[:8, :128] + down_ref[:8, :128] + (cot_ref[:8, :128] + paired_ref[:8, :128])
+    )
+
+
 def norm_two(flag_ref, x_ref, own_ref, received_ref, gain_ref, middle_ref, out_ref):
     def body(at):
         middle = x_ref[at, :].astype(f32) + own_ref[at, :] + received_ref[at, :].astype(f32)
@@ -144,7 +175,8 @@
 
 
 def norm_two_back(
-    flag_ref, middle_ref, own_ref, received_ref, cot_ref, gain_ref, grad_ref, low_ref, gain_out_ref
+    flag_ref, middle_ref, own_ref, received_ref, cot_ref, gain_ref, warm_ref, grad_ref, low_ref,
+    gain_out_ref,
 ):
     sums = []
 
@@ -274,9 +306,17 @@
     second_ref[...] = (local_ref[...] + acc[...]).astype(bf16)
 
 
+def qkv_back(flag_ref, dqkv_ref, near_weight_ref, far_weight_ref, out_ref):
+    split = near_weight_ref.shape[1]
+    for half in range(2):
+        out_ref[half] = mm(dqkv_ref[half, :, :split], near_weight_ref[...], NT) + mm(
+            dqkv_ref[half, :, split:], far_weight_ref[...], NT
+        )
+
+
 def ssm_signal_grad(
-    flag_ref, near_ref, returned_ref, rate_ref, coef_ref, skip_ref, dqkv_ref, near_weight_ref,
-    far_weight_ref, own_ref, send_ref, last_ref, rows_out, total,
+    flag_ref, near_ref, returned_ref, rate_ref, coef_ref, skip_ref, total_ref, own_ref, send_ref,
+    last_ref, rows_out, total,
 ):
     channels = rate_ref.shape[1] // 2
     adjoints = []
@@ -309,11 +349,8 @@
     adjoint = jnp.concatenate(adjoints, axis=1)
     for chunk in (3, 2, 1, 0):
         adjoint = lax.fori_loop(0, 16, partial(step, chunk=chunk), adjoint)
-    split = near_weight_ref.shape[1]
     for half in (1, 0):
-        total[...] = mm(dqkv_ref[half, :, :split], near_weight_ref[...], NT) + mm(
-            dqkv_ref[half, :, split:], far_weight_ref[...], NT
-        )
+        total[...] = total_ref[half]
         source = aligned(jnp.bitwise_xor(flag_ref[ODD], half) * HALF, HALF)
         for slot, name in enumerate((NEAR, FAR)):
             total[:, aligned(flag_ref[name] * channels, channels)] += rows_out[
@@ -396,35 +433,40 @@
     ]
 
 
-def attention_forward(
-    flag_ref, near_ref, far_ref, first_ref, second_ref, out_near_ref, out_far_ref, att_ref, own_ref,
-    send_ref,
-):
+def attend(flag_ref, qkv_ref, first_ref, second_ref, att_ref, slot):
     half0 = flag_ref[ODD]
     half1 = 1 - half0
-    heads = near_ref.shape[2] // (3 * HD)
-    for index in range(2 * heads):
-        qkv_ref = (near_ref, far_ref)[index // heads]
-        q0, k0, v0 = head_parts(qkv_ref, index % heads, half0)
-        q1, k1, v1 = head_parts(qkv_ref, index % heads, half1)
-        at = slice(index * HD, (index + 1) * HD)
+    heads = qkv_ref.shape[2] // (3 * HD)
+    for head in range(heads):
+        q0, k0, v0 = head_parts(qkv_ref, head, half0)
+        q1, k1, v1 = head_parts(qkv_ref, head, half1)
+        at = slice((slot * heads + head) * HD, (slot * heads + head + 1) * HD)
         first = first_ref[:, at]
         second = second_ref[:, at]
         (p00, p0c), (p11, p10, p1c), chosen = block_probs(
             q0, q1, k0, k1, first, second, flag_ref[WHOLE], flag_ref[LATE]
         )
-        att_ref[half0, :, at] = (mm(p00.astype(bf16), v0) + mm(p0c.astype(bf16), first)).astype(
+        to = slice(head * HD, (head + 1) * HD)
+        att_ref[half0, :, to] = (mm(p00.astype(bf16), v0) + mm(p0c.astype(bf16), first)).astype(
             bf16
         )
-        att_ref[half1, :, at] = (
+        att_ref[half1, :, to] = (
             mm(p11.astype(bf16), v1) + mm(p10.astype(bf16), v0) + mm(p1c.astype(bf16), chosen)
         ).astype(bf16)
-    split = heads * HD
+
+
+def attention_near(flag_ref, qkv_ref, first_ref, second_ref, att_ref):
+    attend(flag_ref, qkv_ref, first_ref, second_ref, att_ref, 0)
+
+
+def attention_far(
+    flag_ref, qkv_ref, first_ref, second_ref, near_ref, out_near_ref, out_far_ref, att_ref, own_ref,
+    send_ref,
+):
+    attend(flag_ref, qkv_ref, first_ref, second_ref, att_ref, 1)
 
     def projected(half):
-        return mm(att_ref[half, :, :split], out_near_ref[...]) + mm(
-            att_ref[half, :, split:], out_far_ref[...], NT
-        )
+        return mm(near_ref[half], out_near_ref[...]) + mm(att_ref[half], out_far_ref[...], NT)
 
     send_ref[...] = projected(1).astype(bf16)
     own_ref[...] = projected(0)
@@ -598,7 +640,7 @@
         compiler_params=pltpu.CompilerParams(
             vmem_limit_bytes=24 * 1024 * 1024, dimension_semantics=("arbitrary",)
         ),
-        cost_estimate=pl.CostEstimate(flops=0, bytes_accessed=0, transcendentals=0),
+        cost_estimate=length(0),
     )(flags, rows, cot, up, down, far, far)
 
 
@@ -666,53 +708,79 @@
     left_ref[...] = left + core_ref[half // 2 :, :].astype(f32)
 
 
-def rows_step(
-    flag_ref, up_left, out_left, up_received, out_received, up_own, out_own, send_ref
-):
-    rows = up_own.shape[0]
-    at = 0
-    for left, received, own in ((up_left, up_received, up_own), (out_left, out_received, out_own)):
-        own[...] = left[:rows, :] + received[:rows, :].astype(f32)
-        width = own.shape[1]
-        send_ref[:, at : at + width] = (left[rows:, :] + received[rows:, :].astype(f32)).astype(bf16)
-        at += width
-
-
-def own_slices(
-    flag_ref, down_own, down_received, up_own, out_own, rows_received, near_ref, far_ref
-):
-    rows, hidden, channels = up_own.shape[0], up_own.shape[1] // 2, out_own.shape[1] // 2
+def up_step(flag_ref, left_ref, received_ref, own_ref, send_ref):
+    rows = own_ref.shape[0]
+    own_ref[...] = left_ref[:rows, :] + received_ref[:rows, :].astype(f32)
+    send_ref[...] = (left_ref[rows:, :] + received_ref[rows:, :].astype(f32)).astype(bf16)
+
+
+def own_slices(flag_ref, down_own, down_received, up_own, up_received, near_ref, far_ref):
+    rows, hidden = up_own.shape[0], up_own.shape[1] // 2
     down = down_own[...] + down_received[...].astype(f32)
-    up = up_own[...] + rows_received[:, : 2 * hidden].astype(f32)
-    out = out_own[...] + rows_received[:, 2 * hidden :].astype(f32)
+    up = up_own[...] + up_received[...].astype(f32)
     width = down.shape[1]
     for slot, ref in enumerate((near_ref, far_ref)):
         ref[:, :width] = down[slot * rows : (slot + 1) * rows].astype(ref.dtype)
-        ref[:, width : width + hidden] = up[:, slot * hidden : (slot + 1) * hidden].astype(ref.dtype)
-        ref[:, width + hidden :] = out[:, slot * channels : (slot + 1) * channels].astype(ref.dtype)
-
-
-def attn_pass(flag_ref, lhs0, lhs1, rhs0, rhs1, out_ref):
-    half = lhs0.shape[1] // 2
-    out_ref[...] = products((lhs0, lhs1), (rhs0, rhs1), slice(0, half)).astype(bf16)
-
-
-def attn_keep(flag_ref, lhs0, lhs1, rhs0, rhs1, core_ref, own_ref, *send_refs):
-    half = lhs0.shape[1] // 2
+        ref[:, width:] = up[:, slot * hidden : (slot + 1) * hidden].astype(ref.dtype)
+
+
+def attn_pass(flag_ref, one0, one1, dqkv0, dqkv1, back0, back1, att0, att1, att2, att3, out_ref):
+    half = one0.shape[1] // 2
+    width = dqkv0.shape[1]
+    channels = att0.shape[1]
+    columns = slice(0, half)
+    out_ref[:, :width] = products((one0, one1), (dqkv0, dqkv1), columns).astype(bf16)
+    for slot, pair in enumerate(((att0, att1), (att2, att3))):
+        at = width + slot * channels
+        out_ref[:, at : at + channels] = products((back0, back1), pair, columns).astype(bf16)
+
+
+def attn_keep(
+    flag_ref, one0, one1, dqkv0, dqkv1, back0, back1, att0, att1, att2, att3, core_ref, own_ref,
+    *send_refs,
+):
+    half = one0.shape[1] // 2
     rows = half // 4
-    value = products((lhs0, lhs1), (rhs0, rhs1), slice(half, 2 * half)) + core_ref[...].astype(f32)
-    own_ref[...] = value[:rows]
-    for k, ref in enumerate(send_refs):
-        ref[...] = value[(k + 1) * rows : (k + 2) * rows].astype(bf16)
-
-
-def attn_own(flag_ref, own_ref, r1_ref, r2_ref, r3_ref, near_ref, far_ref):
+    width = dqkv0.shape[1]
+    channels = att0.shape[1]
+    columns = slice(half, 2 * half)
+    blocks = [(0, products((one0, one1), (dqkv0, dqkv1), columns))]
+    for slot, pair in enumerate(((att0, att1), (att2, att3))):
+        blocks.append((width + slot * channels, products((back0, back1), pair, columns)))
+    for at, block in blocks:
+        to = slice(at, at + block.shape[1])
+        block = block + core_ref[:, to].astype(f32)
+        own_ref[:, to] = block[:rows]
+        for k, ref in enumerate(send_refs):
+            ref[:, to] = block[(k + 1) * rows : (k + 2) * rows].astype(bf16)
+
+
+def attn_own(
+    flag_ref, own_ref, r1_ref, r2_ref, r3_ref, param_ref, gains_ref, gains_received, near_ref,
+    far_ref,
+):
+    rows = own_ref.shape[0]
     total = own_ref[...] + (
         r1_ref[...].astype(f32) + r2_ref[...].astype(f32) + r3_ref[...].astype(f32)
     )
-    width = near_ref.shape[1]
-    near_ref[...] = total[:, :width]
-    far_ref[...] = total[:, width:].astype(bf16)
+    channels = total.shape[1] // 8
+    gains = gains_ref[...] + gains_received[...]
+    for slot, ref in enumerate((near_ref, far_ref)):
+        ref[:rows, : 3 * channels] = total[:, slot * 3 * channels : (slot + 1) * 3 * channels].astype(
+            ref.dtype
+        )
+        ref[:rows, 3 * channels :] = total[
+            :, (6 + slot) * channels : (7 + slot) * channels
+        ].astype(ref.dtype)
+        small = jnp.concatenate(
+            [param_ref[:, slot * channels : (slot + 1) * channels], gains], axis=0
+        ).astype(ref.dtype)
+        count = small.shape[0] // 4
+        for quarter in range(4):
+            ref[rows : rows + count, quarter * channels : (quarter + 1) * channels] = small[
+                quarter * count : (quarter + 1) * count
+            ]
+        ref[rows + count :, :] = jnp.zeros((ref.shape[0] - rows - count, 4 * channels), ref.dtype)
 
 
 def add_two(flag_ref, a_ref, b_ref, out_ref):
@@ -723,42 +791,60 @@
     out_ref[...] = (a_ref[...] + b_ref[...] + c_ref[...].astype(f32)).astype(out_ref.dtype)
 
 
-def pack_small(flag_ref, param_ref, gains_ref, received_ref, near_ref, far_ref):
-    gains = gains_ref[...] + received_ref[...]
-    width = gains.shape[1]
-    rows = param_ref.shape[0]
-    for slot, ref in enumerate((near_ref, far_ref)):
-        ref[:rows, :] = param_ref[:, slot * width : (slot + 1) * width]
-        ref[rows:, :] = gains
-
-
-def widen(flag_ref, all_ref, down_ref, up_ref, out_ref):
-    down, up = down_ref.shape[1], up_ref.shape[1]
+def widen(all_ref, down_ref, up_ref):
+    down = down_ref.shape[1]
     down_ref[...] = all_ref[:, :down].astype(f32)
-    up_ref[...] = all_ref[:, down : down + up].astype(f32)
-    out_ref[...] = all_ref[:, down + up :].astype(f32).T
-
-
-def sources(flag_ref, even_ref, odd_ref):
+    up_ref[...] = all_ref[:, down:].astype(f32)
+
+
+def run_widen(value, down_width, up_width):
+    rows = value.shape[0] // 4
+    return pl.pallas_call(
+        widen,
+        grid=(4,),
+        in_specs=[pl.BlockSpec((rows, value.shape[1]), lambda j: (j, 0))],
+        out_specs=(
+            pl.BlockSpec((rows, down_width), lambda j: (j, 0)),
+            pl.BlockSpec((rows, up_width), lambda j: (j, 0)),
+        ),
+        out_shape=(shape((value.shape[0], down_width)), shape((value.shape[0], up_width))),
+        compiler_params=pltpu.CompilerParams(vmem_limit_bytes=56 * 1024 * 1024),
+        cost_estimate=length(0),
+    )(value)
+
+
+def sources(flag_ref, even_ref, odd_ref, rows):
     for pair in range(GROUP // 2):
         for side, ref in enumerate((even_ref, odd_ref)):
             source = jnp.bitwise_xor(flag_ref[PLACE], 2 * pair + side)
-            yield ref, pair, aligned(source * even_ref.shape[1], even_ref.shape[1])
+            yield ref, pair, aligned(source * rows, rows)
 
 
 def assemble_weight(flag_ref, even_ref, odd_ref, tile_ref, weight_ref, out_ref, qkv_ref):
     split = weight_ref.shape[1]
-    for ref, pair, at in sources(flag_ref, even_ref, odd_ref):
+    for ref, pair, at in sources(flag_ref, even_ref, odd_ref, even_ref.shape[1]):
         weight_ref[at, :] = ref[pair, :, :split]
         out_ref[at, :] = ref[pair, :, split:]
     project(flag_ref, tile_ref, weight_ref, qkv_ref)
 
 
-def assemble_grad(flag_ref, even_ref, odd_ref, qkv_ref):
+def assemble_grad(flag_ref, even_ref, odd_ref, qkv_ref, out_ref, small_ref):
     channels = qkv_ref.shape[2]
-    for ref, pair, at in sources(flag_ref, even_ref, odd_ref):
+    rows = qkv_ref.shape[1] // GROUP
+    count = small_ref.shape[0] // 4
+    total = None
+    for ref, pair, at in sources(flag_ref, even_ref, odd_ref, rows):
         for part in range(3):
-            qkv_ref[part, at, :] = ref[pair, :, part * channels : (part + 1) * channels].astype(f32)
+            qkv_ref[part, at, :] = ref[
+                pair, :rows, part * channels : (part + 1) * channels
+            ].astype(f32)
+        out_ref[:, at] = ref[pair, :rows, 3 * channels :].astype(f32).T
+        term = ref[pair, rows:, :].astype(f32)
+        total = term if total is None else total + term
+    for quarter in range(4):
+        small_ref[quarter * count : (quarter + 1) * count, :] = total[
+            :count, quarter * channels : (quarter + 1) * channels
+        ]
 
 
 class Order:
@@ -834,20 +920,22 @@
     normed_one = order.done(call(norm_one, half_low)(flags, row, gain_one))
     paired_one = swap_mp(normed_one, 1)
     qkv_parts = jnp.transpose(qkv_weight, (1, 0, 2))
+    ssm_pack = jnp.concatenate(
+        [ssm_rate.T, ssm_coef.T, ssm_skip[None], jnp.zeros((15, channels), f32)], 0
+    )
     attn_slice, mlp_slice = order.done(
-        run_cut_slices(flags, order(qkv_parts), out_weight, up_weight, down_weight)
+        run_cut_slices(flags, order(qkv_parts), out_weight, up_weight, down_weight, ssm_pack)
     )
     attn_across = swap_mp(attn_slice, 2)
-    ssm_pack = jnp.concatenate(
-        [ssm_rate.T, ssm_coef.T, ssm_skip[None], jnp.zeros((7, channels), f32)], 0
-    )
-    ssm_both = jnp.concatenate([ssm_pack, swap_mp(ssm_pack, 2)], 1)
+    near_qkv = order.done(jnp.concatenate(list(order(*[qkv_parts[k] for k in range(3)])), 1))
+
+    paired_one, attn_across = order.done(order(paired_one, attn_across))
+    attn_mine = attn_across[:rows]
+    attn_x = swap_dp(attn_mine, 2)
+    mlp_across = swap_mp(order(mlp_slice), 2)
+    paired_cot = swap_mp(order(cot), 1)
+    ssm_both = call(join_ssm, shape((48, wide)))(flags, ssm_pack, attn_across)
     rate_t, coef_t, skip_t = ssm_both[:16], ssm_both[16:32], ssm_both[32:33]
-    near_qkv = order.done(jnp.concatenate(list(order(*[qkv_parts[k] for k in range(3)])), 1))
-
-    paired_one, attn_across = order.done(order(paired_one, attn_across))
-    attn_pieces = gather_by_xor(attn_across)
-    mlp_across = swap_mp(order(mlp_slice), 2)
     tile_one, one_sent, second_local, handed = order.done(
         call(
             ssm_forward,
@@ -863,9 +951,28 @@
     handed = lax.ppermute(handed, "mp", [(0, 2), (1, 3)])
 
     qkv_shape = shape((2, HALF, 3 * channels), bf16)
-    qkv_near = order.done(call(project, qkv_shape)(flags, order(tile_one), near_qkv))
-    even = order.done(jnp.stack(list(order(*attn_pieces))))
+    att_shape = shape((2, HALF, channels), bf16)
+    attn_two = order.done(jnp.stack([attn_mine, order(attn_x)]))
+    attn_y = swap_dp(attn_two, 4)
+    paired_cot = order.done(order(paired_cot))
+    mlp_across = order.done(order(mlp_across))
+    qkv_near = order.done(
+        call(project, qkv_shape, micros=4)(flags, order(tile_one), near_qkv)
+    )
+    attn_y = order.done(order(attn_y))
+    ctx_first, ctx_second, enter_state = order.done(
+        call(
+            ssm_carry_in,
+            (shape((CTX, wide), bf16), shape((CTX, wide), bf16), shape((2, STATES, wide))),
+            scratch=[pltpu.VMEM((CTX, wide), f32)],
+        )(flags, second_local, order(handed), rate_t, coef_t)
+    )
+    mlp_far = gather(order(mlp_across)).reshape(GROUP, 2, rows, model_dim)
+    even = order.done(jnp.concatenate(list(order(attn_two, attn_y)), 0))
     odd_part = swap_dp(even, 1)
+    att_near = order.done(
+        call(attention_near, att_shape)(flags, order(qkv_near), ctx_first, ctx_second)
+    )
     far_qkv, far_out, qkv_far = order.done(
         call(
             assemble_weight,
@@ -876,35 +983,30 @@
             ),
         )(flags, even, order(odd_part), tile_one)
     )
-    ctx_first, ctx_second, enter_state = order.done(
-        call(
-            ssm_carry_in,
-            (shape((CTX, wide), bf16), shape((CTX, wide), bf16), shape((2, STATES, wide))),
-            scratch=[pltpu.VMEM((CTX, wide), f32)],
-        )(flags, second_local, order(handed), rate_t, coef_t)
-    )
-    mlp_far = gather(order(mlp_across)).reshape(GROUP, 2, rows, model_dim)
-    paired_cot = swap_mp(order(cot), 1)
-    attended, out_own, out_send = order.done(
-        call(attention_forward, (shape((2, HALF, wide), bf16), half, half_low))(
-            flags, order(qkv_near), qkv_far, ctx_first, ctx_second, out_weight, far_out
+    att_far, out_own, out_send = order.done(
+        call(attention_far, (att_shape, half, half_low))(
+            flags, order(qkv_far), ctx_first, ctx_second, att_near, out_weight, far_out
         )
     )
     out_received = swap_mp(out_send, 1)
-    paired_cot = order.done(order(paired_cot))
     middle, normed_two = order.done(
-        call(norm_two, (half, half_low))(flags, row, out_own, order(out_received), gain_two)
+        call(norm_two, (half, half_low))(
+            flags, row, out_own, order(out_received), gain_two
+        )
     )
 
     paired_two = swap_mp(normed_two, 1)
+    warm = order.done(
+        call(touch, shape((8, 128), bf16))(flags, order(up_weight), down_weight, cot, paired_cot)
+    )
     mlp = (up_weight, down_weight, mlp_far)
+    act_other, gate_other, two_other, down_send, back_send = order.done(
+        run_feed_forward(flags, order(paired_two), paired_cot, *mlp, bf16)
+    )
+    back_received = swap_mp(back_send, 1)
     act_own, gate_own, two_own, down_own, back_own = order.done(
         run_feed_forward(flags, order(normed_two), cot, *mlp, f32)
     )
-    act_other, gate_other, two_other, down_send, back_send = order.done(
-        run_feed_forward(flags, order(paired_two), paired_cot, *mlp, bf16)
-    )
-    back_received = swap_mp(back_send, 1)
 
     def low(*dims):
         return shape(dims, bf16)
@@ -913,18 +1015,15 @@
     acts = (act_own, act_other, cot, paired_cot)
     passed = order.done(call(down_pass, low(hidden, model_dim))(flags, order(act_own), *acts[1:]))
     down_core = swap_dp(passed, 1)
+    ups = (two_own, two_other, gate_own, gate_other)
+    passed = order.done(call(rows_pass, low(side, 2 * hidden))(flags, order(two_own), *ups[1:]))
+    up_core = swap_dp(passed, 1)
     middle_grad, attn_grad, gain_mlp_grad = order.done(
-        call(norm_two_back, (half, half_low, shape((1, model_dim))))(
-            flags, middle, back_own, order(back_received), cot, gain_two
+        call(norm_two_back, (half, half_low, shape((1, model_dim))), micros=12)(
+            flags, middle, back_own, order(back_received), cot, gain_two, warm
         )
     )
     paired_back = swap_mp(attn_grad, 1)
-    passed = order.done(
-        call(rows_pass, low(side, 2 * hidden))(
-            flags, order(two_own), two_other, gate_own, gate_other
-        )
-    )
-    up_core = swap_dp(passed, 1)
     down_send_x, down_left = order.done(
         call(down_keep, (low(side, model_dim), shape((side, model_dim))))(
             flags, *acts, order(down_core)
@@ -933,7 +1032,7 @@
     down_x = swap_dp(down_send_x, 2)
     up_send_y, up_left = order.done(
         call(rows_keep, (low(side // 2, 2 * hidden), shape((side // 2, 2 * hidden))))(
-            flags, two_own, two_other, gate_own, gate_other, order(up_core)
+            flags, *ups, order(up_core)
         )
     )
     up_y = swap_dp(up_send_y, 4)
@@ -942,12 +1041,9 @@
         call(
             attended_grads,
             (shape((2, HALF, wide), bf16), shape((2, HALF, model_dim), bf16)),
+            micros=4,
         )(flags, attn_grad, order(paired_back), out_weight, far_out)
     )
-    down_received = swap_mp(order(down_send), 1)
-    outs = (back_sent[0], back_sent[1], attended[0], attended[1])
-    passed = order.done(call(rows_pass, low(side, wide))(flags, *outs))
-    out_core = swap_dp(passed, 1)
     dqkv, second_grad, returned = order.done(
         call(
             attention_backward,
@@ -959,14 +1055,16 @@
         )(flags, qkv_near, qkv_far, ctx_first, ctx_second, order(att_grad), rate_t)
     )
     returned = lax.ppermute(returned, "mp", [(2, 0), (3, 1)])
-    out_send_y, out_left = order.done(
-        call(rows_keep, (low(side // 2, wide), shape((side // 2, wide))))(
-            flags, *outs, order(out_core)
-        )
-    )
-    out_y = swap_dp(out_send_y, 4)
-    ones = (one_sent[0], one_sent[1], dqkv[0], dqkv[1])
-    passed = order.done(call(attn_pass, low(side, 6 * channels))(flags, order(ones[0]), *ones[1:]))
+    one_total = order.done(
+        call(qkv_back, shape((2, HALF, model_dim)))(flags, order(dqkv), near_qkv, far_qkv)
+    )
+    attns = (
+        one_sent[0], one_sent[1], dqkv[0], dqkv[1], back_sent[0], back_sent[1],
+        att_near[0], att_near[1], att_far[0], att_far[1],
+    )
+    passed = order.done(
+        call(attn_pass, low(side, 8 * channels))(flags, order(attns[0]), *attns[1:])
+    )
     attn_core = swap_dp(passed, 1)
     down_mine, down_send_y = order.done(
         call(down_step, (shape((2 * rows, model_dim)), low(2 * rows, model_dim)))(
@@ -974,34 +1072,40 @@
         )
     )
     down_y = swap_dp(down_send_y, 4)
+    up_mine, up_send_x = order.done(
+        call(up_step, (shape((rows, 2 * hidden)), low(rows, 2 * hidden)))(
+            flags, up_left, order(up_y)
+        )
+    )
+    up_x = swap_dp(up_send_x, 2)
     one_own, one_send, last_grad = order.done(
         call(
             ssm_signal_grad,
             (half, half_low, shape((CTX, wide))),
             scratch=[pltpu.VMEM((2 * HALF, wide), f32), pltpu.VMEM((HALF, model_dim), f32)],
-        )(
-            flags, second_grad, order(returned), rate_t, coef_t, skip_t, dqkv, near_qkv, far_qkv
-        )
+            micros=30,
+        )(flags, second_grad, order(returned), rate_t, coef_t, skip_t, one_total)
     )
     one_received = swap_mp(one_send, 1)
-    up_mine, out_mine, rows_send_x = order.done(
-        call(
-            rows_step,
-            (shape((rows, 2 * hidden)), shape((rows, wide)), low(rows, 2 * hidden + wide)),
-        )(flags, up_left, out_left, *order(up_y, out_y))
-    )
-    rows_x = swap_dp(rows_send_x, 2)
     attn_mine, *attn_sends = order.done(
-        call(attn_keep, (shape((rows, 6 * channels)),) + (low(rows, 6 * channels),) * 3)(
-            flags, *ones, order(attn_core)
+        call(attn_keep, (shape((rows, 8 * channels)),) + (low(rows, 8 * channels),) * 3)(
+            flags, *attns, order(attn_core)
         )
     )
     attn_sent = [swap_dp(part, SENT[5 + k]) for k, part in enumerate(attn_sends)]
+    mlp_width = model_dim + hidden
+    mlp_near, mlp_send = order.done(
+        call(own_slices, (shape((rows, mlp_width)), low(rows, mlp_width)))(
+            flags, down_mine, order(down_y), up_mine, order(up_x)
+        )
+    )
+    mlp_received = swap_mp(mlp_send, 2)
     param_grad = order.done(
         call(
             ssm_param_grad,
             shape((40, wide)),
             scratch=[pltpu.VMEM((2 * HALF, wide), f32)],
+            micros=3,
         )(flags, order(tile_one), second_grad, last_grad, enter_state, rate_t, coef_t)
     )
     input_grad, gains = order.done(
@@ -1009,58 +1113,49 @@
             flags, row, one_own, order(one_received), middle_grad, gain_one, gain_mlp_grad
         )
     )
-    mlp_width = model_dim + hidden + channels
-    mlp_near, mlp_send = order.done(
-        call(own_slices, (shape((rows, mlp_width)), low(rows, mlp_width)))(
-            flags, down_mine, order(down_y), up_mine, out_mine, order(rows_x)
-        )
-    )
-    mlp_received = swap_mp(mlp_send, 2)
+    gains_received = swap_mp(gains, 1)
+    slice_rows = rows + 16
+    *attn_sent, gains_received = order(*attn_sent, gains_received)
     attn_near, attn_send = order.done(
-        call(attn_own, (shape((rows, 3 * channels)), low(rows, 3 * channels)))(
-            flags, attn_mine, *order(*attn_sent)
+        call(attn_own, (shape((slice_rows, 4 * channels)), low(slice_rows, 4 * channels)))(
+            flags, attn_mine, *attn_sent, param_grad, gains, gains_received
         )
     )
     attn_received = swap_mp(attn_send, 2)
-    gains_received = swap_mp(order(gains), 1)
+    mlp_slice_grad = order.done(
+        call(add_two, low(rows, mlp_width))(flags, mlp_near, order(mlp_received))
+    )
+    mlp_full = gather(over_groups(mlp_slice_grad))
+    down_received = swap_mp(order(down_send), 1)
+    attn_slice_grad = order.done(
+        call(add_two, low(slice_rows, 4 * channels))(flags, attn_near, order(attn_received))
+    )
+    attn_pieces = gather_by_xor(over_groups(attn_slice_grad))
     output = order.done(
         call(add_three, half_low)(flags, middle, down_own, order(down_received))
     )
-    attn_slice_grad = order.done(
-        call(add_two, low(rows, 3 * channels))(flags, attn_near, order(attn_received))
-    )
-    attn_pieces = gather_by_xor(over_groups(attn_slice_grad))
-    mlp_slice_grad = order.done(
-        call(add_two, low(rows, mlp_width))(flags, mlp_near, order(mlp_received))
-    )
-    mlp_full = gather(over_groups(mlp_slice_grad))
-    small = shape((48, channels))
-    packed, packed_far = order.done(
-        call(pack_small, (small, small))(flags, param_grad, gains, order(gains_received))
-    )
-    packed = order.done(call(add_two, small)(flags, packed, order(swap_mp(packed_far, 2))))
-    packed = order.done(call(add_two, small)(flags, packed, order(swap_dp(packed, 1))))
     even = order.done(jnp.stack(list(order(*attn_pieces))))
     odd_part = swap_dp(even, 1)
-    mask = 2
-    while mask < dp_size:
-        packed = order.done(call(add_two, small)(flags, packed, order(swap_dp(packed, mask))))
-        mask *= 2
-    qkv_grad = order.done(
-        call(assemble_grad, shape((3, model_dim, channels)))(flags, even, order(odd_part))
-    )
-    down_grad, up_grad, out_grad = call(
-        widen, (shape(down_weight.shape), shape(up_weight.shape), shape(out_weight.shape))
-    )(flags, order(mlp_full))
-    gains = packed[40:].reshape(2, model_dim)
+    qkv_grad, out_grad, small = order.done(
+        call(
+            assemble_grad,
+            (
+                shape((3, model_dim, channels)),
+                shape(out_weight.shape),
+                shape((48, channels)),
+            ),
+        )(flags, even, order(odd_part))
+    )
+    down_grad, up_grad = run_widen(order(mlp_full), model_dim, hidden)
+    gains = small[40:].reshape(2, model_dim)
     return (
         output[None],
         input_grad[None],
         gains[0],
         jnp.transpose(qkv_grad, (1, 0, 2)),
-        packed[:16].T,
-        packed[16:32].T,
-        packed[32],
+        small[:16].T,
+        small[16:32].T,
+        small[32],
         out_grad,
         gains[1],
         up_grad,

time: 316 us -> 271 us (0.86)
  waiting for transfers between devices: 145 us -> 97.7 us
  local copies, waits for them, and re-layouts: 22.4 us -> 19.2 us
  starting transfers between devices: 47.7 us -> 50.9 us
    all_gather x2, waiting for transfers between devices: 15.2 us -> 0.01 us  [gather(): lax.all_gather(value, 'dp', axis=0, tiled=True, axis_index_groups=groups)]
    ppermute x15 -> x13, waiting for transfers between devices: 84.4 us -> 73.1 us  [swap_mp(): return lax.ppermute(value, 'mp', [(k, k ^ mask) for k in range(4)])]
    ppermute x1, waiting for transfers between devices: 10.2 us -> 0.29 us  [per_device(): returned = lax.ppermute(returned, 'mp', [(2, 0), (3, 1)])]
    ppermute x1, waiting for transfers between devices: 8.54 us -> 0.01 us  [per_device(): handed = lax.ppermute(handed, 'mp', [(0, 2), (1, 3)])]
    pallas_call x1 -> x2, Pallas kernels: 0.64 us -> 8.84 us  [the longest x1 5.86 us: run_widen(): pl.pallas_call(widen, grid=(4,), in_specs=[pl.BlockSpec((rows, value.shap...]
    pallas_call x35 -> x31, Pallas kernels: 68.6 us -> 61.2 us  [run(): pl.pallas_call(kernel, out_shape=out_shape, in_specs=[pl.BlockSpec(memory...]
    ppermute x15 -> x13, starting transfers between devices: 21.4 us -> 27.5 us  [swap_mp(): return lax.ppermute(value, 'mp', [(k, k ^ mask) for k in range(4)])]
    unnamed x85 -> x118, local copies, waits for them, and re-layouts: 20.7 us -> 16.3 us
  transfers between devices with their start and end apart: 42 -> 34, of which waited for: 25 -> 19; matrix products, arithmetic and copies ran while one was open for 1% -> 3% of each run, Pallas kernels for 22% -> 25%
where the time goes in v3:
time: 271 us; the launch traced here: 270 us
  waiting for transfers between devices  97.7 us (36%)
  Pallas kernels  84.1 us (31%)
  starting transfers between devices  50.9 us (19%)
  local copies, waits for them, and re-layouts  19.2 us (7%)
  between operations  15.5 us (6%)
    ppermute x13, waiting for transfers between devices, swap_mp(): return lax.ppermute(value, 'mp', [(k, k ^ mask) for k in range(4)])  73.1 us
    pallas_call x31, Pallas kernels, run(): pl.pallas_call(kernel, out_shape=out_shape, in_specs=[pl.BlockSpec(memory...  61.2 us
    ppermute x13, starting transfers between devices, swap_mp(): return lax.ppermute(value, 'mp', [(k, k ^ mask) for k in range(4)])  27.5 us
    ppermute x17, waiting for transfers between devices, swap_dp(): return lax.ppermute(value, 'dp', [(k, k ^ mask) for k in range(dp_size)])  24.2 us
    ppermute x17, starting transfers between devices, swap_dp(): return lax.ppermute(value, 'dp', [(k, k ^ mask) for k in range(dp_size)])  19 us
    unnamed x118, local copies, waits for them, and re-layouts  16.3 us
    pallas_call x2, Pallas kernels, run_feed_forward(): pl.pallas_call(feed_forward, grid=(2 * per,), out_shape=(shape((tokens, 2...  14 us
    pallas_call x1, Pallas kernels, run_widen(): pl.pallas_call(widen, grid=(4,), in_specs=[pl.BlockSpec((rows, value.shap...  5.86 us
  transfers between devices with their start and end apart: 34, of which 19 were waited for; matrix products, arithmetic and copies ran while one was open for 3% of the time, Pallas kernels for 25%

profile of v3, /device:TPU:0, one launch (start us, length us, event | category | flops | bytes accessed | tf_op | source)
XLA Modules:
  0.0 269.9 jit_solution(7597685879564445230)
XLA Ops:
  10.6 3.1 %collective-permute-start = (bf16[256,1024]{1,0:T(8,128)(2,1)S(1)}, bf16[256,1024]{1,0:T(8,128)(2,1)S(1)}, u32[]{:S(2)}, u32[]{:S(2)}) collective-permute-start(bf16[256,1024]{1,0:T(8,128)(2,1)S(1)} %shard_map.203.own_ref), channel_id=1, source_target_pairs={{0,1},{1,0},{2,3},{3,2},{4,5},{5,4},{6,7},{7,6},{8,9},{9,8},{10,11... | collective-permute-start | bytes 1572872 | tf_op jit(solution)/shard_map/ppermute | solution.py:884
  13.8 1.4 maximum_maximum_fusion.ssm_ref.own_ref
  15.2 3.0 %shard_map.204 = (bf16[176,1024]{1,0:T(8,128)(2,1)}, bf16[256,1024]{1,0:T(8,128)(2,1)}) custom-call(s32[6]{0:T(128)} %copy-done.39, bf16[3,1024,256]{2,1,0:T(8,128)(2,1)} %bitcast.79, bf16[256,1024]{1,0:T(8,128)(2,1)} %out_near_ref.3, bf16[1024,1024]{1,0:T(8,128)(2,1)} %up0_ref.3, bf16[1024,1024]{1,0:T(8,128)(2,1)} %down0_ref.3, ...), custom_call_target="tpu_custom_call" | custom-call | tf_op jit(solution)/shard_map/pallas_call | solution.py:115
  18.2 2.7 collective-permute-start.1
  22.3 14.7 %collective-permute-done.1.across_ref = bf16[176,1024]{1,0:T(8,128)(2,1)S(1)} collective-permute-done((bf16[176,1024]{1,0:T(8,128)(2,1)}, bf16[176,1024]{1,0:T(8,128)(2,1)S(1)}, u32[]{:S(2)}, u32[]{:S(2)}) %collective-permute-start.1) | collective-permute-done | bytes 360480 | tf_op jit(solution)/shard_map/ppermute | solution.py:884
  37.1 1.6 collective-permute-start.2
  38.7 3.0 %collective-permute-start.4 = (bf16[256,1024]{1,0:T(8,128)(2,1)S(1)}, bf16[256,1024]{1,0:T(8,128)(2,1)}, u32[]{:S(2)}, u32[]{:S(2)}) collective-permute-start(bf16[256,1024]{1,0:T(8,128)(2,1)S(1)} %copy-done.55), channel_id=1, source_target_pairs={{0,2},{1,3},{2,0},{3,1},{4,6},{5,7},{6,4},{7,5},{8,10},{9,11},{10,... | collective-permute-start | bytes 1572872 | tf_op jit(solution)/shard_map/ppermute | solution.py:884
  42.3 5.8 %shard_map.206 = (bf16[2,256,1024]{2,1,0:T(8,128)(2,1)S(1)}, bf16[2,256,1024]{2,1,0:T(8,128)(2,1)S(1)}, f32[128,512]{1,0:T(8,128)S(1)}, bf16[224,512]{1,0:T(8,128)(2,1)}) custom-call(s32[6]{0:T(128)S(1)} %copy-done.40, bf16[256,1024]{1,0:T(8,128)(2,1)S(1)} %shard_map.203.own_ref, bf16[256,1024]{1,0:T(8,128)(2,1)S(1)} %collective-permute-done.other_ref, ...), custom_call_target="tpu_custom_call" | custom-call | tf_op jit(solution)/shard_map/pallas_call | solution.py:46
  50.0 1.5 collective-permute-start.3
  51.5 2.6 collective-permute-start.6
  54.1 5.8 %collective-permute-done.5.paired_ref.c_ref.cot1 = bf16[256,1024]{1,0:T(8,128)(2,1)S(1)} collective-permute-done((bf16[256,1024]{1,0:T(8,128)(2,1)S(1)}, bf16[256,1024]{1,0:T(8,128)(2,1)S(1)}, u32[]{:S(2)}, u32[]{:S(2)}) %collective-permute-start.5) | collective-permute-done | bytes 524320 | tf_op jit(solution)/shard_map/ppermute | solution.py:884
  59.9 3.4 %collective-permute-done.4 = bf16[256,1024]{1,0:T(8,128)(2,1)} collective-permute-done((bf16[256,1024]{1,0:T(8,128)(2,1)S(1)}, bf16[256,1024]{1,0:T(8,128)(2,1)}, u32[]{:S(2)}, u32[]{:S(2)}) %collective-permute-start.4) | collective-permute-done | bytes 524320 | tf_op jit(solution)/shard_map/ppermute | solution.py:884
  63.3 1.4 copy-done.14
  64.7 1.5 shard_map.207.qkv_ref.near_ref
  66.3 2.1 shard_map.208
  71.1 1.9 shard_map.209.near_ref
  73.7 1.7 shard_map.210
  76.6 2.6 shard_map.211
  79.9 6.6 %collective-permute-start.8 = (bf16[256,1024]{1,0:T(8,128)(2,1)S(1)}, bf16[256,1024]{1,0:T(8,128)(2,1)S(1)}, u32[]{:S(2)}, u32[]{:S(2)}) collective-permute-start(bf16[256,1024]{1,0:T(8,128)(2,1)S(1)} %get-tuple-element.161), channel_id=1, source_target_pairs={{0,1},{1,0},{2,3},{3,2},{4,5},{5,4},{6,7},{7,6},{8,9},{9,8},{10,11... | collective-permute-start | bytes 1572872 | tf_op jit(solution)/shard_map/ppermute | solution.py:884
  86.5 12.2 %collective-permute-done.8.received_ref = bf16[256,1024]{1,0:T(8,128)(2,1)S(1)} collective-permute-done((bf16[256,1024]{1,0:T(8,128)(2,1)S(1)}, bf16[256,1024]{1,0:T(8,128)(2,1)S(1)}, u32[]{:S(2)}, u32[]{:S(2)}) %collective-permute-start.8) | collective-permute-done | bytes 524320 | tf_op jit(solution)/shard_map/ppermute | solution.py:884
  99.7 1.8 collective-permute-start.9
  102.1 11.1 %collective-permute-done.9.n_ref = bf16[256,1024]{1,0:T(8,128)(2,1)S(1)} collective-permute-done((bf16[256,1024]{1,0:T(8,128)(2,1)S(1)}, bf16[256,1024]{1,0:T(8,128)(2,1)S(1)}, u32[]{:S(2)}, u32[]{:S(2)}) %collective-permute-start.9) | collective-permute-done | bytes 524320 | tf_op jit(solution)/shard_map/ppermute | solution.py:884
  114.1 2.2 copy-done
  116.3 1.6 copy-done.4
  118.9 6.9 %shard_map.214 = (bf16[256,2048]{1,0:T(8,128)(2,1)S(1)}, bf16[256,2048]{1,0:T(8,128)(2,1)S(1)}, bf16[256,1024]{1,0:T(8,128)(2,1)S(1)}, bf16[256,1024]{1,0:T(8,128)(2,1)S(1)}, bf16[256,1024]{1,0:T(8,128)(2,1)S(1)}) custom-call(s32[6]{0:T(128)S(1)} %copy-done.40, bf16[256,1024]{1,0:T(8,128)(2,1)S(1)} %copy-done.38, ...), custom_call_target="tpu_custom_call" | custom-call | tf_op jit(solution)/shard_map/pallas_call | solution.py:613
  126.7 1.4 collective-permute-start.11
  128.1 7.1 %shard_map.215 = (bf16[256,2048]{1,0:T(8,128)(2,1)S(1)}, bf16[256,2048]{1,0:T(8,128)(2,1)S(1)}, bf16[256,1024]{1,0:T(8,128)(2,1)S(1)}, f32[256,1024]{1,0:T(8,128)S(1)}, f32[256,1024]{1,0:T(8,128)S(1)}) custom-call(s32[6]{0:T(128)S(1)} %copy-done.40, bf16[256,1024]{1,0:T(8,128)(2,1)S(1)} %copy-done.36, bf16[256,1024]{1,0:T(8,128)(2,1)S(1)} %bitcast.67, ...), custom_call_target="tpu_custom_call" | custom-call | tf_op jit(solution)/shard_map/pallas_call | solution.py:613
  135.3 1.8 shard_map.216
  137.2 1.8 shard_map.217
  139.6 1.4 shard_map.218
  142.0 1.8 shard_map.219
  145.0 1.9 shard_map.220
  146.9 1.3 collective-permute-start.18
  148.2 6.7 %collective-permute-done.13.other_ref = bf16[256,1024]{1,0:T(8,128)(2,1)S(1)} collective-permute-done((bf16[256,1024]{1,0:T(8,128)(2,1)S(1)}, bf16[256,1024]{1,0:T(8,128)(2,1)S(1)}, u32[]{:S(2)}, u32[]{:S(2)}) %collective-permute-start.13) | collective-permute-done | bytes 524320 | tf_op jit(solution)/shard_map/ppermute | solution.py:884
  155.0 1.4 shard_map.221
  156.4 5.4 %shard_map.222 = (bf16[2,256,1536]{2,1,0:T(8,128)(2,1)S(1)}, f32[128,512]{1,0:T(8,128)S(1)}, bf16[176,512]{1,0:T(8,128)(2,1)S(1)}) custom-call(s32[6]{0:T(128)S(1)} %copy-done.40, bf16[2,256,768]{2,1,0:T(8,128)(2,1)S(1)} %copy-done.12, bf16[2,256,768]{2,1,0:T(8,128)(2,1)S(1)} %copy-done.10, bf16[128,512]{1,0:T(8,128)(2,1)S(1)} %get-tuple-element.149.first_ref, ...), custom_call_target="tpu_custom_call" | custom-call | tf_op jit(solution)/shard_map/pallas_call | solution.py:46
  161.8 1.6 collective-permute-start.17
  163.4 2.4 shard_map.223.total_ref
  166.0 1.8 shard_map.224
  169.7 2.0 collective-permute-start.15
  172.5 1.5 collective-permute-start.19
  174.3 5.1 %shard_map.227 = (f32[256,1024]{1,0:T(8,128)S(1)}, bf16[256,1024]{1,0:T(8,128)(2,1)S(1)}, f32[128,512]{1,0:T(8,128)S(1)}) custom-call(s32[6]{0:T(128)S(1)} %copy-done.40, f32[128,512]{1,0:T(8,128)S(1)} %get-tuple-element.195.near_ref, bf16[176,512]{1,0:T(8,128)(2,1)S(1)} %collective-permute-done.17.returned_ref, f32[16,512]{1,0:T(8,128)S(1)} %copy-done.34, ...), custom_call_target="tpu_custom_call" | custom-call | flops 30000001024 | tf_op jit(solution)/shard_map/pallas_call | solution.py:46
  180.5 1.9 shard_map.228
  182.4 1.8 collective-permute-start.21
  185.5 3.6 %collective-permute-start.23 = (bf16[128,2048]{1,0:T(8,128)(2,1)S(1)}, bf16[128,2048]{1,0:T(8,128)(2,1)S(1)}, u32[]{:S(2)}, u32[]{:S(2)}) collective-permute-start(bf16[128,2048]{1,0:T(8,128)(2,1)S(1)} %get-tuple-element.214), channel_id=1, source_target_pairs={{0,24},{4,28},{8,16},{12,20},{16,8},{20,12},{24,0},{28,4},{1,25},{... | collective-permute-start | bytes 1572872 | tf_op jit(solution)/shard_map/ppermute | solution.py:887
  189.8 4.4 %collective-permute-start.20 = (bf16[128,2048]{1,0:T(8,128)(2,1)S(1)}, bf16[128,2048]{1,0:T(8,128)(2,1)S(1)}, u32[]{:S(2)}, u32[]{:S(2)}) collective-permute-start(bf16[128,2048]{1,0:T(8,128)(2,1)S(1)} %get-tuple-element.218), channel_id=1, source_target_pairs={{0,2},{1,3},{2,0},{3,1},{4,6},{5,7},{6,4},{7,5},{8,10},{9,11},{10,... | collective-permute-start | bytes 1572872 | tf_op jit(solution)/shard_map/ppermute | solution.py:884
  194.2 4.3 %shard_map.230.param_ref = f32[40,512]{1,0:T(8,128)S(1)} custom-call(s32[6]{0:T(128)S(1)} %copy-done.40, bf16[2,256,1024]{2,1,0:T(8,128)(2,1)S(1)} %copy-done.26, f32[128,512]{1,0:T(8,128)S(1)} %get-tuple-element.195.near_ref, f32[128,512]{1,0:T(8,128)S(1)} %get-tuple-element.209.last_ref, f32[2,16,512]{2,1,0:T(8,128)S(1)} %copy-done.53, ...), custom_call_target="tpu_custom_call" | custom-call | flops 3000000000 | tf_op jit(solution)/shard_map/pallas_call | solution.py:46
  198.5 2.3 shard_map.231
  200.9 3.6 %collective-permute-done.25.gains_received = f32[8,256]{1,0:T(8,128)S(1)} collective-permute-done((f32[8,256]{1,0:T(8,128)S(1)}, f32[8,256]{1,0:T(8,128)S(1)}, u32[]{:S(2)}, u32[]{:S(2)}) %collective-permute-start.25) | collective-permute-done | bytes 8224 | tf_op jit(solution)/shard_map/ppermute | solution.py:884
  204.5 4.7 %collective-permute-done.23.r3_ref = bf16[128,2048]{1,0:T(8,128)(2,1)S(1)} collective-permute-done((bf16[128,2048]{1,0:T(8,128)(2,1)S(1)}, bf16[128,2048]{1,0:T(8,128)(2,1)S(1)}, u32[]{:S(2)}, u32[]{:S(2)}) %collective-permute-start.23) | collective-permute-done | bytes 524320 | tf_op jit(solution)/shard_map/ppermute | solution.py:887
  210.0 2.6 collective-permute-done.20.b_ref
  212.6 1.4 shard_map.233
  214.1 1.6 collective-permute-start.27
  216.7 10.8 %collective-permute-done.27.b_ref = bf16[144,1024]{1,0:T(8,128)(2,1)S(1)} collective-permute-done((bf16[144,1024]{1,0:T(8,128)(2,1)}, bf16[144,1024]{1,0:T(8,128)(2,1)S(1)}, u32[]{:S(2)}, u32[]{:S(2)}) %collective-permute-start.27) | collective-permute-done | bytes 294944 | tf_op jit(solution)/shard_map/ppermute | solution.py:884
  228.1 1.3 collective-permute-start.28
  229.9 1.8 collective-permute-start.30
  231.6 2.2 collective-permute-done.26.c_ref
  233.8 1.5 shard_map.235
  235.3 2.8 %collective-permute-done.28 = bf16[144,1024]{1,0:T(8,128)(2,1)S(1)} collective-permute-done((bf16[144,1024]{1,0:T(8,128)(2,1)S(1)}, bf16[144,1024]{1,0:T(8,128)(2,1)S(1)}, u32[]{:S(2)}, u32[]{:S(2)}) %collective-permute-start.28) | collective-permute-done | bytes 294944 | tf_op jit(solution)/shard_map/ppermute | solution.py:887
  238.1 4.8 %collective-permute-done.29 = bf16[144,1024]{1,0:T(8,128)(2,1)S(1)} collective-permute-done((bf16[144,1024]{1,0:T(8,128)(2,1)S(1)}, bf16[144,1024]{1,0:T(8,128)(2,1)S(1)}, u32[]{:S(2)}, u32[]{:S(2)}) %collective-permute-start.29) | collective-permute-done | bytes 294944 | tf_op jit(solution)/shard_map/ppermute | solution.py:887
  242.9 5.9 %collective-permute-done.30 = bf16[144,1024]{1,0:T(8,128)(2,1)S(1)} collective-permute-done((bf16[144,1024]{1,0:T(8,128)(2,1)S(1)}, bf16[144,1024]{1,0:T(8,128)(2,1)S(1)}, u32[]{:S(2)}, u32[]{:S(2)}) %collective-permute-start.30) | collective-permute-done | bytes 294944 | tf_op jit(solution)/shard_map/ppermute | solution.py:887
  249.1 2.8 %collective-permute-done.31.odd_ref = bf16[4,144,1024]{2,1,0:T(8,128)(2,1)S(1)} collective-permute-done((bf16[4,144,1024]{2,1,0:T(8,128)(2,1)S(1)}, bf16[4,144,1024]{2,1,0:T(8,128)(2,1)S(1)}, u32[]{:S(2)}, u32[]{:S(2)}) %collective-permute-start.31) | collective-permute-done | bytes 1179680 | tf_op jit(solution)/shard_map/ppermute | solution.py:887
  251.9 2.9 %shard_map.236 = (f32[3,1024,256]{2,1,0:T(8,128)}, f32[256,1024]{1,0:T(8,128)}, f32[48,256]{1,0:T(8,128)S(1)}) custom-call(s32[6]{0:T(128)S(1)} %copy-done.40, bf16[4,144,1024]{2,1,0:T(8,128)(2,1)S(1)} %pad_maximum_fusion.even_ref, bf16[4,144,1024]{2,1,0:T(8,128)(2,1)S(1)} %collective-permute-done.31.odd_ref), custom_call_target="tpu_custom_call" | custom-call | tf_op jit(solution)/shard_map/pallas_call | solution.py:46
  257.2 5.9 %shard_map.237 = (f32[1024,1024]{1,0:T(8,128)}, f32[1024,1024]{1,0:T(8,128)}) custom-call(bf16[1024,2048]{1,0:T(8,128)(2,1)} %all-gather.5.cloned.1.call-done.all_ref), custom_call_target="tpu_custom_call" | custom-call | tf_op jit(solution)/shard_map/pallas_call | solution.py:802
  (178 shorter events, 30.9 us)
Async XLA Ops:
  7.2 106.9 %all-gather.3.cloned.1.call-start = ((), (), s32[]{:S(2)}) async-start(), calls=%async_computation | async-start | bytes 4718592 | tf_op jit(solution)/shard_map/all_gather | solution.py:890
  8.0 7.3 %copy-start.39 = (s32[6]{0:T(128)}, s32[6]{0:T(128)S(1)}, u32[]{:S(2)}) copy-start(s32[6]{0:T(128)S(1)} %stack.48.flag_ref) | copy-start | bytes 76
  10.6 26.4 %collective-permute-start = (bf16[256,1024]{1,0:T(8,128)(2,1)S(1)}, bf16[256,1024]{1,0:T(8,128)(2,1)S(1)}, u32[]{:S(2)}, u32[]{:S(2)}) collective-permute-start(bf16[256,1024]{1,0:T(8,128)(2,1)S(1)} %shard_map.203.own_ref), channel_id=1, source_target_pairs={{0,1},{1,0},{2,3},{3,2},{4,5},{5,4},{6,7},{7,6},{8,9},{9,8},{10,11... | collective-permute-start | bytes 1572872 | tf_op jit(solution)/shard_map/ppermute | solution.py:884
  15.2 5.7 %copy-start.54 = (bf16[1024,3,256]{2,0,1:T(8,128)(2,1)S(1)}, bf16[1024,3,256]{2,0,1:T(8,128)(2,1)}, u32[]{:S(2)}) copy-start(bf16[1024,3,256]{2,0,1:T(8,128)(2,1)} %param.15) | copy-start | bytes 4718596
  18.2 18.8 %collective-permute-start.1 = (bf16[176,1024]{1,0:T(8,128)(2,1)}, bf16[176,1024]{1,0:T(8,128)(2,1)S(1)}, u32[]{:S(2)}, u32[]{:S(2)}) collective-permute-start(bf16[176,1024]{1,0:T(8,128)(2,1)} %get-tuple-element.129), channel_id=1, source_target_pairs={{0,2},{1,3},{2,0},{3,1},{4,6},{5,7},{6,4},{7,5},{8,10},{9,11},{10,... | collective-permute-start | bytes 1081352 | tf_op jit(solution)/shard_map/ppermute | solution.py:884
  21.0 17.6 %copy-start.5 = (bf16[1,256,1024]{2,1,0:T(8,128)(2,1)S(1)}, bf16[1,256,1024]{2,1,0:T(8,128)(2,1)}, u32[]{:S(2)}) copy-start(bf16[1,256,1024]{2,1,0:T(8,128)(2,1)} %param.23) | copy-start | bytes 1572868
  21.0 17.6 %copy-start.55 = (bf16[256,1024]{1,0:T(8,128)(2,1)S(1)}, bf16[256,1024]{1,0:T(8,128)(2,1)}, u32[]{:S(2)}) copy-start(bf16[256,1024]{1,0:T(8,128)(2,1)} %get-tuple-element.142) | copy-start | bytes 1572868
  21.0 20.6 %copy-start.40 = (s32[6]{0:T(128)S(1)}, s32[6]{0:T(128)}, u32[]{:S(2)}) copy-start(s32[6]{0:T(128)} %copy-done.39) | copy-start | bytes 76
  21.0 20.6 %copy-start.41 = (f32[48,256]{1,0:T(8,128)S(1)}, f32[48,256]{1,0:T(8,128)}, u32[]{:S(2)}) copy-start(f32[48,256]{1,0:T(8,128)} %maximum_maximum_fusion.ssm_ref.own_ref) | copy-start | bytes 147460
  37.1 12.0 %collective-permute-start.2 = (bf16[128,1024]{1,0:T(8,128)(2,1)S(1)}, bf16[128,1024]{1,0:T(8,128)(2,1)S(1)}, u32[]{:S(2)}, u32[]{:S(2)}) collective-permute-start(bf16[128,1024]{1,0:T(8,128)(2,1)S(1)} %get-tuple-element.254), channel_id=1, source_target_pairs={{0,8},{4,12},{8,0},{12,4},{16,24},{20,28},{24,16},{28,20},{1,9},{5... | collective-permute-start | bytes 786440 | tf_op jit(solution)/shard_map/ppermute | solution.py:887
  38.7 21.2 %collective-permute-start.5 = (bf16[256,1024]{1,0:T(8,128)(2,1)S(1)}, bf16[256,1024]{1,0:T(8,128)(2,1)S(1)}, u32[]{:S(2)}, u32[]{:S(2)}) collective-permute-start(bf16[256,1024]{1,0:T(8,128)(2,1)S(1)} %bitcast.65), channel_id=1, source_target_pairs={{0,1},{1,0},{2,3},{3,2},{4,5},{5,4},{6,7},{7,6},{8,9},{9,8},{10,11... | collective-permute-start | bytes 1572872 | tf_op jit(solution)/shard_map/ppermute | solution.py:884
  38.7 24.6 %collective-permute-start.4 = (bf16[256,1024]{1,0:T(8,128)(2,1)S(1)}, bf16[256,1024]{1,0:T(8,128)(2,1)}, u32[]{:S(2)}, u32[]{:S(2)}) collective-permute-start(bf16[256,1024]{1,0:T(8,128)(2,1)S(1)} %copy-done.55), channel_id=1, source_target_pairs={{0,2},{1,3},{2,0},{3,1},{4,6},{5,7},{6,4},{7,5},{8,10},{9,11},{10,... | collective-permute-start | bytes 1572872 | tf_op jit(solution)/shard_map/ppermute | solution.py:884
  42.3 24.0 %copy-start.33 = (f32[16,512]{1,0:T(8,128)}, f32[16,512]{1,0:T(8,128)S(1)}, u32[]{:S(2)}) copy-start(f32[16,512]{1,0:T(8,128)S(1)} %get-tuple-element.260.rate_ref) | copy-start | bytes 98308
  42.3 24.0 %copy-start.42 = (f32[16,512]{1,0:T(8,128)}, f32[16,512]{1,0:T(8,128)S(1)}, u32[]{:S(2)}) copy-start(f32[16,512]{1,0:T(8,128)S(1)} %get-tuple-element.259.coef_ref) | copy-start | bytes 98308
  49.0 17.2 %copy-start.24 = (bf16[2,256,1024]{2,1,0:T(8,128)(2,1)}, bf16[2,256,1024]{2,1,0:T(8,128)(2,1)S(1)}, u32[]{:S(2)}) copy-start(bf16[2,256,1024]{2,1,0:T(8,128)(2,1)S(1)} %get-tuple-element.219.tile_ref) | copy-start | bytes 3145732
  50.0 16.3 %collective-permute-start.3 = (bf16[2,128,1024]{2,1,0:T(8,128)(2,1)}, bf16[2,128,1024]{2,1,0:T(8,128)(2,1)}, u32[]{:S(2)}, u32[]{:S(2)}) collective-permute-start(bf16[2,128,1024]{2,1,0:T(8,128)(2,1)} %pad_maximum_fusion.1), channel_id=1, source_target_pairs={{0,16},{4,20},{8,24},{12,28},{16,0},{20,4},{24,8},{28,12},{1,17},{... | collective-permute-start | bytes 1572872 | tf_op jit(solution)/shard_map/ppermute | solution.py:887
  51.5 14.8 %collective-permute-start.6 = (bf16[224,512]{1,0:T(8,128)(2,1)}, bf16[224,512]{1,0:T(8,128)(2,1)}, u32[]{:S(2)}, u32[]{:S(2)}) collective-permute-start(bf16[224,512]{1,0:T(8,128)(2,1)} %get-tuple-element.140), channel_id=1, source_target_pairs={{0,2},{1,3},{4,6},{5,7},{8,10},{9,11},{12,14},{13,15},{16,18},{17,... | collective-permute-start | bytes 688136 | tf_op jit(solution)/shard_map/ppermute | solution.py:951
  66.2 4.8 %copy-start.11 = (bf16[2,256,768]{2,1,0:T(8,128)(2,1)}, bf16[2,256,768]{2,1,0:T(8,128)(2,1)S(1)}, u32[]{:S(2)}) copy-start(bf16[2,256,768]{2,1,0:T(8,128)(2,1)S(1)} %shard_map.207.qkv_ref.near_ref) | copy-start | bytes 2359300
  68.4 4.5 %copy-start.52 = (f32[2,16,512]{2,1,0:T(8,128)}, f32[2,16,512]{2,1,0:T(8,128)S(1)}, u32[]{:S(2)}) copy-start(f32[2,16,512]{2,1,0:T(8,128)S(1)} %get-tuple-element.151.enter_ref) | copy-start | bytes 196612
  68.5 8.1 %copy-start.20 = (bf16[128,512]{1,0:T(8,128)(2,1)}, bf16[128,512]{1,0:T(8,128)(2,1)S(1)}, u32[]{:S(2)}) copy-start(bf16[128,512]{1,0:T(8,128)(2,1)S(1)} %get-tuple-element.150.second_ref) | copy-start | bytes 393220
  68.5 188.7 %all-gather.5.cloned.1.call-start = ((), (), s32[]{:S(2)}) async-start(), calls=%async_computation.1 | async-start | bytes 4718592 | tf_op jit(solution)/shard_map/all_gather | solution.py:890
  68.7 5.0 %copy-start.25 = (bf16[2,256,1024]{2,1,0:T(8,128)(2,1)S(1)}, bf16[2,256,1024]{2,1,0:T(8,128)(2,1)}, u32[]{:S(2)}) copy-start(bf16[2,256,1024]{2,1,0:T(8,128)(2,1)} %copy-done.24) | copy-start | bytes 3145732
  71.0 2.7 %collective-permute-start.7 = (bf16[4,128,1024]{2,1,0:T(8,128)(2,1)S(1)}, bf16[4,128,1024]{2,1,0:T(8,128)(2,1)S(1)}, u32[]{:S(2)}, u32[]{:S(2)}) collective-permute-start(bf16[4,128,1024]{2,1,0:T(8,128)(2,1)S(1)} %constant_dynamic-update-slice_fusion.3.even_ref), channel_id=1, source_target_pairs={{0,4},{4,0},{8,12},{12,8},{16,20},{20,16},{24,28},{28,24},{1,5},{5... | collective-permute-start | bytes 3145736 | tf_op jit(solution)/shard_map/ppermute | solution.py:887
  73.7 25.0 %copy-start.7 = (bf16[1,256,1024]{2,1,0:T(8,128)(2,1)S(1)}, bf16[1,256,1024]{2,1,0:T(8,128)(2,1)}, u32[]{:S(2)}) copy-start(bf16[1,256,1024]{2,1,0:T(8,128)(2,1)} %param.12) | copy-start | bytes 1572868
  76.5 22.2 %copy-start.31 = (bf16[1024,256]{1,0:T(8,128)(2,1)}, bf16[1024,256]{1,0:T(8,128)(2,1)S(1)}, u32[]{:S(2)}) copy-start(bf16[1024,256]{1,0:T(8,128)(2,1)S(1)} %get-tuple-element.158.out_far_ref) | copy-start | bytes 1572868
  76.5 23.2 %copy-start.9 = (bf16[2,256,768]{2,1,0:T(8,128)(2,1)}, bf16[2,256,768]{2,1,0:T(8,128)(2,1)S(1)}, u32[]{:S(2)}) copy-start(bf16[2,256,768]{2,1,0:T(8,128)(2,1)S(1)} %get-tuple-element.159.qkv_ref.far_ref) | copy-start | bytes 2359300
  76.6 22.2 %copy-start.48 = (f32[1024]{0:T(1024)S(1)}, f32[1024]{0:T(1024)}, u32[]{:S(2)}) copy-start(f32[1024]{0:T(1024)} %param.20) | copy-start | bytes 12292
  76.6 25.0 %copy-start.3 = (bf16[1024,1024]{1,0:T(8,128)(2,1)S(1)}, bf16[1024,1024]{1,0:T(8,128)(2,1)}, u32[]{:S(2)}) copy-start(bf16[1024,1024]{1,0:T(8,128)(2,1)} %down0_ref.3) | copy-start | bytes 6291460
  79.9 21.7 %copy-start.2 = (bf16[1024,1024]{1,0:T(8,128)(2,1)S(1)}, bf16[1024,1024]{1,0:T(8,128)(2,1)}, u32[]{:S(2)}) copy-start(bf16[1024,1024]{1,0:T(8,128)(2,1)} %up0_ref.3) | copy-start | bytes 6291460
  79.9 18.8 %collective-permute-start.8 = (bf16[256,1024]{1,0:T(8,128)(2,1)S(1)}, bf16[256,1024]{1,0:T(8,128)(2,1)S(1)}, u32[]{:S(2)}, u32[]{:S(2)}) collective-permute-start(bf16[256,1024]{1,0:T(8,128)(2,1)S(1)} %get-tuple-element.161), channel_id=1, source_target_pairs={{0,1},{1,0},{2,3},{3,2},{4,5},{5,4},{6,7},{7,6},{8,9},{9,8},{10,11... | collective-permute-start | bytes 1572872 | tf_op jit(solution)/shard_map/ppermute | solution.py:884
  99.7 13.5 %collective-permute-start.9 = (bf16[256,1024]{1,0:T(8,128)(2,1)S(1)}, bf16[256,1024]{1,0:T(8,128)(2,1)S(1)}, u32[]{:S(2)}, u32[]{:S(2)}) collective-permute-start(bf16[256,1024]{1,0:T(8,128)(2,1)S(1)} %get-tuple-element.174.n_ref), channel_id=1, source_target_pairs={{0,1},{1,0},{2,3},{3,2},{4,5},{5,4},{6,7},{7,6},{8,9},{9,8},{10,11... | collective-permute-start | bytes 1572872 | tf_op jit(solution)/shard_map/ppermute | solution.py:884
  118.9 9.2 %copy-start.1 = (bf16[2048,1024]{1,0:T(8,128)(2,1)S(1)}, bf16[2048,1024]{1,0:T(8,128)(2,1)}, u32[]{:S(2)}) copy-start(bf16[2048,1024]{1,0:T(8,128)(2,1)} %all-gather.3.cloned.1.call-done) | copy-start | bytes 12582916
  118.9 9.2 %copy-start.36 = (bf16[256,1024]{1,0:T(8,128)(2,1)S(1)}, bf16[256,1024]{1,0:T(8,128)(2,1)}, u32[]{:S(2)}) copy-start(bf16[256,1024]{1,0:T(8,128)(2,1)} %copy-done.35) | copy-start | bytes 1572868
  126.7 13.0 %collective-permute-start.11 = (bf16[256,1024]{1,0:T(8,128)(2,1)S(1)}, bf16[256,1024]{1,0:T(8,128)(2,1)S(1)}, u32[]{:S(2)}, u32[]{:S(2)}) collective-permute-start(bf16[256,1024]{1,0:T(8,128)(2,1)S(1)} %get-tuple-element.173), channel_id=1, source_target_pairs={{0,1},{1,0},{2,3},{3,2},{4,5},{5,4},{6,7},{7,6},{8,9},{9,8},{10,11... | collective-permute-start | bytes 1572872 | tf_op jit(solution)/shard_map/ppermute | solution.py:884
  137.1 4.8 %collective-permute-start.10 = (bf16[1024,1024]{1,0:T(8,128)(2,1)S(1)}, bf16[1024,1024]{1,0:T(8,128)(2,1)S(1)}, u32[]{:S(2)}, u32[]{:S(2)}) collective-permute-start(bf16[1024,1024]{1,0:T(8,128)(2,1)S(1)} %shard_map.216), channel_id=1, source_target_pairs={{0,4},{4,0},{8,12},{12,8},{16,20},{20,16},{24,28},{28,24},{1,5},{5... | collective-permute-start | bytes 6291464 | tf_op jit(solution)/shard_map/ppermute | solution.py:887
  139.1 6.0 %collective-permute-start.14 = (bf16[512,2048]{1,0:T(8,128)(2,1)S(1)}, bf16[512,2048]{1,0:T(8,128)(2,1)S(1)}, u32[]{:S(2)}, u32[]{:S(2)}) collective-permute-start(bf16[512,2048]{1,0:T(8,128)(2,1)S(1)} %shard_map.217), channel_id=1, source_target_pairs={{0,4},{4,0},{8,12},{12,8},{16,20},{20,16},{24,28},{28,24},{1,5},{5... | collective-permute-start | bytes 6291464 | tf_op jit(solution)/shard_map/ppermute | solution.py:887
  141.0 13.9 %collective-permute-start.13 = (bf16[256,1024]{1,0:T(8,128)(2,1)S(1)}, bf16[256,1024]{1,0:T(8,128)(2,1)S(1)}, u32[]{:S(2)}, u32[]{:S(2)}) collective-permute-start(bf16[256,1024]{1,0:T(8,128)(2,1)S(1)} %get-tuple-element.184.own_ref), channel_id=1, source_target_pairs={{0,1},{1,0},{2,3},{3,2},{4,5},{5,4},{6,7},{7,6},{8,9},{9,8},{10,11... | collective-permute-start | bytes 1572872 | tf_op jit(solution)/shard_map/ppermute | solution.py:884
  143.8 25.2 %collective-permute-start.12 = (bf16[512,1024]{1,0:T(8,128)(2,1)S(1)}, bf16[512,1024]{1,0:T(8,128)(2,1)S(1)}, u32[]{:S(2)}, u32[]{:S(2)}) collective-permute-start(bf16[512,1024]{1,0:T(8,128)(2,1)S(1)} %get-tuple-element.188), channel_id=1, source_target_pairs={{0,8},{4,12},{8,0},{12,4},{16,24},{20,28},{24,16},{28,20},{1,9},{5... | collective-permute-start | bytes 3145736 | tf_op jit(solution)/shard_map/ppermute | solution.py:887
  145.0 9.9 %copy-start.17 = (bf16[256,1024]{1,0:T(8,128)(2,1)S(1)}, bf16[256,1024]{1,0:T(8,128)(2,1)}, u32[]{:S(2)}) copy-start(bf16[256,1024]{1,0:T(8,128)(2,1)} %out_near_ref.3) | copy-start | bytes 1572868
  145.0 9.9 %copy-start.32 = (bf16[1024,256]{1,0:T(8,128)(2,1)S(1)}, bf16[1024,256]{1,0:T(8,128)(2,1)}, u32[]{:S(2)}) copy-start(bf16[1024,256]{1,0:T(8,128)(2,1)} %copy-done.31) | copy-start | bytes 1572868
  146.9 24.8 %collective-permute-start.18 = (bf16[256,2048]{1,0:T(8,128)(2,1)S(1)}, bf16[256,2048]{1,0:T(8,128)(2,1)S(1)}, u32[]{:S(2)}, u32[]{:S(2)}) collective-permute-start(bf16[256,2048]{1,0:T(8,128)(2,1)S(1)} %get-tuple-element.190), channel_id=1, source_target_pairs={{0,16},{4,20},{8,24},{12,28},{16,0},{20,4},{24,8},{28,12},{1,17},{... | collective-permute-start | bytes 3145736 | tf_op jit(solution)/shard_map/ppermute | solution.py:887
  155.0 8.4 %copy-start.19 = (bf16[1024,768]{1,0:T(8,128)(2,1)S(1)}, bf16[1024,768]{1,0:T(8,128)(2,1)}, u32[]{:S(2)}) copy-start(bf16[1024,768]{1,0:T(8,128)(2,1)} %copy-done.18) | copy-start | bytes 4718596
  156.3 7.1 %copy-start.15 = (bf16[1024,768]{1,0:T(8,128)(2,1)S(1)}, bf16[1024,768]{1,0:T(8,128)(2,1)}, u32[]{:S(2)}) copy-start(bf16[1024,768]{1,0:T(8,128)(2,1)} %copy-done.13) | copy-start | bytes 4718596
  161.8 12.4 %collective-permute-start.17 = (bf16[176,512]{1,0:T(8,128)(2,1)S(1)}, bf16[176,512]{1,0:T(8,128)(2,1)S(1)}, u32[]{:S(2)}, u32[]{:S(2)}) collective-permute-start(bf16[176,512]{1,0:T(8,128)(2,1)S(1)} %get-tuple-element.196), channel_id=1, source_target_pairs={{2,0},{3,1},{6,4},{7,5},{10,8},{11,9},{14,12},{15,13},{18,16},{19,... | collective-permute-start | bytes 540680 | tf_op jit(solution)/shard_map/ppermute | solution.py:1057
  167.8 12.7 %collective-permute-start.16 = (bf16[512,2048]{1,0:T(8,128)(2,1)S(1)}, bf16[512,2048]{1,0:T(8,128)(2,1)S(1)}, u32[]{:S(2)}, u32[]{:S(2)}) collective-permute-start(bf16[512,2048]{1,0:T(8,128)(2,1)S(1)} %shard_map.224), channel_id=1, source_target_pairs={{0,4},{4,0},{8,12},{12,8},{16,20},{20,16},{24,28},{28,24},{1,5},{5... | collective-permute-start | bytes 6291464 | tf_op jit(solution)/shard_map/ppermute | solution.py:887
  169.7 19.4 %collective-permute-start.15 = (bf16[256,1024]{1,0:T(8,128)(2,1)S(1)}, bf16[256,1024]{1,0:T(8,128)(2,1)S(1)}, u32[]{:S(2)}, u32[]{:S(2)}) collective-permute-start(bf16[256,1024]{1,0:T(8,128)(2,1)S(1)} %get-tuple-element.202), channel_id=1, source_target_pairs={{0,16},{4,20},{8,24},{12,28},{16,0},{20,4},{24,8},{28,12},{1,17},{... | collective-permute-start | bytes 1572872 | tf_op jit(solution)/shard_map/ppermute | solution.py:887
  172.5 13.0 %collective-permute-start.19 = (bf16[128,2048]{1,0:T(8,128)(2,1)S(1)}, bf16[128,2048]{1,0:T(8,128)(2,1)S(1)}, u32[]{:S(2)}, u32[]{:S(2)}) collective-permute-start(bf16[128,2048]{1,0:T(8,128)(2,1)S(1)} %get-tuple-element.205), channel_id=1, source_target_pairs={{0,8},{4,12},{8,0},{12,4},{16,24},{20,28},{24,16},{28,20},{1,9},{5... | collective-permute-start | bytes 1572872 | tf_op jit(solution)/shard_map/ppermute | solution.py:887
  179.3 19.2 %collective-permute-start.24 = (bf16[256,1024]{1,0:T(8,128)(2,1)S(1)}, bf16[256,1024]{1,0:T(8,128)(2,1)S(1)}, u32[]{:S(2)}, u32[]{:S(2)}) collective-permute-start(bf16[256,1024]{1,0:T(8,128)(2,1)S(1)} %get-tuple-element.208), channel_id=1, source_target_pairs={{0,1},{1,0},{2,3},{3,2},{4,5},{5,4},{6,7},{7,6},{8,9},{9,8},{10,11... | collective-permute-start | bytes 1572872 | tf_op jit(solution)/shard_map/ppermute | solution.py:884
  182.4 22.1 %collective-permute-start.21 = (bf16[128,2048]{1,0:T(8,128)(2,1)S(1)}, bf16[128,2048]{1,0:T(8,128)(2,1)S(1)}, u32[]{:S(2)}, u32[]{:S(2)}) collective-permute-start(bf16[128,2048]{1,0:T(8,128)(2,1)S(1)} %get-tuple-element.212), channel_id=1, source_target_pairs={{0,16},{4,20},{8,24},{12,28},{16,0},{20,4},{24,8},{28,12},{1,17},{... | collective-permute-start | bytes 1572872 | tf_op jit(solution)/shard_map/ppermute | solution.py:887
  184.2 20.4 %collective-permute-start.22 = (bf16[128,2048]{1,0:T(8,128)(2,1)S(1)}, bf16[128,2048]{1,0:T(8,128)(2,1)S(1)}, u32[]{:S(2)}, u32[]{:S(2)}) collective-permute-start(bf16[128,2048]{1,0:T(8,128)(2,1)S(1)} %get-tuple-element.213), channel_id=1, source_target_pairs={{0,8},{4,12},{8,0},{12,4},{16,24},{20,28},{24,16},{28,20},{1,9},{5... | collective-permute-start | bytes 1572872 | tf_op jit(solution)/shard_map/ppermute | solution.py:887
  185.5 23.7 %collective-permute-start.23 = (bf16[128,2048]{1,0:T(8,128)(2,1)S(1)}, bf16[128,2048]{1,0:T(8,128)(2,1)S(1)}, u32[]{:S(2)}, u32[]{:S(2)}) collective-permute-start(bf16[128,2048]{1,0:T(8,128)(2,1)S(1)} %get-tuple-element.214), channel_id=1, source_target_pairs={{0,24},{4,28},{8,16},{12,20},{16,8},{20,12},{24,0},{28,4},{1,25},{... | collective-permute-start | bytes 1572872 | tf_op jit(solution)/shard_map/ppermute | solution.py:887
  189.1 5.1 %copy-start.26 = (bf16[2,256,1024]{2,1,0:T(8,128)(2,1)S(1)}, bf16[2,256,1024]{2,1,0:T(8,128)(2,1)}, u32[]{:S(2)}) copy-start(bf16[2,256,1024]{2,1,0:T(8,128)(2,1)} %copy-done.24) | copy-start | bytes 3145732
  189.1 5.1 %copy-start.53 = (f32[2,16,512]{2,1,0:T(8,128)S(1)}, f32[2,16,512]{2,1,0:T(8,128)}, u32[]{:S(2)}) copy-start(f32[2,16,512]{2,1,0:T(8,128)} %copy-done.52) | copy-start | bytes 196612
  189.8 22.8 %collective-permute-start.20 = (bf16[128,2048]{1,0:T(8,128)(2,1)S(1)}, bf16[128,2048]{1,0:T(8,128)(2,1)S(1)}, u32[]{:S(2)}, u32[]{:S(2)}) collective-permute-start(bf16[128,2048]{1,0:T(8,128)(2,1)S(1)} %get-tuple-element.218), channel_id=1, source_target_pairs={{0,2},{1,3},{2,0},{3,1},{4,6},{5,7},{6,4},{7,5},{8,10},{9,11},{10,... | collective-permute-start | bytes 1572872 | tf_op jit(solution)/shard_map/ppermute | solution.py:884
  194.2 4.3 %copy-start.47 = (f32[1024]{0:T(1024)S(1)}, f32[1024]{0:T(1024)}, u32[]{:S(2)}) copy-start(f32[1024]{0:T(1024)} %param.14) | copy-start | bytes 12292
  200.9 3.7 %collective-permute-start.25 = (f32[8,256]{1,0:T(8,128)S(1)}, f32[8,256]{1,0:T(8,128)S(1)}, u32[]{:S(2)}, u32[]{:S(2)}) collective-permute-start(f32[8,256]{1,0:T(8,128)S(1)} %get-tuple-element.221.gains_ref), channel_id=1, source_target_pairs={{0,1},{1,0},{2,3},{3,2},{4,5},{5,4},{6,7},{7,6},{8,9},{9,8},{10,11... | collective-permute-start | bytes 24584 | tf_op jit(solution)/shard_map/ppermute | solution.py:884
  210.0 5.7 %copy-start.50 = (bf16[256,1024]{1,0:T(8,128)(2,1)S(1)}, bf16[256,1024]{1,0:T(8,128)(2,1)}, u32[]{:S(2)}) copy-start(bf16[256,1024]{1,0:T(8,128)(2,1)} %copy-done.49) | copy-start | bytes 1572868
  212.6 21.2 %copy-start.28 = (f32[256,1024]{1,0:T(8,128)S(1)}, f32[256,1024]{1,0:T(8,128)}, u32[]{:S(2)}) copy-start(f32[256,1024]{1,0:T(8,128)} %copy-done.27) | copy-start | bytes 3145732
  214.1 13.4 %collective-permute-start.27 = (bf16[144,1024]{1,0:T(8,128)(2,1)}, bf16[144,1024]{1,0:T(8,128)(2,1)S(1)}, u32[]{:S(2)}, u32[]{:S(2)}) collective-permute-start(bf16[144,1024]{1,0:T(8,128)(2,1)} %copy-done.51), channel_id=1, source_target_pairs={{0,2},{1,3},{2,0},{3,1},{4,6},{5,7},{6,4},{7,5},{8,10},{9,11},{10,... | collective-permute-start | bytes 884744 | tf_op jit(solution)/shard_map/ppermute | solution.py:884
  215.7 18.1 %collective-permute-start.26 = (bf16[256,1024]{1,0:T(8,128)(2,1)S(1)}, bf16[256,1024]{1,0:T(8,128)(2,1)S(1)}, u32[]{:S(2)}, u32[]{:S(2)}) collective-permute-start(bf16[256,1024]{1,0:T(8,128)(2,1)S(1)} %copy-done.50), channel_id=1, source_target_pairs={{0,1},{1,0},{2,3},{3,2},{4,5},{5,4},{6,7},{7,6},{8,9},{9,8},{10,11... | collective-permute-start | bytes 1572872 | tf_op jit(solution)/shard_map/ppermute | solution.py:884
  228.1 10.0 %collective-permute-start.28 = (bf16[144,1024]{1,0:T(8,128)(2,1)S(1)}, bf16[144,1024]{1,0:T(8,128)(2,1)S(1)}, u32[]{:S(2)}, u32[]{:S(2)}) collective-permute-start(bf16[144,1024]{1,0:T(8,128)(2,1)S(1)} %shard_map.234), channel_id=1, source_target_pairs={{0,8},{4,12},{8,0},{12,4},{16,24},{20,28},{24,16},{28,20},{1,9},{5... | collective-permute-start | bytes 884744 | tf_op jit(solution)/shard_map/ppermute | solution.py:887
  229.4 13.5 %collective-permute-start.29 = (bf16[144,1024]{1,0:T(8,128)(2,1)S(1)}, bf16[144,1024]{1,0:T(8,128)(2,1)S(1)}, u32[]{:S(2)}, u32[]{:S(2)}) collective-permute-start(bf16[144,1024]{1,0:T(8,128)(2,1)S(1)} %shard_map.234), channel_id=1, source_target_pairs={{0,16},{4,20},{8,24},{12,28},{16,0},{20,4},{24,8},{28,12},{1,17},{... | collective-permute-start | bytes 884744 | tf_op jit(solution)/shard_map/ppermute | solution.py:887
  229.9 19.0 %collective-permute-start.30 = (bf16[144,1024]{1,0:T(8,128)(2,1)S(1)}, bf16[144,1024]{1,0:T(8,128)(2,1)S(1)}, u32[]{:S(2)}, u32[]{:S(2)}) collective-permute-start(bf16[144,1024]{1,0:T(8,128)(2,1)S(1)} %shard_map.234), channel_id=1, source_target_pairs={{0,24},{4,28},{8,16},{12,20},{16,8},{20,12},{24,0},{28,4},{1,25},{... | collective-permute-start | bytes 884744 | tf_op jit(solution)/shard_map/ppermute | solution.py:887
  249.0 2.9 %collective-permute-start.31 = (bf16[4,144,1024]{2,1,0:T(8,128)(2,1)S(1)}, bf16[4,144,1024]{2,1,0:T(8,128)(2,1)S(1)}, u32[]{:S(2)}, u32[]{:S(2)}) collective-permute-start(bf16[4,144,1024]{2,1,0:T(8,128)(2,1)S(1)} %pad_maximum_fusion.even_ref), channel_id=1, source_target_pairs={{0,4},{4,0},{8,12},{12,8},{16,20},{20,16},{24,28},{28,24},{1,5},{5... | collective-permute-start | bytes 3538952 | tf_op jit(solution)/shard_map/ppermute | solution.py:887
  (26 other events, 45.2 us)
Sparse Core Ops, SparseCore 0:
  68.6 43.2 all-gather.2
  214.2 42.4 all-gather.4

commit v4 on v3

--- a/solution.py
+++ b/solution.py
@@ -158,9 +158,11 @@
     by_rows(body, x_ref.shape[0])
 
 
-def touch(flag_ref, up_ref, down_ref, cot_ref, paired_ref, out_ref):
+def touch(flag_ref, up_ref, down_ref, cot_ref, paired_ref, rows_ref, out_ref):
     out_ref[...] = (
-        up_ref[:8, :128] + down_ref[:8, :128] + (cot_ref[:8, :128] + paired_ref[:8, :128])
+        (up_ref[:8, :128] + down_ref[:8, :128])
+        + (cot_ref[:8, :128] + paired_ref[:8, :128])
+        + rows_ref[:8, :128]
     )
 
 
@@ -542,13 +544,6 @@
         returned_ref[CTX + k * STATES : CTX + (k + 1) * STATES, :] = part
 
 
-def flat(ref):
-    if len(ref.shape) == 2:
-        return ref[...]
-    part = ref[:, 0]
-    return part.reshape(part.shape[0] * part.shape[1], part.shape[2])
-
-
 def feed_forward(
     flag_ref, n_ref, c_ref, up0_ref, down0_ref, up1_ref, down1_ref, act_ref, gate_ref, sent_ref,
     down_out_ref, back_out_ref, acc_down, acc_back,
@@ -588,7 +583,7 @@
 
     @pl.when(step >= per)
     def _():
-        body(flat(up1_ref), flat(down1_ref), 1)
+        body(up1_ref[...], down1_ref[...], 1)
 
     @pl.when(step == steps - 1)
     def _():
@@ -596,12 +591,11 @@
         back_out_ref[...] = acc_back[...].astype(back_out_ref.dtype)
 
 
-def run_feed_forward(flags, rows, cot, up, down, far, kind):
+def run_feed_forward(flags, rows, cot, up, down, up_far, down_far, kind):
     tokens, width = rows.shape
     block = 512
     hidden = up.shape[1]
     per = hidden // block
-    slices, slice_rows = far.shape[0], far.shape[2]
 
     def near_at(j):
         return jnp.minimum(j, per - 1)
@@ -626,8 +620,8 @@
             whole,
             pl.BlockSpec((width, block), lambda j: (0, near_at(j))),
             pl.BlockSpec((block, width), lambda j: (near_at(j), 0)),
-            pl.BlockSpec((slices, 1, slice_rows, block), lambda j: (0, 0, 0, far_at(j))),
-            pl.BlockSpec((slices // per, 1, slice_rows, width), lambda j: (far_at(j), 1, 0, 0)),
+            pl.BlockSpec((width, block), lambda j: (0, far_at(j))),
+            pl.BlockSpec((block, width), lambda j: (far_at(j), 0)),
         ],
         out_specs=(
             pl.BlockSpec((tokens, 2 * hidden), lambda j: (0, 0)),
@@ -641,7 +635,7 @@
             vmem_limit_bytes=24 * 1024 * 1024, dimension_semantics=("arbitrary",)
         ),
         cost_estimate=length(0),
-    )(flags, rows, cot, up, down, far, far)
+    )(flags, rows, cot, up, down, up_far, down_far)
 
 
 def products(lhs_refs, rhs_refs, columns, split=None):
@@ -787,30 +781,21 @@
     out_ref[...] = (a_ref[...].astype(f32) + b_ref[...].astype(f32)).astype(out_ref.dtype)
 
 
+def add_halves(flag_ref, a_ref, b_ref, left_ref, right_ref):
+    width = left_ref.shape[1]
+    total = a_ref[...] + b_ref[...].astype(f32)
+    left_ref[...] = total[:, :width].astype(bf16)
+    right_ref[...] = total[:, width:].astype(bf16)
+
+
+def split_rows(flag_ref, value_ref, top_ref, bottom_ref):
+    rows = top_ref.shape[0]
+    top_ref[...] = value_ref[:rows, :]
+    bottom_ref[...] = value_ref[rows:, :]
+
+
 def add_three(flag_ref, a_ref, b_ref, c_ref, out_ref):
     out_ref[...] = (a_ref[...] + b_ref[...] + c_ref[...].astype(f32)).astype(out_ref.dtype)
-
-
-def widen(all_ref, down_ref, up_ref):
-    down = down_ref.shape[1]
-    down_ref[...] = all_ref[:, :down].astype(f32)
-    up_ref[...] = all_ref[:, down:].astype(f32)
-
-
-def run_widen(value, down_width, up_width):
-    rows = value.shape[0] // 4
-    return pl.pallas_call(
-        widen,
-        grid=(4,),
-        in_specs=[pl.BlockSpec((rows, value.shape[1]), lambda j: (j, 0))],
-        out_specs=(
-            pl.BlockSpec((rows, down_width), lambda j: (j, 0)),
-            pl.BlockSpec((rows, up_width), lambda j: (j, 0)),
-        ),
-        out_shape=(shape((value.shape[0], down_width)), shape((value.shape[0], up_width))),
-        compiler_params=pltpu.CompilerParams(vmem_limit_bytes=56 * 1024 * 1024),
-        cost_estimate=length(0),
-    )(value)
 
 
 def sources(flag_ref, even_ref, odd_ref, rows):
@@ -847,6 +832,62 @@
         ]
 
 
+def stack_two(flag_ref, a_ref, ax_ref, b_ref, by_ref, a_out, b_out):
+    a_out[0], a_out[1] = a_ref[...], ax_ref[...]
+    b_out[0], b_out[1] = b_ref[...], by_ref[...]
+
+
+def stack_four(flag_ref, a_ref, b_ref, c_ref, d_ref, out_ref):
+    for k, ref in enumerate((a_ref, b_ref, c_ref, d_ref)):
+        out_ref[k] = ref[...]
+
+
+def stack_eight(flag_ref, a_ref, ay_ref, b_ref, bx_ref, out_ref):
+    out_ref[0, 0], out_ref[1, 0] = a_ref[0], a_ref[1]
+    out_ref[2, 0], out_ref[3, 0] = ay_ref[0], ay_ref[1]
+    out_ref[0, 1], out_ref[2, 1] = b_ref[0], b_ref[1]
+    out_ref[1, 1], out_ref[3, 1] = bx_ref[0], bx_ref[1]
+
+
+def place_two(flag_ref, even_ref, odd_ref, a_out, b_out):
+    for ref, pair, at in sources(flag_ref, even_ref, odd_ref, even_ref.shape[2]):
+        a_out[at, :] = ref[pair, 0].astype(a_out.dtype)
+        b_out[at, :] = ref[pair, 1].astype(b_out.dtype)
+
+
+def place_wide(flag_ref, even_ref, odd_ref, a_out, b_out):
+    @pl.when(pl.program_id(0) % 2 == 0)
+    def _():
+        a_out[...] = even_ref[0, 0].astype(f32)
+        b_out[...] = even_ref[0, 1].astype(f32)
+
+    @pl.when(pl.program_id(0) % 2 == 1)
+    def _():
+        a_out[...] = odd_ref[0, 0].astype(f32)
+        b_out[...] = odd_ref[0, 1].astype(f32)
+
+
+def run_place_wide(flags, even, odd):
+    rows, width = even.shape[2:]
+    piece = pl.BlockSpec((1, 2, rows, width), lambda j, flag_ref: (j // 2, 0, 0, 0))
+    place = pl.BlockSpec(
+        (rows, width), lambda j, flag_ref: (jnp.bitwise_xor(flag_ref[PLACE], j), 0)
+    )
+    out = shape((GROUP * rows, width))
+    return pl.pallas_call(
+        place_wide,
+        grid_spec=pltpu.PrefetchScalarGridSpec(
+            num_scalar_prefetch=1,
+            grid=(GROUP,),
+            in_specs=[piece, piece],
+            out_specs=(place, place),
+        ),
+        out_shape=(out, out),
+        compiler_params=pltpu.CompilerParams(vmem_limit_bytes=VMEM_LIMIT),
+        cost_estimate=length(0),
+    )(flags, even, odd)
+
+
 class Order:
     def __init__(self):
         self.last = ()
@@ -877,8 +918,6 @@
 ):
     z = lax.axis_index("mp")
     place = jnp.bitwise_and(lax.axis_index("dp"), GROUP - 1)
-    groups = [[g * GROUP + k for k in range(GROUP)] for g in range(dp_size // GROUP)]
-    groups = groups if len(groups) > 1 else None
 
     def swap_mp(value, mask):
         return lax.ppermute(value, "mp", [(k, k ^ mask) for k in range(4)])
@@ -886,11 +925,11 @@
     def swap_dp(value, mask):
         return lax.ppermute(value, "dp", [(k, k ^ mask) for k in range(dp_size)])
 
-    def gather(value):
-        return lax.all_gather(value, "dp", axis=0, tiled=True, axis_index_groups=groups)
-
     def gather_by_xor(piece):
         return [piece] + [swap_dp(piece, 2 * k) for k in range(1, GROUP // 2)]
+
+    def low(*dims):
+        return shape(dims, bf16)
 
     def over_groups(own):
         mask = GROUP
@@ -930,8 +969,9 @@
     near_qkv = order.done(jnp.concatenate(list(order(*[qkv_parts[k] for k in range(3)])), 1))
 
     paired_one, attn_across = order.done(order(paired_one, attn_across))
-    attn_mine = attn_across[:rows]
-    attn_x = swap_dp(attn_mine, 2)
+    attn_own_slice = attn_across[:rows]
+    attn_x = swap_dp(attn_own_slice, 2)
+    attn_y = swap_dp(attn_own_slice, 4)
     mlp_across = swap_mp(order(mlp_slice), 2)
     paired_cot = swap_mp(order(cot), 1)
     ssm_both = call(join_ssm, shape((48, wide)))(flags, ssm_pack, attn_across)
@@ -952,24 +992,30 @@
 
     qkv_shape = shape((2, HALF, 3 * channels), bf16)
     att_shape = shape((2, HALF, channels), bf16)
-    attn_two = order.done(jnp.stack([attn_mine, order(attn_x)]))
-    attn_y = swap_dp(attn_two, 4)
-    paired_cot = order.done(order(paired_cot))
-    mlp_across = order.done(order(mlp_across))
-    qkv_near = order.done(
-        call(project, qkv_shape, micros=4)(flags, order(tile_one), near_qkv)
-    )
-    attn_y = order.done(order(attn_y))
+    attn_x = order.done(order(attn_x))
+    attn_xy = swap_dp(attn_x, 4)
+    qkv_near = order.done(call(project, qkv_shape)(flags, order(tile_one), near_qkv))
+    attn_y, paired_cot = order.done(order(attn_y, paired_cot))
+    even = order.done(
+        call(stack_four, shape((4,) + attn_x.shape, bf16))(
+            flags, attn_own_slice, attn_x, attn_y, order(attn_xy)
+        )
+    )
+    odd_part = swap_dp(even, 1)
+    slice_shape = low(rows, model_dim)
+    mlp_up, mlp_down = order.done(
+        call(split_rows, (slice_shape, slice_shape))(flags, order(mlp_across))
+    )
+    mlp_up_x = swap_dp(mlp_up, 2)
+    mlp_down_y = swap_dp(mlp_down, 4)
     ctx_first, ctx_second, enter_state = order.done(
         call(
             ssm_carry_in,
             (shape((CTX, wide), bf16), shape((CTX, wide), bf16), shape((2, STATES, wide))),
             scratch=[pltpu.VMEM((CTX, wide), f32)],
+            micros=6,
         )(flags, second_local, order(handed), rate_t, coef_t)
     )
-    mlp_far = gather(order(mlp_across)).reshape(GROUP, 2, rows, model_dim)
-    even = order.done(jnp.concatenate(list(order(attn_two, attn_y)), 0))
-    odd_part = swap_dp(even, 1)
     att_near = order.done(
         call(attention_near, att_shape)(flags, order(qkv_near), ctx_first, ctx_second)
     )
@@ -989,17 +1035,40 @@
         )
     )
     out_received = swap_mp(out_send, 1)
+    pair_shape = low(2, rows, model_dim)
+    mlp_up_two, mlp_down_two = order.done(
+        call(stack_two, (pair_shape, pair_shape), micros=3)(
+            flags, mlp_up, order(mlp_up_x), mlp_down, order(mlp_down_y)
+        )
+    )
+    mlp_up_y = swap_dp(mlp_up_two, 4)
+    mlp_down_x = swap_dp(mlp_down_two, 2)
     middle, normed_two = order.done(
-        call(norm_two, (half, half_low))(
+        call(norm_two, (half, half_low), micros=3)(
             flags, row, out_own, order(out_received), gain_two
         )
     )
 
     paired_two = swap_mp(normed_two, 1)
+    eight_shape = low(GROUP // 2, 2, rows, model_dim)
+    mlp_even = order.done(
+        call(stack_eight, eight_shape, micros=1)(
+            flags, mlp_up_two, order(mlp_up_y), mlp_down_two, order(mlp_down_x)
+        )
+    )
+    mlp_odd = swap_dp(mlp_even, 1)
+    paired_two = order(paired_two)
     warm = order.done(
-        call(touch, shape((8, 128), bf16))(flags, order(up_weight), down_weight, cot, paired_cot)
-    )
-    mlp = (up_weight, down_weight, mlp_far)
+        call(touch, shape((8, 128), bf16), micros=12)(
+            flags, up_weight, down_weight, cot, paired_cot, paired_two
+        )
+    )
+    up_far, down_far = order.done(
+        call(place_two, (low(model_dim, hidden), low(hidden, model_dim)))(
+            flags, mlp_even, order(mlp_odd)
+        )
+    )
+    mlp = (up_weight, down_weight, up_far, down_far)
     act_other, gate_other, two_other, down_send, back_send = order.done(
         run_feed_forward(flags, order(paired_two), paired_cot, *mlp, bf16)
     )
@@ -1007,9 +1076,6 @@
     act_own, gate_own, two_own, down_own, back_own = order.done(
         run_feed_forward(flags, order(normed_two), cot, *mlp, f32)
     )
-
-    def low(*dims):
-        return shape(dims, bf16)
 
     side = model_dim // 2
     acts = (act_own, act_other, cot, paired_cot)
@@ -1044,6 +1110,7 @@
             micros=4,
         )(flags, attn_grad, order(paired_back), out_weight, far_out)
     )
+    down_received = swap_mp(order(down_send), 1)
     dqkv, second_grad, returned = order.done(
         call(
             attention_backward,
@@ -1087,6 +1154,9 @@
         )(flags, second_grad, order(returned), rate_t, coef_t, skip_t, one_total)
     )
     one_received = swap_mp(one_send, 1)
+    output = order.done(
+        call(add_three, half_low)(flags, middle, down_own, order(down_received))
+    )
     attn_mine, *attn_sends = order.done(
         call(attn_keep, (shape((rows, 8 * channels)),) + (low(rows, 8 * channels),) * 3)(
             flags, *attns, order(attn_core)
@@ -1114,6 +1184,12 @@
         )
     )
     gains_received = swap_mp(gains, 1)
+    down_mine, up_mine = order.done(
+        call(add_halves, (slice_shape, slice_shape))(flags, mlp_near, order(mlp_received))
+    )
+    down_mine, up_mine = over_groups(down_mine), over_groups(up_mine)
+    down_x = swap_dp(down_mine, 2)
+    up_y = swap_dp(up_mine, 4)
     slice_rows = rows + 16
     *attn_sent, gains_received = order(*attn_sent, gains_received)
     attn_near, attn_send = order.done(
@@ -1122,20 +1198,32 @@
         )
     )
     attn_received = swap_mp(attn_send, 2)
-    mlp_slice_grad = order.done(
-        call(add_two, low(rows, mlp_width))(flags, mlp_near, order(mlp_received))
-    )
-    mlp_full = gather(over_groups(mlp_slice_grad))
-    down_received = swap_mp(order(down_send), 1)
+    down_two, up_two = order.done(
+        call(stack_two, (pair_shape, pair_shape), micros=3)(
+            flags, down_mine, order(down_x), up_mine, order(up_y)
+        )
+    )
+    down_y = swap_dp(down_two, 4)
+    up_x = swap_dp(up_two, 2)
     attn_slice_grad = order.done(
-        call(add_two, low(slice_rows, 4 * channels))(flags, attn_near, order(attn_received))
-    )
-    attn_pieces = gather_by_xor(over_groups(attn_slice_grad))
-    output = order.done(
-        call(add_three, half_low)(flags, middle, down_own, order(down_received))
-    )
-    even = order.done(jnp.stack(list(order(*attn_pieces))))
+        call(add_two, low(slice_rows, 4 * channels), micros=3)(
+            flags, attn_near, order(attn_received)
+        )
+    )
+    attn_slice_grad = over_groups(attn_slice_grad)
+    attn_sent = [swap_dp(attn_slice_grad, 2 * k) for k in range(1, GROUP // 2)]
+    even = order.done(
+        call(stack_four, low(4, slice_rows, 4 * channels))(
+            flags, attn_slice_grad, *order(*attn_sent)
+        )
+    )
     odd_part = swap_dp(even, 1)
+    mlp_even = order.done(
+        call(stack_eight, eight_shape, micros=5)(
+            flags, down_two, order(down_y), up_two, order(up_x)
+        )
+    )
+    mlp_odd = swap_dp(mlp_even, 1)
     qkv_grad, out_grad, small = order.done(
         call(
             assemble_grad,
@@ -1144,9 +1232,10 @@
                 shape(out_weight.shape),
                 shape((48, channels)),
             ),
+            micros=6,
         )(flags, even, order(odd_part))
     )
-    down_grad, up_grad = run_widen(order(mlp_full), model_dim, hidden)
+    down_grad, up_grad = run_place_wide(flags, mlp_even, order(mlp_odd))
     gains = small[40:].reshape(2, model_dim)
     return (
         output[None],

time: 271 us -> 252 us (0.930)
  local copies, waits for them, and re-layouts: 19.2 us -> 4.84 us
  between operations: 15.5 us -> 1.86 us
  starting transfers between devices: 50.9 us -> 58.4 us
    unnamed x118 -> x33, local copies, waits for them, and re-layouts: 16.3 us -> 3.05 us
    ppermute x17 -> x28, starting transfers between devices: 19 us -> 27.4 us  [swap_dp(): return lax.ppermute(value, 'dp', [(k, k ^ mask) for k in range(dp_size)])]
    ppermute x13, starting transfers between devices: 27.5 us -> 24.4 us  [swap_mp(): return lax.ppermute(value, 'mp', [(k, k ^ mask) for k in range(4)])]
    pallas_call x31 -> x39, Pallas kernels: 61.2 us -> 64.2 us  [run(): pl.pallas_call(kernel, out_shape=out_shape, in_specs=[pl.BlockSpec(memory...]
    ppermute x17 -> x28, waiting for transfers between devices: 24.2 us -> 25.3 us  [swap_dp(): return lax.ppermute(value, 'dp', [(k, k ^ mask) for k in range(dp_size)])]
  transfers between devices with their start and end apart: 34 -> 43, of which waited for: 19 -> 20; matrix products, arithmetic and copies ran while one was open for 3% -> 2% of each run, Pallas kernels for 25% -> 29%
where the time goes in v4:
time: 252 us; the launch traced here: 251 us
  waiting for transfers between devices  98.7 us (39%)
  Pallas kernels  86.1 us (34%)
  starting transfers between devices  58.4 us (23%)
  local copies, waits for them, and re-layouts  4.84 us (2%)
    ppermute x13, waiting for transfers between devices, swap_mp(): return lax.ppermute(value, 'mp', [(k, k ^ mask) for k in range(4)])  73.4 us
    pallas_call x39, Pallas kernels, run(): pl.pallas_call(kernel, out_shape=out_shape, in_specs=[pl.BlockSpec(memory...  64.2 us
    ppermute x28, starting transfers between devices, swap_dp(): return lax.ppermute(value, 'dp', [(k, k ^ mask) for k in range(dp_size)])  27.4 us
    ppermute x28, waiting for transfers between devices, swap_dp(): return lax.ppermute(value, 'dp', [(k, k ^ mask) for k in range(dp_size)])  25.3 us
    ppermute x13, starting transfers between devices, swap_mp(): return lax.ppermute(value, 'mp', [(k, k ^ mask) for k in range(4)])  24.4 us
    pallas_call x2, Pallas kernels, run_feed_forward(): pl.pallas_call(feed_forward, grid=(2 * per,), out_shape=(shape((tokens, 2...  13.9 us
    ppermute x1, starting transfers between devices, per_device(): handed = lax.ppermute(handed, 'mp', [(0, 2), (1, 3)])  5.09 us
    pallas_call x1, Pallas kernels, run_place_wide(): pl.pallas_call(place_wide, grid_spec=pltpu.PrefetchScalarGridSpec(num_sca...  5.05 us
  transfers between devices with their start and end apart: 43, of which 20 were waited for; matrix products, arithmetic and copies ran while one was open for 2% of the time, Pallas kernels for 29%

profile of v4, /device:TPU:0, one launch (start us, length us, event | category | flops | bytes accessed | tf_op | source)
XLA Modules:
  0.0 251.4 jit_solution(5966811048582467517)
XLA Ops:
  4.0 3.1 %collective-permute-start = (bf16[256,1024]{1,0:T(8,128)(2,1)S(1)}, bf16[256,1024]{1,0:T(8,128)(2,1)S(1)}, u32[]{:S(2)}, u32[]{:S(2)}) collective-permute-start(bf16[256,1024]{1,0:T(8,128)(2,1)S(1)} %shard_map.203.own_ref), channel_id=1, source_target_pairs={{0,1},{1,0},{2,3},{3,2},{4,5},{5,4},{6,7},{7,6},{8,9},{9,8},{10,11... | collective-permute-start | bytes 1572872 | tf_op jit(solution)/shard_map/ppermute | solution.py:923
  7.2 1.4 maximum_maximum_fusion.ssm_ref.own_ref
  8.6 3.0 %shard_map.204 = (bf16[176,1024]{1,0:T(8,128)(2,1)}, bf16[256,1024]{1,0:T(8,128)(2,1)}) custom-call(s32[6]{0:T(128)} %copy-done.6, bf16[3,1024,256]{2,1,0:T(8,128)(2,1)} %bitcast.66, bf16[256,1024]{1,0:T(8,128)(2,1)} %out_near_ref.3, bf16[1024,1024]{1,0:T(8,128)(2,1)} %up0_ref.3, bf16[1024,1024]{1,0:T(8,128)(2,1)} %down0_ref.3, ...), custom_call_target="tpu_custom_call" | custom-call | tf_op jit(solution)/shard_map/pallas_call | solution.py:115
  11.6 2.7 %collective-permute-start.1 = (bf16[176,1024]{1,0:T(8,128)(2,1)}, bf16[176,1024]{1,0:T(8,128)(2,1)S(1)}, u32[]{:S(2)}, u32[]{:S(2)}) collective-permute-start(bf16[176,1024]{1,0:T(8,128)(2,1)} %get-tuple-element.145), channel_id=1, source_target_pairs={{0,2},{1,3},{2,0},{3,1},{4,6},{5,7},{6,4},{7,5},{8,10},{9,11},{10,... | collective-permute-start | bytes 1081352 | tf_op jit(solution)/shard_map/ppermute | solution.py:923
  14.6 15.9 %collective-permute-done.1.across_ref = bf16[176,1024]{1,0:T(8,128)(2,1)S(1)} collective-permute-done((bf16[176,1024]{1,0:T(8,128)(2,1)}, bf16[176,1024]{1,0:T(8,128)(2,1)S(1)}, u32[]{:S(2)}, u32[]{:S(2)}) %collective-permute-start.1) | collective-permute-done | bytes 360480 | tf_op jit(solution)/shard_map/ppermute | solution.py:923
  30.5 1.6 collective-permute-start.2
  32.6 1.6 collective-permute-start.3
  34.2 5.1 %shard_map.206 = (bf16[2,256,1024]{2,1,0:T(8,128)(2,1)S(1)}, bf16[2,256,1024]{2,1,0:T(8,128)(2,1)S(1)}, f32[128,512]{1,0:T(8,128)S(1)}, bf16[224,512]{1,0:T(8,128)(2,1)S(1)}) custom-call(s32[6]{0:T(128)S(1)} %copy-done.7, bf16[256,1024]{1,0:T(8,128)(2,1)S(1)} %shard_map.203.own_ref, bf16[256,1024]{1,0:T(8,128)(2,1)S(1)} %collective-permute-done.other_ref, ...), custom_call_target="tpu_custom_call" | custom-call | tf_op jit(solution)/shard_map/pallas_call | solution.py:46
  39.9 3.0 %collective-permute-start.8 = (bf16[256,1024]{1,0:T(8,128)(2,1)S(1)}, bf16[256,1024]{1,0:T(8,128)(2,1)S(1)}, u32[]{:S(2)}, u32[]{:S(2)}) collective-permute-start(bf16[256,1024]{1,0:T(8,128)(2,1)S(1)} %copy-done.13), channel_id=1, source_target_pairs={{0,2},{1,3},{2,0},{3,1},{4,6},{5,7},{6,4},{7,5},{8,10},{9,11},{10,... | collective-permute-start | bytes 1572872 | tf_op jit(solution)/shard_map/ppermute | solution.py:923
  42.9 1.5 shard_map.207.qkv_ref.near_ref
  44.5 1.2 collective-permute-done.5.d_ref
  46.4 5.1 %collective-permute-start.7 = (bf16[224,512]{1,0:T(8,128)(2,1)S(1)}, bf16[224,512]{1,0:T(8,128)(2,1)S(1)}, u32[]{:S(2)}, u32[]{:S(2)}) collective-permute-start(bf16[224,512]{1,0:T(8,128)(2,1)S(1)} %get-tuple-element.156), channel_id=1, source_target_pairs={{0,2},{1,3},{4,6},{5,7},{8,10},{9,11},{12,14},{13,15},{16,18},{17,... | collective-permute-start | bytes 688136 | tf_op jit(solution)/shard_map/ppermute | solution.py:991
  51.5 12.3 %collective-permute-done.8.value_ref = bf16[256,1024]{1,0:T(8,128)(2,1)S(1)} collective-permute-done((bf16[256,1024]{1,0:T(8,128)(2,1)S(1)}, bf16[256,1024]{1,0:T(8,128)(2,1)S(1)}, u32[]{:S(2)}, u32[]{:S(2)}) %collective-permute-start.8) | collective-permute-done | bytes 524320 | tf_op jit(solution)/shard_map/ppermute | solution.py:923
  64.4 1.6 collective-permute-start.11
  66.5 1.5 shard_map.210
  68.0 1.9 shard_map.211.near_ref
  69.9 1.7 shard_map.212
  71.6 2.6 %shard_map.213 = (bf16[2,256,256]{2,1,0:T(8,128)(2,1)S(1)}, f32[256,1024]{1,0:T(8,128)S(1)}, bf16[256,1024]{1,0:T(8,128)(2,1)S(1)}) custom-call(s32[6]{0:T(128)S(1)} %copy-done.7, bf16[2,256,768]{2,1,0:T(8,128)(2,1)S(1)} %get-tuple-element.176.qkv_ref.far_ref, bf16[128,512]{1,0:T(8,128)(2,1)S(1)} %get-tuple-element.168.first_ref, ...), custom_call_target="tpu_custom_call" | custom-call | tf_op jit(solution)/shard_map/pallas_call | solution.py:46
  74.2 6.8 %collective-permute-start.9 = (bf16[256,1024]{1,0:T(8,128)(2,1)S(1)}, bf16[256,1024]{1,0:T(8,128)(2,1)S(1)}, u32[]{:S(2)}, u32[]{:S(2)}) collective-permute-start(bf16[256,1024]{1,0:T(8,128)(2,1)S(1)} %get-tuple-element.178), channel_id=1, source_target_pairs={{0,1},{1,0},{2,3},{3,2},{4,5},{5,4},{6,7},{7,6},{8,9},{9,8},{10,11... | collective-permute-start | bytes 1572872 | tf_op jit(solution)/shard_map/ppermute | solution.py:923
  81.6 1.6 collective-permute-start.14
  83.7 7.2 %collective-permute-done.9.received_ref = bf16[256,1024]{1,0:T(8,128)(2,1)S(1)} collective-permute-done((bf16[256,1024]{1,0:T(8,128)(2,1)S(1)}, bf16[256,1024]{1,0:T(8,128)(2,1)S(1)}, u32[]{:S(2)}, u32[]{:S(2)}) %collective-permute-start.9) | collective-permute-done | bytes 524320 | tf_op jit(solution)/shard_map/ppermute | solution.py:923
  91.9 1.2 collective-permute-done.14.bx_ref
  94.5 13.9 %collective-permute-done.12.rows_ref.n_ref = bf16[256,1024]{1,0:T(8,128)(2,1)S(1)} collective-permute-done((bf16[256,1024]{1,0:T(8,128)(2,1)S(1)}, bf16[256,1024]{1,0:T(8,128)(2,1)S(1)}, u32[]{:S(2)}, u32[]{:S(2)}) %collective-permute-start.12) | collective-permute-done | bytes 524320 | tf_op jit(solution)/shard_map/ppermute | solution.py:923
  109.8 6.8 %shard_map.219 = (bf16[256,2048]{1,0:T(8,128)(2,1)S(1)}, bf16[256,2048]{1,0:T(8,128)(2,1)S(1)}, bf16[256,1024]{1,0:T(8,128)(2,1)S(1)}, bf16[256,1024]{1,0:T(8,128)(2,1)S(1)}, bf16[256,1024]{1,0:T(8,128)(2,1)S(1)}) custom-call(s32[6]{0:T(128)S(1)} %copy-done.7, bf16[256,1024]{1,0:T(8,128)(2,1)S(1)} %collective-permute-done.12.rows_ref.n_ref, ...), custom_call_target="tpu_custom_call" | custom-call | tf_op jit(solution)/shard_map/pallas_call | solution.py:607
  117.1 7.1 %shard_map.220 = (bf16[256,2048]{1,0:T(8,128)(2,1)S(1)}, bf16[256,2048]{1,0:T(8,128)(2,1)S(1)}, bf16[256,1024]{1,0:T(8,128)(2,1)S(1)}, f32[256,1024]{1,0:T(8,128)S(1)}, f32[256,1024]{1,0:T(8,128)S(1)}) custom-call(s32[6]{0:T(128)S(1)} %copy-done.7, bf16[256,1024]{1,0:T(8,128)(2,1)S(1)} %get-tuple-element.199.n_ref, bf16[256,1024]{1,0:T(8,128)(2,1)S(1)} %bitcast.55, ...), custom_call_target="tpu_custom_call" | custom-call | tf_op jit(solution)/shard_map/pallas_call | solution.py:607
  124.2 1.8 shard_map.221
  126.1 1.8 shard_map.222
  128.5 1.7 collective-permute-done.16.received_ref
  130.2 1.4 shard_map.223
  132.2 1.8 shard_map.224
  134.0 1.5 collective-permute-start.23
  135.5 1.9 shard_map.225
  137.4 1.6 collective-permute-start.22
  139.0 5.2 %collective-permute-done.17.other_ref = bf16[256,1024]{1,0:T(8,128)(2,1)S(1)} collective-permute-done((bf16[256,1024]{1,0:T(8,128)(2,1)S(1)}, bf16[256,1024]{1,0:T(8,128)(2,1)S(1)}, u32[]{:S(2)}, u32[]{:S(2)}) %collective-permute-start.17) | collective-permute-done | bytes 524320 | tf_op jit(solution)/shard_map/ppermute | solution.py:923
  144.2 1.4 shard_map.226
  145.6 5.4 %shard_map.227 = (bf16[2,256,1536]{2,1,0:T(8,128)(2,1)S(1)}, f32[128,512]{1,0:T(8,128)S(1)}, bf16[176,512]{1,0:T(8,128)(2,1)S(1)}) custom-call(s32[6]{0:T(128)S(1)} %copy-done.7, bf16[2,256,768]{2,1,0:T(8,128)(2,1)S(1)} %shard_map.207.qkv_ref.near_ref, bf16[2,256,768]{2,1,0:T(8,128)(2,1)S(1)} %get-tuple-element.176.qkv_ref.far_ref, ...), custom_call_target="tpu_custom_call" | custom-call | tf_op jit(solution)/shard_map/pallas_call | solution.py:46
  151.0 1.6 collective-permute-start.21
  152.6 2.4 shard_map.228.total_ref
  155.0 1.3 collective-permute-start.20
  156.4 1.8 shard_map.229
  159.1 1.6 collective-permute-start.25
  163.0 5.1 %shard_map.232 = (f32[256,1024]{1,0:T(8,128)S(1)}, bf16[256,1024]{1,0:T(8,128)(2,1)S(1)}, f32[128,512]{1,0:T(8,128)S(1)}) custom-call(s32[6]{0:T(128)S(1)} %copy-done.7, f32[128,512]{1,0:T(8,128)S(1)} %get-tuple-element.222.near_ref, bf16[176,512]{1,0:T(8,128)(2,1)S(1)} %collective-permute-done.21.returned_ref, f32[16,512]{1,0:T(8,128)S(1)} %get-tuple-element.291.rate_ref, ...), custom_call_target="tpu_custom_call" | custom-call | flops 30000001024 | tf_op jit(solution)/shard_map/pallas_call | solution.py:46
  168.1 1.4 collective-permute-start.24
  169.5 1.5 shard_map.233
  170.9 1.9 shard_map.234
  172.8 2.8 %collective-permute-done.27.up_received = bf16[128,2048]{1,0:T(8,128)(2,1)S(1)} collective-permute-done((bf16[128,2048]{1,0:T(8,128)(2,1)S(1)}, bf16[128,2048]{1,0:T(8,128)(2,1)S(1)}, u32[]{:S(2)}, u32[]{:S(2)}) %collective-permute-start.27) | collective-permute-done | bytes 524320 | tf_op jit(solution)/shard_map/ppermute | solution.py:926
  176.3 3.6 %collective-permute-start.32 = (bf16[128,2048]{1,0:T(8,128)(2,1)S(1)}, bf16[128,2048]{1,0:T(8,128)(2,1)S(1)}, u32[]{:S(2)}, u32[]{:S(2)}) collective-permute-start(bf16[128,2048]{1,0:T(8,128)(2,1)S(1)} %get-tuple-element.246), channel_id=1, source_target_pairs={{0,2},{1,3},{2,0},{3,1},{4,6},{5,7},{6,4},{7,5},{8,10},{9,11},{10,... | collective-permute-start | bytes 1572872 | tf_op jit(solution)/shard_map/ppermute | solution.py:923
  180.3 1.5 collective-permute-start.29
  181.8 1.5 collective-permute-start.30
  183.4 4.3 %shard_map.236.param_ref = f32[40,512]{1,0:T(8,128)S(1)} custom-call(s32[6]{0:T(128)S(1)} %copy-done.7, bf16[2,256,1024]{2,1,0:T(8,128)(2,1)S(1)} %get-tuple-element.247.tile_ref, f32[128,512]{1,0:T(8,128)S(1)} %get-tuple-element.222.near_ref, f32[128,512]{1,0:T(8,128)S(1)} %get-tuple-element.236.last_ref, f32[2,16,512]{2,1,0:T(8,128)S(1)} %get-tuple-element.170.enter_ref, ...), custom_call_target="tpu_custom_call" | custom-call | flops 3000000000 | tf_op jit(solution)/shard_map/pallas_call | solution.py:46
  187.6 2.4 shard_map.237
  190.8 11.0 %collective-permute-done.32.b_ref = bf16[128,2048]{1,0:T(8,128)(2,1)S(1)} collective-permute-done((bf16[128,2048]{1,0:T(8,128)(2,1)S(1)}, bf16[128,2048]{1,0:T(8,128)(2,1)S(1)}, u32[]{:S(2)}, u32[]{:S(2)}) %collective-permute-start.32) | collective-permute-done | bytes 524320 | tf_op jit(solution)/shard_map/ppermute | solution.py:923
  203.1 1.7 collective-permute-start.34
  206.3 4.3 %collective-permute-done.35.by_ref = bf16[128,1024]{1,0:T(8,128)(2,1)S(1)} collective-permute-done((bf16[128,1024]{1,0:T(8,128)(2,1)S(1)}, bf16[128,1024]{1,0:T(8,128)(2,1)S(1)}, u32[]{:S(2)}, u32[]{:S(2)}) %collective-permute-start.35) | collective-permute-done | bytes 262176 | tf_op jit(solution)/shard_map/ppermute | solution.py:926
  211.2 1.8 collective-permute-start.41
  213.0 1.3 collective-permute-start.40
  214.2 6.1 %collective-permute-done.33.b_ref = bf16[144,1024]{1,0:T(8,128)(2,1)S(1)} collective-permute-done((bf16[144,1024]{1,0:T(8,128)(2,1)S(1)}, bf16[144,1024]{1,0:T(8,128)(2,1)S(1)}, u32[]{:S(2)}, u32[]{:S(2)}) %collective-permute-start.33) | collective-permute-done | bytes 294944 | tf_op jit(solution)/shard_map/ppermute | solution.py:923
  221.7 1.3 collective-permute-start.37
  223.0 1.5 collective-permute-start.38
  224.5 6.4 %collective-permute-done.36.b_ref = bf16[144,1024]{1,0:T(8,128)(2,1)S(1)} collective-permute-done((bf16[144,1024]{1,0:T(8,128)(2,1)S(1)}, bf16[144,1024]{1,0:T(8,128)(2,1)S(1)}, u32[]{:S(2)}, u32[]{:S(2)}) %collective-permute-start.36) | collective-permute-done | bytes 294944 | tf_op jit(solution)/shard_map/ppermute | solution.py:926
  230.9 6.6 %collective-permute-done.37.c_ref = bf16[144,1024]{1,0:T(8,128)(2,1)S(1)} collective-permute-done((bf16[144,1024]{1,0:T(8,128)(2,1)S(1)}, bf16[144,1024]{1,0:T(8,128)(2,1)S(1)}, u32[]{:S(2)}, u32[]{:S(2)}) %collective-permute-start.37) | collective-permute-done | bytes 294944 | tf_op jit(solution)/shard_map/ppermute | solution.py:926
  239.5 1.6 collective-permute-done.39.odd_ref
  241.1 2.9 %shard_map.244 = (f32[3,1024,256]{2,1,0:T(8,128)}, f32[256,1024]{1,0:T(8,128)}, f32[48,256]{1,0:T(8,128)S(1)}) custom-call(s32[6]{0:T(128)S(1)} %copy-done.7, bf16[4,144,1024]{2,1,0:T(8,128)(2,1)S(1)} %shard_map.242.even_ref, bf16[4,144,1024]{2,1,0:T(8,128)(2,1)S(1)} %collective-permute-done.39.odd_ref), custom_call_target="tpu_custom_call" | custom-call | flops 6000000000 | tf_op jit(solution)/shard_map/pallas_call | solution.py:46
  246.4 5.0 %shard_map.245 = (f32[1024,1024]{1,0:T(8,128)}, f32[1024,1024]{1,0:T(8,128)}) custom-call(s32[6]{0:T(128)S(1)} %copy-done.7, bf16[4,2,128,1024]{3,2,1,0:T(8,128)(2,1)S(1)} %shard_map.243.even_ref, bf16[4,2,128,1024]{3,2,1,0:T(8,128)(2,1)S(1)} %collective-permute-done.42.odd_ref), custom_call_target="tpu_custom_call" | custom-call | tf_op jit(solution)/shard_map/pallas_call | solution.py:877
  (114 shorter events, 26.8 us)
Async XLA Ops:
  1.4 7.3 %copy-start.6 = (s32[6]{0:T(128)}, s32[6]{0:T(128)S(1)}, u32[]{:S(2)}) copy-start(s32[6]{0:T(128)S(1)} %stack.24.flag_ref) | copy-start | bytes 76
  1.4 1.0 copy-start.4
  2.4 0.7 copy-start.9
  4.0 26.4 %collective-permute-start = (bf16[256,1024]{1,0:T(8,128)(2,1)S(1)}, bf16[256,1024]{1,0:T(8,128)(2,1)S(1)}, u32[]{:S(2)}, u32[]{:S(2)}) collective-permute-start(bf16[256,1024]{1,0:T(8,128)(2,1)S(1)} %shard_map.203.own_ref), channel_id=1, source_target_pairs={{0,1},{1,0},{2,3},{3,2},{4,5},{5,4},{6,7},{7,6},{8,9},{9,8},{10,11... | collective-permute-start | bytes 1572872 | tf_op jit(solution)/shard_map/ppermute | solution.py:923
  8.6 5.6 %copy-start.12 = (bf16[1024,3,256]{2,0,1:T(8,128)(2,1)S(1)}, bf16[1024,3,256]{2,0,1:T(8,128)(2,1)}, u32[]{:S(2)}) copy-start(bf16[1024,3,256]{2,0,1:T(8,128)(2,1)} %param.15) | copy-start | bytes 4718596
  11.6 18.8 %collective-permute-start.1 = (bf16[176,1024]{1,0:T(8,128)(2,1)}, bf16[176,1024]{1,0:T(8,128)(2,1)S(1)}, u32[]{:S(2)}, u32[]{:S(2)}) collective-permute-start(bf16[176,1024]{1,0:T(8,128)(2,1)} %get-tuple-element.145), channel_id=1, source_target_pairs={{0,2},{1,3},{2,0},{3,1},{4,6},{5,7},{6,4},{7,5},{8,10},{9,11},{10,... | collective-permute-start | bytes 1081352 | tf_op jit(solution)/shard_map/ppermute | solution.py:923
  14.4 17.7 %copy-start.2 = (bf16[1,256,1024]{2,1,0:T(8,128)(2,1)S(1)}, bf16[1,256,1024]{2,1,0:T(8,128)(2,1)}, u32[]{:S(2)}) copy-start(bf16[1,256,1024]{2,1,0:T(8,128)(2,1)} %param.23) | copy-start | bytes 1572868
  14.4 17.7 %copy-start.7 = (s32[6]{0:T(128)S(1)}, s32[6]{0:T(128)}, u32[]{:S(2)}) copy-start(s32[6]{0:T(128)} %copy-done.6) | copy-start | bytes 76
  14.4 17.7 %copy-start.8 = (f32[48,256]{1,0:T(8,128)S(1)}, f32[48,256]{1,0:T(8,128)}, u32[]{:S(2)}) copy-start(f32[48,256]{1,0:T(8,128)} %maximum_maximum_fusion.ssm_ref.own_ref) | copy-start | bytes 147460
  14.5 25.4 %copy-start.13 = (bf16[256,1024]{1,0:T(8,128)(2,1)S(1)}, bf16[256,1024]{1,0:T(8,128)(2,1)}, u32[]{:S(2)}) copy-start(bf16[256,1024]{1,0:T(8,128)(2,1)} %get-tuple-element.163) | copy-start | bytes 1572868
  30.5 8.8 %collective-permute-start.2 = (bf16[128,1024]{1,0:T(8,128)(2,1)S(1)}, bf16[128,1024]{1,0:T(8,128)(2,1)S(1)}, u32[]{:S(2)}, u32[]{:S(2)}) collective-permute-start(bf16[128,1024]{1,0:T(8,128)(2,1)S(1)} %slice.74.a_ref), channel_id=1, source_target_pairs={{0,8},{4,12},{8,0},{12,4},{16,24},{20,28},{24,16},{28,20},{1,9},{5... | collective-permute-start | bytes 786440 | tf_op jit(solution)/shard_map/ppermute | solution.py:926
  32.0 12.5 %collective-permute-start.4 = (bf16[256,1024]{1,0:T(8,128)(2,1)S(1)}, bf16[256,1024]{1,0:T(8,128)(2,1)S(1)}, u32[]{:S(2)}, u32[]{:S(2)}) collective-permute-start(bf16[256,1024]{1,0:T(8,128)(2,1)S(1)} %bitcast.53), channel_id=1, source_target_pairs={{0,1},{1,0},{2,3},{3,2},{4,5},{5,4},{6,7},{7,6},{8,9},{9,8},{10,11... | collective-permute-start | bytes 1572872 | tf_op jit(solution)/shard_map/ppermute | solution.py:923
  32.6 11.8 %collective-permute-start.3 = (bf16[128,1024]{1,0:T(8,128)(2,1)S(1)}, bf16[128,1024]{1,0:T(8,128)(2,1)S(1)}, u32[]{:S(2)}, u32[]{:S(2)}) collective-permute-start(bf16[128,1024]{1,0:T(8,128)(2,1)S(1)} %slice.74.a_ref), channel_id=1, source_target_pairs={{0,16},{4,20},{8,24},{12,28},{16,0},{20,4},{24,8},{28,12},{1,17},{... | collective-permute-start | bytes 786440 | tf_op jit(solution)/shard_map/ppermute | solution.py:926
  39.3 6.4 %collective-permute-start.5 = (bf16[128,1024]{1,0:T(8,128)(2,1)S(1)}, bf16[128,1024]{1,0:T(8,128)(2,1)S(1)}, u32[]{:S(2)}, u32[]{:S(2)}) collective-permute-start(bf16[128,1024]{1,0:T(8,128)(2,1)S(1)} %collective-permute-done.2.b_ref), channel_id=1, source_target_pairs={{0,16},{4,20},{8,24},{12,28},{16,0},{20,4},{24,8},{28,12},{1,17},{... | collective-permute-start | bytes 786440 | tf_op jit(solution)/shard_map/ppermute | solution.py:926
  39.9 23.9 %collective-permute-start.8 = (bf16[256,1024]{1,0:T(8,128)(2,1)S(1)}, bf16[256,1024]{1,0:T(8,128)(2,1)S(1)}, u32[]{:S(2)}, u32[]{:S(2)}) collective-permute-start(bf16[256,1024]{1,0:T(8,128)(2,1)S(1)} %copy-done.13), channel_id=1, source_target_pairs={{0,2},{1,3},{2,0},{3,1},{4,6},{5,7},{6,4},{7,5},{8,10},{9,11},{10,... | collective-permute-start | bytes 1572872 | tf_op jit(solution)/shard_map/ppermute | solution.py:923
  46.4 23.6 %collective-permute-start.6 = (bf16[4,128,1024]{2,1,0:T(8,128)(2,1)S(1)}, bf16[4,128,1024]{2,1,0:T(8,128)(2,1)S(1)}, u32[]{:S(2)}, u32[]{:S(2)}) collective-permute-start(bf16[4,128,1024]{2,1,0:T(8,128)(2,1)S(1)} %shard_map.208.even_ref), channel_id=1, source_target_pairs={{0,4},{4,0},{8,12},{12,8},{16,20},{20,16},{24,28},{28,24},{1,5},{5... | collective-permute-start | bytes 3145736 | tf_op jit(solution)/shard_map/ppermute | solution.py:926
  46.4 20.1 %collective-permute-start.7 = (bf16[224,512]{1,0:T(8,128)(2,1)S(1)}, bf16[224,512]{1,0:T(8,128)(2,1)S(1)}, u32[]{:S(2)}, u32[]{:S(2)}) collective-permute-start(bf16[224,512]{1,0:T(8,128)(2,1)S(1)} %get-tuple-element.156), channel_id=1, source_target_pairs={{0,2},{1,3},{4,6},{5,7},{8,10},{9,11},{12,14},{13,15},{16,18},{17,... | collective-permute-start | bytes 688136 | tf_op jit(solution)/shard_map/ppermute | solution.py:991
  64.4 16.6 %collective-permute-start.11 = (bf16[128,1024]{1,0:T(8,128)(2,1)S(1)}, bf16[128,1024]{1,0:T(8,128)(2,1)S(1)}, u32[]{:S(2)}, u32[]{:S(2)}) collective-permute-start(bf16[128,1024]{1,0:T(8,128)(2,1)S(1)} %get-tuple-element.166.b_ref), channel_id=1, source_target_pairs={{0,16},{4,20},{8,24},{12,28},{16,0},{20,4},{24,8},{28,12},{1,17},{... | collective-permute-start | bytes 786440 | tf_op jit(solution)/shard_map/ppermute | solution.py:926
  66.0 15.0 %collective-permute-start.10 = (bf16[128,1024]{1,0:T(8,128)(2,1)S(1)}, bf16[128,1024]{1,0:T(8,128)(2,1)S(1)}, u32[]{:S(2)}, u32[]{:S(2)}) collective-permute-start(bf16[128,1024]{1,0:T(8,128)(2,1)S(1)} %get-tuple-element.165.a_ref), channel_id=1, source_target_pairs={{0,8},{4,12},{8,0},{12,4},{16,24},{20,28},{24,16},{28,20},{1,9},{5... | collective-permute-start | bytes 786440 | tf_op jit(solution)/shard_map/ppermute | solution.py:926
  68.0 3.6 %copy-start.3 = (bf16[256,1024]{1,0:T(8,128)(2,1)S(1)}, bf16[256,1024]{1,0:T(8,128)(2,1)}, u32[]{:S(2)}) copy-start(bf16[256,1024]{1,0:T(8,128)(2,1)} %out_near_ref.3) | copy-start | bytes 1572868
  74.2 16.7 %collective-permute-start.9 = (bf16[256,1024]{1,0:T(8,128)(2,1)S(1)}, bf16[256,1024]{1,0:T(8,128)(2,1)S(1)}, u32[]{:S(2)}, u32[]{:S(2)}) collective-permute-start(bf16[256,1024]{1,0:T(8,128)(2,1)S(1)} %get-tuple-element.178), channel_id=1, source_target_pairs={{0,1},{1,0},{2,3},{3,2},{4,5},{5,4},{6,7},{7,6},{8,9},{9,8},{10,11... | collective-permute-start | bytes 1572872 | tf_op jit(solution)/shard_map/ppermute | solution.py:923
  81.0 10.0 %copy-start.5 = (bf16[1,256,1024]{2,1,0:T(8,128)(2,1)S(1)}, bf16[1,256,1024]{2,1,0:T(8,128)(2,1)}, u32[]{:S(2)}) copy-start(bf16[1,256,1024]{2,1,0:T(8,128)(2,1)} %param.12) | copy-start | bytes 1572868
  81.0 10.0 %copy-start.11 = (f32[1024]{0:T(1024)S(1)}, f32[1024]{0:T(1024)}, u32[]{:S(2)}) copy-start(f32[1024]{0:T(1024)} %param.20) | copy-start | bytes 12292
  81.6 11.5 %collective-permute-start.14 = (bf16[2,128,1024]{2,1,0:T(8,128)(2,1)S(1)}, bf16[2,128,1024]{2,1,0:T(8,128)(2,1)S(1)}, u32[]{:S(2)}, u32[]{:S(2)}) collective-permute-start(bf16[2,128,1024]{2,1,0:T(8,128)(2,1)S(1)} %get-tuple-element.183.b_ref), channel_id=1, source_target_pairs={{0,8},{4,12},{8,0},{12,4},{16,24},{20,28},{24,16},{28,20},{1,9},{5... | collective-permute-start | bytes 1572872 | tf_op jit(solution)/shard_map/ppermute | solution.py:926
  83.1 10.1 %collective-permute-start.13 = (bf16[2,128,1024]{2,1,0:T(8,128)(2,1)S(1)}, bf16[2,128,1024]{2,1,0:T(8,128)(2,1)S(1)}, u32[]{:S(2)}, u32[]{:S(2)}) collective-permute-start(bf16[2,128,1024]{2,1,0:T(8,128)(2,1)S(1)} %get-tuple-element.182.a_ref), channel_id=1, source_target_pairs={{0,16},{4,20},{8,24},{12,28},{16,0},{20,4},{24,8},{28,12},{1,17},{... | collective-permute-start | bytes 1572872 | tf_op jit(solution)/shard_map/ppermute | solution.py:926
  93.1 15.3 %copy-start = (bf16[1024,1024]{1,0:T(8,128)(2,1)S(1)}, bf16[1024,1024]{1,0:T(8,128)(2,1)}, u32[]{:S(2)}) copy-start(bf16[1024,1024]{1,0:T(8,128)(2,1)} %up0_ref.3) | copy-start | bytes 6291460
  93.1 15.3 %copy-start.1 = (bf16[1024,1024]{1,0:T(8,128)(2,1)S(1)}, bf16[1024,1024]{1,0:T(8,128)(2,1)}, u32[]{:S(2)}) copy-start(bf16[1024,1024]{1,0:T(8,128)(2,1)} %down0_ref.3) | copy-start | bytes 6291460
  94.0 15.0 %collective-permute-start.15 = (bf16[4,2,128,1024]{3,2,1,0:T(8,128)(2,1)S(1)}, bf16[4,2,128,1024]{3,2,1,0:T(8,128)(2,1)S(1)}, u32[]{:S(2)}, u32[]{:S(2)}) collective-permute-start(bf16[4,2,128,1024]{3,2,1,0:T(8,128)(2,1)S(1)} %shard_map.216.even_ref), channel_id=1, source_target_pairs={{0,4},{4,0},{8,12},{12,8},{16,20},{20,16},{24,28},{28,24},{1,5},{5... | collective-permute-start | bytes 6291464 | tf_op jit(solution)/shard_map/ppermute | solution.py:926
  94.1 14.3 %collective-permute-start.12 = (bf16[256,1024]{1,0:T(8,128)(2,1)S(1)}, bf16[256,1024]{1,0:T(8,128)(2,1)S(1)}, u32[]{:S(2)}, u32[]{:S(2)}) collective-permute-start(bf16[256,1024]{1,0:T(8,128)(2,1)S(1)} %get-tuple-element.199.n_ref), channel_id=1, source_target_pairs={{0,1},{1,0},{2,3},{3,2},{4,5},{5,4},{6,7},{7,6},{8,9},{9,8},{10,11... | collective-permute-start | bytes 1572872 | tf_op jit(solution)/shard_map/ppermute | solution.py:923
  116.7 13.5 %collective-permute-start.16 = (bf16[256,1024]{1,0:T(8,128)(2,1)S(1)}, bf16[256,1024]{1,0:T(8,128)(2,1)S(1)}, u32[]{:S(2)}, u32[]{:S(2)}) collective-permute-start(bf16[256,1024]{1,0:T(8,128)(2,1)S(1)} %get-tuple-element.198), channel_id=1, source_target_pairs={{0,1},{1,0},{2,3},{3,2},{4,5},{5,4},{6,7},{7,6},{8,9},{9,8},{10,11... | collective-permute-start | bytes 1572872 | tf_op jit(solution)/shard_map/ppermute | solution.py:923
  126.0 6.1 %collective-permute-start.19 = (bf16[1024,1024]{1,0:T(8,128)(2,1)S(1)}, bf16[1024,1024]{1,0:T(8,128)(2,1)S(1)}, u32[]{:S(2)}, u32[]{:S(2)}) collective-permute-start(bf16[1024,1024]{1,0:T(8,128)(2,1)S(1)} %shard_map.221), channel_id=1, source_target_pairs={{0,4},{4,0},{8,12},{12,8},{16,20},{20,16},{24,28},{28,24},{1,5},{5... | collective-permute-start | bytes 6291464 | tf_op jit(solution)/shard_map/ppermute | solution.py:926
  127.9 7.6 %collective-permute-start.18 = (bf16[512,2048]{1,0:T(8,128)(2,1)S(1)}, bf16[512,2048]{1,0:T(8,128)(2,1)S(1)}, u32[]{:S(2)}, u32[]{:S(2)}) collective-permute-start(bf16[512,2048]{1,0:T(8,128)(2,1)S(1)} %shard_map.222), channel_id=1, source_target_pairs={{0,4},{4,0},{8,12},{12,8},{16,20},{20,16},{24,28},{28,24},{1,5},{5... | collective-permute-start | bytes 6291464 | tf_op jit(solution)/shard_map/ppermute | solution.py:926
  131.6 12.6 %collective-permute-start.17 = (bf16[256,1024]{1,0:T(8,128)(2,1)S(1)}, bf16[256,1024]{1,0:T(8,128)(2,1)S(1)}, u32[]{:S(2)}, u32[]{:S(2)}) collective-permute-start(bf16[256,1024]{1,0:T(8,128)(2,1)S(1)} %get-tuple-element.208.own_ref), channel_id=1, source_target_pairs={{0,1},{1,0},{2,3},{3,2},{4,5},{5,4},{6,7},{7,6},{8,9},{9,8},{10,11... | collective-permute-start | bytes 1572872 | tf_op jit(solution)/shard_map/ppermute | solution.py:923
  134.0 24.4 %collective-permute-start.23 = (bf16[512,1024]{1,0:T(8,128)(2,1)S(1)}, bf16[512,1024]{1,0:T(8,128)(2,1)S(1)}, u32[]{:S(2)}, u32[]{:S(2)}) collective-permute-start(bf16[512,1024]{1,0:T(8,128)(2,1)S(1)} %get-tuple-element.212), channel_id=1, source_target_pairs={{0,8},{4,12},{8,0},{12,4},{16,24},{20,28},{24,16},{28,20},{1,9},{5... | collective-permute-start | bytes 3145736 | tf_op jit(solution)/shard_map/ppermute | solution.py:926
  137.4 24.2 %collective-permute-start.22 = (bf16[256,2048]{1,0:T(8,128)(2,1)S(1)}, bf16[256,2048]{1,0:T(8,128)(2,1)S(1)}, u32[]{:S(2)}, u32[]{:S(2)}) collective-permute-start(bf16[256,2048]{1,0:T(8,128)(2,1)S(1)} %get-tuple-element.215), channel_id=1, source_target_pairs={{0,16},{4,20},{8,24},{12,28},{16,0},{20,4},{24,8},{28,12},{1,17},{... | collective-permute-start | bytes 3145736 | tf_op jit(solution)/shard_map/ppermute | solution.py:926
  151.0 12.0 %collective-permute-start.21 = (bf16[176,512]{1,0:T(8,128)(2,1)S(1)}, bf16[176,512]{1,0:T(8,128)(2,1)S(1)}, u32[]{:S(2)}, u32[]{:S(2)}) collective-permute-start(bf16[176,512]{1,0:T(8,128)(2,1)S(1)} %get-tuple-element.223), channel_id=1, source_target_pairs={{2,0},{3,1},{6,4},{7,5},{10,8},{11,9},{14,12},{15,13},{18,16},{19,... | collective-permute-start | bytes 540680 | tf_op jit(solution)/shard_map/ppermute | solution.py:1124
  155.0 14.5 %collective-permute-start.20 = (bf16[256,1024]{1,0:T(8,128)(2,1)S(1)}, bf16[256,1024]{1,0:T(8,128)(2,1)S(1)}, u32[]{:S(2)}, u32[]{:S(2)}) collective-permute-start(bf16[256,1024]{1,0:T(8,128)(2,1)S(1)} %get-tuple-element.220), channel_id=1, source_target_pairs={{0,1},{1,0},{2,3},{3,2},{4,5},{5,4},{6,7},{7,6},{8,9},{9,8},{10,11... | collective-permute-start | bytes 1572872 | tf_op jit(solution)/shard_map/ppermute | solution.py:923
  158.3 12.6 %collective-permute-start.26 = (bf16[512,2048]{1,0:T(8,128)(2,1)S(1)}, bf16[512,2048]{1,0:T(8,128)(2,1)S(1)}, u32[]{:S(2)}, u32[]{:S(2)}) collective-permute-start(bf16[512,2048]{1,0:T(8,128)(2,1)S(1)} %shard_map.229), channel_id=1, source_target_pairs={{0,4},{4,0},{8,12},{12,8},{16,20},{20,16},{24,28},{28,24},{1,5},{5... | collective-permute-start | bytes 6291464 | tf_op jit(solution)/shard_map/ppermute | solution.py:926
  159.1 16.4 %collective-permute-start.25 = (bf16[256,1024]{1,0:T(8,128)(2,1)S(1)}, bf16[256,1024]{1,0:T(8,128)(2,1)S(1)}, u32[]{:S(2)}, u32[]{:S(2)}) collective-permute-start(bf16[256,1024]{1,0:T(8,128)(2,1)S(1)} %get-tuple-element.229), channel_id=1, source_target_pairs={{0,16},{4,20},{8,24},{12,28},{16,0},{20,4},{24,8},{28,12},{1,17},{... | collective-permute-start | bytes 1572872 | tf_op jit(solution)/shard_map/ppermute | solution.py:926
  162.3 13.2 %collective-permute-start.27 = (bf16[128,2048]{1,0:T(8,128)(2,1)S(1)}, bf16[128,2048]{1,0:T(8,128)(2,1)S(1)}, u32[]{:S(2)}, u32[]{:S(2)}) collective-permute-start(bf16[128,2048]{1,0:T(8,128)(2,1)S(1)} %get-tuple-element.232), channel_id=1, source_target_pairs={{0,8},{4,12},{8,0},{12,4},{16,24},{20,28},{24,16},{28,20},{1,9},{5... | collective-permute-start | bytes 1572872 | tf_op jit(solution)/shard_map/ppermute | solution.py:926
  168.1 19.5 %collective-permute-start.24 = (bf16[256,1024]{1,0:T(8,128)(2,1)S(1)}, bf16[256,1024]{1,0:T(8,128)(2,1)S(1)}, u32[]{:S(2)}, u32[]{:S(2)}) collective-permute-start(bf16[256,1024]{1,0:T(8,128)(2,1)S(1)} %get-tuple-element.235), channel_id=1, source_target_pairs={{0,1},{1,0},{2,3},{3,2},{4,5},{5,4},{6,7},{7,6},{8,9},{9,8},{10,11... | collective-permute-start | bytes 1572872 | tf_op jit(solution)/shard_map/ppermute | solution.py:923
  176.3 25.5 %collective-permute-start.32 = (bf16[128,2048]{1,0:T(8,128)(2,1)S(1)}, bf16[128,2048]{1,0:T(8,128)(2,1)S(1)}, u32[]{:S(2)}, u32[]{:S(2)}) collective-permute-start(bf16[128,2048]{1,0:T(8,128)(2,1)S(1)} %get-tuple-element.246), channel_id=1, source_target_pairs={{0,2},{1,3},{2,0},{3,1},{4,6},{5,7},{6,4},{7,5},{8,10},{9,11},{10,... | collective-permute-start | bytes 1572872 | tf_op jit(solution)/shard_map/ppermute | solution.py:923
  179.9 25.0 %collective-permute-start.28 = (bf16[128,2048]{1,0:T(8,128)(2,1)S(1)}, bf16[128,2048]{1,0:T(8,128)(2,1)S(1)}, u32[]{:S(2)}, u32[]{:S(2)}) collective-permute-start(bf16[128,2048]{1,0:T(8,128)(2,1)S(1)} %get-tuple-element.240), channel_id=1, source_target_pairs={{0,16},{4,20},{8,24},{12,28},{16,0},{20,4},{24,8},{28,12},{1,17},{... | collective-permute-start | bytes 1572872 | tf_op jit(solution)/shard_map/ppermute | solution.py:926
  180.3 24.5 %collective-permute-start.29 = (bf16[128,2048]{1,0:T(8,128)(2,1)S(1)}, bf16[128,2048]{1,0:T(8,128)(2,1)S(1)}, u32[]{:S(2)}, u32[]{:S(2)}) collective-permute-start(bf16[128,2048]{1,0:T(8,128)(2,1)S(1)} %get-tuple-element.241), channel_id=1, source_target_pairs={{0,8},{4,12},{8,0},{12,4},{16,24},{20,28},{24,16},{28,20},{1,9},{5... | collective-permute-start | bytes 1572872 | tf_op jit(solution)/shard_map/ppermute | solution.py:926
  181.8 23.2 %collective-permute-start.30 = (bf16[128,2048]{1,0:T(8,128)(2,1)S(1)}, bf16[128,2048]{1,0:T(8,128)(2,1)S(1)}, u32[]{:S(2)}, u32[]{:S(2)}) collective-permute-start(bf16[128,2048]{1,0:T(8,128)(2,1)S(1)} %get-tuple-element.242), channel_id=1, source_target_pairs={{0,24},{4,28},{8,16},{12,20},{16,8},{20,12},{24,0},{28,4},{1,25},{... | collective-permute-start | bytes 1572872 | tf_op jit(solution)/shard_map/ppermute | solution.py:926
  183.4 4.3 %copy-start.10 = (f32[1024]{0:T(1024)S(1)}, f32[1024]{0:T(1024)}, u32[]{:S(2)}) copy-start(f32[1024]{0:T(1024)} %param.14) | copy-start | bytes 12292
  190.0 13.1 %collective-permute-start.31 = (f32[8,256]{1,0:T(8,128)S(1)}, f32[8,256]{1,0:T(8,128)S(1)}, u32[]{:S(2)}, u32[]{:S(2)}) collective-permute-start(f32[8,256]{1,0:T(8,128)S(1)} %get-tuple-element.250.gains_ref), channel_id=1, source_target_pairs={{0,1},{1,0},{2,3},{3,2},{4,5},{5,4},{6,7},{7,6},{8,9},{9,8},{10,11... | collective-permute-start | bytes 24584 | tf_op jit(solution)/shard_map/ppermute | solution.py:923
  202.4 8.1 %collective-permute-start.35 = (bf16[128,1024]{1,0:T(8,128)(2,1)S(1)}, bf16[128,1024]{1,0:T(8,128)(2,1)S(1)}, u32[]{:S(2)}, u32[]{:S(2)}) collective-permute-start(bf16[128,1024]{1,0:T(8,128)(2,1)S(1)} %get-tuple-element.253.b_ref), channel_id=1, source_target_pairs={{0,16},{4,20},{8,24},{12,28},{16,0},{20,4},{24,8},{28,12},{1,17},{... | collective-permute-start | bytes 786440 | tf_op jit(solution)/shard_map/ppermute | solution.py:926
  203.1 7.4 %collective-permute-start.34 = (bf16[128,1024]{1,0:T(8,128)(2,1)S(1)}, bf16[128,1024]{1,0:T(8,128)(2,1)S(1)}, u32[]{:S(2)}, u32[]{:S(2)}) collective-permute-start(bf16[128,1024]{1,0:T(8,128)(2,1)S(1)} %get-tuple-element.252.a_ref), channel_id=1, source_target_pairs={{0,8},{4,12},{8,0},{12,4},{16,24},{20,28},{24,16},{28,20},{1,9},{5... | collective-permute-start | bytes 786440 | tf_op jit(solution)/shard_map/ppermute | solution.py:926
  205.8 14.6 %collective-permute-start.33 = (bf16[144,1024]{1,0:T(8,128)(2,1)S(1)}, bf16[144,1024]{1,0:T(8,128)(2,1)S(1)}, u32[]{:S(2)}, u32[]{:S(2)}) collective-permute-start(bf16[144,1024]{1,0:T(8,128)(2,1)S(1)} %get-tuple-element.259), channel_id=1, source_target_pairs={{0,2},{1,3},{2,0},{3,1},{4,6},{5,7},{6,4},{7,5},{8,10},{9,11},{10,... | collective-permute-start | bytes 884744 | tf_op jit(solution)/shard_map/ppermute | solution.py:923
  211.2 27.1 %collective-permute-start.41 = (bf16[2,128,1024]{2,1,0:T(8,128)(2,1)S(1)}, bf16[2,128,1024]{2,1,0:T(8,128)(2,1)S(1)}, u32[]{:S(2)}, u32[]{:S(2)}) collective-permute-start(bf16[2,128,1024]{2,1,0:T(8,128)(2,1)S(1)} %get-tuple-element.263.b_ref), channel_id=1, source_target_pairs={{0,8},{4,12},{8,0},{12,4},{16,24},{20,28},{24,16},{28,20},{1,9},{5... | collective-permute-start | bytes 1572872 | tf_op jit(solution)/shard_map/ppermute | solution.py:926
  213.0 25.3 %collective-permute-start.40 = (bf16[2,128,1024]{2,1,0:T(8,128)(2,1)S(1)}, bf16[2,128,1024]{2,1,0:T(8,128)(2,1)S(1)}, u32[]{:S(2)}, u32[]{:S(2)}) collective-permute-start(bf16[2,128,1024]{2,1,0:T(8,128)(2,1)S(1)} %get-tuple-element.262.a_ref), channel_id=1, source_target_pairs={{0,16},{4,20},{8,24},{12,28},{16,0},{20,4},{24,8},{28,12},{1,17},{... | collective-permute-start | bytes 1572872 | tf_op jit(solution)/shard_map/ppermute | solution.py:926
  221.0 9.9 %collective-permute-start.36 = (bf16[144,1024]{1,0:T(8,128)(2,1)S(1)}, bf16[144,1024]{1,0:T(8,128)(2,1)S(1)}, u32[]{:S(2)}, u32[]{:S(2)}) collective-permute-start(bf16[144,1024]{1,0:T(8,128)(2,1)S(1)} %shard_map.241.a_ref), channel_id=1, source_target_pairs={{0,8},{4,12},{8,0},{12,4},{16,24},{20,28},{24,16},{28,20},{1,9},{5... | collective-permute-start | bytes 884744 | tf_op jit(solution)/shard_map/ppermute | solution.py:926
  221.7 15.9 %collective-permute-start.37 = (bf16[144,1024]{1,0:T(8,128)(2,1)S(1)}, bf16[144,1024]{1,0:T(8,128)(2,1)S(1)}, u32[]{:S(2)}, u32[]{:S(2)}) collective-permute-start(bf16[144,1024]{1,0:T(8,128)(2,1)S(1)} %shard_map.241.a_ref), channel_id=1, source_target_pairs={{0,16},{4,20},{8,24},{12,28},{16,0},{20,4},{24,8},{28,12},{1,17},{... | collective-permute-start | bytes 884744 | tf_op jit(solution)/shard_map/ppermute | solution.py:926
  223.0 14.5 %collective-permute-start.38 = (bf16[144,1024]{1,0:T(8,128)(2,1)S(1)}, bf16[144,1024]{1,0:T(8,128)(2,1)S(1)}, u32[]{:S(2)}, u32[]{:S(2)}) collective-permute-start(bf16[144,1024]{1,0:T(8,128)(2,1)S(1)} %shard_map.241.a_ref), channel_id=1, source_target_pairs={{0,24},{4,28},{8,16},{12,20},{16,8},{20,12},{24,0},{28,4},{1,25},{... | collective-permute-start | bytes 884744 | tf_op jit(solution)/shard_map/ppermute | solution.py:926
  238.2 2.9 %collective-permute-start.39 = (bf16[4,144,1024]{2,1,0:T(8,128)(2,1)S(1)}, bf16[4,144,1024]{2,1,0:T(8,128)(2,1)S(1)}, u32[]{:S(2)}, u32[]{:S(2)}) collective-permute-start(bf16[4,144,1024]{2,1,0:T(8,128)(2,1)S(1)} %shard_map.242.even_ref), channel_id=1, source_target_pairs={{0,4},{4,0},{8,12},{12,8},{16,20},{20,16},{24,28},{28,24},{1,5},{5... | collective-permute-start | bytes 3538952 | tf_op jit(solution)/shard_map/ppermute | solution.py:926
  239.0 7.4 %collective-permute-start.42 = (bf16[4,2,128,1024]{3,2,1,0:T(8,128)(2,1)S(1)}, bf16[4,2,128,1024]{3,2,1,0:T(8,128)(2,1)S(1)}, u32[]{:S(2)}, u32[]{:S(2)}) collective-permute-start(bf16[4,2,128,1024]{3,2,1,0:T(8,128)(2,1)S(1)} %shard_map.243.even_ref), channel_id=1, source_target_pairs={{0,4},{4,0},{8,12},{12,8},{16,20},{20,16},{24,28},{28,24},{1,5},{5... | collective-permute-start | bytes 6291464 | tf_op jit(solution)/shard_map/ppermute | solution.py:926

commit v5 on v4

--- a/solution.py
+++ b/solution.py
@@ -71,11 +71,16 @@
 
 
 def cut_slices(
-    flag_ref, qkv_ref, out_ref, up_ref, down_ref, ssm_ref, attn_ref, mlp_ref, out_slice, *sems
+    flag_ref, qkv_ref, out_ref, up_ref, down_ref, rate_ref, coef_ref, skip_ref, attn_ref, up_slice,
+    down_slice, ssm_ref, out_slice, *sems,
 ):
-    rows = mlp_ref.shape[0] // 2
+    rows = up_slice.shape[0]
     channels = out_slice.shape[0]
     count = ssm_ref.shape[0]
+    ssm_ref[:STATES, :] = rate_ref[...]
+    ssm_ref[STATES : 2 * STATES, :] = coef_ref[...]
+    ssm_ref[2 * STATES :, :] = jnp.zeros((count - 2 * STATES, channels), f32)
+    ssm_ref[2 * STATES : 2 * STATES + 1, :] = skip_ref[...]
     for k, part in enumerate(split_three(ssm_ref[...])):
         attn_ref[rows : rows + count, k * channels : (k + 1) * channels] = part
     attn_ref[rows : rows + count, 3 * channels :] = jnp.zeros((count, channels), bf16)
@@ -89,8 +94,8 @@
         for part in range(3)
     ] + [
         pltpu.make_async_copy(out_ref.at[:, at], out_slice, sems[3]),
-        pltpu.make_async_copy(up_ref.at[at, :], mlp_ref.at[:rows, :], sems[4]),
-        pltpu.make_async_copy(down_ref.at[at, :], mlp_ref.at[rows:, :], sems[5]),
+        pltpu.make_async_copy(up_ref.at[at, :], up_slice, sems[4]),
+        pltpu.make_async_copy(down_ref.at[at, :], down_slice, sems[5]),
     ]
     for copy in copies:
         copy.start()
@@ -107,7 +112,7 @@
     out_ref[:, channels:] = (parts[0] + parts[1]) + parts[2]
 
 
-def run_cut_slices(flags, qkv_parts, out_weight, up_weight, down_weight, ssm_pack):
+def run_cut_slices(flags, qkv_parts, out_weight, up_weight, down_weight, *ssm_parts):
     channels = qkv_parts.shape[2]
     width = out_weight.shape[1]
     rows = width // GROUP
@@ -116,16 +121,18 @@
         cut_slices,
         in_specs=[pl.BlockSpec(memory_space=pltpu.SMEM)]
         + [pl.BlockSpec(memory_space=pltpu.HBM)] * 4
-        + [vmem],
-        out_specs=(vmem, vmem),
+        + [vmem] * 3,
+        out_specs=(vmem,) * 4,
         out_shape=(
-            shape((rows + ssm_pack.shape[0], 4 * channels), bf16),
-            shape((2 * rows, width), bf16),
+            shape((rows + 48, 4 * channels), bf16),
+            shape((rows, width), bf16),
+            shape((rows, width), bf16),
+            shape((48, channels)),
         ),
         scratch_shapes=[pltpu.VMEM((channels, rows), bf16)] + [pltpu.SemaphoreType.DMA] * 6,
         compiler_params=pltpu.CompilerParams(vmem_limit_bytes=56 * 1024 * 1024),
         cost_estimate=length(0),
-    )(flags, qkv_parts, out_weight, up_weight, down_weight, ssm_pack)
+    )(flags, qkv_parts, out_weight, up_weight, down_weight, *ssm_parts)
 
 
 def normalise(values):
@@ -249,14 +256,11 @@
     decay = jnp.exp(-rate_ref[...])
     coef = coef_ref[...]
     skip = skip_ref[...]
-    zero = jnp.zeros_like(decay)
-
-    def step(eight, carry, chunk):
-        state, slope = carry
+
+    def step(eight, state, chunk):
         x8 = xs[aligned((chunk * 16 + eight) * 8, 8), :]
         rows = []
         for k in range(8):
-            slope = decay * (slope + state)
             state = decay * state + x8[k : k + 1]
             if chunk % 2:
                 rows.append(jnp.sum(coef * state, axis=0, keepdims=True))
@@ -267,13 +271,13 @@
                 second_ref[at, :] = y8
             else:
                 xs[at, :] = y8
-        return state, slope
-
-    carry = (zero, zero)
+        return state
+
+    state = jnp.zeros_like(decay)
     for chunk in range(4):
-        carry = lax.fori_loop(0, 16, partial(step, chunk=chunk), carry)
+        state = lax.fori_loop(0, 16, partial(step, chunk=chunk), state)
     handed_ref[:CTX, :] = xs[:CTX, :].astype(bf16)
-    for k, part in enumerate(split_three(carry[0]) + split_three(carry[1])):
+    for k, part in enumerate(split_three(state)):
         handed_ref[CTX + k * STATES : CTX + (k + 1) * STATES, :] = part
 
 
@@ -290,8 +294,7 @@
         to = slice(slot * channels, (slot + 1) * channels)
         source = slice((1 - slot) * channels, (2 - slot) * channels)
         first_ref[:, to] = handed_ref[:CTX, source]
-        enter_ref[0, :, to] = join_three(handed_ref, CTX, source)
-        enter_ref[1, :, to] = join_three(handed_ref, CTX + 3 * STATES, source)
+        enter_ref[:, to] = join_three(handed_ref, CTX, source)
     rate = rate_ref[...]
     decay = jnp.exp(-rate)
     coef = coef_ref[...]
@@ -304,7 +307,7 @@
         acc[aligned(eight * 8, 8), :] = jnp.concatenate(rows, axis=0)
         return state
 
-    lax.fori_loop(0, 16, step, enter_ref[0] * jnp.exp(-129.0 * rate))
+    lax.fori_loop(0, 16, step, enter_ref[...] * jnp.exp(-129.0 * rate))
     second_ref[...] = (local_ref[...] + acc[...]).astype(bf16)
 
 
@@ -318,7 +321,7 @@
 
 def ssm_signal_grad(
     flag_ref, near_ref, returned_ref, rate_ref, coef_ref, skip_ref, total_ref, own_ref, send_ref,
-    last_ref, rows_out, total,
+    last_ref, adjoint_ref, rows_out, total,
 ):
     channels = rate_ref.shape[1] // 2
     adjoints = []
@@ -349,6 +352,7 @@
         return adjoint
 
     adjoint = jnp.concatenate(adjoints, axis=1)
+    adjoint_ref[...] = adjoint
     for chunk in (3, 2, 1, 0):
         adjoint = lax.fori_loop(0, 16, partial(step, chunk=chunk), adjoint)
     for half in (1, 0):
@@ -365,7 +369,7 @@
 
 
 def ssm_param_grad(
-    flag_ref, tile_ref, near_ref, last_ref, enter_ref, rate_ref, coef_ref, out_ref, xs
+    flag_ref, tile_ref, near_ref, last_ref, enter_ref, adjoint_ref, rate_ref, coef_ref, out_ref, xs
 ):
     load_signal(flag_ref, tile_ref, xs)
     decay = jnp.exp(-rate_ref[...])
@@ -384,10 +388,11 @@
                 for_rate = for_rate + slope * g8[k : k + 1]
         return state, slope, for_coef, for_rate
 
-    carry = (enter_ref[0], enter_ref[1], zero, zero)
+    carry = (enter_ref[...], zero, zero, zero)
     for chunk in range(4):
         carry = lax.fori_loop(0, 16, partial(step, chunk=chunk), carry)
-    out_ref[:STATES, :] = -coef_ref[...] * carry[3]
+    for_rate = carry[3] + decay * adjoint_ref[...] * carry[1]
+    out_ref[:STATES, :] = -coef_ref[...] * for_rate
     out_ref[STATES : 2 * STATES, :] = carry[2]
     skip = jnp.sum(xs[CTX : 2 * CTX] * near_ref[...], axis=0, keepdims=True) + jnp.sum(
         xs[3 * CTX :] * last_ref[...], axis=0, keepdims=True
@@ -708,14 +713,16 @@
     send_ref[...] = (left_ref[rows:, :] + received_ref[rows:, :].astype(f32)).astype(bf16)
 
 
-def own_slices(flag_ref, down_own, down_received, up_own, up_received, near_ref, far_ref):
-    rows, hidden = up_own.shape[0], up_own.shape[1] // 2
-    down = down_own[...] + down_received[...].astype(f32)
-    up = up_own[...] + up_received[...].astype(f32)
-    width = down.shape[1]
-    for slot, ref in enumerate((near_ref, far_ref)):
-        ref[:, :width] = down[slot * rows : (slot + 1) * rows].astype(ref.dtype)
-        ref[:, width:] = up[:, slot * hidden : (slot + 1) * hidden].astype(ref.dtype)
+def own_down(flag_ref, own_ref, received_ref, near_ref, far_ref):
+    rows = near_ref.shape[0]
+    near_ref[...] = own_ref[:rows, :] + received_ref[:rows, :].astype(f32)
+    far_ref[...] = (own_ref[rows:, :] + received_ref[rows:, :].astype(f32)).astype(bf16)
+
+
+def own_up(flag_ref, own_ref, received_ref, near_ref, far_ref):
+    width = near_ref.shape[1]
+    near_ref[...] = own_ref[:, :width] + received_ref[:, :width].astype(f32)
+    far_ref[...] = (own_ref[:, width:] + received_ref[:, width:].astype(f32)).astype(bf16)
 
 
 def attn_pass(flag_ref, one0, one1, dqkv0, dqkv1, back0, back1, att0, att1, att2, att3, out_ref):
@@ -781,19 +788,6 @@
     out_ref[...] = (a_ref[...].astype(f32) + b_ref[...].astype(f32)).astype(out_ref.dtype)
 
 
-def add_halves(flag_ref, a_ref, b_ref, left_ref, right_ref):
-    width = left_ref.shape[1]
-    total = a_ref[...] + b_ref[...].astype(f32)
-    left_ref[...] = total[:, :width].astype(bf16)
-    right_ref[...] = total[:, width:].astype(bf16)
-
-
-def split_rows(flag_ref, value_ref, top_ref, bottom_ref):
-    rows = top_ref.shape[0]
-    top_ref[...] = value_ref[:rows, :]
-    bottom_ref[...] = value_ref[rows:, :]
-
-
 def add_three(flag_ref, a_ref, b_ref, c_ref, out_ref):
     out_ref[...] = (a_ref[...] + b_ref[...] + c_ref[...].astype(f32)).astype(out_ref.dtype)
 
@@ -813,10 +807,12 @@
     project(flag_ref, tile_ref, weight_ref, qkv_ref)
 
 
-def assemble_grad(flag_ref, even_ref, odd_ref, qkv_ref, out_ref, small_ref):
+def assemble_grad(
+    flag_ref, even_ref, odd_ref, qkv_ref, out_ref, rate_ref, coef_ref, skip_ref, gain_one_ref,
+    gain_two_ref,
+):
     channels = qkv_ref.shape[2]
     rows = qkv_ref.shape[1] // GROUP
-    count = small_ref.shape[0] // 4
     total = None
     for ref, pair, at in sources(flag_ref, even_ref, odd_ref, rows):
         for part in range(3):
@@ -826,15 +822,34 @@
         out_ref[:, at] = ref[pair, :rows, 3 * channels :].astype(f32).T
         term = ref[pair, rows:, :].astype(f32)
         total = term if total is None else total + term
-    for quarter in range(4):
-        small_ref[quarter * count : (quarter + 1) * count, :] = total[
-            :count, quarter * channels : (quarter + 1) * channels
-        ]
+    count = (2 * STATES + 8 + 8) // 4
+
+    def row(k):
+        return total[k % count : k % count + 1, k // count * channels : (k // count + 1) * channels]
+
+    for k in range(STATES):
+        rate_ref[k : k + 1, :] = row(k)
+        coef_ref[k : k + 1, :] = row(STATES + k)
+    skip_ref[...] = row(2 * STATES)
+    for which, ref in enumerate((gain_one_ref, gain_two_ref)):
+        for k in range(4):
+            ref[:, k * channels : (k + 1) * channels] = row(2 * STATES + 8 + which * 4 + k)
 
 
 def stack_two(flag_ref, a_ref, ax_ref, b_ref, by_ref, a_out, b_out):
     a_out[0], a_out[1] = a_ref[...], ax_ref[...]
     b_out[0], b_out[1] = b_ref[...], by_ref[...]
+
+
+def stack_three(flag_ref, a_ref, ax_ref, b_ref, by_ref, a_out, b_out, both_out):
+    stack_two(flag_ref, a_ref, ax_ref, b_ref, by_ref, a_out, b_out)
+    both_out[0, 0], both_out[0, 1] = a_ref[...], b_ref[...]
+    both_out[1, 0], both_out[1, 1] = ax_ref[...], by_ref[...]
+
+
+def stack_pairs(flag_ref, a_ref, b_ref, out_ref):
+    out_ref[0, 0], out_ref[0, 1] = a_ref[0], b_ref[0]
+    out_ref[1, 0], out_ref[1, 1] = a_ref[1], b_ref[1]
 
 
 def stack_four(flag_ref, a_ref, b_ref, c_ref, d_ref, out_ref):
@@ -855,37 +870,44 @@
         b_out[at, :] = ref[pair, 1].astype(b_out.dtype)
 
 
-def place_wide(flag_ref, even_ref, odd_ref, a_out, b_out):
-    @pl.when(pl.program_id(0) % 2 == 0)
-    def _():
-        a_out[...] = even_ref[0, 0].astype(f32)
-        b_out[...] = even_ref[0, 1].astype(f32)
-
-    @pl.when(pl.program_id(0) % 2 == 1)
-    def _():
-        a_out[...] = odd_ref[0, 0].astype(f32)
-        b_out[...] = odd_ref[0, 1].astype(f32)
-
-
-def run_place_wide(flags, even, odd):
-    rows, width = even.shape[2:]
+def place_wide(flag_ref, own_ref, other_ref, *refs):
+    for side, ref in enumerate((own_ref, other_ref)):
+
+        @pl.when(pl.program_id(0) % 2 == side)
+        def _():
+            refs[-2][...] = ref[0, 0].astype(f32)
+            refs[-1][...] = ref[0, 1].astype(f32)
+
+
+def run_place_wide(flags, own, other, starts, steps, filled=()):
+    rows, width = own.shape[2:]
     piece = pl.BlockSpec((1, 2, rows, width), lambda j, flag_ref: (j // 2, 0, 0, 0))
-    place = pl.BlockSpec(
-        (rows, width), lambda j, flag_ref: (jnp.bitwise_xor(flag_ref[PLACE], j), 0)
-    )
+
+    def place(which):
+        return pl.BlockSpec(
+            (rows, width),
+            lambda j, flag_ref: (
+                jnp.bitwise_xor(
+                    flag_ref[PLACE], starts[which] + (j // 2) * steps[which] + j % 2
+                ),
+                0,
+            ),
+        )
+
     out = shape((GROUP * rows, width))
     return pl.pallas_call(
         place_wide,
         grid_spec=pltpu.PrefetchScalarGridSpec(
             num_scalar_prefetch=1,
-            grid=(GROUP,),
-            in_specs=[piece, piece],
-            out_specs=(place, place),
+            grid=(GROUP // 2,),
+            in_specs=[piece, piece] + [pl.BlockSpec(memory_space=pl.ANY)] * len(filled),
+            out_specs=(place(0), place(1)),
         ),
         out_shape=(out, out),
+        input_output_aliases={3 + k: k for k in range(len(filled))},
         compiler_params=pltpu.CompilerParams(vmem_limit_bytes=VMEM_LIMIT),
         cost_estimate=length(0),
-    )(flags, even, odd)
+    )(flags, own, other, *filled)
 
 
 class Order:
@@ -959,11 +981,11 @@
     normed_one = order.done(call(norm_one, half_low)(flags, row, gain_one))
     paired_one = swap_mp(normed_one, 1)
     qkv_parts = jnp.transpose(qkv_weight, (1, 0, 2))
-    ssm_pack = jnp.concatenate(
-        [ssm_rate.T, ssm_coef.T, ssm_skip[None], jnp.zeros((15, channels), f32)], 0
-    )
-    attn_slice, mlp_slice = order.done(
-        run_cut_slices(flags, order(qkv_parts), out_weight, up_weight, down_weight, ssm_pack)
+    attn_slice, up_slice, down_slice, ssm_pack = order.done(
+        run_cut_slices(
+            flags, order(qkv_parts), out_weight, up_weight, down_weight, ssm_rate.T, ssm_coef.T,
+            ssm_skip[None],
+        )
     )
     attn_across = swap_mp(attn_slice, 2)
     near_qkv = order.done(jnp.concatenate(list(order(*[qkv_parts[k] for k in range(3)])), 1))
@@ -972,7 +994,7 @@
     attn_own_slice = attn_across[:rows]
     attn_x = swap_dp(attn_own_slice, 2)
     attn_y = swap_dp(attn_own_slice, 4)
-    mlp_across = swap_mp(order(mlp_slice), 2)
+    up_across = swap_mp(order(up_slice), 2)
     paired_cot = swap_mp(order(cot), 1)
     ssm_both = call(join_ssm, shape((48, wide)))(flags, ssm_pack, attn_across)
     rate_t, coef_t, skip_t = ssm_both[:16], ssm_both[16:32], ssm_both[32:33]
@@ -983,7 +1005,7 @@
                 shape((2, HALF, model_dim), bf16),
                 shape((2, HALF, model_dim), bf16),
                 shape((CTX, wide)),
-                shape((CTX + 6 * STATES, wide), bf16),
+                shape((CTX + 3 * STATES, wide), bf16),
             ),
             scratch=[pltpu.VMEM((2 * HALF, wide), f32)],
         )(flags, normed_one, order(paired_one), rate_t, coef_t, skip_t)
@@ -994,8 +1016,9 @@
     att_shape = shape((2, HALF, channels), bf16)
     attn_x = order.done(order(attn_x))
     attn_xy = swap_dp(attn_x, 4)
+    attn_y, paired_cot, mlp_up = order.done(order(attn_y, paired_cot, up_across))
+    mlp_up_x = swap_dp(mlp_up, 2)
     qkv_near = order.done(call(project, qkv_shape)(flags, order(tile_one), near_qkv))
-    attn_y, paired_cot = order.done(order(attn_y, paired_cot))
     even = order.done(
         call(stack_four, shape((4,) + attn_x.shape, bf16))(
             flags, attn_own_slice, attn_x, attn_y, order(attn_xy)
@@ -1003,18 +1026,15 @@
     )
     odd_part = swap_dp(even, 1)
     slice_shape = low(rows, model_dim)
-    mlp_up, mlp_down = order.done(
-        call(split_rows, (slice_shape, slice_shape))(flags, order(mlp_across))
-    )
-    mlp_up_x = swap_dp(mlp_up, 2)
-    mlp_down_y = swap_dp(mlp_down, 4)
+    handed = order.done(order(handed))
+    down_across = swap_mp(order(down_slice), 2)
     ctx_first, ctx_second, enter_state = order.done(
         call(
             ssm_carry_in,
-            (shape((CTX, wide), bf16), shape((CTX, wide), bf16), shape((2, STATES, wide))),
+            (shape((CTX, wide), bf16), shape((CTX, wide), bf16), shape((STATES, wide))),
             scratch=[pltpu.VMEM((CTX, wide), f32)],
-            micros=6,
-        )(flags, second_local, order(handed), rate_t, coef_t)
+            micros=16,
+        )(flags, order(second_local), handed, rate_t, coef_t)
     )
     att_near = order.done(
         call(attention_near, att_shape)(flags, order(qkv_near), ctx_first, ctx_second)
@@ -1036,8 +1056,10 @@
     )
     out_received = swap_mp(out_send, 1)
     pair_shape = low(2, rows, model_dim)
+    mlp_down = order.done(order(down_across))
+    mlp_down_y = swap_dp(mlp_down, 4)
     mlp_up_two, mlp_down_two = order.done(
-        call(stack_two, (pair_shape, pair_shape), micros=3)(
+        call(stack_two, (pair_shape, pair_shape), micros=0.5)(
             flags, mlp_up, order(mlp_up_x), mlp_down, order(mlp_down_y)
         )
     )
@@ -1059,7 +1081,7 @@
     mlp_odd = swap_dp(mlp_even, 1)
     paired_two = order(paired_two)
     warm = order.done(
-        call(touch, shape((8, 128), bf16), micros=12)(
+        call(touch, shape((8, 128), bf16), micros=30)(
             flags, up_weight, down_weight, cot, paired_cot, paired_two
         )
     )
@@ -1145,38 +1167,40 @@
         )
     )
     up_x = swap_dp(up_send_x, 2)
-    one_own, one_send, last_grad = order.done(
+    one_own, one_send, last_grad, enter_adjoint = order.done(
         call(
             ssm_signal_grad,
-            (half, half_low, shape((CTX, wide))),
+            (half, half_low, shape((CTX, wide)), shape((STATES, wide))),
             scratch=[pltpu.VMEM((2 * HALF, wide), f32), pltpu.VMEM((HALF, model_dim), f32)],
             micros=30,
         )(flags, second_grad, order(returned), rate_t, coef_t, skip_t, one_total)
     )
     one_received = swap_mp(one_send, 1)
-    output = order.done(
-        call(add_three, half_low)(flags, middle, down_own, order(down_received))
-    )
+    down_received = order.done(order(down_received))
     attn_mine, *attn_sends = order.done(
         call(attn_keep, (shape((rows, 8 * channels)),) + (low(rows, 8 * channels),) * 3)(
             flags, *attns, order(attn_core)
         )
     )
     attn_sent = [swap_dp(part, SENT[5 + k]) for k, part in enumerate(attn_sends)]
-    mlp_width = model_dim + hidden
-    mlp_near, mlp_send = order.done(
-        call(own_slices, (shape((rows, mlp_width)), low(rows, mlp_width)))(
-            flags, down_mine, order(down_y), up_mine, order(up_x)
-        )
-    )
-    mlp_received = swap_mp(mlp_send, 2)
+    wide_slice = shape((rows, model_dim))
+    down_near, down_far_grad = order.done(
+        call(own_down, (wide_slice, slice_shape))(flags, down_mine, order(down_y))
+    )
+    down_received_far = swap_mp(down_far_grad, 2)
+    up_near, up_far_grad = order.done(
+        call(own_up, (wide_slice, slice_shape))(flags, up_mine, order(up_x))
+    )
+    up_received_far = swap_mp(up_far_grad, 2)
     param_grad = order.done(
         call(
             ssm_param_grad,
             shape((40, wide)),
             scratch=[pltpu.VMEM((2 * HALF, wide), f32)],
             micros=3,
-        )(flags, order(tile_one), second_grad, last_grad, enter_state, rate_t, coef_t)
+        )(
+            flags, order(tile_one), second_grad, last_grad, enter_state, enter_adjoint, rate_t, coef_t
+        )
     )
     input_grad, gains = order.done(
         call(norm_one_back, (half, shape((2 * model_dim // channels, channels))))(
@@ -1184,11 +1208,16 @@
         )
     )
     gains_received = swap_mp(gains, 1)
-    down_mine, up_mine = order.done(
-        call(add_halves, (slice_shape, slice_shape))(flags, mlp_near, order(mlp_received))
-    )
-    down_mine, up_mine = over_groups(down_mine), over_groups(up_mine)
+    output = order.done(
+        call(add_three, half_low)(flags, middle, order(down_own), down_received)
+    )
+    down_mine = order.done(
+        call(add_two, slice_shape)(flags, down_near, order(down_received_far))
+    )
+    down_mine = over_groups(down_mine)
     down_x = swap_dp(down_mine, 2)
+    up_mine = order.done(call(add_two, slice_shape)(flags, up_near, order(up_received_far)))
+    up_mine = over_groups(up_mine)
     up_y = swap_dp(up_mine, 4)
     slice_rows = rows + 16
     *attn_sent, gains_received = order(*attn_sent, gains_received)
@@ -1198,55 +1227,64 @@
         )
     )
     attn_received = swap_mp(attn_send, 2)
-    down_two, up_two = order.done(
-        call(stack_two, (pair_shape, pair_shape), micros=3)(
+    both_shape = low(2, 2, rows, model_dim)
+    down_two, up_two, first_pieces = order.done(
+        call(stack_three, (pair_shape, pair_shape, both_shape), micros=3)(
             flags, down_mine, order(down_x), up_mine, order(up_y)
         )
     )
     down_y = swap_dp(down_two, 4)
     up_x = swap_dp(up_two, 2)
+    first_others = swap_dp(first_pieces, 1)
     attn_slice_grad = order.done(
-        call(add_two, low(slice_rows, 4 * channels), micros=3)(
+        call(add_two, low(slice_rows, 4 * channels), micros=20)(
             flags, attn_near, order(attn_received)
         )
     )
-    attn_slice_grad = over_groups(attn_slice_grad)
+    first_others = order.done(order(first_others))
+    attn_slice_grad = over_groups(order(attn_slice_grad))
     attn_sent = [swap_dp(attn_slice_grad, 2 * k) for k in range(1, GROUP // 2)]
+    wide_grads = order.done(
+        run_place_wide(flags, first_pieces, order(first_others), (0, 0), (2, 4))
+    )
     even = order.done(
         call(stack_four, low(4, slice_rows, 4 * channels))(
             flags, attn_slice_grad, *order(*attn_sent)
         )
     )
     odd_part = swap_dp(even, 1)
-    mlp_even = order.done(
-        call(stack_eight, eight_shape, micros=5)(
-            flags, down_two, order(down_y), up_two, order(up_x)
-        )
-    )
-    mlp_odd = swap_dp(mlp_even, 1)
-    qkv_grad, out_grad, small = order.done(
+    last_pieces = order.done(
+        call(stack_pairs, both_shape, micros=8)(flags, *order(down_y, up_x))
+    )
+    last_others = swap_dp(last_pieces, 1)
+    qkv_grad, out_grad, rate_grad, coef_grad, skip_grad, gain_one_grad, gain_two_grad = order.done(
         call(
             assemble_grad,
             (
                 shape((3, model_dim, channels)),
                 shape(out_weight.shape),
-                shape((48, channels)),
+                shape((STATES, channels)),
+                shape((STATES, channels)),
+                shape((1, channels)),
+                shape((1, model_dim)),
+                shape((1, model_dim)),
             ),
-            micros=6,
+            micros=8,
         )(flags, even, order(odd_part))
     )
-    down_grad, up_grad = run_place_wide(flags, mlp_even, order(mlp_odd))
-    gains = small[40:].reshape(2, model_dim)
+    down_grad, up_grad = run_place_wide(
+        flags, last_pieces, order(last_others), (4, 2), (2, 4), wide_grads
+    )
     return (
         output[None],
         input_grad[None],
-        gains[0],
+        gain_one_grad[0],
         jnp.transpose(qkv_grad, (1, 0, 2)),
-        small[:16].T,
-        small[16:32].T,
-        small[32],
+        rate_grad.T,
+        coef_grad.T,
+        skip_grad[0],
         out_grad,
-        gains[1],
+        gain_two_grad[0],
         up_grad,
         down_grad,
     )

time: 252 us -> 233 us (0.925)
  waiting for transfers between devices: 98.7 us -> 82.7 us
    ppermute x13 -> x15, waiting for transfers between devices: 73.4 us -> 47.5 us  [swap_mp(): return lax.ppermute(value, 'mp', [(k, k ^ mask) for k in range(4)])]
    ppermute x28 -> x29, waiting for transfers between devices: 25.3 us -> 35.2 us  [swap_dp(): return lax.ppermute(value, 'dp', [(k, k ^ mask) for k in range(dp_size)])]
    ppermute x1, starting transfers between devices: 5.09 us -> 2.42 us  [per_device(): handed = lax.ppermute(handed, 'mp', [(0, 2), (1, 3)])]
    ppermute x13 -> x15, starting transfers between devices: 24.4 us -> 26.4 us  [swap_mp(): return lax.ppermute(value, 'mp', [(k, k ^ mask) for k in range(4)])]
    pallas_call x1 -> x2, Pallas kernels: 5.05 us -> 6.09 us  [run_place_wide(): pl.pallas_call(place_wide, grid_spec=pltpu.PrefetchScalarGridSpec(num_sca...]
    ppermute x28 -> x29, starting transfers between devices: 27.4 us -> 28.3 us  [swap_dp(): return lax.ppermute(value, 'dp', [(k, k ^ mask) for k in range(dp_size)])]
    pallas_call x39 -> x40, Pallas kernels: 64.2 us -> 63.7 us  [run(): pl.pallas_call(kernel, out_shape=out_shape, in_specs=[pl.BlockSpec(memory...]
  transfers between devices with their start and end apart: 43 -> 46, of which waited for: 20 -> 23; matrix products, arithmetic and copies ran while one was open for 2% -> 0% of each run, Pallas kernels for 29% -> 32%
where the time goes in v5:
time: 233 us; the launch traced here: 232 us
  Pallas kernels  86.6 us (37%)
  waiting for transfers between devices  82.7 us (35%)
  starting transfers between devices  58.8 us (25%)
  local copies, waits for them, and re-layouts  2.4 us (1%)
    pallas_call x40, Pallas kernels, run(): pl.pallas_call(kernel, out_shape=out_shape, in_specs=[pl.BlockSpec(memory...  63.7 us
    ppermute x15, waiting for transfers between devices, swap_mp(): return lax.ppermute(value, 'mp', [(k, k ^ mask) for k in range(4)])  47.5 us
    ppermute x29, waiting for transfers between devices, swap_dp(): return lax.ppermute(value, 'dp', [(k, k ^ mask) for k in range(dp_size)])  35.2 us
    ppermute x29, starting transfers between devices, swap_dp(): return lax.ppermute(value, 'dp', [(k, k ^ mask) for k in range(dp_size)])  28.3 us
    ppermute x15, starting transfers between devices, swap_mp(): return lax.ppermute(value, 'mp', [(k, k ^ mask) for k in range(4)])  26.4 us
    pallas_call x2, Pallas kernels, run_feed_forward(): pl.pallas_call(feed_forward, grid=(2 * per,), out_shape=(shape((tokens, 2...  13.9 us
    pallas_call x2, Pallas kernels, run_place_wide(): pl.pallas_call(place_wide, grid_spec=pltpu.PrefetchScalarGridSpec(num_sca...  6.09 us
  transfers between devices with their start and end apart: 46, of which 23 were waited for; matrix products, arithmetic and copies ran while one was open for 0% of the time, Pallas kernels for 32%

profile of v5, /device:TPU:0, one launch (start us, length us, event | category | flops | bytes accessed | tf_op | source)
XLA Modules:
  0.0 232.5 jit_solution(17313707693015068669)
XLA Ops:
  4.0 3.1 %collective-permute-start = (bf16[256,1024]{1,0:T(8,128)(2,1)S(1)}, bf16[256,1024]{1,0:T(8,128)(2,1)S(1)}, u32[]{:S(2)}, u32[]{:S(2)}) collective-permute-start(bf16[256,1024]{1,0:T(8,128)(2,1)S(1)} %shard_map.203.own_ref), channel_id=1, source_target_pairs={{0,1},{1,0},{2,3},{3,2},{4,5},{5,4},{6,7},{7,6},{8,9},{9,8},{10,11... | collective-permute-start | bytes 1572872 | tf_op jit(solution)/shard_map/ppermute | solution.py:945
  7.1 2.9 %shard_map.204 = (bf16[176,1024]{1,0:T(8,128)(2,1)}, bf16[128,1024]{1,0:T(8,128)(2,1)}, bf16[128,1024]{1,0:T(8,128)(2,1)}, f32[48,256]{1,0:T(8,128)}) custom-call(s32[6]{0:T(128)} %copy-done.6, bf16[3,1024,256]{2,1,0:T(8,128)(2,1)} %bitcast.60, bf16[256,1024]{1,0:T(8,128)(2,1)} %out_near_ref.3, bf16[1024,1024]{1,0:T(8,128)(2,1)} %up0_ref.3, ...), custom_call_target="tpu_custom_call" | custom-call | tf_op jit(solution)/shard_map/pallas_call | solution.py:120
  10.0 2.7 %collective-permute-start.1 = (bf16[176,1024]{1,0:T(8,128)(2,1)}, bf16[176,1024]{1,0:T(8,128)(2,1)S(1)}, u32[]{:S(2)}, u32[]{:S(2)}) collective-permute-start(bf16[176,1024]{1,0:T(8,128)(2,1)} %get-tuple-element.161), channel_id=1, source_target_pairs={{0,2},{1,3},{2,0},{3,1},{4,6},{5,7},{6,4},{7,5},{8,10},{9,11},{10,... | collective-permute-start | bytes 1081352 | tf_op jit(solution)/shard_map/ppermute | solution.py:945
  13.0 13.2 %collective-permute-done.1.across_ref = bf16[176,1024]{1,0:T(8,128)(2,1)S(1)} collective-permute-done((bf16[176,1024]{1,0:T(8,128)(2,1)}, bf16[176,1024]{1,0:T(8,128)(2,1)S(1)}, u32[]{:S(2)}, u32[]{:S(2)}) %collective-permute-start.1) | collective-permute-done | bytes 360480 | tf_op jit(solution)/shard_map/ppermute | solution.py:945
  26.8 2.8 %collective-permute-start.4 = (bf16[256,1024]{1,0:T(8,128)(2,1)S(1)}, bf16[256,1024]{1,0:T(8,128)(2,1)S(1)}, u32[]{:S(2)}, u32[]{:S(2)}) collective-permute-start(bf16[256,1024]{1,0:T(8,128)(2,1)S(1)} %bitcast.47), channel_id=1, source_target_pairs={{0,1},{1,0},{2,3},{3,2},{4,5},{5,4},{6,7},{7,6},{8,9},{9,8},{10,11... | collective-permute-start | bytes 1572872 | tf_op jit(solution)/shard_map/ppermute | solution.py:945
  29.5 1.6 collective-permute-start.2
  31.7 1.6 collective-permute-start.3
  33.2 2.4 %collective-permute-start.5 = (bf16[128,1024]{1,0:T(8,128)(2,1)S(1)}, bf16[128,1024]{1,0:T(8,128)(2,1)S(1)}, u32[]{:S(2)}, u32[]{:S(2)}) collective-permute-start(bf16[128,1024]{1,0:T(8,128)(2,1)S(1)} %copy-done.14), channel_id=1, source_target_pairs={{0,2},{1,3},{2,0},{3,1},{4,6},{5,7},{6,4},{7,5},{8,10},{9,11},{10,... | collective-permute-start | bytes 786440 | tf_op jit(solution)/shard_map/ppermute | solution.py:945
  35.7 3.9 %shard_map.206 = (bf16[2,256,1024]{2,1,0:T(8,128)(2,1)S(1)}, bf16[2,256,1024]{2,1,0:T(8,128)(2,1)S(1)}, f32[128,512]{1,0:T(8,128)S(1)}, bf16[176,512]{1,0:T(8,128)(2,1)S(1)}) custom-call(s32[6]{0:T(128)S(1)} %copy-done.7, bf16[256,1024]{1,0:T(8,128)(2,1)S(1)} %shard_map.203.own_ref, bf16[256,1024]{1,0:T(8,128)(2,1)S(1)} %collective-permute-done.other_ref, ...), custom_call_target="tpu_custom_call" | custom-call | tf_op jit(solution)/shard_map/pallas_call | solution.py:46
  40.2 2.4 %collective-permute-start.8 = (bf16[176,512]{1,0:T(8,128)(2,1)S(1)}, bf16[176,512]{1,0:T(8,128)(2,1)S(1)}, u32[]{:S(2)}, u32[]{:S(2)}) collective-permute-start(bf16[176,512]{1,0:T(8,128)(2,1)S(1)} %get-tuple-element.174), channel_id=1, source_target_pairs={{0,2},{1,3},{4,6},{5,7},{8,10},{9,11},{12,14},{13,15},{16,18},{17,... | collective-permute-start | bytes 540680 | tf_op jit(solution)/shard_map/ppermute | solution.py:1013
  42.6 4.8 %collective-permute-done.5.a_ref = bf16[128,1024]{1,0:T(8,128)(2,1)S(1)} collective-permute-done((bf16[128,1024]{1,0:T(8,128)(2,1)S(1)}, bf16[128,1024]{1,0:T(8,128)(2,1)S(1)}, u32[]{:S(2)}, u32[]{:S(2)}) %collective-permute-start.5) | collective-permute-done | bytes 262176 | tf_op jit(solution)/shard_map/ppermute | solution.py:945
  47.4 1.5 shard_map.207.qkv_ref.near_ref
  49.7 3.5 %collective-permute-start.11 = (bf16[128,1024]{1,0:T(8,128)(2,1)S(1)}, bf16[128,1024]{1,0:T(8,128)(2,1)S(1)}, u32[]{:S(2)}, u32[]{:S(2)}) collective-permute-start(bf16[128,1024]{1,0:T(8,128)(2,1)S(1)} %copy-done.13), channel_id=1, source_target_pairs={{0,2},{1,3},{2,0},{3,1},{4,6},{5,7},{6,4},{7,5},{8,10},{9,11},{10,... | collective-permute-start | bytes 786440 | tf_op jit(solution)/shard_map/ppermute | solution.py:945
  53.2 1.7 shard_map.209
  54.9 1.9 shard_map.210.near_ref
  56.8 1.7 shard_map.211
  58.5 2.6 %shard_map.212 = (bf16[2,256,256]{2,1,0:T(8,128)(2,1)S(1)}, f32[256,1024]{1,0:T(8,128)S(1)}, bf16[256,1024]{1,0:T(8,128)(2,1)S(1)}) custom-call(s32[6]{0:T(128)S(1)} %copy-done.7, bf16[2,256,768]{2,1,0:T(8,128)(2,1)S(1)} %get-tuple-element.193.qkv_ref.far_ref, bf16[128,512]{1,0:T(8,128)(2,1)S(1)} %get-tuple-element.185.first_ref, ...), custom_call_target="tpu_custom_call" | custom-call | tf_op jit(solution)/shard_map/pallas_call | solution.py:46
  61.1 3.5 %collective-permute-start.9 = (bf16[256,1024]{1,0:T(8,128)(2,1)S(1)}, bf16[256,1024]{1,0:T(8,128)(2,1)S(1)}, u32[]{:S(2)}, u32[]{:S(2)}) collective-permute-start(bf16[256,1024]{1,0:T(8,128)(2,1)S(1)} %get-tuple-element.195), channel_id=1, source_target_pairs={{0,1},{1,0},{2,3},{3,2},{4,5},{5,4},{6,7},{7,6},{8,9},{9,8},{10,11... | collective-permute-start | bytes 1572872 | tf_op jit(solution)/shard_map/ppermute | solution.py:945
  65.8 1.5 collective-permute-start.12
  67.3 3.6 %collective-permute-done.10.ax_ref = bf16[128,1024]{1,0:T(8,128)(2,1)S(1)} collective-permute-done((bf16[128,1024]{1,0:T(8,128)(2,1)S(1)}, bf16[128,1024]{1,0:T(8,128)(2,1)S(1)}, u32[]{:S(2)}, u32[]{:S(2)}) %collective-permute-start.10) | collective-permute-done | bytes 262176 | tf_op jit(solution)/shard_map/ppermute | solution.py:948
  71.0 2.8 %collective-permute-done.12.by_ref = bf16[128,1024]{1,0:T(8,128)(2,1)S(1)} collective-permute-done((bf16[128,1024]{1,0:T(8,128)(2,1)S(1)}, bf16[128,1024]{1,0:T(8,128)(2,1)S(1)}, u32[]{:S(2)}, u32[]{:S(2)}) %collective-permute-start.12) | collective-permute-done | bytes 262176 | tf_op jit(solution)/shard_map/ppermute | solution.py:948
  74.4 1.6 collective-permute-start.15
  75.9 1.5 collective-permute-start.14
  78.5 8.6 %collective-permute-done.15.bx_ref = bf16[2,128,1024]{2,1,0:T(8,128)(2,1)S(1)} collective-permute-done((bf16[2,128,1024]{2,1,0:T(8,128)(2,1)S(1)}, bf16[2,128,1024]{2,1,0:T(8,128)(2,1)S(1)}, u32[]{:S(2)}, u32[]{:S(2)}) %collective-permute-start.15) | collective-permute-done | bytes 524320 | tf_op jit(solution)/shard_map/ppermute | solution.py:948
  89.1 2.3 %collective-permute-done.13.rows_ref.n_ref = bf16[256,1024]{1,0:T(8,128)(2,1)S(1)} collective-permute-done((bf16[256,1024]{1,0:T(8,128)(2,1)S(1)}, bf16[256,1024]{1,0:T(8,128)(2,1)S(1)}, u32[]{:S(2)}, u32[]{:S(2)}) %collective-permute-start.13) | collective-permute-done | bytes 524320 | tf_op jit(solution)/shard_map/ppermute | solution.py:945
  94.0 6.8 %shard_map.218 = (bf16[256,2048]{1,0:T(8,128)(2,1)S(1)}, bf16[256,2048]{1,0:T(8,128)(2,1)S(1)}, bf16[256,1024]{1,0:T(8,128)(2,1)S(1)}, bf16[256,1024]{1,0:T(8,128)(2,1)S(1)}, bf16[256,1024]{1,0:T(8,128)(2,1)S(1)}) custom-call(s32[6]{0:T(128)S(1)} %copy-done.7, bf16[256,1024]{1,0:T(8,128)(2,1)S(1)} %collective-permute-done.13.rows_ref.n_ref, ...), custom_call_target="tpu_custom_call" | custom-call | tf_op jit(solution)/shard_map/pallas_call | solution.py:612
  101.1 7.1 %shard_map.219 = (bf16[256,2048]{1,0:T(8,128)(2,1)S(1)}, bf16[256,2048]{1,0:T(8,128)(2,1)S(1)}, bf16[256,1024]{1,0:T(8,128)(2,1)S(1)}, f32[256,1024]{1,0:T(8,128)S(1)}, f32[256,1024]{1,0:T(8,128)S(1)}) custom-call(s32[6]{0:T(128)S(1)} %copy-done.7, bf16[256,1024]{1,0:T(8,128)(2,1)S(1)} %get-tuple-element.218.n_ref, bf16[256,1024]{1,0:T(8,128)(2,1)S(1)} %bitcast.49, ...), custom_call_target="tpu_custom_call" | custom-call | tf_op jit(solution)/shard_map/pallas_call | solution.py:612
  108.2 1.8 shard_map.220
  110.1 1.8 shard_map.221
  112.5 2.4 %collective-permute-done.17.received_ref = bf16[256,1024]{1,0:T(8,128)(2,1)S(1)} collective-permute-done((bf16[256,1024]{1,0:T(8,128)(2,1)S(1)}, bf16[256,1024]{1,0:T(8,128)(2,1)S(1)}, u32[]{:S(2)}, u32[]{:S(2)}) %collective-permute-start.17) | collective-permute-done | bytes 524320 | tf_op jit(solution)/shard_map/ppermute | solution.py:945
  116.8 1.8 shard_map.223
  118.6 1.6 collective-permute-start.23
  120.2 1.9 shard_map.224
  122.1 1.6 collective-permute-start.22
  123.7 5.8 %collective-permute-done.18.other_ref = bf16[256,1024]{1,0:T(8,128)(2,1)S(1)} collective-permute-done((bf16[256,1024]{1,0:T(8,128)(2,1)S(1)}, bf16[256,1024]{1,0:T(8,128)(2,1)S(1)}, u32[]{:S(2)}, u32[]{:S(2)}) %collective-permute-start.18) | collective-permute-done | bytes 524320 | tf_op jit(solution)/shard_map/ppermute | solution.py:945
  131.4 5.4 %shard_map.226 = (bf16[2,256,1536]{2,1,0:T(8,128)(2,1)S(1)}, f32[128,512]{1,0:T(8,128)S(1)}, bf16[176,512]{1,0:T(8,128)(2,1)S(1)}) custom-call(s32[6]{0:T(128)S(1)} %copy-done.7, bf16[2,256,768]{2,1,0:T(8,128)(2,1)S(1)} %shard_map.207.qkv_ref.near_ref, bf16[2,256,768]{2,1,0:T(8,128)(2,1)S(1)} %get-tuple-element.193.qkv_ref.far_ref, ...), custom_call_target="tpu_custom_call" | custom-call | tf_op jit(solution)/shard_map/pallas_call | solution.py:46
  136.8 1.6 collective-permute-start.21
  138.4 2.4 %shard_map.227.total_ref = f32[2,256,1024]{2,1,0:T(8,128)S(1)} custom-call(s32[6]{0:T(128)S(1)} %copy-done.7, bf16[2,256,1536]{2,1,0:T(8,128)(2,1)S(1)} %get-tuple-element.243.dqkv_ref, bf16[1024,768]{1,0:T(8,128)(2,1)S(1)} %constant_dynamic-update-slice_fusion.weight_ref.near_weight_ref, bf16[1024,768]{1,0:T(8,128)(2,1)S(1)} %get-tuple-element.191.far_weight_ref), custom_call_target="tpu_custom_call" | custom-call | tf_op jit(solution)/shard_map/pallas_call | solution.py:46
  140.9 1.8 shard_map.228
  143.6 1.6 collective-permute-start.26
  147.4 5.1 %shard_map.231 = (f32[256,1024]{1,0:T(8,128)S(1)}, bf16[256,1024]{1,0:T(8,128)(2,1)S(1)}, f32[128,512]{1,0:T(8,128)S(1)}, f32[16,512]{1,0:T(8,128)S(1)}) custom-call(s32[6]{0:T(128)S(1)} %copy-done.7, f32[128,512]{1,0:T(8,128)S(1)} %get-tuple-element.240.near_ref, bf16[176,512]{1,0:T(8,128)(2,1)S(1)} %collective-permute-done.21.returned_ref, ...), custom_call_target="tpu_custom_call" | custom-call | flops 30000001024 | tf_op jit(solution)/shard_map/pallas_call | solution.py:46
  152.5 1.8 collective-permute-start.24
  154.3 1.9 shard_map.232
  156.2 1.6 collective-permute-start.29
  157.7 2.0 collective-permute-start.30
  160.3 2.3 collective-permute-start.34
  163.3 2.4 %collective-permute-start.33 = (bf16[128,1024]{1,0:T(8,128)(2,1)S(1)}, bf16[128,1024]{1,0:T(8,128)(2,1)S(1)}, u32[]{:S(2)}, u32[]{:S(2)}) collective-permute-start(bf16[128,1024]{1,0:T(8,128)(2,1)S(1)} %get-tuple-element.268), channel_id=1, source_target_pairs={{0,2},{1,3},{2,0},{3,1},{4,6},{5,7},{6,4},{7,5},{8,10},{9,11},{10,... | collective-permute-start | bytes 786440 | tf_op jit(solution)/shard_map/ppermute | solution.py:945
  165.6 7.1 %collective-permute-done.24.received_ref = bf16[256,1024]{1,0:T(8,128)(2,1)S(1)} collective-permute-done((bf16[256,1024]{1,0:T(8,128)(2,1)S(1)}, bf16[256,1024]{1,0:T(8,128)(2,1)S(1)}, u32[]{:S(2)}, u32[]{:S(2)}) %collective-permute-start.24) | collective-permute-done | bytes 524320 | tf_op jit(solution)/shard_map/ppermute | solution.py:945
  172.7 4.3 %shard_map.235.param_ref = f32[40,512]{1,0:T(8,128)S(1)} custom-call(s32[6]{0:T(128)S(1)} %copy-done.7, bf16[2,256,1024]{2,1,0:T(8,128)(2,1)S(1)} %get-tuple-element.269.tile_ref, f32[128,512]{1,0:T(8,128)S(1)} %get-tuple-element.240.near_ref, f32[128,512]{1,0:T(8,128)S(1)} %get-tuple-element.255.last_ref, f32[16,512]{1,0:T(8,128)S(1)} %get-tuple-element.187.enter_ref, ...), custom_call_target="tpu_custom_call" | custom-call | flops 3000000000 | tf_op jit(solution)/shard_map/pallas_call | solution.py:46
  177.1 2.4 %shard_map.236 = (f32[256,1024]{1,0:T(8,128)}, f32[8,256]{1,0:T(8,128)S(1)}) custom-call(s32[6]{0:T(128)S(1)} %copy-done.7, bf16[256,1024]{1,0:T(8,128)(2,1)S(1)} %bitcast.55, f32[256,1024]{1,0:T(8,128)S(1)} %get-tuple-element.252.own_ref, bf16[256,1024]{1,0:T(8,128)(2,1)S(1)} %collective-permute-done.24.received_ref, ...), custom_call_target="tpu_custom_call" | custom-call | tf_op jit(solution)/shard_map/pallas_call | solution.py:46
  179.5 2.4 %collective-permute-done.34.b_ref = bf16[128,1024]{1,0:T(8,128)(2,1)S(1)} collective-permute-done((bf16[128,1024]{1,0:T(8,128)(2,1)S(1)}, bf16[128,1024]{1,0:T(8,128)(2,1)S(1)}, u32[]{:S(2)}, u32[]{:S(2)}) %collective-permute-start.34) | collective-permute-done | bytes 262176 | tf_op jit(solution)/shard_map/ppermute | solution.py:945
  183.9 1.5 collective-permute-done.33.b_ref
  186.0 1.6 collective-permute-start.37
  190.7 2.0 collective-permute-done.37.by_ref
  192.7 1.5 collective-permute-done.36.ax_ref
  195.3 1.5 collective-permute-start.44
  196.8 7.2 %collective-permute-done.35.b_ref = bf16[144,1024]{1,0:T(8,128)(2,1)S(1)} collective-permute-done((bf16[144,1024]{1,0:T(8,128)(2,1)S(1)}, bf16[144,1024]{1,0:T(8,128)(2,1)S(1)}, u32[]{:S(2)}, u32[]{:S(2)}) %collective-permute-start.35) | collective-permute-done | bytes 294944 | tf_op jit(solution)/shard_map/ppermute | solution.py:945
  205.7 2.5 %collective-permute-start.41 = (bf16[144,1024]{1,0:T(8,128)(2,1)S(1)}, bf16[144,1024]{1,0:T(8,128)(2,1)S(1)}, u32[]{:S(2)}, u32[]{:S(2)}) collective-permute-start(bf16[144,1024]{1,0:T(8,128)(2,1)S(1)} %shard_map.242.a_ref), channel_id=1, source_target_pairs={{0,24},{4,28},{8,16},{12,20},{16,8},{20,12},{24,0},{28,4},{1,25},{... | collective-permute-start | bytes 884744 | tf_op jit(solution)/shard_map/ppermute | solution.py:948
  208.2 3.0 %shard_map.243 = (f32[1024,1024]{1,0:T(8,128)}, f32[1024,1024]{1,0:T(8,128)}) custom-call(s32[6]{0:T(128)S(1)} %copy-done.7, bf16[2,2,128,1024]{3,2,1,0:T(8,128)(2,1)S(1)} %get-tuple-element.286.own_ref, bf16[2,2,128,1024]{3,2,1,0:T(8,128)(2,1)S(1)} %collective-permute-done.38.other_ref), custom_call_target="tpu_custom_call" | custom-call | tf_op jit(solution)/shard_map/pallas_call | solution.py:898
  211.3 5.2 %collective-permute-done.39.b_ref = bf16[144,1024]{1,0:T(8,128)(2,1)S(1)} collective-permute-done((bf16[144,1024]{1,0:T(8,128)(2,1)S(1)}, bf16[144,1024]{1,0:T(8,128)(2,1)S(1)}, u32[]{:S(2)}, u32[]{:S(2)}) %collective-permute-start.39) | collective-permute-done | bytes 294944 | tf_op jit(solution)/shard_map/ppermute | solution.py:948
  216.4 6.6 %collective-permute-done.41.d_ref = bf16[144,1024]{1,0:T(8,128)(2,1)S(1)} collective-permute-done((bf16[144,1024]{1,0:T(8,128)(2,1)S(1)}, bf16[144,1024]{1,0:T(8,128)(2,1)S(1)}, u32[]{:S(2)}, u32[]{:S(2)}) %collective-permute-start.41) | collective-permute-done | bytes 294944 | tf_op jit(solution)/shard_map/ppermute | solution.py:948
  224.9 1.6 collective-permute-done.42.odd_ref
  226.6 2.8 %shard_map.246 = (f32[3,1024,256]{2,1,0:T(8,128)}, f32[256,1024]{1,0:T(8,128)}, f32[16,256]{1,0:T(8,128)}, f32[16,256]{1,0:T(8,128)}, f32[1,256]{1,0:T(1,128)}, /*index=5*/f32[1,1024]{1,0:T(1,128)}, f32[1,1024]{1,0:T(1,128)}) custom-call(s32[6]{0:T(128)S(1)} %copy-done.7, bf16[4,144,1024]{2,1,0:T(8,128)(2,1)S(1)} %shard_map.244.even_ref, ...), custom_call_target="tpu_custom_call" | custom-call | flops 8000000000 | tf_op jit(solution)/shard_map/pallas_call | solution.py:46
  229.4 3.1 %shard_map.247 = (f32[1024,1024]{1,0:T(8,128)}, f32[1024,1024]{1,0:T(8,128)}) custom-call(s32[6]{0:T(128)S(1)} %copy-done.7, bf16[2,2,128,1024]{3,2,1,0:T(8,128)(2,1)S(1)} %shard_map.245.own_ref, bf16[2,2,128,1024]{3,2,1,0:T(8,128)(2,1)S(1)} %collective-permute-done.45.other_ref, ...), custom_call_target="tpu_custom_call", output_to_operand_aliasing={{0}: (3, {}), {1}: (4, {})} | custom-call | tf_op jit(solution)/shard_map/pallas_call | solution.py:898
  (116 shorter events, 32.4 us)
Async XLA Ops:
  1.4 5.7 %copy-start.6 = (s32[6]{0:T(128)}, s32[6]{0:T(128)S(1)}, u32[]{:S(2)}) copy-start(s32[6]{0:T(128)S(1)} %stack.24.flag_ref) | copy-start | bytes 76
  1.4 1.0 copy-start.4
  2.4 0.7 copy-start.9
  4.0 22.7 %collective-permute-start = (bf16[256,1024]{1,0:T(8,128)(2,1)S(1)}, bf16[256,1024]{1,0:T(8,128)(2,1)S(1)}, u32[]{:S(2)}, u32[]{:S(2)}) collective-permute-start(bf16[256,1024]{1,0:T(8,128)(2,1)S(1)} %shard_map.203.own_ref), channel_id=1, source_target_pairs={{0,1},{1,0},{2,3},{3,2},{4,5},{5,4},{6,7},{7,6},{8,9},{9,8},{10,11... | collective-permute-start | bytes 1572872 | tf_op jit(solution)/shard_map/ppermute | solution.py:945
  7.1 5.6 %copy-start.12 = (bf16[1024,3,256]{2,0,1:T(8,128)(2,1)S(1)}, bf16[1024,3,256]{2,0,1:T(8,128)(2,1)}, u32[]{:S(2)}) copy-start(bf16[1024,3,256]{2,0,1:T(8,128)(2,1)} %param.15) | copy-start | bytes 4718596
  10.0 16.1 %collective-permute-start.1 = (bf16[176,1024]{1,0:T(8,128)(2,1)}, bf16[176,1024]{1,0:T(8,128)(2,1)S(1)}, u32[]{:S(2)}, u32[]{:S(2)}) collective-permute-start(bf16[176,1024]{1,0:T(8,128)(2,1)} %get-tuple-element.161), channel_id=1, source_target_pairs={{0,2},{1,3},{2,0},{3,1},{4,6},{5,7},{6,4},{7,5},{8,10},{9,11},{10,... | collective-permute-start | bytes 1081352 | tf_op jit(solution)/shard_map/ppermute | solution.py:945
  12.8 13.9 %copy-start.2 = (bf16[1,256,1024]{2,1,0:T(8,128)(2,1)S(1)}, bf16[1,256,1024]{2,1,0:T(8,128)(2,1)}, u32[]{:S(2)}) copy-start(bf16[1,256,1024]{2,1,0:T(8,128)(2,1)} %param.23) | copy-start | bytes 1572868
  12.8 18.3 %copy-start.7 = (s32[6]{0:T(128)S(1)}, s32[6]{0:T(128)}, u32[]{:S(2)}) copy-start(s32[6]{0:T(128)} %copy-done.6) | copy-start | bytes 76
  12.8 18.3 %copy-start.8 = (f32[48,256]{1,0:T(8,128)S(1)}, f32[48,256]{1,0:T(8,128)}, u32[]{:S(2)}) copy-start(f32[48,256]{1,0:T(8,128)} %get-tuple-element.164.own_ref) | copy-start | bytes 147460
  12.8 20.4 %copy-start.14 = (bf16[128,1024]{1,0:T(8,128)(2,1)S(1)}, bf16[128,1024]{1,0:T(8,128)(2,1)}, u32[]{:S(2)}) copy-start(bf16[128,1024]{1,0:T(8,128)(2,1)} %get-tuple-element.177) | copy-start | bytes 786436
  26.8 20.7 %collective-permute-start.4 = (bf16[256,1024]{1,0:T(8,128)(2,1)S(1)}, bf16[256,1024]{1,0:T(8,128)(2,1)S(1)}, u32[]{:S(2)}, u32[]{:S(2)}) collective-permute-start(bf16[256,1024]{1,0:T(8,128)(2,1)S(1)} %bitcast.47), channel_id=1, source_target_pairs={{0,1},{1,0},{2,3},{3,2},{4,5},{5,4},{6,7},{7,6},{8,9},{9,8},{10,11... | collective-permute-start | bytes 1572872 | tf_op jit(solution)/shard_map/ppermute | solution.py:945
  29.5 10.1 %collective-permute-start.2 = (bf16[128,1024]{1,0:T(8,128)(2,1)S(1)}, bf16[128,1024]{1,0:T(8,128)(2,1)S(1)}, u32[]{:S(2)}, u32[]{:S(2)}) collective-permute-start(bf16[128,1024]{1,0:T(8,128)(2,1)S(1)} %slice.54.a_ref), channel_id=1, source_target_pairs={{0,8},{4,12},{8,0},{12,4},{16,24},{20,28},{24,16},{28,20},{1,9},{5... | collective-permute-start | bytes 786440 | tf_op jit(solution)/shard_map/ppermute | solution.py:948
  31.7 15.8 %collective-permute-start.3 = (bf16[128,1024]{1,0:T(8,128)(2,1)S(1)}, bf16[128,1024]{1,0:T(8,128)(2,1)S(1)}, u32[]{:S(2)}, u32[]{:S(2)}) collective-permute-start(bf16[128,1024]{1,0:T(8,128)(2,1)S(1)} %slice.54.a_ref), channel_id=1, source_target_pairs={{0,16},{4,20},{8,24},{12,28},{16,0},{20,4},{24,8},{28,12},{1,17},{... | collective-permute-start | bytes 786440 | tf_op jit(solution)/shard_map/ppermute | solution.py:948
  33.2 14.2 %collective-permute-start.5 = (bf16[128,1024]{1,0:T(8,128)(2,1)S(1)}, bf16[128,1024]{1,0:T(8,128)(2,1)S(1)}, u32[]{:S(2)}, u32[]{:S(2)}) collective-permute-start(bf16[128,1024]{1,0:T(8,128)(2,1)S(1)} %copy-done.14), channel_id=1, source_target_pairs={{0,2},{1,3},{2,0},{3,1},{4,6},{5,7},{6,4},{7,5},{8,10},{9,11},{10,... | collective-permute-start | bytes 786440 | tf_op jit(solution)/shard_map/ppermute | solution.py:945
  39.6 10.1 %copy-start.13 = (bf16[128,1024]{1,0:T(8,128)(2,1)S(1)}, bf16[128,1024]{1,0:T(8,128)(2,1)}, u32[]{:S(2)}) copy-start(bf16[128,1024]{1,0:T(8,128)(2,1)} %get-tuple-element.196) | copy-start | bytes 786436
  39.6 9.3 %collective-permute-start.6 = (bf16[128,1024]{1,0:T(8,128)(2,1)S(1)}, bf16[128,1024]{1,0:T(8,128)(2,1)S(1)}, u32[]{:S(2)}, u32[]{:S(2)}) collective-permute-start(bf16[128,1024]{1,0:T(8,128)(2,1)S(1)} %collective-permute-done.2.b_ref), channel_id=1, source_target_pairs={{0,16},{4,20},{8,24},{12,28},{16,0},{20,4},{24,8},{28,12},{1,17},{... | collective-permute-start | bytes 786440 | tf_op jit(solution)/shard_map/ppermute | solution.py:948
  40.2 9.5 %collective-permute-start.8 = (bf16[176,512]{1,0:T(8,128)(2,1)S(1)}, bf16[176,512]{1,0:T(8,128)(2,1)S(1)}, u32[]{:S(2)}, u32[]{:S(2)}) collective-permute-start(bf16[176,512]{1,0:T(8,128)(2,1)S(1)} %get-tuple-element.174), channel_id=1, source_target_pairs={{0,2},{1,3},{4,6},{5,7},{8,10},{9,11},{12,14},{13,15},{16,18},{17,... | collective-permute-start | bytes 540680 | tf_op jit(solution)/shard_map/ppermute | solution.py:1013
  49.6 7.2 %collective-permute-start.7 = (bf16[4,128,1024]{2,1,0:T(8,128)(2,1)S(1)}, bf16[4,128,1024]{2,1,0:T(8,128)(2,1)S(1)}, u32[]{:S(2)}, u32[]{:S(2)}) collective-permute-start(bf16[4,128,1024]{2,1,0:T(8,128)(2,1)S(1)} %shard_map.208.even_ref), channel_id=1, source_target_pairs={{0,4},{4,0},{8,12},{12,8},{16,20},{20,16},{24,28},{28,24},{1,5},{5... | collective-permute-start | bytes 3145736 | tf_op jit(solution)/shard_map/ppermute | solution.py:948
  49.7 16.1 %collective-permute-start.11 = (bf16[128,1024]{1,0:T(8,128)(2,1)S(1)}, bf16[128,1024]{1,0:T(8,128)(2,1)S(1)}, u32[]{:S(2)}, u32[]{:S(2)}) collective-permute-start(bf16[128,1024]{1,0:T(8,128)(2,1)S(1)} %copy-done.13), channel_id=1, source_target_pairs={{0,2},{1,3},{2,0},{3,1},{4,6},{5,7},{6,4},{7,5},{8,10},{9,11},{10,... | collective-permute-start | bytes 786440 | tf_op jit(solution)/shard_map/ppermute | solution.py:945
  54.9 3.6 %copy-start.3 = (bf16[256,1024]{1,0:T(8,128)(2,1)S(1)}, bf16[256,1024]{1,0:T(8,128)(2,1)}, u32[]{:S(2)}) copy-start(bf16[256,1024]{1,0:T(8,128)(2,1)} %out_near_ref.3) | copy-start | bytes 1572868
  58.5 19.0 %copy-start.5 = (bf16[1,256,1024]{2,1,0:T(8,128)(2,1)S(1)}, bf16[1,256,1024]{2,1,0:T(8,128)(2,1)}, u32[]{:S(2)}) copy-start(bf16[1,256,1024]{2,1,0:T(8,128)(2,1)} %param.12) | copy-start | bytes 1572868
  58.5 19.0 %copy-start.11 = (f32[1024]{0:T(1024)S(1)}, f32[1024]{0:T(1024)}, u32[]{:S(2)}) copy-start(f32[1024]{0:T(1024)} %param.20) | copy-start | bytes 12292
  61.1 16.3 %collective-permute-start.9 = (bf16[256,1024]{1,0:T(8,128)(2,1)S(1)}, bf16[256,1024]{1,0:T(8,128)(2,1)S(1)}, u32[]{:S(2)}, u32[]{:S(2)}) collective-permute-start(bf16[256,1024]{1,0:T(8,128)(2,1)S(1)} %get-tuple-element.195), channel_id=1, source_target_pairs={{0,1},{1,0},{2,3},{3,2},{4,5},{5,4},{6,7},{7,6},{8,9},{9,8},{10,11... | collective-permute-start | bytes 1572872 | tf_op jit(solution)/shard_map/ppermute | solution.py:945
  64.6 6.4 %collective-permute-start.10 = (bf16[128,1024]{1,0:T(8,128)(2,1)S(1)}, bf16[128,1024]{1,0:T(8,128)(2,1)S(1)}, u32[]{:S(2)}, u32[]{:S(2)}) collective-permute-start(bf16[128,1024]{1,0:T(8,128)(2,1)S(1)} %collective-permute-done.5.a_ref), channel_id=1, source_target_pairs={{0,8},{4,12},{8,0},{12,4},{16,24},{20,28},{24,16},{28,20},{1,9},{5... | collective-permute-start | bytes 786440 | tf_op jit(solution)/shard_map/ppermute | solution.py:948
  65.8 7.9 %collective-permute-start.12 = (bf16[128,1024]{1,0:T(8,128)(2,1)S(1)}, bf16[128,1024]{1,0:T(8,128)(2,1)S(1)}, u32[]{:S(2)}, u32[]{:S(2)}) collective-permute-start(bf16[128,1024]{1,0:T(8,128)(2,1)S(1)} %collective-permute-done.11.b_ref), channel_id=1, source_target_pairs={{0,16},{4,20},{8,24},{12,28},{16,0},{20,4},{24,8},{28,12},{1,17},{... | collective-permute-start | bytes 786440 | tf_op jit(solution)/shard_map/ppermute | solution.py:948
  74.4 12.7 %collective-permute-start.15 = (bf16[2,128,1024]{2,1,0:T(8,128)(2,1)S(1)}, bf16[2,128,1024]{2,1,0:T(8,128)(2,1)S(1)}, u32[]{:S(2)}, u32[]{:S(2)}) collective-permute-start(bf16[2,128,1024]{2,1,0:T(8,128)(2,1)S(1)} %get-tuple-element.202.b_ref), channel_id=1, source_target_pairs={{0,8},{4,12},{8,0},{12,4},{16,24},{20,28},{24,16},{28,20},{1,9},{5... | collective-permute-start | bytes 1572872 | tf_op jit(solution)/shard_map/ppermute | solution.py:948
  75.9 12.4 %collective-permute-start.14 = (bf16[2,128,1024]{2,1,0:T(8,128)(2,1)S(1)}, bf16[2,128,1024]{2,1,0:T(8,128)(2,1)S(1)}, u32[]{:S(2)}, u32[]{:S(2)}) collective-permute-start(bf16[2,128,1024]{2,1,0:T(8,128)(2,1)S(1)} %get-tuple-element.201.a_ref), channel_id=1, source_target_pairs={{0,16},{4,20},{8,24},{12,28},{16,0},{20,4},{24,8},{28,12},{1,17},{... | collective-permute-start | bytes 1572872 | tf_op jit(solution)/shard_map/ppermute | solution.py:948
  78.4 13.0 %collective-permute-start.13 = (bf16[256,1024]{1,0:T(8,128)(2,1)S(1)}, bf16[256,1024]{1,0:T(8,128)(2,1)S(1)}, u32[]{:S(2)}, u32[]{:S(2)}) collective-permute-start(bf16[256,1024]{1,0:T(8,128)(2,1)S(1)} %get-tuple-element.218.n_ref), channel_id=1, source_target_pairs={{0,1},{1,0},{2,3},{3,2},{4,5},{5,4},{6,7},{7,6},{8,9},{9,8},{10,11... | collective-permute-start | bytes 1572872 | tf_op jit(solution)/shard_map/ppermute | solution.py:945
  87.1 4.3 %copy-start = (bf16[1024,1024]{1,0:T(8,128)(2,1)S(1)}, bf16[1024,1024]{1,0:T(8,128)(2,1)}, u32[]{:S(2)}) copy-start(bf16[1024,1024]{1,0:T(8,128)(2,1)} %up0_ref.3) | copy-start | bytes 6291460
  87.1 4.3 %copy-start.1 = (bf16[1024,1024]{1,0:T(8,128)(2,1)S(1)}, bf16[1024,1024]{1,0:T(8,128)(2,1)}, u32[]{:S(2)}) copy-start(bf16[1024,1024]{1,0:T(8,128)(2,1)} %down0_ref.3) | copy-start | bytes 6291460
  89.0 4.2 %collective-permute-start.16 = (bf16[4,2,128,1024]{3,2,1,0:T(8,128)(2,1)S(1)}, bf16[4,2,128,1024]{3,2,1,0:T(8,128)(2,1)S(1)}, u32[]{:S(2)}, u32[]{:S(2)}) collective-permute-start(bf16[4,2,128,1024]{3,2,1,0:T(8,128)(2,1)S(1)} %shard_map.215.even_ref), channel_id=1, source_target_pairs={{0,4},{4,0},{8,12},{12,8},{16,20},{20,16},{24,28},{28,24},{1,5},{5... | collective-permute-start | bytes 6291464 | tf_op jit(solution)/shard_map/ppermute | solution.py:948
  100.9 14.0 %collective-permute-start.17 = (bf16[256,1024]{1,0:T(8,128)(2,1)S(1)}, bf16[256,1024]{1,0:T(8,128)(2,1)S(1)}, u32[]{:S(2)}, u32[]{:S(2)}) collective-permute-start(bf16[256,1024]{1,0:T(8,128)(2,1)S(1)} %get-tuple-element.217), channel_id=1, source_target_pairs={{0,1},{1,0},{2,3},{3,2},{4,5},{5,4},{6,7},{7,6},{8,9},{9,8},{10,11... | collective-permute-start | bytes 1572872 | tf_op jit(solution)/shard_map/ppermute | solution.py:945
  110.0 6.7 %collective-permute-start.20 = (bf16[1024,1024]{1,0:T(8,128)(2,1)S(1)}, bf16[1024,1024]{1,0:T(8,128)(2,1)S(1)}, u32[]{:S(2)}, u32[]{:S(2)}) collective-permute-start(bf16[1024,1024]{1,0:T(8,128)(2,1)S(1)} %shard_map.220), channel_id=1, source_target_pairs={{0,4},{4,0},{8,12},{12,8},{16,20},{20,16},{24,28},{28,24},{1,5},{5... | collective-permute-start | bytes 6291464 | tf_op jit(solution)/shard_map/ppermute | solution.py:948
  111.9 8.3 %collective-permute-start.19 = (bf16[512,2048]{1,0:T(8,128)(2,1)S(1)}, bf16[512,2048]{1,0:T(8,128)(2,1)S(1)}, u32[]{:S(2)}, u32[]{:S(2)}) collective-permute-start(bf16[512,2048]{1,0:T(8,128)(2,1)S(1)} %shard_map.221), channel_id=1, source_target_pairs={{0,4},{4,0},{8,12},{12,8},{16,20},{20,16},{24,28},{28,24},{1,5},{5... | collective-permute-start | bytes 6291464 | tf_op jit(solution)/shard_map/ppermute | solution.py:948
  116.3 13.2 %collective-permute-start.18 = (bf16[256,1024]{1,0:T(8,128)(2,1)S(1)}, bf16[256,1024]{1,0:T(8,128)(2,1)S(1)}, u32[]{:S(2)}, u32[]{:S(2)}) collective-permute-start(bf16[256,1024]{1,0:T(8,128)(2,1)S(1)} %get-tuple-element.227.own_ref), channel_id=1, source_target_pairs={{0,1},{1,0},{2,3},{3,2},{4,5},{5,4},{6,7},{7,6},{8,9},{9,8},{10,11... | collective-permute-start | bytes 1572872 | tf_op jit(solution)/shard_map/ppermute | solution.py:945
  118.6 24.3 %collective-permute-start.23 = (bf16[512,1024]{1,0:T(8,128)(2,1)S(1)}, bf16[512,1024]{1,0:T(8,128)(2,1)S(1)}, u32[]{:S(2)}, u32[]{:S(2)}) collective-permute-start(bf16[512,1024]{1,0:T(8,128)(2,1)S(1)} %get-tuple-element.231), channel_id=1, source_target_pairs={{0,8},{4,12},{8,0},{12,4},{16,24},{20,28},{24,16},{28,20},{1,9},{5... | collective-permute-start | bytes 3145736 | tf_op jit(solution)/shard_map/ppermute | solution.py:948
  122.1 23.9 %collective-permute-start.22 = (bf16[256,2048]{1,0:T(8,128)(2,1)S(1)}, bf16[256,2048]{1,0:T(8,128)(2,1)S(1)}, u32[]{:S(2)}, u32[]{:S(2)}) collective-permute-start(bf16[256,2048]{1,0:T(8,128)(2,1)S(1)} %get-tuple-element.234), channel_id=1, source_target_pairs={{0,16},{4,20},{8,24},{12,28},{16,0},{20,4},{24,8},{28,12},{1,17},{... | collective-permute-start | bytes 3145736 | tf_op jit(solution)/shard_map/ppermute | solution.py:948
  130.9 23.4 %collective-permute-start.28 = (bf16[256,1024]{1,0:T(8,128)(2,1)S(1)}, bf16[256,1024]{1,0:T(8,128)(2,1)S(1)}, u32[]{:S(2)}, u32[]{:S(2)}) collective-permute-start(bf16[256,1024]{1,0:T(8,128)(2,1)S(1)} %get-tuple-element.254), channel_id=1, source_target_pairs={{0,1},{1,0},{2,3},{3,2},{4,5},{5,4},{6,7},{7,6},{8,9},{9,8},{10,11... | collective-permute-start | bytes 1572872 | tf_op jit(solution)/shard_map/ppermute | solution.py:945
  136.8 10.6 %collective-permute-start.21 = (bf16[176,512]{1,0:T(8,128)(2,1)S(1)}, bf16[176,512]{1,0:T(8,128)(2,1)S(1)}, u32[]{:S(2)}, u32[]{:S(2)}) collective-permute-start(bf16[176,512]{1,0:T(8,128)(2,1)S(1)} %get-tuple-element.241), channel_id=1, source_target_pairs={{2,0},{3,1},{6,4},{7,5},{10,8},{11,9},{14,12},{15,13},{18,16},{19,... | collective-permute-start | bytes 540680 | tf_op jit(solution)/shard_map/ppermute | solution.py:1146
  142.8 11.5 %collective-permute-start.27 = (bf16[512,2048]{1,0:T(8,128)(2,1)S(1)}, bf16[512,2048]{1,0:T(8,128)(2,1)S(1)}, u32[]{:S(2)}, u32[]{:S(2)}) collective-permute-start(bf16[512,2048]{1,0:T(8,128)(2,1)S(1)} %shard_map.228), channel_id=1, source_target_pairs={{0,4},{4,0},{8,12},{12,8},{16,20},{20,16},{24,28},{28,24},{1,5},{5... | collective-permute-start | bytes 6291464 | tf_op jit(solution)/shard_map/ppermute | solution.py:948
  143.6 16.1 %collective-permute-start.26 = (bf16[256,1024]{1,0:T(8,128)(2,1)S(1)}, bf16[256,1024]{1,0:T(8,128)(2,1)S(1)}, u32[]{:S(2)}, u32[]{:S(2)}) collective-permute-start(bf16[256,1024]{1,0:T(8,128)(2,1)S(1)} %get-tuple-element.247), channel_id=1, source_target_pairs={{0,16},{4,20},{8,24},{12,28},{16,0},{20,4},{24,8},{28,12},{1,17},{... | collective-permute-start | bytes 1572872 | tf_op jit(solution)/shard_map/ppermute | solution.py:948
  146.7 16.0 %collective-permute-start.25 = (bf16[128,2048]{1,0:T(8,128)(2,1)S(1)}, bf16[128,2048]{1,0:T(8,128)(2,1)S(1)}, u32[]{:S(2)}, u32[]{:S(2)}) collective-permute-start(bf16[128,2048]{1,0:T(8,128)(2,1)S(1)} %get-tuple-element.250), channel_id=1, source_target_pairs={{0,8},{4,12},{8,0},{12,4},{16,24},{20,28},{24,16},{28,20},{1,9},{5... | collective-permute-start | bytes 1572872 | tf_op jit(solution)/shard_map/ppermute | solution.py:948
  152.5 20.3 %collective-permute-start.24 = (bf16[256,1024]{1,0:T(8,128)(2,1)S(1)}, bf16[256,1024]{1,0:T(8,128)(2,1)S(1)}, u32[]{:S(2)}, u32[]{:S(2)}) collective-permute-start(bf16[256,1024]{1,0:T(8,128)(2,1)S(1)} %get-tuple-element.253), channel_id=1, source_target_pairs={{0,1},{1,0},{2,3},{3,2},{4,5},{5,4},{6,7},{7,6},{8,9},{9,8},{10,11... | collective-permute-start | bytes 1572872 | tf_op jit(solution)/shard_map/ppermute | solution.py:945
  156.2 32.8 %collective-permute-start.29 = (bf16[128,2048]{1,0:T(8,128)(2,1)S(1)}, bf16[128,2048]{1,0:T(8,128)(2,1)S(1)}, u32[]{:S(2)}, u32[]{:S(2)}) collective-permute-start(bf16[128,2048]{1,0:T(8,128)(2,1)S(1)} %get-tuple-element.260), channel_id=1, source_target_pairs={{0,16},{4,20},{8,24},{12,28},{16,0},{20,4},{24,8},{28,12},{1,17},{... | collective-permute-start | bytes 1572872 | tf_op jit(solution)/shard_map/ppermute | solution.py:948
  157.7 31.2 %collective-permute-start.30 = (bf16[128,2048]{1,0:T(8,128)(2,1)S(1)}, bf16[128,2048]{1,0:T(8,128)(2,1)S(1)}, u32[]{:S(2)}, u32[]{:S(2)}) collective-permute-start(bf16[128,2048]{1,0:T(8,128)(2,1)S(1)} %get-tuple-element.261), channel_id=1, source_target_pairs={{0,8},{4,12},{8,0},{12,4},{16,24},{20,28},{24,16},{28,20},{1,9},{5... | collective-permute-start | bytes 1572872 | tf_op jit(solution)/shard_map/ppermute | solution.py:948
  160.3 21.5 %collective-permute-start.34 = (bf16[128,1024]{1,0:T(8,128)(2,1)S(1)}, bf16[128,1024]{1,0:T(8,128)(2,1)S(1)}, u32[]{:S(2)}, u32[]{:S(2)}) collective-permute-start(bf16[128,1024]{1,0:T(8,128)(2,1)S(1)} %get-tuple-element.265), channel_id=1, source_target_pairs={{0,2},{1,3},{2,0},{3,1},{4,6},{5,7},{6,4},{7,5},{8,10},{9,11},{10,... | collective-permute-start | bytes 786440 | tf_op jit(solution)/shard_map/ppermute | solution.py:945
  163.3 22.1 %collective-permute-start.33 = (bf16[128,1024]{1,0:T(8,128)(2,1)S(1)}, bf16[128,1024]{1,0:T(8,128)(2,1)S(1)}, u32[]{:S(2)}, u32[]{:S(2)}) collective-permute-start(bf16[128,1024]{1,0:T(8,128)(2,1)S(1)} %get-tuple-element.268), channel_id=1, source_target_pairs={{0,2},{1,3},{2,0},{3,1},{4,6},{5,7},{6,4},{7,5},{8,10},{9,11},{10,... | collective-permute-start | bytes 786440 | tf_op jit(solution)/shard_map/ppermute | solution.py:945
  165.6 11.4 %copy-start.10 = (f32[1024]{0:T(1024)S(1)}, f32[1024]{0:T(1024)}, u32[]{:S(2)}) copy-start(f32[1024]{0:T(1024)} %param.14) | copy-start | bytes 12292
  172.7 16.2 %collective-permute-start.31 = (bf16[128,2048]{1,0:T(8,128)(2,1)S(1)}, bf16[128,2048]{1,0:T(8,128)(2,1)S(1)}, u32[]{:S(2)}, u32[]{:S(2)}) collective-permute-start(bf16[128,2048]{1,0:T(8,128)(2,1)S(1)} %get-tuple-element.262), channel_id=1, source_target_pairs={{0,24},{4,28},{8,16},{12,20},{16,8},{20,12},{24,0},{28,4},{1,25},{... | collective-permute-start | bytes 1572872 | tf_op jit(solution)/shard_map/ppermute | solution.py:948
  181.8 5.7 %collective-permute-start.32 = (f32[8,256]{1,0:T(8,128)S(1)}, f32[8,256]{1,0:T(8,128)S(1)}, u32[]{:S(2)}, u32[]{:S(2)}) collective-permute-start(f32[8,256]{1,0:T(8,128)S(1)} %get-tuple-element.272.gains_ref), channel_id=1, source_target_pairs={{0,1},{1,0},{2,3},{3,2},{4,5},{5,4},{6,7},{7,6},{8,9},{9,8},{10,11... | collective-permute-start | bytes 24584 | tf_op jit(solution)/shard_map/ppermute | solution.py:945
  186.0 6.7 %collective-permute-start.37 = (bf16[128,1024]{1,0:T(8,128)(2,1)S(1)}, bf16[128,1024]{1,0:T(8,128)(2,1)S(1)}, u32[]{:S(2)}, u32[]{:S(2)}) collective-permute-start(bf16[128,1024]{1,0:T(8,128)(2,1)S(1)} %shard_map.239.b_ref), channel_id=1, source_target_pairs={{0,16},{4,20},{8,24},{12,28},{16,0},{20,4},{24,8},{28,12},{1,17},{... | collective-permute-start | bytes 786440 | tf_op jit(solution)/shard_map/ppermute | solution.py:948
  187.5 6.6 %collective-permute-start.36 = (bf16[128,1024]{1,0:T(8,128)(2,1)S(1)}, bf16[128,1024]{1,0:T(8,128)(2,1)S(1)}, u32[]{:S(2)}, u32[]{:S(2)}) collective-permute-start(bf16[128,1024]{1,0:T(8,128)(2,1)S(1)} %shard_map.238.a_ref), channel_id=1, source_target_pairs={{0,8},{4,12},{8,0},{12,4},{16,24},{20,28},{24,16},{28,20},{1,9},{5... | collective-permute-start | bytes 786440 | tf_op jit(solution)/shard_map/ppermute | solution.py:948
  189.8 14.3 %collective-permute-start.35 = (bf16[144,1024]{1,0:T(8,128)(2,1)S(1)}, bf16[144,1024]{1,0:T(8,128)(2,1)S(1)}, u32[]{:S(2)}, u32[]{:S(2)}) collective-permute-start(bf16[144,1024]{1,0:T(8,128)(2,1)S(1)} %get-tuple-element.281), channel_id=1, source_target_pairs={{0,2},{1,3},{2,0},{3,1},{4,6},{5,7},{6,4},{7,5},{8,10},{9,11},{10,... | collective-permute-start | bytes 884744 | tf_op jit(solution)/shard_map/ppermute | solution.py:945
  194.8 9.8 %collective-permute-start.38 = (bf16[2,2,128,1024]{3,2,1,0:T(8,128)(2,1)S(1)}, bf16[2,2,128,1024]{3,2,1,0:T(8,128)(2,1)S(1)}, u32[]{:S(2)}, u32[]{:S(2)}) collective-permute-start(bf16[2,2,128,1024]{3,2,1,0:T(8,128)(2,1)S(1)} %get-tuple-element.286.own_ref), channel_id=1, source_target_pairs={{0,4},{4,0},{8,12},{12,8},{16,20},{20,16},{24,28},{28,24},{1,5},{5... | collective-permute-start | bytes 3145736 | tf_op jit(solution)/shard_map/ppermute | solution.py:948
  194.9 28.9 %collective-permute-start.43 = (bf16[2,128,1024]{2,1,0:T(8,128)(2,1)S(1)}, bf16[2,128,1024]{2,1,0:T(8,128)(2,1)S(1)}, u32[]{:S(2)}, u32[]{:S(2)}) collective-permute-start(bf16[2,128,1024]{2,1,0:T(8,128)(2,1)S(1)} %get-tuple-element.284), channel_id=1, source_target_pairs={{0,16},{4,20},{8,24},{12,28},{16,0},{20,4},{24,8},{28,12},{1,17},{... | collective-permute-start | bytes 1572872 | tf_op jit(solution)/shard_map/ppermute | solution.py:948
  195.3 28.4 %collective-permute-start.44 = (bf16[2,128,1024]{2,1,0:T(8,128)(2,1)S(1)}, bf16[2,128,1024]{2,1,0:T(8,128)(2,1)S(1)}, u32[]{:S(2)}, u32[]{:S(2)}) collective-permute-start(bf16[2,128,1024]{2,1,0:T(8,128)(2,1)S(1)} %get-tuple-element.285), channel_id=1, source_target_pairs={{0,8},{4,12},{8,0},{12,4},{16,24},{20,28},{24,16},{28,20},{1,9},{5... | collective-permute-start | bytes 1572872 | tf_op jit(solution)/shard_map/ppermute | solution.py:948
  204.7 11.8 %collective-permute-start.39 = (bf16[144,1024]{1,0:T(8,128)(2,1)S(1)}, bf16[144,1024]{1,0:T(8,128)(2,1)S(1)}, u32[]{:S(2)}, u32[]{:S(2)}) collective-permute-start(bf16[144,1024]{1,0:T(8,128)(2,1)S(1)} %shard_map.242.a_ref), channel_id=1, source_target_pairs={{0,8},{4,12},{8,0},{12,4},{16,24},{20,28},{24,16},{28,20},{1,9},{5... | collective-permute-start | bytes 884744 | tf_op jit(solution)/shard_map/ppermute | solution.py:948
  205.3 11.1 %collective-permute-start.40 = (bf16[144,1024]{1,0:T(8,128)(2,1)S(1)}, bf16[144,1024]{1,0:T(8,128)(2,1)S(1)}, u32[]{:S(2)}, u32[]{:S(2)}) collective-permute-start(bf16[144,1024]{1,0:T(8,128)(2,1)S(1)} %shard_map.242.a_ref), channel_id=1, source_target_pairs={{0,16},{4,20},{8,24},{12,28},{16,0},{20,4},{24,8},{28,12},{1,17},{... | collective-permute-start | bytes 884744 | tf_op jit(solution)/shard_map/ppermute | solution.py:948
  205.7 17.4 %collective-permute-start.41 = (bf16[144,1024]{1,0:T(8,128)(2,1)S(1)}, bf16[144,1024]{1,0:T(8,128)(2,1)S(1)}, u32[]{:S(2)}, u32[]{:S(2)}) collective-permute-start(bf16[144,1024]{1,0:T(8,128)(2,1)S(1)} %shard_map.242.a_ref), channel_id=1, source_target_pairs={{0,24},{4,28},{8,16},{12,20},{16,8},{20,12},{24,0},{28,4},{1,25},{... | collective-permute-start | bytes 884744 | tf_op jit(solution)/shard_map/ppermute | solution.py:948
  223.7 2.9 %collective-permute-start.42 = (bf16[4,144,1024]{2,1,0:T(8,128)(2,1)S(1)}, bf16[4,144,1024]{2,1,0:T(8,128)(2,1)S(1)}, u32[]{:S(2)}, u32[]{:S(2)}) collective-permute-start(bf16[4,144,1024]{2,1,0:T(8,128)(2,1)S(1)} %shard_map.244.even_ref), channel_id=1, source_target_pairs={{0,4},{4,0},{8,12},{12,8},{16,20},{20,16},{24,28},{28,24},{1,5},{5... | collective-permute-start | bytes 3538952 | tf_op jit(solution)/shard_map/ppermute | solution.py:948
  224.4 5.0 %collective-permute-start.45 = (bf16[2,2,128,1024]{3,2,1,0:T(8,128)(2,1)S(1)}, bf16[2,2,128,1024]{3,2,1,0:T(8,128)(2,1)S(1)}, u32[]{:S(2)}, u32[]{:S(2)}) collective-permute-start(bf16[2,2,128,1024]{3,2,1,0:T(8,128)(2,1)S(1)} %shard_map.245.own_ref), channel_id=1, source_target_pairs={{0,4},{4,0},{8,12},{12,8},{16,20},{20,16},{24,28},{28,24},{1,5},{5... | collective-permute-start | bytes 3145736 | tf_op jit(solution)/shard_map/ppermute | solution.py:948

commit v6 on v5

--- a/solution.py
+++ b/solution.py
@@ -167,9 +167,9 @@
 
 def touch(flag_ref, up_ref, down_ref, cot_ref, paired_ref, rows_ref, out_ref):
     out_ref[...] = (
-        (up_ref[:8, :128] + down_ref[:8, :128])
-        + (cot_ref[:8, :128] + paired_ref[:8, :128])
-        + rows_ref[:8, :128]
+        (up_ref[:16, :128] + down_ref[:16, :128])
+        + (cot_ref[:16, :128] + paired_ref[:16, :128])
+        + rows_ref[:16, :128]
     )
 
 
@@ -775,13 +775,13 @@
         ].astype(ref.dtype)
         small = jnp.concatenate(
             [param_ref[:, slot * channels : (slot + 1) * channels], gains], axis=0
-        ).astype(ref.dtype)
+        )
         count = small.shape[0] // 4
+        rest = jnp.zeros((ref.shape[0] - rows - count, channels), f32)
         for quarter in range(4):
-            ref[rows : rows + count, quarter * channels : (quarter + 1) * channels] = small[
-                quarter * count : (quarter + 1) * count
-            ]
-        ref[rows + count :, :] = jnp.zeros((ref.shape[0] - rows - count, 4 * channels), ref.dtype)
+            ref[rows:, quarter * channels : (quarter + 1) * channels] = jnp.concatenate(
+                [small[quarter * count : (quarter + 1) * count], rest], axis=0
+            ).astype(ref.dtype)
 
 
 def add_two(flag_ref, a_ref, b_ref, out_ref):
@@ -1081,7 +1081,7 @@
     mlp_odd = swap_dp(mlp_even, 1)
     paired_two = order(paired_two)
     warm = order.done(
-        call(touch, shape((8, 128), bf16), micros=30)(
+        call(touch, shape((16, 128), bf16), micros=30)(
             flags, up_weight, down_weight, cot, paired_cot, paired_two
         )
     )
@@ -1208,9 +1208,6 @@
         )
     )
     gains_received = swap_mp(gains, 1)
-    output = order.done(
-        call(add_three, half_low)(flags, middle, order(down_own), down_received)
-    )
     down_mine = order.done(
         call(add_two, slice_shape)(flags, down_near, order(down_received_far))
     )
@@ -1236,6 +1233,9 @@
     down_y = swap_dp(down_two, 4)
     up_x = swap_dp(up_two, 2)
     first_others = swap_dp(first_pieces, 1)
+    output = order.done(
+        call(add_three, half_low)(flags, middle, order(down_own), down_received)
+    )
     attn_slice_grad = order.done(
         call(add_two, low(slice_rows, 4 * channels), micros=20)(
             flags, attn_near, order(attn_received)

time: 233 us -> 233 us (level)
  starting transfers between devices: 58.8 us -> 54.3 us
  waiting for transfers between devices: 82.7 us -> 87 us
    ppermute x15, starting transfers between devices: 26.4 us -> 23.8 us  [swap_mp(): return lax.ppermute(value, 'mp', [(k, k ^ mask) for k in range(4)])]
  transfers between devices with their start and end apart: 46 -> 46, of which waited for: 23 -> 25; matrix products, arithmetic and copies ran while one was open for 0% -> 0% of each run, Pallas kernels for 32% -> 32%
where the time goes in v6:
time: 233 us; the launch traced here: 232 us
  waiting for transfers between devices  87 us (37%)
  Pallas kernels  86.6 us (37%)
  starting transfers between devices  54.3 us (23%)
  local copies, waits for them, and re-layouts  2.4 us (1%)
    pallas_call x40, Pallas kernels, run(): pl.pallas_call(kernel, out_shape=out_shape, in_specs=[pl.BlockSpec(memory...  63.7 us
    ppermute x15, waiting for transfers between devices, swap_mp(): return lax.ppermute(value, 'mp', [(k, k ^ mask) for k in range(4)])  49.8 us
    ppermute x29, waiting for transfers between devices, swap_dp(): return lax.ppermute(value, 'dp', [(k, k ^ mask) for k in range(dp_size)])  36.7 us
    ppermute x29, starting transfers between devices, swap_dp(): return lax.ppermute(value, 'dp', [(k, k ^ mask) for k in range(dp_size)])  26.5 us
    ppermute x15, starting transfers between devices, swap_mp(): return lax.ppermute(value, 'mp', [(k, k ^ mask) for k in range(4)])  23.8 us
    pallas_call x2, Pallas kernels, run_feed_forward(): pl.pallas_call(feed_forward, grid=(2 * per,), out_shape=(shape((tokens, 2...  13.9 us
    pallas_call x2, Pallas kernels, run_place_wide(): pl.pallas_call(place_wide, grid_spec=pltpu.PrefetchScalarGridSpec(num_sca...  6.09 us
  transfers between devices with their start and end apart: 46, of which 25 were waited for; matrix products, arithmetic and copies ran while one was open for 0% of the time, Pallas kernels for 32%

profile of v6, /device:TPU:0, one launch (start us, length us, event | category | flops | bytes accessed | tf_op | source)
XLA Modules:
  0.0 232.2 jit_solution(6662990708960992260)
XLA Ops:
  4.0 3.1 %collective-permute-start = (bf16[256,1024]{1,0:T(8,128)(2,1)S(1)}, bf16[256,1024]{1,0:T(8,128)(2,1)S(1)}, u32[]{:S(2)}, u32[]{:S(2)}) collective-permute-start(bf16[256,1024]{1,0:T(8,128)(2,1)S(1)} %shard_map.203.own_ref), channel_id=1, source_target_pairs={{0,1},{1,0},{2,3},{3,2},{4,5},{5,4},{6,7},{7,6},{8,9},{9,8},{10,11... | collective-permute-start | bytes 1572872 | tf_op jit(solution)/shard_map/ppermute | solution.py:945
  7.1 2.9 %shard_map.204 = (bf16[176,1024]{1,0:T(8,128)(2,1)}, bf16[128,1024]{1,0:T(8,128)(2,1)}, bf16[128,1024]{1,0:T(8,128)(2,1)}, f32[48,256]{1,0:T(8,128)}) custom-call(s32[6]{0:T(128)} %copy-done.6, bf16[3,1024,256]{2,1,0:T(8,128)(2,1)} %bitcast.60, bf16[256,1024]{1,0:T(8,128)(2,1)} %out_near_ref.3, bf16[1024,1024]{1,0:T(8,128)(2,1)} %up0_ref.3, ...), custom_call_target="tpu_custom_call" | custom-call | tf_op jit(solution)/shard_map/pallas_call | solution.py:120
  10.0 2.7 %collective-permute-start.1 = (bf16[176,1024]{1,0:T(8,128)(2,1)}, bf16[176,1024]{1,0:T(8,128)(2,1)S(1)}, u32[]{:S(2)}, u32[]{:S(2)}) collective-permute-start(bf16[176,1024]{1,0:T(8,128)(2,1)} %get-tuple-element.161), channel_id=1, source_target_pairs={{0,2},{1,3},{2,0},{3,1},{4,6},{5,7},{6,4},{7,5},{8,10},{9,11},{10,... | collective-permute-start | bytes 1081352 | tf_op jit(solution)/shard_map/ppermute | solution.py:945
  13.0 13.2 %collective-permute-done.1.across_ref = bf16[176,1024]{1,0:T(8,128)(2,1)S(1)} collective-permute-done((bf16[176,1024]{1,0:T(8,128)(2,1)}, bf16[176,1024]{1,0:T(8,128)(2,1)S(1)}, u32[]{:S(2)}, u32[]{:S(2)}) %collective-permute-start.1) | collective-permute-done | bytes 360480 | tf_op jit(solution)/shard_map/ppermute | solution.py:945
  26.8 2.8 %collective-permute-start.4 = (bf16[256,1024]{1,0:T(8,128)(2,1)S(1)}, bf16[256,1024]{1,0:T(8,128)(2,1)S(1)}, u32[]{:S(2)}, u32[]{:S(2)}) collective-permute-start(bf16[256,1024]{1,0:T(8,128)(2,1)S(1)} %bitcast.47), channel_id=1, source_target_pairs={{0,1},{1,0},{2,3},{3,2},{4,5},{5,4},{6,7},{7,6},{8,9},{9,8},{10,11... | collective-permute-start | bytes 1572872 | tf_op jit(solution)/shard_map/ppermute | solution.py:945
  29.5 1.6 collective-permute-start.2
  31.7 1.6 collective-permute-start.3
  33.2 2.4 %collective-permute-start.5 = (bf16[128,1024]{1,0:T(8,128)(2,1)S(1)}, bf16[128,1024]{1,0:T(8,128)(2,1)S(1)}, u32[]{:S(2)}, u32[]{:S(2)}) collective-permute-start(bf16[128,1024]{1,0:T(8,128)(2,1)S(1)} %copy-done.14), channel_id=1, source_target_pairs={{0,2},{1,3},{2,0},{3,1},{4,6},{5,7},{6,4},{7,5},{8,10},{9,11},{10,... | collective-permute-start | bytes 786440 | tf_op jit(solution)/shard_map/ppermute | solution.py:945
  35.7 3.9 %shard_map.206 = (bf16[2,256,1024]{2,1,0:T(8,128)(2,1)S(1)}, bf16[2,256,1024]{2,1,0:T(8,128)(2,1)S(1)}, f32[128,512]{1,0:T(8,128)S(1)}, bf16[176,512]{1,0:T(8,128)(2,1)S(1)}) custom-call(s32[6]{0:T(128)S(1)} %copy-done.7, bf16[256,1024]{1,0:T(8,128)(2,1)S(1)} %shard_map.203.own_ref, bf16[256,1024]{1,0:T(8,128)(2,1)S(1)} %collective-permute-done.other_ref, ...), custom_call_target="tpu_custom_call" | custom-call | tf_op jit(solution)/shard_map/pallas_call | solution.py:46
  40.2 2.4 %collective-permute-start.8 = (bf16[176,512]{1,0:T(8,128)(2,1)S(1)}, bf16[176,512]{1,0:T(8,128)(2,1)S(1)}, u32[]{:S(2)}, u32[]{:S(2)}) collective-permute-start(bf16[176,512]{1,0:T(8,128)(2,1)S(1)} %get-tuple-element.174), channel_id=1, source_target_pairs={{0,2},{1,3},{4,6},{5,7},{8,10},{9,11},{12,14},{13,15},{16,18},{17,... | collective-permute-start | bytes 540680 | tf_op jit(solution)/shard_map/ppermute | solution.py:1013
  42.6 4.8 %collective-permute-done.5.a_ref = bf16[128,1024]{1,0:T(8,128)(2,1)S(1)} collective-permute-done((bf16[128,1024]{1,0:T(8,128)(2,1)S(1)}, bf16[128,1024]{1,0:T(8,128)(2,1)S(1)}, u32[]{:S(2)}, u32[]{:S(2)}) %collective-permute-start.5) | collective-permute-done | bytes 262176 | tf_op jit(solution)/shard_map/ppermute | solution.py:945
  47.4 1.5 shard_map.207.qkv_ref.near_ref
  49.7 3.5 %collective-permute-start.11 = (bf16[128,1024]{1,0:T(8,128)(2,1)S(1)}, bf16[128,1024]{1,0:T(8,128)(2,1)S(1)}, u32[]{:S(2)}, u32[]{:S(2)}) collective-permute-start(bf16[128,1024]{1,0:T(8,128)(2,1)S(1)} %copy-done.13), channel_id=1, source_target_pairs={{0,2},{1,3},{2,0},{3,1},{4,6},{5,7},{6,4},{7,5},{8,10},{9,11},{10,... | collective-permute-start | bytes 786440 | tf_op jit(solution)/shard_map/ppermute | solution.py:945
  53.2 1.7 shard_map.209
  54.9 1.9 shard_map.210.near_ref
  56.8 1.7 shard_map.211
  58.5 2.6 %shard_map.212 = (bf16[2,256,256]{2,1,0:T(8,128)(2,1)S(1)}, f32[256,1024]{1,0:T(8,128)S(1)}, bf16[256,1024]{1,0:T(8,128)(2,1)S(1)}) custom-call(s32[6]{0:T(128)S(1)} %copy-done.7, bf16[2,256,768]{2,1,0:T(8,128)(2,1)S(1)} %get-tuple-element.193.qkv_ref.far_ref, bf16[128,512]{1,0:T(8,128)(2,1)S(1)} %get-tuple-element.185.first_ref, ...), custom_call_target="tpu_custom_call" | custom-call | tf_op jit(solution)/shard_map/pallas_call | solution.py:46
  61.1 3.5 %collective-permute-start.9 = (bf16[256,1024]{1,0:T(8,128)(2,1)S(1)}, bf16[256,1024]{1,0:T(8,128)(2,1)S(1)}, u32[]{:S(2)}, u32[]{:S(2)}) collective-permute-start(bf16[256,1024]{1,0:T(8,128)(2,1)S(1)} %get-tuple-element.195), channel_id=1, source_target_pairs={{0,1},{1,0},{2,3},{3,2},{4,5},{5,4},{6,7},{7,6},{8,9},{9,8},{10,11... | collective-permute-start | bytes 1572872 | tf_op jit(solution)/shard_map/ppermute | solution.py:945
  65.8 1.5 collective-permute-start.12
  67.3 3.6 %collective-permute-done.10.ax_ref = bf16[128,1024]{1,0:T(8,128)(2,1)S(1)} collective-permute-done((bf16[128,1024]{1,0:T(8,128)(2,1)S(1)}, bf16[128,1024]{1,0:T(8,128)(2,1)S(1)}, u32[]{:S(2)}, u32[]{:S(2)}) %collective-permute-start.10) | collective-permute-done | bytes 262176 | tf_op jit(solution)/shard_map/ppermute | solution.py:948
  71.0 2.8 %collective-permute-done.12.by_ref = bf16[128,1024]{1,0:T(8,128)(2,1)S(1)} collective-permute-done((bf16[128,1024]{1,0:T(8,128)(2,1)S(1)}, bf16[128,1024]{1,0:T(8,128)(2,1)S(1)}, u32[]{:S(2)}, u32[]{:S(2)}) %collective-permute-start.12) | collective-permute-done | bytes 262176 | tf_op jit(solution)/shard_map/ppermute | solution.py:948
  74.4 1.6 collective-permute-start.15
  75.9 1.5 collective-permute-start.14
  78.5 8.6 %collective-permute-done.15.bx_ref = bf16[2,128,1024]{2,1,0:T(8,128)(2,1)S(1)} collective-permute-done((bf16[2,128,1024]{2,1,0:T(8,128)(2,1)S(1)}, bf16[2,128,1024]{2,1,0:T(8,128)(2,1)S(1)}, u32[]{:S(2)}, u32[]{:S(2)}) %collective-permute-start.15) | collective-permute-done | bytes 524320 | tf_op jit(solution)/shard_map/ppermute | solution.py:948
  89.1 2.3 %collective-permute-done.13.rows_ref.n_ref = bf16[256,1024]{1,0:T(8,128)(2,1)S(1)} collective-permute-done((bf16[256,1024]{1,0:T(8,128)(2,1)S(1)}, bf16[256,1024]{1,0:T(8,128)(2,1)S(1)}, u32[]{:S(2)}, u32[]{:S(2)}) %collective-permute-start.13) | collective-permute-done | bytes 524320 | tf_op jit(solution)/shard_map/ppermute | solution.py:945
  94.0 6.8 %shard_map.218 = (bf16[256,2048]{1,0:T(8,128)(2,1)S(1)}, bf16[256,2048]{1,0:T(8,128)(2,1)S(1)}, bf16[256,1024]{1,0:T(8,128)(2,1)S(1)}, bf16[256,1024]{1,0:T(8,128)(2,1)S(1)}, bf16[256,1024]{1,0:T(8,128)(2,1)S(1)}) custom-call(s32[6]{0:T(128)S(1)} %copy-done.7, bf16[256,1024]{1,0:T(8,128)(2,1)S(1)} %collective-permute-done.13.rows_ref.n_ref, ...), custom_call_target="tpu_custom_call" | custom-call | tf_op jit(solution)/shard_map/pallas_call | solution.py:612
  101.1 7.1 %shard_map.219 = (bf16[256,2048]{1,0:T(8,128)(2,1)S(1)}, bf16[256,2048]{1,0:T(8,128)(2,1)S(1)}, bf16[256,1024]{1,0:T(8,128)(2,1)S(1)}, f32[256,1024]{1,0:T(8,128)S(1)}, f32[256,1024]{1,0:T(8,128)S(1)}) custom-call(s32[6]{0:T(128)S(1)} %copy-done.7, bf16[256,1024]{1,0:T(8,128)(2,1)S(1)} %get-tuple-element.218.n_ref, bf16[256,1024]{1,0:T(8,128)(2,1)S(1)} %bitcast.49, ...), custom_call_target="tpu_custom_call" | custom-call | tf_op jit(solution)/shard_map/pallas_call | solution.py:612
  108.2 1.8 shard_map.220
  110.1 1.8 shard_map.221
  112.5 2.4 %collective-permute-done.18.received_ref = bf16[256,1024]{1,0:T(8,128)(2,1)S(1)} collective-permute-done((bf16[256,1024]{1,0:T(8,128)(2,1)S(1)}, bf16[256,1024]{1,0:T(8,128)(2,1)S(1)}, u32[]{:S(2)}, u32[]{:S(2)}) %collective-permute-start.18) | collective-permute-done | bytes 524320 | tf_op jit(solution)/shard_map/ppermute | solution.py:945
  114.9 1.4 shard_map.222
  116.8 1.8 shard_map.223
  118.6 1.6 collective-permute-start.19
  120.2 1.9 shard_map.224
  122.1 1.6 collective-permute-start.26
  123.7 5.8 %collective-permute-done.20.other_ref = bf16[256,1024]{1,0:T(8,128)(2,1)S(1)} collective-permute-done((bf16[256,1024]{1,0:T(8,128)(2,1)S(1)}, bf16[256,1024]{1,0:T(8,128)(2,1)S(1)}, u32[]{:S(2)}, u32[]{:S(2)}) %collective-permute-start.20) | collective-permute-done | bytes 524320 | tf_op jit(solution)/shard_map/ppermute | solution.py:945
  129.5 1.4 shard_map.225
  130.9 5.4 %shard_map.226 = (bf16[2,256,1536]{2,1,0:T(8,128)(2,1)S(1)}, f32[128,512]{1,0:T(8,128)S(1)}, bf16[176,512]{1,0:T(8,128)(2,1)S(1)}) custom-call(s32[6]{0:T(128)S(1)} %copy-done.7, bf16[2,256,768]{2,1,0:T(8,128)(2,1)S(1)} %shard_map.207.qkv_ref.near_ref, bf16[2,256,768]{2,1,0:T(8,128)(2,1)S(1)} %get-tuple-element.193.qkv_ref.far_ref, ...), custom_call_target="tpu_custom_call" | custom-call | tf_op jit(solution)/shard_map/pallas_call | solution.py:46
  136.3 1.6 collective-permute-start.25
  137.9 2.4 %shard_map.227.total_ref = f32[2,256,1024]{2,1,0:T(8,128)S(1)} custom-call(s32[6]{0:T(128)S(1)} %copy-done.7, bf16[2,256,1536]{2,1,0:T(8,128)(2,1)S(1)} %get-tuple-element.243.dqkv_ref, bf16[1024,768]{1,0:T(8,128)(2,1)S(1)} %constant_dynamic-update-slice_fusion.weight_ref.near_weight_ref, bf16[1024,768]{1,0:T(8,128)(2,1)S(1)} %get-tuple-element.191.far_weight_ref), custom_call_target="tpu_custom_call" | custom-call | tf_op jit(solution)/shard_map/pallas_call | solution.py:46
  140.9 1.8 shard_map.228
  143.6 1.6 collective-permute-start.22
  147.9 5.1 %shard_map.231 = (f32[256,1024]{1,0:T(8,128)S(1)}, bf16[256,1024]{1,0:T(8,128)(2,1)S(1)}, f32[128,512]{1,0:T(8,128)S(1)}, f32[16,512]{1,0:T(8,128)S(1)}) custom-call(s32[6]{0:T(128)S(1)} %copy-done.7, f32[128,512]{1,0:T(8,128)S(1)} %get-tuple-element.241.near_ref, bf16[176,512]{1,0:T(8,128)(2,1)S(1)} %collective-permute-done.25.returned_ref, ...), custom_call_target="tpu_custom_call" | custom-call | flops 30000001024 | tf_op jit(solution)/shard_map/pallas_call | solution.py:46
  154.1 3.2 %collective-permute-done.24.c_ref = bf16[256,1024]{1,0:T(8,128)(2,1)S(1)} collective-permute-done((bf16[256,1024]{1,0:T(8,128)(2,1)S(1)}, bf16[256,1024]{1,0:T(8,128)(2,1)S(1)}, u32[]{:S(2)}, u32[]{:S(2)}) %collective-permute-start.24) | collective-permute-done | bytes 524320 | tf_op jit(solution)/shard_map/ppermute | solution.py:945
  157.3 1.9 shard_map.232
  159.2 1.6 collective-permute-start.31
  163.2 2.4 %collective-permute-start.35 = (bf16[128,1024]{1,0:T(8,128)(2,1)S(1)}, bf16[128,1024]{1,0:T(8,128)(2,1)S(1)}, u32[]{:S(2)}, u32[]{:S(2)}) collective-permute-start(bf16[128,1024]{1,0:T(8,128)(2,1)S(1)} %get-tuple-element.268), channel_id=1, source_target_pairs={{0,2},{1,3},{2,0},{3,1},{4,6},{5,7},{6,4},{7,5},{8,10},{9,11},{10,... | collective-permute-start | bytes 786440 | tf_op jit(solution)/shard_map/ppermute | solution.py:945
  165.6 8.1 %collective-permute-done.28.received_ref = bf16[256,1024]{1,0:T(8,128)(2,1)S(1)} collective-permute-done((bf16[256,1024]{1,0:T(8,128)(2,1)S(1)}, bf16[256,1024]{1,0:T(8,128)(2,1)S(1)}, u32[]{:S(2)}, u32[]{:S(2)}) %collective-permute-start.28) | collective-permute-done | bytes 524320 | tf_op jit(solution)/shard_map/ppermute | solution.py:945
  173.7 4.3 %shard_map.235.param_ref = f32[40,512]{1,0:T(8,128)S(1)} custom-call(s32[6]{0:T(128)S(1)} %copy-done.7, bf16[2,256,1024]{2,1,0:T(8,128)(2,1)S(1)} %get-tuple-element.269.tile_ref, f32[128,512]{1,0:T(8,128)S(1)} %get-tuple-element.241.near_ref, f32[128,512]{1,0:T(8,128)S(1)} %get-tuple-element.255.last_ref, f32[16,512]{1,0:T(8,128)S(1)} %get-tuple-element.187.enter_ref, ...), custom_call_target="tpu_custom_call" | custom-call | flops 3000000000 | tf_op jit(solution)/shard_map/pallas_call | solution.py:46
  178.1 2.4 %shard_map.236 = (f32[256,1024]{1,0:T(8,128)}, f32[8,256]{1,0:T(8,128)S(1)}) custom-call(s32[6]{0:T(128)S(1)} %copy-done.7, bf16[256,1024]{1,0:T(8,128)(2,1)S(1)} %bitcast.55, f32[256,1024]{1,0:T(8,128)S(1)} %get-tuple-element.253.own_ref, bf16[256,1024]{1,0:T(8,128)(2,1)S(1)} %collective-permute-done.28.received_ref, ...), custom_call_target="tpu_custom_call" | custom-call | tf_op jit(solution)/shard_map/pallas_call | solution.py:46
  180.5 2.3 collective-permute-done.27.b_ref
  183.3 2.2 collective-permute-done.35.b_ref
  187.5 1.4 collective-permute-start.30
  189.8 3.3 %collective-permute-done.36.by_ref = bf16[128,1024]{1,0:T(8,128)(2,1)S(1)} collective-permute-done((bf16[128,1024]{1,0:T(8,128)(2,1)S(1)}, bf16[128,1024]{1,0:T(8,128)(2,1)S(1)}, u32[]{:S(2)}, u32[]{:S(2)}) %collective-permute-start.36) | collective-permute-done | bytes 262176 | tf_op jit(solution)/shard_map/ppermute | solution.py:948
  195.5 1.4 collective-permute-start.44
  196.8 1.5 shard_map.241
  198.3 4.7 %collective-permute-done.37.b_ref = bf16[144,1024]{1,0:T(8,128)(2,1)S(1)} collective-permute-done((bf16[144,1024]{1,0:T(8,128)(2,1)S(1)}, bf16[144,1024]{1,0:T(8,128)(2,1)S(1)}, u32[]{:S(2)}, u32[]{:S(2)}) %collective-permute-start.37) | collective-permute-done | bytes 294944 | tf_op jit(solution)/shard_map/ppermute | solution.py:945
  204.8 2.3 %collective-permute-start.41 = (bf16[144,1024]{1,0:T(8,128)(2,1)S(1)}, bf16[144,1024]{1,0:T(8,128)(2,1)S(1)}, u32[]{:S(2)}, u32[]{:S(2)}) collective-permute-start(bf16[144,1024]{1,0:T(8,128)(2,1)S(1)} %shard_map.242.a_ref), channel_id=1, source_target_pairs={{0,24},{4,28},{8,16},{12,20},{16,8},{20,12},{24,0},{28,4},{1,25},{... | collective-permute-start | bytes 884744 | tf_op jit(solution)/shard_map/ppermute | solution.py:948
  207.2 3.0 %shard_map.243 = (f32[1024,1024]{1,0:T(8,128)}, f32[1024,1024]{1,0:T(8,128)}) custom-call(s32[6]{0:T(128)S(1)} %copy-done.7, bf16[2,2,128,1024]{3,2,1,0:T(8,128)(2,1)S(1)} %get-tuple-element.285.own_ref, bf16[2,2,128,1024]{3,2,1,0:T(8,128)(2,1)S(1)} %collective-permute-done.38.other_ref), custom_call_target="tpu_custom_call" | custom-call | tf_op jit(solution)/shard_map/pallas_call | solution.py:898
  210.2 6.3 %collective-permute-done.39.b_ref = bf16[144,1024]{1,0:T(8,128)(2,1)S(1)} collective-permute-done((bf16[144,1024]{1,0:T(8,128)(2,1)S(1)}, bf16[144,1024]{1,0:T(8,128)(2,1)S(1)}, u32[]{:S(2)}, u32[]{:S(2)}) %collective-permute-start.39) | collective-permute-done | bytes 294944 | tf_op jit(solution)/shard_map/ppermute | solution.py:948
  216.6 6.3 %collective-permute-done.41.d_ref = bf16[144,1024]{1,0:T(8,128)(2,1)S(1)} collective-permute-done((bf16[144,1024]{1,0:T(8,128)(2,1)S(1)}, bf16[144,1024]{1,0:T(8,128)(2,1)S(1)}, u32[]{:S(2)}, u32[]{:S(2)}) %collective-permute-start.41) | collective-permute-done | bytes 294944 | tf_op jit(solution)/shard_map/ppermute | solution.py:948
  224.7 1.6 collective-permute-done.42.odd_ref
  226.4 2.8 %shard_map.246 = (f32[3,1024,256]{2,1,0:T(8,128)}, f32[256,1024]{1,0:T(8,128)}, f32[16,256]{1,0:T(8,128)}, f32[16,256]{1,0:T(8,128)}, f32[1,256]{1,0:T(1,128)}, /*index=5*/f32[1,1024]{1,0:T(1,128)}, f32[1,1024]{1,0:T(1,128)}) custom-call(s32[6]{0:T(128)S(1)} %copy-done.7, bf16[4,144,1024]{2,1,0:T(8,128)(2,1)S(1)} %shard_map.244.even_ref, ...), custom_call_target="tpu_custom_call" | custom-call | flops 8000000000 | tf_op jit(solution)/shard_map/pallas_call | solution.py:46
  229.2 3.1 %shard_map.247 = (f32[1024,1024]{1,0:T(8,128)}, f32[1024,1024]{1,0:T(8,128)}) custom-call(s32[6]{0:T(128)S(1)} %copy-done.7, bf16[2,2,128,1024]{3,2,1,0:T(8,128)(2,1)S(1)} %shard_map.245.own_ref, bf16[2,2,128,1024]{3,2,1,0:T(8,128)(2,1)S(1)} %collective-permute-done.45.other_ref, ...), custom_call_target="tpu_custom_call", output_to_operand_aliasing={{0}: (3, {}), {1}: (4, {})} | custom-call | tf_op jit(solution)/shard_map/pallas_call | solution.py:898
  (116 shorter events, 31.3 us)
Async XLA Ops:
  1.4 5.7 %copy-start.6 = (s32[6]{0:T(128)}, s32[6]{0:T(128)S(1)}, u32[]{:S(2)}) copy-start(s32[6]{0:T(128)S(1)} %stack.24.flag_ref) | copy-start | bytes 76
  1.4 1.0 copy-start.4
  2.4 0.7 copy-start.9
  4.0 22.7 %collective-permute-start = (bf16[256,1024]{1,0:T(8,128)(2,1)S(1)}, bf16[256,1024]{1,0:T(8,128)(2,1)S(1)}, u32[]{:S(2)}, u32[]{:S(2)}) collective-permute-start(bf16[256,1024]{1,0:T(8,128)(2,1)S(1)} %shard_map.203.own_ref), channel_id=1, source_target_pairs={{0,1},{1,0},{2,3},{3,2},{4,5},{5,4},{6,7},{7,6},{8,9},{9,8},{10,11... | collective-permute-start | bytes 1572872 | tf_op jit(solution)/shard_map/ppermute | solution.py:945
  7.1 5.6 %copy-start.12 = (bf16[1024,3,256]{2,0,1:T(8,128)(2,1)S(1)}, bf16[1024,3,256]{2,0,1:T(8,128)(2,1)}, u32[]{:S(2)}) copy-start(bf16[1024,3,256]{2,0,1:T(8,128)(2,1)} %param.15) | copy-start | bytes 4718596
  10.0 16.1 %collective-permute-start.1 = (bf16[176,1024]{1,0:T(8,128)(2,1)}, bf16[176,1024]{1,0:T(8,128)(2,1)S(1)}, u32[]{:S(2)}, u32[]{:S(2)}) collective-permute-start(bf16[176,1024]{1,0:T(8,128)(2,1)} %get-tuple-element.161), channel_id=1, source_target_pairs={{0,2},{1,3},{2,0},{3,1},{4,6},{5,7},{6,4},{7,5},{8,10},{9,11},{10,... | collective-permute-start | bytes 1081352 | tf_op jit(solution)/shard_map/ppermute | solution.py:945
  12.8 13.9 %copy-start.2 = (bf16[1,256,1024]{2,1,0:T(8,128)(2,1)S(1)}, bf16[1,256,1024]{2,1,0:T(8,128)(2,1)}, u32[]{:S(2)}) copy-start(bf16[1,256,1024]{2,1,0:T(8,128)(2,1)} %param.23) | copy-start | bytes 1572868
  12.8 18.3 %copy-start.7 = (s32[6]{0:T(128)S(1)}, s32[6]{0:T(128)}, u32[]{:S(2)}) copy-start(s32[6]{0:T(128)} %copy-done.6) | copy-start | bytes 76
  12.8 18.3 %copy-start.8 = (f32[48,256]{1,0:T(8,128)S(1)}, f32[48,256]{1,0:T(8,128)}, u32[]{:S(2)}) copy-start(f32[48,256]{1,0:T(8,128)} %get-tuple-element.164.own_ref) | copy-start | bytes 147460
  12.8 20.4 %copy-start.14 = (bf16[128,1024]{1,0:T(8,128)(2,1)S(1)}, bf16[128,1024]{1,0:T(8,128)(2,1)}, u32[]{:S(2)}) copy-start(bf16[128,1024]{1,0:T(8,128)(2,1)} %get-tuple-element.177) | copy-start | bytes 786436
  26.8 20.7 %collective-permute-start.4 = (bf16[256,1024]{1,0:T(8,128)(2,1)S(1)}, bf16[256,1024]{1,0:T(8,128)(2,1)S(1)}, u32[]{:S(2)}, u32[]{:S(2)}) collective-permute-start(bf16[256,1024]{1,0:T(8,128)(2,1)S(1)} %bitcast.47), channel_id=1, source_target_pairs={{0,1},{1,0},{2,3},{3,2},{4,5},{5,4},{6,7},{7,6},{8,9},{9,8},{10,11... | collective-permute-start | bytes 1572872 | tf_op jit(solution)/shard_map/ppermute | solution.py:945
  29.5 10.1 %collective-permute-start.2 = (bf16[128,1024]{1,0:T(8,128)(2,1)S(1)}, bf16[128,1024]{1,0:T(8,128)(2,1)S(1)}, u32[]{:S(2)}, u32[]{:S(2)}) collective-permute-start(bf16[128,1024]{1,0:T(8,128)(2,1)S(1)} %slice.54.a_ref), channel_id=1, source_target_pairs={{0,8},{4,12},{8,0},{12,4},{16,24},{20,28},{24,16},{28,20},{1,9},{5... | collective-permute-start | bytes 786440 | tf_op jit(solution)/shard_map/ppermute | solution.py:948
  31.7 15.8 %collective-permute-start.3 = (bf16[128,1024]{1,0:T(8,128)(2,1)S(1)}, bf16[128,1024]{1,0:T(8,128)(2,1)S(1)}, u32[]{:S(2)}, u32[]{:S(2)}) collective-permute-start(bf16[128,1024]{1,0:T(8,128)(2,1)S(1)} %slice.54.a_ref), channel_id=1, source_target_pairs={{0,16},{4,20},{8,24},{12,28},{16,0},{20,4},{24,8},{28,12},{1,17},{... | collective-permute-start | bytes 786440 | tf_op jit(solution)/shard_map/ppermute | solution.py:948
  33.2 14.2 %collective-permute-start.5 = (bf16[128,1024]{1,0:T(8,128)(2,1)S(1)}, bf16[128,1024]{1,0:T(8,128)(2,1)S(1)}, u32[]{:S(2)}, u32[]{:S(2)}) collective-permute-start(bf16[128,1024]{1,0:T(8,128)(2,1)S(1)} %copy-done.14), channel_id=1, source_target_pairs={{0,2},{1,3},{2,0},{3,1},{4,6},{5,7},{6,4},{7,5},{8,10},{9,11},{10,... | collective-permute-start | bytes 786440 | tf_op jit(solution)/shard_map/ppermute | solution.py:945
  39.6 10.1 %copy-start.13 = (bf16[128,1024]{1,0:T(8,128)(2,1)S(1)}, bf16[128,1024]{1,0:T(8,128)(2,1)}, u32[]{:S(2)}) copy-start(bf16[128,1024]{1,0:T(8,128)(2,1)} %get-tuple-element.196) | copy-start | bytes 786436
  39.6 9.3 %collective-permute-start.6 = (bf16[128,1024]{1,0:T(8,128)(2,1)S(1)}, bf16[128,1024]{1,0:T(8,128)(2,1)S(1)}, u32[]{:S(2)}, u32[]{:S(2)}) collective-permute-start(bf16[128,1024]{1,0:T(8,128)(2,1)S(1)} %collective-permute-done.2.b_ref), channel_id=1, source_target_pairs={{0,16},{4,20},{8,24},{12,28},{16,0},{20,4},{24,8},{28,12},{1,17},{... | collective-permute-start | bytes 786440 | tf_op jit(solution)/shard_map/ppermute | solution.py:948
  40.2 9.5 %collective-permute-start.8 = (bf16[176,512]{1,0:T(8,128)(2,1)S(1)}, bf16[176,512]{1,0:T(8,128)(2,1)S(1)}, u32[]{:S(2)}, u32[]{:S(2)}) collective-permute-start(bf16[176,512]{1,0:T(8,128)(2,1)S(1)} %get-tuple-element.174), channel_id=1, source_target_pairs={{0,2},{1,3},{4,6},{5,7},{8,10},{9,11},{12,14},{13,15},{16,18},{17,... | collective-permute-start | bytes 540680 | tf_op jit(solution)/shard_map/ppermute | solution.py:1013
  49.6 7.2 %collective-permute-start.7 = (bf16[4,128,1024]{2,1,0:T(8,128)(2,1)S(1)}, bf16[4,128,1024]{2,1,0:T(8,128)(2,1)S(1)}, u32[]{:S(2)}, u32[]{:S(2)}) collective-permute-start(bf16[4,128,1024]{2,1,0:T(8,128)(2,1)S(1)} %shard_map.208.even_ref), channel_id=1, source_target_pairs={{0,4},{4,0},{8,12},{12,8},{16,20},{20,16},{24,28},{28,24},{1,5},{5... | collective-permute-start | bytes 3145736 | tf_op jit(solution)/shard_map/ppermute | solution.py:948
  49.7 16.1 %collective-permute-start.11 = (bf16[128,1024]{1,0:T(8,128)(2,1)S(1)}, bf16[128,1024]{1,0:T(8,128)(2,1)S(1)}, u32[]{:S(2)}, u32[]{:S(2)}) collective-permute-start(bf16[128,1024]{1,0:T(8,128)(2,1)S(1)} %copy-done.13), channel_id=1, source_target_pairs={{0,2},{1,3},{2,0},{3,1},{4,6},{5,7},{6,4},{7,5},{8,10},{9,11},{10,... | collective-permute-start | bytes 786440 | tf_op jit(solution)/shard_map/ppermute | solution.py:945
  54.9 3.6 %copy-start.3 = (bf16[256,1024]{1,0:T(8,128)(2,1)S(1)}, bf16[256,1024]{1,0:T(8,128)(2,1)}, u32[]{:S(2)}) copy-start(bf16[256,1024]{1,0:T(8,128)(2,1)} %out_near_ref.3) | copy-start | bytes 1572868
  58.5 19.0 %copy-start.5 = (bf16[1,256,1024]{2,1,0:T(8,128)(2,1)S(1)}, bf16[1,256,1024]{2,1,0:T(8,128)(2,1)}, u32[]{:S(2)}) copy-start(bf16[1,256,1024]{2,1,0:T(8,128)(2,1)} %param.12) | copy-start | bytes 1572868
  58.5 19.0 %copy-start.11 = (f32[1024]{0:T(1024)S(1)}, f32[1024]{0:T(1024)}, u32[]{:S(2)}) copy-start(f32[1024]{0:T(1024)} %param.20) | copy-start | bytes 12292
  61.1 16.3 %collective-permute-start.9 = (bf16[256,1024]{1,0:T(8,128)(2,1)S(1)}, bf16[256,1024]{1,0:T(8,128)(2,1)S(1)}, u32[]{:S(2)}, u32[]{:S(2)}) collective-permute-start(bf16[256,1024]{1,0:T(8,128)(2,1)S(1)} %get-tuple-element.195), channel_id=1, source_target_pairs={{0,1},{1,0},{2,3},{3,2},{4,5},{5,4},{6,7},{7,6},{8,9},{9,8},{10,11... | collective-permute-start | bytes 1572872 | tf_op jit(solution)/shard_map/ppermute | solution.py:945
  64.6 6.4 %collective-permute-start.10 = (bf16[128,1024]{1,0:T(8,128)(2,1)S(1)}, bf16[128,1024]{1,0:T(8,128)(2,1)S(1)}, u32[]{:S(2)}, u32[]{:S(2)}) collective-permute-start(bf16[128,1024]{1,0:T(8,128)(2,1)S(1)} %collective-permute-done.5.a_ref), channel_id=1, source_target_pairs={{0,8},{4,12},{8,0},{12,4},{16,24},{20,28},{24,16},{28,20},{1,9},{5... | collective-permute-start | bytes 786440 | tf_op jit(solution)/shard_map/ppermute | solution.py:948
  65.8 7.9 %collective-permute-start.12 = (bf16[128,1024]{1,0:T(8,128)(2,1)S(1)}, bf16[128,1024]{1,0:T(8,128)(2,1)S(1)}, u32[]{:S(2)}, u32[]{:S(2)}) collective-permute-start(bf16[128,1024]{1,0:T(8,128)(2,1)S(1)} %collective-permute-done.11.b_ref), channel_id=1, source_target_pairs={{0,16},{4,20},{8,24},{12,28},{16,0},{20,4},{24,8},{28,12},{1,17},{... | collective-permute-start | bytes 786440 | tf_op jit(solution)/shard_map/ppermute | solution.py:948
  74.4 12.7 %collective-permute-start.15 = (bf16[2,128,1024]{2,1,0:T(8,128)(2,1)S(1)}, bf16[2,128,1024]{2,1,0:T(8,128)(2,1)S(1)}, u32[]{:S(2)}, u32[]{:S(2)}) collective-permute-start(bf16[2,128,1024]{2,1,0:T(8,128)(2,1)S(1)} %get-tuple-element.202.b_ref), channel_id=1, source_target_pairs={{0,8},{4,12},{8,0},{12,4},{16,24},{20,28},{24,16},{28,20},{1,9},{5... | collective-permute-start | bytes 1572872 | tf_op jit(solution)/shard_map/ppermute | solution.py:948
  75.9 12.4 %collective-permute-start.14 = (bf16[2,128,1024]{2,1,0:T(8,128)(2,1)S(1)}, bf16[2,128,1024]{2,1,0:T(8,128)(2,1)S(1)}, u32[]{:S(2)}, u32[]{:S(2)}) collective-permute-start(bf16[2,128,1024]{2,1,0:T(8,128)(2,1)S(1)} %get-tuple-element.201.a_ref), channel_id=1, source_target_pairs={{0,16},{4,20},{8,24},{12,28},{16,0},{20,4},{24,8},{28,12},{1,17},{... | collective-permute-start | bytes 1572872 | tf_op jit(solution)/shard_map/ppermute | solution.py:948
  78.4 13.0 %collective-permute-start.13 = (bf16[256,1024]{1,0:T(8,128)(2,1)S(1)}, bf16[256,1024]{1,0:T(8,128)(2,1)S(1)}, u32[]{:S(2)}, u32[]{:S(2)}) collective-permute-start(bf16[256,1024]{1,0:T(8,128)(2,1)S(1)} %get-tuple-element.218.n_ref), channel_id=1, source_target_pairs={{0,1},{1,0},{2,3},{3,2},{4,5},{5,4},{6,7},{7,6},{8,9},{9,8},{10,11... | collective-permute-start | bytes 1572872 | tf_op jit(solution)/shard_map/ppermute | solution.py:945
  87.1 4.3 %copy-start = (bf16[1024,1024]{1,0:T(8,128)(2,1)S(1)}, bf16[1024,1024]{1,0:T(8,128)(2,1)}, u32[]{:S(2)}) copy-start(bf16[1024,1024]{1,0:T(8,128)(2,1)} %up0_ref.3) | copy-start | bytes 6291460
  87.1 4.3 %copy-start.1 = (bf16[1024,1024]{1,0:T(8,128)(2,1)S(1)}, bf16[1024,1024]{1,0:T(8,128)(2,1)}, u32[]{:S(2)}) copy-start(bf16[1024,1024]{1,0:T(8,128)(2,1)} %down0_ref.3) | copy-start | bytes 6291460
  89.0 4.2 %collective-permute-start.16 = (bf16[4,2,128,1024]{3,2,1,0:T(8,128)(2,1)S(1)}, bf16[4,2,128,1024]{3,2,1,0:T(8,128)(2,1)S(1)}, u32[]{:S(2)}, u32[]{:S(2)}) collective-permute-start(bf16[4,2,128,1024]{3,2,1,0:T(8,128)(2,1)S(1)} %shard_map.215.even_ref), channel_id=1, source_target_pairs={{0,4},{4,0},{8,12},{12,8},{16,20},{20,16},{24,28},{28,24},{1,5},{5... | collective-permute-start | bytes 6291464 | tf_op jit(solution)/shard_map/ppermute | solution.py:948
  100.9 14.0 %collective-permute-start.18 = (bf16[256,1024]{1,0:T(8,128)(2,1)S(1)}, bf16[256,1024]{1,0:T(8,128)(2,1)S(1)}, u32[]{:S(2)}, u32[]{:S(2)}) collective-permute-start(bf16[256,1024]{1,0:T(8,128)(2,1)S(1)} %get-tuple-element.217), channel_id=1, source_target_pairs={{0,1},{1,0},{2,3},{3,2},{4,5},{5,4},{6,7},{7,6},{8,9},{9,8},{10,11... | collective-permute-start | bytes 1572872 | tf_op jit(solution)/shard_map/ppermute | solution.py:945
  110.0 6.7 %collective-permute-start.17 = (bf16[1024,1024]{1,0:T(8,128)(2,1)S(1)}, bf16[1024,1024]{1,0:T(8,128)(2,1)S(1)}, u32[]{:S(2)}, u32[]{:S(2)}) collective-permute-start(bf16[1024,1024]{1,0:T(8,128)(2,1)S(1)} %shard_map.220), channel_id=1, source_target_pairs={{0,4},{4,0},{8,12},{12,8},{16,20},{20,16},{24,28},{28,24},{1,5},{5... | collective-permute-start | bytes 6291464 | tf_op jit(solution)/shard_map/ppermute | solution.py:948
  111.9 8.3 %collective-permute-start.21 = (bf16[512,2048]{1,0:T(8,128)(2,1)S(1)}, bf16[512,2048]{1,0:T(8,128)(2,1)S(1)}, u32[]{:S(2)}, u32[]{:S(2)}) collective-permute-start(bf16[512,2048]{1,0:T(8,128)(2,1)S(1)} %shard_map.221), channel_id=1, source_target_pairs={{0,4},{4,0},{8,12},{12,8},{16,20},{20,16},{24,28},{28,24},{1,5},{5... | collective-permute-start | bytes 6291464 | tf_op jit(solution)/shard_map/ppermute | solution.py:948
  116.3 13.2 %collective-permute-start.20 = (bf16[256,1024]{1,0:T(8,128)(2,1)S(1)}, bf16[256,1024]{1,0:T(8,128)(2,1)S(1)}, u32[]{:S(2)}, u32[]{:S(2)}) collective-permute-start(bf16[256,1024]{1,0:T(8,128)(2,1)S(1)} %get-tuple-element.228.own_ref), channel_id=1, source_target_pairs={{0,1},{1,0},{2,3},{3,2},{4,5},{5,4},{6,7},{7,6},{8,9},{9,8},{10,11... | collective-permute-start | bytes 1572872 | tf_op jit(solution)/shard_map/ppermute | solution.py:945
  118.6 24.3 %collective-permute-start.19 = (bf16[512,1024]{1,0:T(8,128)(2,1)S(1)}, bf16[512,1024]{1,0:T(8,128)(2,1)S(1)}, u32[]{:S(2)}, u32[]{:S(2)}) collective-permute-start(bf16[512,1024]{1,0:T(8,128)(2,1)S(1)} %get-tuple-element.232), channel_id=1, source_target_pairs={{0,8},{4,12},{8,0},{12,4},{16,24},{20,28},{24,16},{28,20},{1,9},{5... | collective-permute-start | bytes 3145736 | tf_op jit(solution)/shard_map/ppermute | solution.py:948
  122.1 23.8 %collective-permute-start.26 = (bf16[256,2048]{1,0:T(8,128)(2,1)S(1)}, bf16[256,2048]{1,0:T(8,128)(2,1)S(1)}, u32[]{:S(2)}, u32[]{:S(2)}) collective-permute-start(bf16[256,2048]{1,0:T(8,128)(2,1)S(1)} %get-tuple-element.234), channel_id=1, source_target_pairs={{0,16},{4,20},{8,24},{12,28},{16,0},{20,4},{24,8},{28,12},{1,17},{... | collective-permute-start | bytes 3145736 | tf_op jit(solution)/shard_map/ppermute | solution.py:948
  136.3 11.6 %collective-permute-start.25 = (bf16[176,512]{1,0:T(8,128)(2,1)S(1)}, bf16[176,512]{1,0:T(8,128)(2,1)S(1)}, u32[]{:S(2)}, u32[]{:S(2)}) collective-permute-start(bf16[176,512]{1,0:T(8,128)(2,1)S(1)} %get-tuple-element.242), channel_id=1, source_target_pairs={{2,0},{3,1},{6,4},{7,5},{10,8},{11,9},{14,12},{15,13},{18,16},{19,... | collective-permute-start | bytes 540680 | tf_op jit(solution)/shard_map/ppermute | solution.py:1146
  140.2 17.1 %collective-permute-start.24 = (bf16[256,1024]{1,0:T(8,128)(2,1)S(1)}, bf16[256,1024]{1,0:T(8,128)(2,1)S(1)}, u32[]{:S(2)}, u32[]{:S(2)}) collective-permute-start(bf16[256,1024]{1,0:T(8,128)(2,1)S(1)} %get-tuple-element.248), channel_id=1, source_target_pairs={{0,1},{1,0},{2,3},{3,2},{4,5},{5,4},{6,7},{7,6},{8,9},{9,8},{10,11... | collective-permute-start | bytes 1572872 | tf_op jit(solution)/shard_map/ppermute | solution.py:945
  142.8 14.5 %collective-permute-start.23 = (bf16[512,2048]{1,0:T(8,128)(2,1)S(1)}, bf16[512,2048]{1,0:T(8,128)(2,1)S(1)}, u32[]{:S(2)}, u32[]{:S(2)}) collective-permute-start(bf16[512,2048]{1,0:T(8,128)(2,1)S(1)} %shard_map.228), channel_id=1, source_target_pairs={{0,4},{4,0},{8,12},{12,8},{16,20},{20,16},{24,28},{28,24},{1,5},{5... | collective-permute-start | bytes 6291464 | tf_op jit(solution)/shard_map/ppermute | solution.py:948
  143.6 17.2 %collective-permute-start.22 = (bf16[256,1024]{1,0:T(8,128)(2,1)S(1)}, bf16[256,1024]{1,0:T(8,128)(2,1)S(1)}, u32[]{:S(2)}, u32[]{:S(2)}) collective-permute-start(bf16[256,1024]{1,0:T(8,128)(2,1)S(1)} %get-tuple-element.247), channel_id=1, source_target_pairs={{0,16},{4,20},{8,24},{12,28},{16,0},{20,4},{24,8},{28,12},{1,17},{... | collective-permute-start | bytes 1572872 | tf_op jit(solution)/shard_map/ppermute | solution.py:948
  146.7 15.9 %collective-permute-start.29 = (bf16[128,2048]{1,0:T(8,128)(2,1)S(1)}, bf16[128,2048]{1,0:T(8,128)(2,1)S(1)}, u32[]{:S(2)}, u32[]{:S(2)}) collective-permute-start(bf16[128,2048]{1,0:T(8,128)(2,1)S(1)} %get-tuple-element.251), channel_id=1, source_target_pairs={{0,8},{4,12},{8,0},{12,4},{16,24},{20,28},{24,16},{28,20},{1,9},{5... | collective-permute-start | bytes 1572872 | tf_op jit(solution)/shard_map/ppermute | solution.py:948
  152.9 20.8 %collective-permute-start.28 = (bf16[256,1024]{1,0:T(8,128)(2,1)S(1)}, bf16[256,1024]{1,0:T(8,128)(2,1)S(1)}, u32[]{:S(2)}, u32[]{:S(2)}) collective-permute-start(bf16[256,1024]{1,0:T(8,128)(2,1)S(1)} %get-tuple-element.254), channel_id=1, source_target_pairs={{0,1},{1,0},{2,3},{3,2},{4,5},{5,4},{6,7},{7,6},{8,9},{9,8},{10,11... | collective-permute-start | bytes 1572872 | tf_op jit(solution)/shard_map/ppermute | solution.py:945
  159.2 29.8 %collective-permute-start.31 = (bf16[128,2048]{1,0:T(8,128)(2,1)S(1)}, bf16[128,2048]{1,0:T(8,128)(2,1)S(1)}, u32[]{:S(2)}, u32[]{:S(2)}) collective-permute-start(bf16[128,2048]{1,0:T(8,128)(2,1)S(1)} %get-tuple-element.260), channel_id=1, source_target_pairs={{0,16},{4,20},{8,24},{12,28},{16,0},{20,4},{24,8},{28,12},{1,17},{... | collective-permute-start | bytes 1572872 | tf_op jit(solution)/shard_map/ppermute | solution.py:948
  160.8 28.1 %collective-permute-start.32 = (bf16[128,2048]{1,0:T(8,128)(2,1)S(1)}, bf16[128,2048]{1,0:T(8,128)(2,1)S(1)}, u32[]{:S(2)}, u32[]{:S(2)}) collective-permute-start(bf16[128,2048]{1,0:T(8,128)(2,1)S(1)} %get-tuple-element.261), channel_id=1, source_target_pairs={{0,8},{4,12},{8,0},{12,4},{16,24},{20,28},{24,16},{28,20},{1,9},{5... | collective-permute-start | bytes 1572872 | tf_op jit(solution)/shard_map/ppermute | solution.py:948
  161.5 21.3 %collective-permute-start.27 = (bf16[128,1024]{1,0:T(8,128)(2,1)S(1)}, bf16[128,1024]{1,0:T(8,128)(2,1)S(1)}, u32[]{:S(2)}, u32[]{:S(2)}) collective-permute-start(bf16[128,1024]{1,0:T(8,128)(2,1)S(1)} %get-tuple-element.265), channel_id=1, source_target_pairs={{0,2},{1,3},{2,0},{3,1},{4,6},{5,7},{6,4},{7,5},{8,10},{9,11},{10,... | collective-permute-start | bytes 786440 | tf_op jit(solution)/shard_map/ppermute | solution.py:945
  163.2 22.3 %collective-permute-start.35 = (bf16[128,1024]{1,0:T(8,128)(2,1)S(1)}, bf16[128,1024]{1,0:T(8,128)(2,1)S(1)}, u32[]{:S(2)}, u32[]{:S(2)}) collective-permute-start(bf16[128,1024]{1,0:T(8,128)(2,1)S(1)} %get-tuple-element.268), channel_id=1, source_target_pairs={{0,2},{1,3},{2,0},{3,1},{4,6},{5,7},{6,4},{7,5},{8,10},{9,11},{10,... | collective-permute-start | bytes 786440 | tf_op jit(solution)/shard_map/ppermute | solution.py:945
  165.6 12.4 %copy-start.10 = (f32[1024]{0:T(1024)S(1)}, f32[1024]{0:T(1024)}, u32[]{:S(2)}) copy-start(f32[1024]{0:T(1024)} %param.14) | copy-start | bytes 12292
  173.7 15.2 %collective-permute-start.33 = (bf16[128,2048]{1,0:T(8,128)(2,1)S(1)}, bf16[128,2048]{1,0:T(8,128)(2,1)S(1)}, u32[]{:S(2)}, u32[]{:S(2)}) collective-permute-start(bf16[128,2048]{1,0:T(8,128)(2,1)S(1)} %get-tuple-element.262), channel_id=1, source_target_pairs={{0,24},{4,28},{8,16},{12,20},{16,8},{20,12},{24,0},{28,4},{1,25},{... | collective-permute-start | bytes 1572872 | tf_op jit(solution)/shard_map/ppermute | solution.py:948
  182.7 4.8 %collective-permute-start.34 = (f32[8,256]{1,0:T(8,128)S(1)}, f32[8,256]{1,0:T(8,128)S(1)}, u32[]{:S(2)}, u32[]{:S(2)}) collective-permute-start(f32[8,256]{1,0:T(8,128)S(1)} %get-tuple-element.272.gains_ref), channel_id=1, source_target_pairs={{0,1},{1,0},{2,3},{3,2},{4,5},{5,4},{6,7},{7,6},{8,9},{9,8},{10,11... | collective-permute-start | bytes 24584 | tf_op jit(solution)/shard_map/ppermute | solution.py:945
  186.2 6.9 %collective-permute-start.36 = (bf16[128,1024]{1,0:T(8,128)(2,1)S(1)}, bf16[128,1024]{1,0:T(8,128)(2,1)S(1)}, u32[]{:S(2)}, u32[]{:S(2)}) collective-permute-start(bf16[128,1024]{1,0:T(8,128)(2,1)S(1)} %shard_map.238.b_ref), channel_id=1, source_target_pairs={{0,16},{4,20},{8,24},{12,28},{16,0},{20,4},{24,8},{28,12},{1,17},{... | collective-permute-start | bytes 786440 | tf_op jit(solution)/shard_map/ppermute | solution.py:948
  187.5 6.4 %collective-permute-start.30 = (bf16[128,1024]{1,0:T(8,128)(2,1)S(1)}, bf16[128,1024]{1,0:T(8,128)(2,1)S(1)}, u32[]{:S(2)}, u32[]{:S(2)}) collective-permute-start(bf16[128,1024]{1,0:T(8,128)(2,1)S(1)} %shard_map.237.a_ref), channel_id=1, source_target_pairs={{0,8},{4,12},{8,0},{12,4},{16,24},{20,28},{24,16},{28,20},{1,9},{5... | collective-permute-start | bytes 786440 | tf_op jit(solution)/shard_map/ppermute | solution.py:948
  189.7 13.3 %collective-permute-start.37 = (bf16[144,1024]{1,0:T(8,128)(2,1)S(1)}, bf16[144,1024]{1,0:T(8,128)(2,1)S(1)}, u32[]{:S(2)}, u32[]{:S(2)}) collective-permute-start(bf16[144,1024]{1,0:T(8,128)(2,1)S(1)} %get-tuple-element.280), channel_id=1, source_target_pairs={{0,2},{1,3},{2,0},{3,1},{4,6},{5,7},{6,4},{7,5},{8,10},{9,11},{10,... | collective-permute-start | bytes 884744 | tf_op jit(solution)/shard_map/ppermute | solution.py:945
  194.6 9.0 %collective-permute-start.38 = (bf16[2,2,128,1024]{3,2,1,0:T(8,128)(2,1)S(1)}, bf16[2,2,128,1024]{3,2,1,0:T(8,128)(2,1)S(1)}, u32[]{:S(2)}, u32[]{:S(2)}) collective-permute-start(bf16[2,2,128,1024]{3,2,1,0:T(8,128)(2,1)S(1)} %get-tuple-element.285.own_ref), channel_id=1, source_target_pairs={{0,4},{4,0},{8,12},{12,8},{16,20},{20,16},{24,28},{28,24},{1,5},{5... | collective-permute-start | bytes 3145736 | tf_op jit(solution)/shard_map/ppermute | solution.py:948
  194.7 28.9 %collective-permute-start.43 = (bf16[2,128,1024]{2,1,0:T(8,128)(2,1)S(1)}, bf16[2,128,1024]{2,1,0:T(8,128)(2,1)S(1)}, u32[]{:S(2)}, u32[]{:S(2)}) collective-permute-start(bf16[2,128,1024]{2,1,0:T(8,128)(2,1)S(1)} %get-tuple-element.283), channel_id=1, source_target_pairs={{0,16},{4,20},{8,24},{12,28},{16,0},{20,4},{24,8},{28,12},{1,17},{... | collective-permute-start | bytes 1572872 | tf_op jit(solution)/shard_map/ppermute | solution.py:948
  195.5 28.1 %collective-permute-start.44 = (bf16[2,128,1024]{2,1,0:T(8,128)(2,1)S(1)}, bf16[2,128,1024]{2,1,0:T(8,128)(2,1)S(1)}, u32[]{:S(2)}, u32[]{:S(2)}) collective-permute-start(bf16[2,128,1024]{2,1,0:T(8,128)(2,1)S(1)} %get-tuple-element.284), channel_id=1, source_target_pairs={{0,8},{4,12},{8,0},{12,4},{16,24},{20,28},{24,16},{28,20},{1,9},{5... | collective-permute-start | bytes 1572872 | tf_op jit(solution)/shard_map/ppermute | solution.py:948
  203.6 12.9 %collective-permute-start.39 = (bf16[144,1024]{1,0:T(8,128)(2,1)S(1)}, bf16[144,1024]{1,0:T(8,128)(2,1)S(1)}, u32[]{:S(2)}, u32[]{:S(2)}) collective-permute-start(bf16[144,1024]{1,0:T(8,128)(2,1)S(1)} %shard_map.242.a_ref), channel_id=1, source_target_pairs={{0,8},{4,12},{8,0},{12,4},{16,24},{20,28},{24,16},{28,20},{1,9},{5... | collective-permute-start | bytes 884744 | tf_op jit(solution)/shard_map/ppermute | solution.py:948
  204.5 12.1 %collective-permute-start.40 = (bf16[144,1024]{1,0:T(8,128)(2,1)S(1)}, bf16[144,1024]{1,0:T(8,128)(2,1)S(1)}, u32[]{:S(2)}, u32[]{:S(2)}) collective-permute-start(bf16[144,1024]{1,0:T(8,128)(2,1)S(1)} %shard_map.242.a_ref), channel_id=1, source_target_pairs={{0,16},{4,20},{8,24},{12,28},{16,0},{20,4},{24,8},{28,12},{1,17},{... | collective-permute-start | bytes 884744 | tf_op jit(solution)/shard_map/ppermute | solution.py:948
  204.8 18.0 %collective-permute-start.41 = (bf16[144,1024]{1,0:T(8,128)(2,1)S(1)}, bf16[144,1024]{1,0:T(8,128)(2,1)S(1)}, u32[]{:S(2)}, u32[]{:S(2)}) collective-permute-start(bf16[144,1024]{1,0:T(8,128)(2,1)S(1)} %shard_map.242.a_ref), channel_id=1, source_target_pairs={{0,24},{4,28},{8,16},{12,20},{16,8},{20,12},{24,0},{28,4},{1,25},{... | collective-permute-start | bytes 884744 | tf_op jit(solution)/shard_map/ppermute | solution.py:948
  223.4 2.9 %collective-permute-start.42 = (bf16[4,144,1024]{2,1,0:T(8,128)(2,1)S(1)}, bf16[4,144,1024]{2,1,0:T(8,128)(2,1)S(1)}, u32[]{:S(2)}, u32[]{:S(2)}) collective-permute-start(bf16[4,144,1024]{2,1,0:T(8,128)(2,1)S(1)} %shard_map.244.even_ref), channel_id=1, source_target_pairs={{0,4},{4,0},{8,12},{12,8},{16,20},{20,16},{24,28},{28,24},{1,5},{5... | collective-permute-start | bytes 3538952 | tf_op jit(solution)/shard_map/ppermute | solution.py:948
  224.2 5.0 %collective-permute-start.45 = (bf16[2,2,128,1024]{3,2,1,0:T(8,128)(2,1)S(1)}, bf16[2,2,128,1024]{3,2,1,0:T(8,128)(2,1)S(1)}, u32[]{:S(2)}, u32[]{:S(2)}) collective-permute-start(bf16[2,2,128,1024]{3,2,1,0:T(8,128)(2,1)S(1)} %shard_map.245.own_ref), channel_id=1, source_target_pairs={{0,4},{4,0},{8,12},{12,8},{16,20},{20,16},{24,28},{28,24},{1,5},{5... | collective-permute-start | bytes 3145736 | tf_op jit(solution)/shard_map/ppermute | solution.py:948

commit v7 on v6

--- a/solution.py
+++ b/solution.py
@@ -234,6 +234,20 @@
     return (parts[0].astype(f32) + parts[1].astype(f32)) + parts[2].astype(f32)
 
 
+def sums_over_states(parts):
+    parts = [part[:8] + part[8:] for part in parts]
+    rows = lax.broadcasted_iota(jnp.int32, parts[0].shape, 0)
+    distance = 1
+    while len(parts) > 1:
+        first = jnp.bitwise_and(rows, distance) == 0
+        parts = [
+            jnp.where(first, a, b) + pltpu.roll(jnp.where(first, b, a), distance, 0)
+            for a, b in zip(parts[::2], parts[1::2])
+        ]
+        distance *= 2
+    return parts[0]
+
+
 def load_signal(flag_ref, tile_ref, xs):
     channels = xs.shape[1] // 2
     for half in range(2):
@@ -263,9 +277,9 @@
         for k in range(8):
             state = decay * state + x8[k : k + 1]
             if chunk % 2:
-                rows.append(jnp.sum(coef * state, axis=0, keepdims=True))
+                rows.append(coef * state)
         if chunk % 2:
-            y8 = jnp.concatenate(rows, axis=0) + skip * x8
+            y8 = sums_over_states(rows) + skip * x8
             at = aligned(eight * 8, 8)
             if chunk == 1:
                 second_ref[at, :] = y8
@@ -302,9 +316,9 @@
     def step(eight, state):
         rows = []
         for k in range(8):
-            rows.append(jnp.sum(coef * state, axis=0, keepdims=True))
+            rows.append(coef * state)
             state = decay * state
-        acc[aligned(eight * 8, 8), :] = jnp.concatenate(rows, axis=0)
+        acc[aligned(eight * 8, 8), :] = sums_over_states(rows)
         return state
 
     lax.fori_loop(0, 16, step, enter_ref[...] * jnp.exp(-129.0 * rate))
@@ -344,8 +358,8 @@
             adjoint = decay * adjoint
             if chunk % 2:
                 adjoint = adjoint + g8[k : k + 1]
-            rows[k] = jnp.sum(coef * adjoint, axis=0, keepdims=True)
-        y8 = jnp.concatenate(rows, axis=0)
+            rows[k] = coef * adjoint
+        y8 = sums_over_states(rows)
         if chunk % 2:
             y8 = y8 + skip * g8
         rows_out[aligned((chunk * 16 + eight) * 8, 8), :] = y8
@@ -910,6 +924,48 @@
     )(flags, own, other, *filled)
 
 
+def place_last(flag_ref, own_ref, other_ref, *refs, starts, steps):
+    outs, (wide, sems) = refs[2:4], refs[4:]
+    rows = own_ref.shape[2]
+    copies = []
+    for j in range(GROUP // 2):
+        ref = (own_ref, other_ref)[j % 2]
+        for which in range(2):
+            source = jnp.bitwise_xor(
+                flag_ref[PLACE], starts[which] + (j // 2) * steps[which] + j % 2
+            )
+            wide[2 * j + which] = ref[j // 2, which].astype(f32)
+            copy = pltpu.make_async_copy(
+                wide.at[2 * j + which],
+                outs[which].at[aligned(source * rows, rows), :],
+                sems.at[2 * j + which],
+            )
+            copy.start()
+            copies.append(copy)
+    for copy in copies:
+        copy.wait()
+
+
+def run_place_last(flags, own, other, starts, steps, filled):
+    rows, width = own.shape[2:]
+    vmem = pl.BlockSpec(memory_space=pltpu.VMEM)
+    out = shape((GROUP * rows, width))
+    return pl.pallas_call(
+        partial(place_last, starts=starts, steps=steps),
+        in_specs=[pl.BlockSpec(memory_space=pltpu.SMEM), vmem, vmem]
+        + [pl.BlockSpec(memory_space=pl.ANY)] * 2,
+        out_specs=(pl.BlockSpec(memory_space=pl.ANY),) * 2,
+        out_shape=(out, out),
+        input_output_aliases={3: 0, 4: 1},
+        scratch_shapes=[
+            pltpu.VMEM((GROUP, rows, width), f32),
+            pltpu.SemaphoreType.DMA((GROUP,)),
+        ],
+        compiler_params=pltpu.CompilerParams(vmem_limit_bytes=VMEM_LIMIT),
+        cost_estimate=length(0),
+    )(flags, own, other, *filled)
+
+
 class Order:
     def __init__(self):
         self.last = ()
@@ -1272,7 +1328,7 @@
             micros=8,
         )(flags, even, order(odd_part))
     )
-    down_grad, up_grad = run_place_wide(
+    down_grad, up_grad = run_place_last(
         flags, last_pieces, order(last_others), (4, 2), (2, 4), wide_grads
     )
     return (

time: 233 us -> 233 us (level)
    pallas_call x2 -> x1, Pallas kernels: 6.09 us -> 3.04 us  [run_place_wide(): pl.pallas_call(place_wide, grid_spec=pltpu.PrefetchScalarGridSpec(num_sca...]
    pallas_call x0 -> x1, Pallas kernels: none -> 2.65 us  [run_place_last(): pl.pallas_call(partial(place_last, starts=starts, steps=steps), in_specs=...]
  transfers between devices with their start and end apart: 46 -> 46, of which waited for: 25 -> 24; matrix products, arithmetic and copies ran while one was open for 0% -> 0% of each run, Pallas kernels for 32% -> 32%
where the time goes in v7:
time: 233 us
  waiting for transfers between devices  89 us (38%)
  Pallas kernels  84.8 us (36%)
  starting transfers between devices  54.2 us (23%)
  local copies, waits for them, and re-layouts  2.4 us (1%)
    pallas_call x40, Pallas kernels, run(): pl.pallas_call(kernel, out_shape=out_shape, in_specs=[pl.BlockSpec(memory...  62.2 us
    ppermute x15, waiting for transfers between devices, swap_mp(): return lax.ppermute(value, 'mp', [(k, k ^ mask) for k in range(4)])  50.1 us
    ppermute x29, waiting for transfers between devices, swap_dp(): return lax.ppermute(value, 'dp', [(k, k ^ mask) for k in range(dp_size)])  38.5 us
    ppermute x29, starting transfers between devices, swap_dp(): return lax.ppermute(value, 'dp', [(k, k ^ mask) for k in range(dp_size)])  27.1 us
    ppermute x15, starting transfers between devices, swap_mp(): return lax.ppermute(value, 'mp', [(k, k ^ mask) for k in range(4)])  23.1 us
    pallas_call x2, Pallas kernels, run_feed_forward(): pl.pallas_call(feed_forward, grid=(2 * per,), out_shape=(shape((tokens, 2...  13.9 us
  transfers between devices with their start and end apart: 46, of which 24 were waited for; matrix products, arithmetic and copies ran while one was open for 0% of the time, Pallas kernels for 32%

profile of v7, /device:TPU:0, one launch (start us, length us, event | category | flops | bytes accessed | tf_op | source)
XLA Modules:
  0.0 232.5 jit_solution(4566692879751147084)
XLA Ops:
  4.0 3.1 %collective-permute-start = (bf16[256,1024]{1,0:T(8,128)(2,1)S(1)}, bf16[256,1024]{1,0:T(8,128)(2,1)S(1)}, u32[]{:S(2)}, u32[]{:S(2)}) collective-permute-start(bf16[256,1024]{1,0:T(8,128)(2,1)S(1)} %shard_map.203.own_ref), channel_id=1, source_target_pairs={{0,1},{1,0},{2,3},{3,2},{4,5},{5,4},{6,7},{7,6},{8,9},{9,8},{10,11... | collective-permute-start | bytes 1572872 | tf_op jit(solution)/shard_map/ppermute | solution.py:1001
  7.1 2.9 %shard_map.204 = (bf16[176,1024]{1,0:T(8,128)(2,1)}, bf16[128,1024]{1,0:T(8,128)(2,1)}, bf16[128,1024]{1,0:T(8,128)(2,1)}, f32[48,256]{1,0:T(8,128)}) custom-call(s32[6]{0:T(128)} %copy-done.6, bf16[3,1024,256]{2,1,0:T(8,128)(2,1)} %bitcast.60, bf16[256,1024]{1,0:T(8,128)(2,1)} %out_near_ref.3, bf16[1024,1024]{1,0:T(8,128)(2,1)} %up0_ref.3, ...), custom_call_target="tpu_custom_call" | custom-call | tf_op jit(solution)/shard_map/pallas_call | solution.py:120
  10.0 2.7 %collective-permute-start.1 = (bf16[176,1024]{1,0:T(8,128)(2,1)}, bf16[176,1024]{1,0:T(8,128)(2,1)S(1)}, u32[]{:S(2)}, u32[]{:S(2)}) collective-permute-start(bf16[176,1024]{1,0:T(8,128)(2,1)} %get-tuple-element.161), channel_id=1, source_target_pairs={{0,2},{1,3},{2,0},{3,1},{4,6},{5,7},{6,4},{7,5},{8,10},{9,11},{10,... | collective-permute-start | bytes 1081352 | tf_op jit(solution)/shard_map/ppermute | solution.py:1001
  13.0 13.2 %collective-permute-done.1.across_ref = bf16[176,1024]{1,0:T(8,128)(2,1)S(1)} collective-permute-done((bf16[176,1024]{1,0:T(8,128)(2,1)}, bf16[176,1024]{1,0:T(8,128)(2,1)S(1)}, u32[]{:S(2)}, u32[]{:S(2)}) %collective-permute-start.1) | collective-permute-done | bytes 360480 | tf_op jit(solution)/shard_map/ppermute | solution.py:1001
  26.8 2.8 %collective-permute-start.4 = (bf16[256,1024]{1,0:T(8,128)(2,1)S(1)}, bf16[256,1024]{1,0:T(8,128)(2,1)S(1)}, u32[]{:S(2)}, u32[]{:S(2)}) collective-permute-start(bf16[256,1024]{1,0:T(8,128)(2,1)S(1)} %bitcast.47), channel_id=1, source_target_pairs={{0,1},{1,0},{2,3},{3,2},{4,5},{5,4},{6,7},{7,6},{8,9},{9,8},{10,11... | collective-permute-start | bytes 1572872 | tf_op jit(solution)/shard_map/ppermute | solution.py:1001
  29.5 1.6 collective-permute-start.2
  31.7 1.6 collective-permute-start.3
  33.2 2.4 %collective-permute-start.5 = (bf16[128,1024]{1,0:T(8,128)(2,1)S(1)}, bf16[128,1024]{1,0:T(8,128)(2,1)S(1)}, u32[]{:S(2)}, u32[]{:S(2)}) collective-permute-start(bf16[128,1024]{1,0:T(8,128)(2,1)S(1)} %copy-done.14), channel_id=1, source_target_pairs={{0,2},{1,3},{2,0},{3,1},{4,6},{5,7},{6,4},{7,5},{8,10},{9,11},{10,... | collective-permute-start | bytes 786440 | tf_op jit(solution)/shard_map/ppermute | solution.py:1001
  35.7 3.5 %shard_map.206 = (bf16[2,256,1024]{2,1,0:T(8,128)(2,1)S(1)}, bf16[2,256,1024]{2,1,0:T(8,128)(2,1)S(1)}, f32[128,512]{1,0:T(8,128)S(1)}, bf16[176,512]{1,0:T(8,128)(2,1)S(1)}) custom-call(s32[6]{0:T(128)S(1)} %copy-done.7, bf16[256,1024]{1,0:T(8,128)(2,1)S(1)} %shard_map.203.own_ref, bf16[256,1024]{1,0:T(8,128)(2,1)S(1)} %collective-permute-done.other_ref, ...), custom_call_target="tpu_custom_call" | custom-call | tf_op jit(solution)/shard_map/pallas_call | solution.py:46
  39.8 2.4 %collective-permute-start.8 = (bf16[176,512]{1,0:T(8,128)(2,1)S(1)}, bf16[176,512]{1,0:T(8,128)(2,1)S(1)}, u32[]{:S(2)}, u32[]{:S(2)}) collective-permute-start(bf16[176,512]{1,0:T(8,128)(2,1)S(1)} %get-tuple-element.174), channel_id=1, source_target_pairs={{0,2},{1,3},{4,6},{5,7},{8,10},{9,11},{12,14},{13,15},{16,18},{17,... | collective-permute-start | bytes 540680 | tf_op jit(solution)/shard_map/ppermute | solution.py:1069
  42.2 5.2 %collective-permute-done.5.a_ref = bf16[128,1024]{1,0:T(8,128)(2,1)S(1)} collective-permute-done((bf16[128,1024]{1,0:T(8,128)(2,1)S(1)}, bf16[128,1024]{1,0:T(8,128)(2,1)S(1)}, u32[]{:S(2)}, u32[]{:S(2)}) %collective-permute-start.5) | collective-permute-done | bytes 262176 | tf_op jit(solution)/shard_map/ppermute | solution.py:1001
  47.4 1.5 shard_map.207.qkv_ref.near_ref
  49.7 3.5 %collective-permute-start.11 = (bf16[128,1024]{1,0:T(8,128)(2,1)S(1)}, bf16[128,1024]{1,0:T(8,128)(2,1)S(1)}, u32[]{:S(2)}, u32[]{:S(2)}) collective-permute-start(bf16[128,1024]{1,0:T(8,128)(2,1)S(1)} %copy-done.13), channel_id=1, source_target_pairs={{0,2},{1,3},{2,0},{3,1},{4,6},{5,7},{6,4},{7,5},{8,10},{9,11},{10,... | collective-permute-start | bytes 786440 | tf_op jit(solution)/shard_map/ppermute | solution.py:1001
  53.2 1.5 shard_map.209
  54.7 1.9 shard_map.210.near_ref
  56.6 1.7 shard_map.211
  58.3 2.6 %shard_map.212 = (bf16[2,256,256]{2,1,0:T(8,128)(2,1)S(1)}, f32[256,1024]{1,0:T(8,128)S(1)}, bf16[256,1024]{1,0:T(8,128)(2,1)S(1)}) custom-call(s32[6]{0:T(128)S(1)} %copy-done.7, bf16[2,256,768]{2,1,0:T(8,128)(2,1)S(1)} %get-tuple-element.193.qkv_ref.far_ref, bf16[128,512]{1,0:T(8,128)(2,1)S(1)} %get-tuple-element.185.first_ref, ...), custom_call_target="tpu_custom_call" | custom-call | tf_op jit(solution)/shard_map/pallas_call | solution.py:46
  60.9 3.3 %collective-permute-start.9 = (bf16[256,1024]{1,0:T(8,128)(2,1)S(1)}, bf16[256,1024]{1,0:T(8,128)(2,1)S(1)}, u32[]{:S(2)}, u32[]{:S(2)}) collective-permute-start(bf16[256,1024]{1,0:T(8,128)(2,1)S(1)} %get-tuple-element.195), channel_id=1, source_target_pairs={{0,1},{1,0},{2,3},{3,2},{4,5},{5,4},{6,7},{7,6},{8,9},{9,8},{10,11... | collective-permute-start | bytes 1572872 | tf_op jit(solution)/shard_map/ppermute | solution.py:1001
  65.8 1.5 collective-permute-start.12
  67.3 3.2 %collective-permute-done.10.ax_ref = bf16[128,1024]{1,0:T(8,128)(2,1)S(1)} collective-permute-done((bf16[128,1024]{1,0:T(8,128)(2,1)S(1)}, bf16[128,1024]{1,0:T(8,128)(2,1)S(1)}, u32[]{:S(2)}, u32[]{:S(2)}) %collective-permute-start.10) | collective-permute-done | bytes 262176 | tf_op jit(solution)/shard_map/ppermute | solution.py:1004
  70.5 3.2 %collective-permute-done.12.by_ref = bf16[128,1024]{1,0:T(8,128)(2,1)S(1)} collective-permute-done((bf16[128,1024]{1,0:T(8,128)(2,1)S(1)}, bf16[128,1024]{1,0:T(8,128)(2,1)S(1)}, u32[]{:S(2)}, u32[]{:S(2)}) %collective-permute-start.12) | collective-permute-done | bytes 262176 | tf_op jit(solution)/shard_map/ppermute | solution.py:1004
  75.7 1.5 collective-permute-start.14
  78.3 8.9 %collective-permute-done.15.bx_ref = bf16[2,128,1024]{2,1,0:T(8,128)(2,1)S(1)} collective-permute-done((bf16[2,128,1024]{2,1,0:T(8,128)(2,1)S(1)}, bf16[2,128,1024]{2,1,0:T(8,128)(2,1)S(1)}, u32[]{:S(2)}, u32[]{:S(2)}) %collective-permute-start.15) | collective-permute-done | bytes 524320 | tf_op jit(solution)/shard_map/ppermute | solution.py:1004
  89.2 2.7 %collective-permute-done.13.rows_ref.n_ref = bf16[256,1024]{1,0:T(8,128)(2,1)S(1)} collective-permute-done((bf16[256,1024]{1,0:T(8,128)(2,1)S(1)}, bf16[256,1024]{1,0:T(8,128)(2,1)S(1)}, u32[]{:S(2)}, u32[]{:S(2)}) %collective-permute-start.13) | collective-permute-done | bytes 524320 | tf_op jit(solution)/shard_map/ppermute | solution.py:1001
  94.1 6.8 %shard_map.218 = (bf16[256,2048]{1,0:T(8,128)(2,1)S(1)}, bf16[256,2048]{1,0:T(8,128)(2,1)S(1)}, bf16[256,1024]{1,0:T(8,128)(2,1)S(1)}, bf16[256,1024]{1,0:T(8,128)(2,1)S(1)}, bf16[256,1024]{1,0:T(8,128)(2,1)S(1)}) custom-call(s32[6]{0:T(128)S(1)} %copy-done.7, bf16[256,1024]{1,0:T(8,128)(2,1)S(1)} %collective-permute-done.13.rows_ref.n_ref, ...), custom_call_target="tpu_custom_call" | custom-call | tf_op jit(solution)/shard_map/pallas_call | solution.py:626
  101.1 7.1 %shard_map.219 = (bf16[256,2048]{1,0:T(8,128)(2,1)S(1)}, bf16[256,2048]{1,0:T(8,128)(2,1)S(1)}, bf16[256,1024]{1,0:T(8,128)(2,1)S(1)}, f32[256,1024]{1,0:T(8,128)S(1)}, f32[256,1024]{1,0:T(8,128)S(1)}) custom-call(s32[6]{0:T(128)S(1)} %copy-done.7, bf16[256,1024]{1,0:T(8,128)(2,1)S(1)} %get-tuple-element.218.n_ref, bf16[256,1024]{1,0:T(8,128)(2,1)S(1)} %bitcast.49, ...), custom_call_target="tpu_custom_call" | custom-call | tf_op jit(solution)/shard_map/pallas_call | solution.py:626
  108.2 1.8 shard_map.220
  110.2 1.8 shard_map.221
  112.5 2.5 %collective-permute-done.18.received_ref = bf16[256,1024]{1,0:T(8,128)(2,1)S(1)} collective-permute-done((bf16[256,1024]{1,0:T(8,128)(2,1)S(1)}, bf16[256,1024]{1,0:T(8,128)(2,1)S(1)}, u32[]{:S(2)}, u32[]{:S(2)}) %collective-permute-start.18) | collective-permute-done | bytes 524320 | tf_op jit(solution)/shard_map/ppermute | solution.py:1001
  116.9 1.8 shard_map.223
  119.6 1.9 shard_map.224
  121.5 1.6 collective-permute-start.26
  123.1 6.5 %collective-permute-done.20.other_ref = bf16[256,1024]{1,0:T(8,128)(2,1)S(1)} collective-permute-done((bf16[256,1024]{1,0:T(8,128)(2,1)S(1)}, bf16[256,1024]{1,0:T(8,128)(2,1)S(1)}, u32[]{:S(2)}, u32[]{:S(2)}) %collective-permute-start.20) | collective-permute-done | bytes 524320 | tf_op jit(solution)/shard_map/ppermute | solution.py:1001
  129.6 1.4 shard_map.225
  131.0 5.4 %shard_map.226 = (bf16[2,256,1536]{2,1,0:T(8,128)(2,1)S(1)}, f32[128,512]{1,0:T(8,128)S(1)}, bf16[176,512]{1,0:T(8,128)(2,1)S(1)}) custom-call(s32[6]{0:T(128)S(1)} %copy-done.7, bf16[2,256,768]{2,1,0:T(8,128)(2,1)S(1)} %shard_map.207.qkv_ref.near_ref, bf16[2,256,768]{2,1,0:T(8,128)(2,1)S(1)} %get-tuple-element.193.qkv_ref.far_ref, ...), custom_call_target="tpu_custom_call" | custom-call | tf_op jit(solution)/shard_map/pallas_call | solution.py:46
  136.4 1.6 collective-permute-start.25
  138.0 2.4 %shard_map.227.total_ref = f32[2,256,1024]{2,1,0:T(8,128)S(1)} custom-call(s32[6]{0:T(128)S(1)} %copy-done.7, bf16[2,256,1536]{2,1,0:T(8,128)(2,1)S(1)} %get-tuple-element.243.dqkv_ref, bf16[1024,768]{1,0:T(8,128)(2,1)S(1)} %constant_dynamic-update-slice_fusion.weight_ref.near_weight_ref, bf16[1024,768]{1,0:T(8,128)(2,1)S(1)} %get-tuple-element.191.far_weight_ref), custom_call_target="tpu_custom_call" | custom-call | tf_op jit(solution)/shard_map/pallas_call | solution.py:46
  141.2 1.8 shard_map.228
  143.9 1.6 collective-permute-start.22
  146.2 1.4 collective-permute-start.29
  148.0 4.2 %shard_map.231 = (f32[256,1024]{1,0:T(8,128)S(1)}, bf16[256,1024]{1,0:T(8,128)(2,1)S(1)}, f32[128,512]{1,0:T(8,128)S(1)}, f32[16,512]{1,0:T(8,128)S(1)}) custom-call(s32[6]{0:T(128)S(1)} %copy-done.7, f32[128,512]{1,0:T(8,128)S(1)} %get-tuple-element.241.near_ref, bf16[176,512]{1,0:T(8,128)(2,1)S(1)} %collective-permute-done.25.returned_ref, ...), custom_call_target="tpu_custom_call" | custom-call | flops 30000001024 | tf_op jit(solution)/shard_map/pallas_call | solution.py:46
  153.3 4.4 %collective-permute-done.24.c_ref = bf16[256,1024]{1,0:T(8,128)(2,1)S(1)} collective-permute-done((bf16[256,1024]{1,0:T(8,128)(2,1)S(1)}, bf16[256,1024]{1,0:T(8,128)(2,1)S(1)}, u32[]{:S(2)}, u32[]{:S(2)}) %collective-permute-start.24) | collective-permute-done | bytes 524320 | tf_op jit(solution)/shard_map/ppermute | solution.py:1001
  157.7 1.9 shard_map.232
  159.6 1.6 collective-permute-start.31
  163.6 3.0 %collective-permute-start.35 = (bf16[128,1024]{1,0:T(8,128)(2,1)S(1)}, bf16[128,1024]{1,0:T(8,128)(2,1)S(1)}, u32[]{:S(2)}, u32[]{:S(2)}) collective-permute-start(bf16[128,1024]{1,0:T(8,128)(2,1)S(1)} %get-tuple-element.268), channel_id=1, source_target_pairs={{0,2},{1,3},{2,0},{3,1},{4,6},{5,7},{6,4},{7,5},{8,10},{9,11},{10,... | collective-permute-start | bytes 786440 | tf_op jit(solution)/shard_map/ppermute | solution.py:1001
  166.6 5.1 %collective-permute-done.28.received_ref = bf16[256,1024]{1,0:T(8,128)(2,1)S(1)} collective-permute-done((bf16[256,1024]{1,0:T(8,128)(2,1)S(1)}, bf16[256,1024]{1,0:T(8,128)(2,1)S(1)}, u32[]{:S(2)}, u32[]{:S(2)}) %collective-permute-start.28) | collective-permute-done | bytes 524320 | tf_op jit(solution)/shard_map/ppermute | solution.py:1001
  171.7 1.8 collective-permute-start.33
  173.5 4.3 %shard_map.235.param_ref = f32[40,512]{1,0:T(8,128)S(1)} custom-call(s32[6]{0:T(128)S(1)} %copy-done.7, bf16[2,256,1024]{2,1,0:T(8,128)(2,1)S(1)} %get-tuple-element.269.tile_ref, f32[128,512]{1,0:T(8,128)S(1)} %get-tuple-element.241.near_ref, f32[128,512]{1,0:T(8,128)S(1)} %get-tuple-element.255.last_ref, f32[16,512]{1,0:T(8,128)S(1)} %get-tuple-element.187.enter_ref, ...), custom_call_target="tpu_custom_call" | custom-call | flops 3000000000 | tf_op jit(solution)/shard_map/pallas_call | solution.py:46
  177.8 2.4 %shard_map.236 = (f32[256,1024]{1,0:T(8,128)}, f32[8,256]{1,0:T(8,128)S(1)}) custom-call(s32[6]{0:T(128)S(1)} %copy-done.7, bf16[256,1024]{1,0:T(8,128)(2,1)S(1)} %bitcast.55, f32[256,1024]{1,0:T(8,128)S(1)} %get-tuple-element.253.own_ref, bf16[256,1024]{1,0:T(8,128)(2,1)S(1)} %collective-permute-done.28.received_ref, ...), custom_call_target="tpu_custom_call" | custom-call | tf_op jit(solution)/shard_map/pallas_call | solution.py:46
  180.2 2.8 %collective-permute-done.27.b_ref = bf16[128,1024]{1,0:T(8,128)(2,1)S(1)} collective-permute-done((bf16[128,1024]{1,0:T(8,128)(2,1)S(1)}, bf16[128,1024]{1,0:T(8,128)(2,1)S(1)}, u32[]{:S(2)}, u32[]{:S(2)}) %collective-permute-start.27) | collective-permute-done | bytes 262176 | tf_op jit(solution)/shard_map/ppermute | solution.py:1001
  183.6 2.2 collective-permute-done.35.b_ref
  186.4 1.6 collective-permute-start.36
  189.3 3.6 %collective-permute-done.36.by_ref = bf16[128,1024]{1,0:T(8,128)(2,1)S(1)} collective-permute-done((bf16[128,1024]{1,0:T(8,128)(2,1)S(1)}, bf16[128,1024]{1,0:T(8,128)(2,1)S(1)}, u32[]{:S(2)}, u32[]{:S(2)}) %collective-permute-start.36) | collective-permute-done | bytes 262176 | tf_op jit(solution)/shard_map/ppermute | solution.py:1004
  192.9 1.5 collective-permute-done.30.ax_ref
  196.2 1.5 shard_map.241
  197.7 4.2 %collective-permute-done.37.b_ref = bf16[144,1024]{1,0:T(8,128)(2,1)S(1)} collective-permute-done((bf16[144,1024]{1,0:T(8,128)(2,1)S(1)}, bf16[144,1024]{1,0:T(8,128)(2,1)S(1)}, u32[]{:S(2)}, u32[]{:S(2)}) %collective-permute-start.37) | collective-permute-done | bytes 294944 | tf_op jit(solution)/shard_map/ppermute | solution.py:1001
  202.6 1.8 collective-permute-start.39
  204.7 1.4 collective-permute-start.41
  206.1 3.0 %shard_map.243 = (f32[1024,1024]{1,0:T(8,128)}, f32[1024,1024]{1,0:T(8,128)}) custom-call(s32[6]{0:T(128)S(1)} %copy-done.7, bf16[2,2,128,1024]{3,2,1,0:T(8,128)(2,1)S(1)} %get-tuple-element.285.own_ref, bf16[2,2,128,1024]{3,2,1,0:T(8,128)(2,1)S(1)} %collective-permute-done.38.other_ref), custom_call_target="tpu_custom_call" | custom-call | tf_op jit(solution)/shard_map/pallas_call | solution.py:912
  209.2 7.7 %collective-permute-done.39.b_ref = bf16[144,1024]{1,0:T(8,128)(2,1)S(1)} collective-permute-done((bf16[144,1024]{1,0:T(8,128)(2,1)S(1)}, bf16[144,1024]{1,0:T(8,128)(2,1)S(1)}, u32[]{:S(2)}, u32[]{:S(2)}) %collective-permute-start.39) | collective-permute-done | bytes 294944 | tf_op jit(solution)/shard_map/ppermute | solution.py:1004
  216.8 6.5 %collective-permute-done.41.d_ref = bf16[144,1024]{1,0:T(8,128)(2,1)S(1)} collective-permute-done((bf16[144,1024]{1,0:T(8,128)(2,1)S(1)}, bf16[144,1024]{1,0:T(8,128)(2,1)S(1)}, u32[]{:S(2)}, u32[]{:S(2)}) %collective-permute-start.41) | collective-permute-done | bytes 294944 | tf_op jit(solution)/shard_map/ppermute | solution.py:1004
  225.2 1.6 collective-permute-done.42.odd_ref
  226.9 2.8 %shard_map.246 = (f32[3,1024,256]{2,1,0:T(8,128)}, f32[256,1024]{1,0:T(8,128)}, f32[16,256]{1,0:T(8,128)}, f32[16,256]{1,0:T(8,128)}, f32[1,256]{1,0:T(1,128)}, /*index=5*/f32[1,1024]{1,0:T(1,128)}, f32[1,1024]{1,0:T(1,128)}) custom-call(s32[6]{0:T(128)S(1)} %copy-done.7, bf16[4,144,1024]{2,1,0:T(8,128)(2,1)S(1)} %shard_map.244.even_ref, ...), custom_call_target="tpu_custom_call" | custom-call | flops 8000000000 | tf_op jit(solution)/shard_map/pallas_call | solution.py:46
  229.7 2.6 %shard_map.247 = (f32[1024,1024]{1,0:T(8,128)}, f32[1024,1024]{1,0:T(8,128)}) custom-call(s32[6]{0:T(128)S(1)} %copy-done.7, bf16[2,2,128,1024]{3,2,1,0:T(8,128)(2,1)S(1)} %shard_map.245.own_ref, bf16[2,2,128,1024]{3,2,1,0:T(8,128)(2,1)S(1)} %collective-permute-done.45.other_ref, ...), custom_call_target="tpu_custom_call", output_to_operand_aliasing={{0}: (3, {}), {1}: (4, {})} | custom-call | tf_op jit(solution)/shard_map/pallas_call | solution.py:953
  (116 shorter events, 31.1 us)
Async XLA Ops:
  1.4 5.7 %copy-start.6 = (s32[6]{0:T(128)}, s32[6]{0:T(128)S(1)}, u32[]{:S(2)}) copy-start(s32[6]{0:T(128)S(1)} %stack.24.flag_ref) | copy-start | bytes 76
  1.4 1.0 copy-start.4
  2.4 0.7 copy-start.9
  4.0 22.7 %collective-permute-start = (bf16[256,1024]{1,0:T(8,128)(2,1)S(1)}, bf16[256,1024]{1,0:T(8,128)(2,1)S(1)}, u32[]{:S(2)}, u32[]{:S(2)}) collective-permute-start(bf16[256,1024]{1,0:T(8,128)(2,1)S(1)} %shard_map.203.own_ref), channel_id=1, source_target_pairs={{0,1},{1,0},{2,3},{3,2},{4,5},{5,4},{6,7},{7,6},{8,9},{9,8},{10,11... | collective-permute-start | bytes 1572872 | tf_op jit(solution)/shard_map/ppermute | solution.py:1001
  7.1 5.6 %copy-start.12 = (bf16[1024,3,256]{2,0,1:T(8,128)(2,1)S(1)}, bf16[1024,3,256]{2,0,1:T(8,128)(2,1)}, u32[]{:S(2)}) copy-start(bf16[1024,3,256]{2,0,1:T(8,128)(2,1)} %param.15) | copy-start | bytes 4718596
  10.0 16.1 %collective-permute-start.1 = (bf16[176,1024]{1,0:T(8,128)(2,1)}, bf16[176,1024]{1,0:T(8,128)(2,1)S(1)}, u32[]{:S(2)}, u32[]{:S(2)}) collective-permute-start(bf16[176,1024]{1,0:T(8,128)(2,1)} %get-tuple-element.161), channel_id=1, source_target_pairs={{0,2},{1,3},{2,0},{3,1},{4,6},{5,7},{6,4},{7,5},{8,10},{9,11},{10,... | collective-permute-start | bytes 1081352 | tf_op jit(solution)/shard_map/ppermute | solution.py:1001
  12.8 13.9 %copy-start.2 = (bf16[1,256,1024]{2,1,0:T(8,128)(2,1)S(1)}, bf16[1,256,1024]{2,1,0:T(8,128)(2,1)}, u32[]{:S(2)}) copy-start(bf16[1,256,1024]{2,1,0:T(8,128)(2,1)} %param.23) | copy-start | bytes 1572868
  12.8 18.3 %copy-start.7 = (s32[6]{0:T(128)S(1)}, s32[6]{0:T(128)}, u32[]{:S(2)}) copy-start(s32[6]{0:T(128)} %copy-done.6) | copy-start | bytes 76
  12.8 18.3 %copy-start.8 = (f32[48,256]{1,0:T(8,128)S(1)}, f32[48,256]{1,0:T(8,128)}, u32[]{:S(2)}) copy-start(f32[48,256]{1,0:T(8,128)} %get-tuple-element.164.own_ref) | copy-start | bytes 147460
  12.8 20.4 %copy-start.14 = (bf16[128,1024]{1,0:T(8,128)(2,1)S(1)}, bf16[128,1024]{1,0:T(8,128)(2,1)}, u32[]{:S(2)}) copy-start(bf16[128,1024]{1,0:T(8,128)(2,1)} %get-tuple-element.177) | copy-start | bytes 786436
  26.8 20.7 %collective-permute-start.4 = (bf16[256,1024]{1,0:T(8,128)(2,1)S(1)}, bf16[256,1024]{1,0:T(8,128)(2,1)S(1)}, u32[]{:S(2)}, u32[]{:S(2)}) collective-permute-start(bf16[256,1024]{1,0:T(8,128)(2,1)S(1)} %bitcast.47), channel_id=1, source_target_pairs={{0,1},{1,0},{2,3},{3,2},{4,5},{5,4},{6,7},{7,6},{8,9},{9,8},{10,11... | collective-permute-start | bytes 1572872 | tf_op jit(solution)/shard_map/ppermute | solution.py:1001
  29.5 9.6 %collective-permute-start.2 = (bf16[128,1024]{1,0:T(8,128)(2,1)S(1)}, bf16[128,1024]{1,0:T(8,128)(2,1)S(1)}, u32[]{:S(2)}, u32[]{:S(2)}) collective-permute-start(bf16[128,1024]{1,0:T(8,128)(2,1)S(1)} %slice.54.a_ref), channel_id=1, source_target_pairs={{0,8},{4,12},{8,0},{12,4},{16,24},{20,28},{24,16},{28,20},{1,9},{5... | collective-permute-start | bytes 786440 | tf_op jit(solution)/shard_map/ppermute | solution.py:1004
  31.7 15.8 %collective-permute-start.3 = (bf16[128,1024]{1,0:T(8,128)(2,1)S(1)}, bf16[128,1024]{1,0:T(8,128)(2,1)S(1)}, u32[]{:S(2)}, u32[]{:S(2)}) collective-permute-start(bf16[128,1024]{1,0:T(8,128)(2,1)S(1)} %slice.54.a_ref), channel_id=1, source_target_pairs={{0,16},{4,20},{8,24},{12,28},{16,0},{20,4},{24,8},{28,12},{1,17},{... | collective-permute-start | bytes 786440 | tf_op jit(solution)/shard_map/ppermute | solution.py:1004
  33.2 14.2 %collective-permute-start.5 = (bf16[128,1024]{1,0:T(8,128)(2,1)S(1)}, bf16[128,1024]{1,0:T(8,128)(2,1)S(1)}, u32[]{:S(2)}, u32[]{:S(2)}) collective-permute-start(bf16[128,1024]{1,0:T(8,128)(2,1)S(1)} %copy-done.14), channel_id=1, source_target_pairs={{0,2},{1,3},{2,0},{3,1},{4,6},{5,7},{6,4},{7,5},{8,10},{9,11},{10,... | collective-permute-start | bytes 786440 | tf_op jit(solution)/shard_map/ppermute | solution.py:1001
  39.2 10.5 %copy-start.13 = (bf16[128,1024]{1,0:T(8,128)(2,1)S(1)}, bf16[128,1024]{1,0:T(8,128)(2,1)}, u32[]{:S(2)}) copy-start(bf16[128,1024]{1,0:T(8,128)(2,1)} %get-tuple-element.196) | copy-start | bytes 786436
  39.2 9.8 %collective-permute-start.6 = (bf16[128,1024]{1,0:T(8,128)(2,1)S(1)}, bf16[128,1024]{1,0:T(8,128)(2,1)S(1)}, u32[]{:S(2)}, u32[]{:S(2)}) collective-permute-start(bf16[128,1024]{1,0:T(8,128)(2,1)S(1)} %collective-permute-done.2.b_ref), channel_id=1, source_target_pairs={{0,16},{4,20},{8,24},{12,28},{16,0},{20,4},{24,8},{28,12},{1,17},{... | collective-permute-start | bytes 786440 | tf_op jit(solution)/shard_map/ppermute | solution.py:1004
  39.8 9.9 %collective-permute-start.8 = (bf16[176,512]{1,0:T(8,128)(2,1)S(1)}, bf16[176,512]{1,0:T(8,128)(2,1)S(1)}, u32[]{:S(2)}, u32[]{:S(2)}) collective-permute-start(bf16[176,512]{1,0:T(8,128)(2,1)S(1)} %get-tuple-element.174), channel_id=1, source_target_pairs={{0,2},{1,3},{4,6},{5,7},{8,10},{9,11},{12,14},{13,15},{16,18},{17,... | collective-permute-start | bytes 540680 | tf_op jit(solution)/shard_map/ppermute | solution.py:1069
  49.6 7.0 %collective-permute-start.7 = (bf16[4,128,1024]{2,1,0:T(8,128)(2,1)S(1)}, bf16[4,128,1024]{2,1,0:T(8,128)(2,1)S(1)}, u32[]{:S(2)}, u32[]{:S(2)}) collective-permute-start(bf16[4,128,1024]{2,1,0:T(8,128)(2,1)S(1)} %shard_map.208.even_ref), channel_id=1, source_target_pairs={{0,4},{4,0},{8,12},{12,8},{16,20},{20,16},{24,28},{28,24},{1,5},{5... | collective-permute-start | bytes 3145736 | tf_op jit(solution)/shard_map/ppermute | solution.py:1004
  49.7 16.1 %collective-permute-start.11 = (bf16[128,1024]{1,0:T(8,128)(2,1)S(1)}, bf16[128,1024]{1,0:T(8,128)(2,1)S(1)}, u32[]{:S(2)}, u32[]{:S(2)}) collective-permute-start(bf16[128,1024]{1,0:T(8,128)(2,1)S(1)} %copy-done.13), channel_id=1, source_target_pairs={{0,2},{1,3},{2,0},{3,1},{4,6},{5,7},{6,4},{7,5},{8,10},{9,11},{10,... | collective-permute-start | bytes 786440 | tf_op jit(solution)/shard_map/ppermute | solution.py:1001
  54.7 3.6 %copy-start.3 = (bf16[256,1024]{1,0:T(8,128)(2,1)S(1)}, bf16[256,1024]{1,0:T(8,128)(2,1)}, u32[]{:S(2)}) copy-start(bf16[256,1024]{1,0:T(8,128)(2,1)} %out_near_ref.3) | copy-start | bytes 1572868
  58.3 19.0 %copy-start.5 = (bf16[1,256,1024]{2,1,0:T(8,128)(2,1)S(1)}, bf16[1,256,1024]{2,1,0:T(8,128)(2,1)}, u32[]{:S(2)}) copy-start(bf16[1,256,1024]{2,1,0:T(8,128)(2,1)} %param.12) | copy-start | bytes 1572868
  58.3 19.0 %copy-start.11 = (f32[1024]{0:T(1024)S(1)}, f32[1024]{0:T(1024)}, u32[]{:S(2)}) copy-start(f32[1024]{0:T(1024)} %param.20) | copy-start | bytes 12292
  60.9 16.3 %collective-permute-start.9 = (bf16[256,1024]{1,0:T(8,128)(2,1)S(1)}, bf16[256,1024]{1,0:T(8,128)(2,1)S(1)}, u32[]{:S(2)}, u32[]{:S(2)}) collective-permute-start(bf16[256,1024]{1,0:T(8,128)(2,1)S(1)} %get-tuple-element.195), channel_id=1, source_target_pairs={{0,1},{1,0},{2,3},{3,2},{4,5},{5,4},{6,7},{7,6},{8,9},{9,8},{10,11... | collective-permute-start | bytes 1572872 | tf_op jit(solution)/shard_map/ppermute | solution.py:1001
  64.2 6.4 %collective-permute-start.10 = (bf16[128,1024]{1,0:T(8,128)(2,1)S(1)}, bf16[128,1024]{1,0:T(8,128)(2,1)S(1)}, u32[]{:S(2)}, u32[]{:S(2)}) collective-permute-start(bf16[128,1024]{1,0:T(8,128)(2,1)S(1)} %collective-permute-done.5.a_ref), channel_id=1, source_target_pairs={{0,8},{4,12},{8,0},{12,4},{16,24},{20,28},{24,16},{28,20},{1,9},{5... | collective-permute-start | bytes 786440 | tf_op jit(solution)/shard_map/ppermute | solution.py:1004
  65.8 8.0 %collective-permute-start.12 = (bf16[128,1024]{1,0:T(8,128)(2,1)S(1)}, bf16[128,1024]{1,0:T(8,128)(2,1)S(1)}, u32[]{:S(2)}, u32[]{:S(2)}) collective-permute-start(bf16[128,1024]{1,0:T(8,128)(2,1)S(1)} %collective-permute-done.11.b_ref), channel_id=1, source_target_pairs={{0,16},{4,20},{8,24},{12,28},{16,0},{20,4},{24,8},{28,12},{1,17},{... | collective-permute-start | bytes 786440 | tf_op jit(solution)/shard_map/ppermute | solution.py:1004
  74.4 12.8 %collective-permute-start.15 = (bf16[2,128,1024]{2,1,0:T(8,128)(2,1)S(1)}, bf16[2,128,1024]{2,1,0:T(8,128)(2,1)S(1)}, u32[]{:S(2)}, u32[]{:S(2)}) collective-permute-start(bf16[2,128,1024]{2,1,0:T(8,128)(2,1)S(1)} %get-tuple-element.202.b_ref), channel_id=1, source_target_pairs={{0,8},{4,12},{8,0},{12,4},{16,24},{20,28},{24,16},{28,20},{1,9},{5... | collective-permute-start | bytes 1572872 | tf_op jit(solution)/shard_map/ppermute | solution.py:1004
  75.7 12.7 %collective-permute-start.14 = (bf16[2,128,1024]{2,1,0:T(8,128)(2,1)S(1)}, bf16[2,128,1024]{2,1,0:T(8,128)(2,1)S(1)}, u32[]{:S(2)}, u32[]{:S(2)}) collective-permute-start(bf16[2,128,1024]{2,1,0:T(8,128)(2,1)S(1)} %get-tuple-element.201.a_ref), channel_id=1, source_target_pairs={{0,16},{4,20},{8,24},{12,28},{16,0},{20,4},{24,8},{28,12},{1,17},{... | collective-permute-start | bytes 1572872 | tf_op jit(solution)/shard_map/ppermute | solution.py:1004
  78.2 13.6 %collective-permute-start.13 = (bf16[256,1024]{1,0:T(8,128)(2,1)S(1)}, bf16[256,1024]{1,0:T(8,128)(2,1)S(1)}, u32[]{:S(2)}, u32[]{:S(2)}) collective-permute-start(bf16[256,1024]{1,0:T(8,128)(2,1)S(1)} %get-tuple-element.218.n_ref), channel_id=1, source_target_pairs={{0,1},{1,0},{2,3},{3,2},{4,5},{5,4},{6,7},{7,6},{8,9},{9,8},{10,11... | collective-permute-start | bytes 1572872 | tf_op jit(solution)/shard_map/ppermute | solution.py:1001
  87.2 4.7 %copy-start = (bf16[1024,1024]{1,0:T(8,128)(2,1)S(1)}, bf16[1024,1024]{1,0:T(8,128)(2,1)}, u32[]{:S(2)}) copy-start(bf16[1024,1024]{1,0:T(8,128)(2,1)} %up0_ref.3) | copy-start | bytes 6291460
  87.2 4.7 %copy-start.1 = (bf16[1024,1024]{1,0:T(8,128)(2,1)S(1)}, bf16[1024,1024]{1,0:T(8,128)(2,1)}, u32[]{:S(2)}) copy-start(bf16[1024,1024]{1,0:T(8,128)(2,1)} %down0_ref.3) | copy-start | bytes 6291460
  89.1 4.2 %collective-permute-start.16 = (bf16[4,2,128,1024]{3,2,1,0:T(8,128)(2,1)S(1)}, bf16[4,2,128,1024]{3,2,1,0:T(8,128)(2,1)S(1)}, u32[]{:S(2)}, u32[]{:S(2)}) collective-permute-start(bf16[4,2,128,1024]{3,2,1,0:T(8,128)(2,1)S(1)} %shard_map.215.even_ref), channel_id=1, source_target_pairs={{0,4},{4,0},{8,12},{12,8},{16,20},{20,16},{24,28},{28,24},{1,5},{5... | collective-permute-start | bytes 6291464 | tf_op jit(solution)/shard_map/ppermute | solution.py:1004
  101.0 14.0 %collective-permute-start.18 = (bf16[256,1024]{1,0:T(8,128)(2,1)S(1)}, bf16[256,1024]{1,0:T(8,128)(2,1)S(1)}, u32[]{:S(2)}, u32[]{:S(2)}) collective-permute-start(bf16[256,1024]{1,0:T(8,128)(2,1)S(1)} %get-tuple-element.217), channel_id=1, source_target_pairs={{0,1},{1,0},{2,3},{3,2},{4,5},{5,4},{6,7},{7,6},{8,9},{9,8},{10,11... | collective-permute-start | bytes 1572872 | tf_op jit(solution)/shard_map/ppermute | solution.py:1001
  110.0 6.9 %collective-permute-start.17 = (bf16[1024,1024]{1,0:T(8,128)(2,1)S(1)}, bf16[1024,1024]{1,0:T(8,128)(2,1)S(1)}, u32[]{:S(2)}, u32[]{:S(2)}) collective-permute-start(bf16[1024,1024]{1,0:T(8,128)(2,1)S(1)} %shard_map.220), channel_id=1, source_target_pairs={{0,4},{4,0},{8,12},{12,8},{16,20},{20,16},{24,28},{28,24},{1,5},{5... | collective-permute-start | bytes 6291464 | tf_op jit(solution)/shard_map/ppermute | solution.py:1004
  112.0 7.6 %collective-permute-start.21 = (bf16[512,2048]{1,0:T(8,128)(2,1)S(1)}, bf16[512,2048]{1,0:T(8,128)(2,1)S(1)}, u32[]{:S(2)}, u32[]{:S(2)}) collective-permute-start(bf16[512,2048]{1,0:T(8,128)(2,1)S(1)} %shard_map.221), channel_id=1, source_target_pairs={{0,4},{4,0},{8,12},{12,8},{16,20},{20,16},{24,28},{28,24},{1,5},{5... | collective-permute-start | bytes 6291464 | tf_op jit(solution)/shard_map/ppermute | solution.py:1004
  116.4 13.2 %collective-permute-start.20 = (bf16[256,1024]{1,0:T(8,128)(2,1)S(1)}, bf16[256,1024]{1,0:T(8,128)(2,1)S(1)}, u32[]{:S(2)}, u32[]{:S(2)}) collective-permute-start(bf16[256,1024]{1,0:T(8,128)(2,1)S(1)} %get-tuple-element.228.own_ref), channel_id=1, source_target_pairs={{0,1},{1,0},{2,3},{3,2},{4,5},{5,4},{6,7},{7,6},{8,9},{9,8},{10,11... | collective-permute-start | bytes 1572872 | tf_op jit(solution)/shard_map/ppermute | solution.py:1001
  118.7 24.5 %collective-permute-start.19 = (bf16[512,1024]{1,0:T(8,128)(2,1)S(1)}, bf16[512,1024]{1,0:T(8,128)(2,1)S(1)}, u32[]{:S(2)}, u32[]{:S(2)}) collective-permute-start(bf16[512,1024]{1,0:T(8,128)(2,1)S(1)} %get-tuple-element.232), channel_id=1, source_target_pairs={{0,8},{4,12},{8,0},{12,4},{16,24},{20,28},{24,16},{28,20},{1,9},{5... | collective-permute-start | bytes 3145736 | tf_op jit(solution)/shard_map/ppermute | solution.py:1004
  121.5 24.0 %collective-permute-start.26 = (bf16[256,2048]{1,0:T(8,128)(2,1)S(1)}, bf16[256,2048]{1,0:T(8,128)(2,1)S(1)}, u32[]{:S(2)}, u32[]{:S(2)}) collective-permute-start(bf16[256,2048]{1,0:T(8,128)(2,1)S(1)} %get-tuple-element.234), channel_id=1, source_target_pairs={{0,16},{4,20},{8,24},{12,28},{16,0},{20,4},{24,8},{28,12},{1,17},{... | collective-permute-start | bytes 3145736 | tf_op jit(solution)/shard_map/ppermute | solution.py:1004
  136.4 11.6 %collective-permute-start.25 = (bf16[176,512]{1,0:T(8,128)(2,1)S(1)}, bf16[176,512]{1,0:T(8,128)(2,1)S(1)}, u32[]{:S(2)}, u32[]{:S(2)}) collective-permute-start(bf16[176,512]{1,0:T(8,128)(2,1)S(1)} %get-tuple-element.242), channel_id=1, source_target_pairs={{2,0},{3,1},{6,4},{7,5},{10,8},{11,9},{14,12},{15,13},{18,16},{19,... | collective-permute-start | bytes 540680 | tf_op jit(solution)/shard_map/ppermute | solution.py:1202
  140.3 17.4 %collective-permute-start.24 = (bf16[256,1024]{1,0:T(8,128)(2,1)S(1)}, bf16[256,1024]{1,0:T(8,128)(2,1)S(1)}, u32[]{:S(2)}, u32[]{:S(2)}) collective-permute-start(bf16[256,1024]{1,0:T(8,128)(2,1)S(1)} %get-tuple-element.248), channel_id=1, source_target_pairs={{0,1},{1,0},{2,3},{3,2},{4,5},{5,4},{6,7},{7,6},{8,9},{9,8},{10,11... | collective-permute-start | bytes 1572872 | tf_op jit(solution)/shard_map/ppermute | solution.py:1001
  143.0 14.7 %collective-permute-start.23 = (bf16[512,2048]{1,0:T(8,128)(2,1)S(1)}, bf16[512,2048]{1,0:T(8,128)(2,1)S(1)}, u32[]{:S(2)}, u32[]{:S(2)}) collective-permute-start(bf16[512,2048]{1,0:T(8,128)(2,1)S(1)} %shard_map.228), channel_id=1, source_target_pairs={{0,4},{4,0},{8,12},{12,8},{16,20},{20,16},{24,28},{28,24},{1,5},{5... | collective-permute-start | bytes 6291464 | tf_op jit(solution)/shard_map/ppermute | solution.py:1004
  143.9 18.4 %collective-permute-start.22 = (bf16[256,1024]{1,0:T(8,128)(2,1)S(1)}, bf16[256,1024]{1,0:T(8,128)(2,1)S(1)}, u32[]{:S(2)}, u32[]{:S(2)}) collective-permute-start(bf16[256,1024]{1,0:T(8,128)(2,1)S(1)} %get-tuple-element.247), channel_id=1, source_target_pairs={{0,16},{4,20},{8,24},{12,28},{16,0},{20,4},{24,8},{28,12},{1,17},{... | collective-permute-start | bytes 1572872 | tf_op jit(solution)/shard_map/ppermute | solution.py:1004
  146.2 16.8 %collective-permute-start.29 = (bf16[128,2048]{1,0:T(8,128)(2,1)S(1)}, bf16[128,2048]{1,0:T(8,128)(2,1)S(1)}, u32[]{:S(2)}, u32[]{:S(2)}) collective-permute-start(bf16[128,2048]{1,0:T(8,128)(2,1)S(1)} %get-tuple-element.251), channel_id=1, source_target_pairs={{0,8},{4,12},{8,0},{12,4},{16,24},{20,28},{24,16},{28,20},{1,9},{5... | collective-permute-start | bytes 1572872 | tf_op jit(solution)/shard_map/ppermute | solution.py:1004
  152.1 19.6 %collective-permute-start.28 = (bf16[256,1024]{1,0:T(8,128)(2,1)S(1)}, bf16[256,1024]{1,0:T(8,128)(2,1)S(1)}, u32[]{:S(2)}, u32[]{:S(2)}) collective-permute-start(bf16[256,1024]{1,0:T(8,128)(2,1)S(1)} %get-tuple-element.254), channel_id=1, source_target_pairs={{0,1},{1,0},{2,3},{3,2},{4,5},{5,4},{6,7},{7,6},{8,9},{9,8},{10,11... | collective-permute-start | bytes 1572872 | tf_op jit(solution)/shard_map/ppermute | solution.py:1001
  159.6 28.8 %collective-permute-start.31 = (bf16[128,2048]{1,0:T(8,128)(2,1)S(1)}, bf16[128,2048]{1,0:T(8,128)(2,1)S(1)}, u32[]{:S(2)}, u32[]{:S(2)}) collective-permute-start(bf16[128,2048]{1,0:T(8,128)(2,1)S(1)} %get-tuple-element.260), channel_id=1, source_target_pairs={{0,16},{4,20},{8,24},{12,28},{16,0},{20,4},{24,8},{28,12},{1,17},{... | collective-permute-start | bytes 1572872 | tf_op jit(solution)/shard_map/ppermute | solution.py:1004
  161.2 27.2 %collective-permute-start.32 = (bf16[128,2048]{1,0:T(8,128)(2,1)S(1)}, bf16[128,2048]{1,0:T(8,128)(2,1)S(1)}, u32[]{:S(2)}, u32[]{:S(2)}) collective-permute-start(bf16[128,2048]{1,0:T(8,128)(2,1)S(1)} %get-tuple-element.261), channel_id=1, source_target_pairs={{0,8},{4,12},{8,0},{12,4},{16,24},{20,28},{24,16},{28,20},{1,9},{5... | collective-permute-start | bytes 1572872 | tf_op jit(solution)/shard_map/ppermute | solution.py:1004
  162.9 20.1 %collective-permute-start.27 = (bf16[128,1024]{1,0:T(8,128)(2,1)S(1)}, bf16[128,1024]{1,0:T(8,128)(2,1)S(1)}, u32[]{:S(2)}, u32[]{:S(2)}) collective-permute-start(bf16[128,1024]{1,0:T(8,128)(2,1)S(1)} %get-tuple-element.265), channel_id=1, source_target_pairs={{0,2},{1,3},{2,0},{3,1},{4,6},{5,7},{6,4},{7,5},{8,10},{9,11},{10,... | collective-permute-start | bytes 786440 | tf_op jit(solution)/shard_map/ppermute | solution.py:1001
  163.6 22.2 %collective-permute-start.35 = (bf16[128,1024]{1,0:T(8,128)(2,1)S(1)}, bf16[128,1024]{1,0:T(8,128)(2,1)S(1)}, u32[]{:S(2)}, u32[]{:S(2)}) collective-permute-start(bf16[128,1024]{1,0:T(8,128)(2,1)S(1)} %get-tuple-element.268), channel_id=1, source_target_pairs={{0,2},{1,3},{2,0},{3,1},{4,6},{5,7},{6,4},{7,5},{8,10},{9,11},{10,... | collective-permute-start | bytes 786440 | tf_op jit(solution)/shard_map/ppermute | solution.py:1001
  166.6 11.2 %copy-start.10 = (f32[1024]{0:T(1024)S(1)}, f32[1024]{0:T(1024)}, u32[]{:S(2)}) copy-start(f32[1024]{0:T(1024)} %param.14) | copy-start | bytes 12292
  171.7 16.7 %collective-permute-start.33 = (bf16[128,2048]{1,0:T(8,128)(2,1)S(1)}, bf16[128,2048]{1,0:T(8,128)(2,1)S(1)}, u32[]{:S(2)}, u32[]{:S(2)}) collective-permute-start(bf16[128,2048]{1,0:T(8,128)(2,1)S(1)} %get-tuple-element.262), channel_id=1, source_target_pairs={{0,24},{4,28},{8,16},{12,20},{16,8},{20,12},{24,0},{28,4},{1,25},{... | collective-permute-start | bytes 1572872 | tf_op jit(solution)/shard_map/ppermute | solution.py:1004
  183.0 5.0 %collective-permute-start.34 = (f32[8,256]{1,0:T(8,128)S(1)}, f32[8,256]{1,0:T(8,128)S(1)}, u32[]{:S(2)}, u32[]{:S(2)}) collective-permute-start(f32[8,256]{1,0:T(8,128)S(1)} %get-tuple-element.272.gains_ref), channel_id=1, source_target_pairs={{0,1},{1,0},{2,3},{3,2},{4,5},{5,4},{6,7},{7,6},{8,9},{9,8},{10,11... | collective-permute-start | bytes 24584 | tf_op jit(solution)/shard_map/ppermute | solution.py:1001
  186.4 6.4 %collective-permute-start.36 = (bf16[128,1024]{1,0:T(8,128)(2,1)S(1)}, bf16[128,1024]{1,0:T(8,128)(2,1)S(1)}, u32[]{:S(2)}, u32[]{:S(2)}) collective-permute-start(bf16[128,1024]{1,0:T(8,128)(2,1)S(1)} %shard_map.238.b_ref), channel_id=1, source_target_pairs={{0,16},{4,20},{8,24},{12,28},{16,0},{20,4},{24,8},{28,12},{1,17},{... | collective-permute-start | bytes 786440 | tf_op jit(solution)/shard_map/ppermute | solution.py:1004
  188.0 6.4 %collective-permute-start.30 = (bf16[128,1024]{1,0:T(8,128)(2,1)S(1)}, bf16[128,1024]{1,0:T(8,128)(2,1)S(1)}, u32[]{:S(2)}, u32[]{:S(2)}) collective-permute-start(bf16[128,1024]{1,0:T(8,128)(2,1)S(1)} %shard_map.237.a_ref), channel_id=1, source_target_pairs={{0,8},{4,12},{8,0},{12,4},{16,24},{20,28},{24,16},{28,20},{1,9},{5... | collective-permute-start | bytes 786440 | tf_op jit(solution)/shard_map/ppermute | solution.py:1004
  189.2 12.7 %collective-permute-start.37 = (bf16[144,1024]{1,0:T(8,128)(2,1)S(1)}, bf16[144,1024]{1,0:T(8,128)(2,1)S(1)}, u32[]{:S(2)}, u32[]{:S(2)}) collective-permute-start(bf16[144,1024]{1,0:T(8,128)(2,1)S(1)} %get-tuple-element.280), channel_id=1, source_target_pairs={{0,2},{1,3},{2,0},{3,1},{4,6},{5,7},{6,4},{7,5},{8,10},{9,11},{10,... | collective-permute-start | bytes 884744 | tf_op jit(solution)/shard_map/ppermute | solution.py:1001
  195.1 7.5 %collective-permute-start.38 = (bf16[2,2,128,1024]{3,2,1,0:T(8,128)(2,1)S(1)}, bf16[2,2,128,1024]{3,2,1,0:T(8,128)(2,1)S(1)}, u32[]{:S(2)}, u32[]{:S(2)}) collective-permute-start(bf16[2,2,128,1024]{3,2,1,0:T(8,128)(2,1)S(1)} %get-tuple-element.285.own_ref), channel_id=1, source_target_pairs={{0,4},{4,0},{8,12},{12,8},{16,20},{20,16},{24,28},{28,24},{1,5},{5... | collective-permute-start | bytes 3145736 | tf_op jit(solution)/shard_map/ppermute | solution.py:1004
  195.2 28.9 %collective-permute-start.43 = (bf16[2,128,1024]{2,1,0:T(8,128)(2,1)S(1)}, bf16[2,128,1024]{2,1,0:T(8,128)(2,1)S(1)}, u32[]{:S(2)}, u32[]{:S(2)}) collective-permute-start(bf16[2,128,1024]{2,1,0:T(8,128)(2,1)S(1)} %get-tuple-element.283), channel_id=1, source_target_pairs={{0,16},{4,20},{8,24},{12,28},{16,0},{20,4},{24,8},{28,12},{1,17},{... | collective-permute-start | bytes 1572872 | tf_op jit(solution)/shard_map/ppermute | solution.py:1004
  195.7 28.3 %collective-permute-start.44 = (bf16[2,128,1024]{2,1,0:T(8,128)(2,1)S(1)}, bf16[2,128,1024]{2,1,0:T(8,128)(2,1)S(1)}, u32[]{:S(2)}, u32[]{:S(2)}) collective-permute-start(bf16[2,128,1024]{2,1,0:T(8,128)(2,1)S(1)} %get-tuple-element.284), channel_id=1, source_target_pairs={{0,8},{4,12},{8,0},{12,4},{16,24},{20,28},{24,16},{28,20},{1,9},{5... | collective-permute-start | bytes 1572872 | tf_op jit(solution)/shard_map/ppermute | solution.py:1004
  202.6 14.3 %collective-permute-start.39 = (bf16[144,1024]{1,0:T(8,128)(2,1)S(1)}, bf16[144,1024]{1,0:T(8,128)(2,1)S(1)}, u32[]{:S(2)}, u32[]{:S(2)}) collective-permute-start(bf16[144,1024]{1,0:T(8,128)(2,1)S(1)} %shard_map.242.a_ref), channel_id=1, source_target_pairs={{0,8},{4,12},{8,0},{12,4},{16,24},{20,28},{24,16},{28,20},{1,9},{5... | collective-permute-start | bytes 884744 | tf_op jit(solution)/shard_map/ppermute | solution.py:1004
  204.4 12.5 %collective-permute-start.40 = (bf16[144,1024]{1,0:T(8,128)(2,1)S(1)}, bf16[144,1024]{1,0:T(8,128)(2,1)S(1)}, u32[]{:S(2)}, u32[]{:S(2)}) collective-permute-start(bf16[144,1024]{1,0:T(8,128)(2,1)S(1)} %shard_map.242.a_ref), channel_id=1, source_target_pairs={{0,16},{4,20},{8,24},{12,28},{16,0},{20,4},{24,8},{28,12},{1,17},{... | collective-permute-start | bytes 884744 | tf_op jit(solution)/shard_map/ppermute | solution.py:1004
  204.7 18.6 %collective-permute-start.41 = (bf16[144,1024]{1,0:T(8,128)(2,1)S(1)}, bf16[144,1024]{1,0:T(8,128)(2,1)S(1)}, u32[]{:S(2)}, u32[]{:S(2)}) collective-permute-start(bf16[144,1024]{1,0:T(8,128)(2,1)S(1)} %shard_map.242.a_ref), channel_id=1, source_target_pairs={{0,24},{4,28},{8,16},{12,20},{16,8},{20,12},{24,0},{28,4},{1,25},{... | collective-permute-start | bytes 884744 | tf_op jit(solution)/shard_map/ppermute | solution.py:1004
  224.0 2.9 %collective-permute-start.42 = (bf16[4,144,1024]{2,1,0:T(8,128)(2,1)S(1)}, bf16[4,144,1024]{2,1,0:T(8,128)(2,1)S(1)}, u32[]{:S(2)}, u32[]{:S(2)}) collective-permute-start(bf16[4,144,1024]{2,1,0:T(8,128)(2,1)S(1)} %shard_map.244.even_ref), channel_id=1, source_target_pairs={{0,4},{4,0},{8,12},{12,8},{16,20},{20,16},{24,28},{28,24},{1,5},{5... | collective-permute-start | bytes 3538952 | tf_op jit(solution)/shard_map/ppermute | solution.py:1004
  224.7 5.0 %collective-permute-start.45 = (bf16[2,2,128,1024]{3,2,1,0:T(8,128)(2,1)S(1)}, bf16[2,2,128,1024]{3,2,1,0:T(8,128)(2,1)S(1)}, u32[]{:S(2)}, u32[]{:S(2)}) collective-permute-start(bf16[2,2,128,1024]{3,2,1,0:T(8,128)(2,1)S(1)} %shard_map.245.own_ref), channel_id=1, source_target_pairs={{0,4},{4,0},{8,12},{12,8},{16,20},{20,16},{24,28},{28,24},{1,5},{5... | collective-permute-start | bytes 3145736 | tf_op jit(solution)/shard_map/ppermute | solution.py:1004
